TPU v7x, 32 devices: a whole 2x2x4 slice. The times are simulated.
32 devices in a mesh: recon: 2 (over y), blk: 4 (over z), probe: 4 (over x, core).
Axes of the slice: x: 2, y: 2, z: 4, core: 2. Of those that a mesh axis runs over, the one named last changes fastest.
Arguments:
- tiles: bfloat16 [8, 2, 512, 512], P(('recon', 'blk')), parts along dimension 0, may hold values from -5 to 5
- eigenprobes: bfloat16 [12, 2, 256, 256], P('recon'), parts along dimension 0, may hold values from -6 to 6
- coefficients: float32 [320, 6], P(('recon', 'blk', 'probe')), parts along dimension 0, may hold values from -2.4 to 2.4
- tile_list: int32 [320, 2], P(('recon', 'blk', 'probe')), parts along dimension 0, may hold values from 0 to 3, as said below
- offsets: int32 [320, 4], P(('recon', 'blk', 'probe')), parts along dimension 0, may hold values from 0 to 256
- amplitudes: bfloat16 [320, 256, 256], P(('recon', 'blk', 'probe')), parts along dimension 0, may hold values from 0 to 2
- group_counts: int32 [8], P(('recon', 'blk')), parts along dimension 0, may hold values from 10 to 40, as said below
Outputs:
- object_grad: float32 [8, 2, 512, 512], P(('recon', 'blk'), None, 'probe'), parts along dimension 0
- eigen_grad: float32 [12, 2, 256, 256], P('recon', None, 'probe'), parts along dimension 0
- coef_grad: float32 [320, 6], P(('recon', 'blk', 'probe')), parts along dimension 0
There are 2 independent parts, one for each index of `recon`. A program takes and returns all parts, laid end to end along the dimension named above; each array names one. Nothing has to cross between parts.
Inputs may be any that keep to these rules, and one draw needn't show every extreme that they name: `tile_list`: A position of group g lists two different tiles among (g + r) mod 4 for r from 0 to 2. `group_counts`: some group is full in every draw.
All inputs are finite; a program needn't handle non-finite values.
Results may differ from a plain program's by a relative error of at most 0.0034.
Values may be sent and summed in bfloat16 or wider, within the bound.
No kernel may reach another device: no remote copies, remote signals or barrier semaphores. Data moves between devices by JAX's collectives and lax.ppermute only.
A program may use at most 64 MiB of HBM per device.

v0:
```python
import math

import jax
import jax.numpy as jnp
from jax import lax
from jax.sharding import PartitionSpec as P

REACH = 3


def from_behind(array, axis, by):
    peers = lax.axis_size(axis)
    return lax.ppermute(array, axis, [(i, (i + by) % peers) for i in range(peers)])


def tables(frame):
    indices = jnp.arange(frame, dtype=jnp.int32)
    product = indices[:, None] * indices[None, :] % frame
    angle = product.astype(jnp.float32) * (2.0 * math.pi / frame)
    cos_part = jnp.cos(angle) / math.sqrt(frame)
    sin_part = -jnp.sin(angle) / math.sqrt(frame)
    forward = jnp.concatenate(
        [jnp.concatenate([cos_part, sin_part], 1), jnp.concatenate([-sin_part, cos_part], 1)], 0
    )
    backward = jnp.concatenate(
        [jnp.concatenate([cos_part, -sin_part], 1), jnp.concatenate([sin_part, cos_part], 1)], 0
    )
    return (forward.astype(jnp.bfloat16), backward.astype(jnp.bfloat16))


def transform(in_real, in_imag, dft_table):
    width_n = in_real.shape[0]
    section_one = jnp.dot(
        jnp.concatenate([in_real, in_imag], 1), dft_table, preferred_element_type=jnp.float32
    ).astype(jnp.bfloat16)
    joined = jnp.concatenate([section_one[:, :width_n].T, section_one[:, width_n:].T], 1)
    second = jnp.dot(joined, dft_table, preferred_element_type=jnp.float32)
    return (second[:, :width_n].T, second[:, width_n:].T)


def position_terms(obj_re, obj_im, probe_re, probe_im, measured, living, forward, backward):
    exit_re = (probe_re * obj_re - probe_im * obj_im).astype(jnp.bfloat16)
    exit_im = (probe_re * obj_im + probe_im * obj_re).astype(jnp.bfloat16)
    far_re, far_im = transform(exit_re, exit_im, forward)
    modulus = jnp.sqrt(far_re * far_re + far_im * far_im + 1.0)
    factor = (1.0 - measured / modulus) * living
    back_re, back_im = transform(
        (far_re * factor).astype(jnp.bfloat16), (far_im * factor).astype(jnp.bfloat16), backward
    )
    grad_obj = jnp.stack(
        [probe_re * back_re + probe_im * back_im, probe_re * back_im - probe_im * back_re]
    )
    grad_probe = jnp.stack(
        [obj_re * back_re + obj_im * back_im, obj_re * back_im - obj_im * back_re]
    )
    return (grad_obj, grad_probe)


def take_block(source, which, row_at, col_at, frame):
    start_at = (jnp.asarray(which), jnp.int32(0), jnp.asarray(row_at), jnp.asarray(col_at))
    return lax.dynamic_slice(source, start_at, (1, 2, frame, frame))[0].astype(jnp.float32)


def add_block(target, which, row_at, col_at, piece):
    frame = piece.shape[1]
    start_at = (jnp.asarray(which), jnp.int32(0), jnp.asarray(row_at), jnp.asarray(col_at))
    present = lax.dynamic_slice(target, start_at, (1, 2, frame, frame))
    return lax.dynamic_update_slice(target, present + piece[None], start_at)


def on_device(tiles, eigenprobes, coefficients, tile_list, offsets, amplitudes, group_counts):
    frame = eigenprobes.shape[2]
    tile_side = tiles.shape[2]
    pos_dev = coefficients.shape[0]
    blocks = lax.axis_size("blk")
    shares = lax.axis_size("probe")
    my_block = lax.axis_index("blk")
    member = lax.axis_index("probe")
    own_tile = tiles[0]
    fetched = [own_tile]
    current = own_tile
    for section in range(1, REACH):
        current = from_behind(current, "blk", -1)
        fetched.append(current)
    visiting = jnp.stack(fetched)
    forward, backward = tables(frame)
    probes_wide = eigenprobes.astype(jnp.float32)
    alive_count = jnp.clip(group_counts[0] - member * pos_dev, 0, pos_dev)

    def visit(position, carried):
        grad_tiles, eigen_acc, coef_rows = carried
        position = jnp.asarray(position).astype(jnp.int32)
        tile_ids = tile_list[position]
        corner = offsets[position]
        reach_ids = (tile_ids - my_block) % blocks
        obj_patch = 0.5 * (
            take_block(visiting, reach_ids[0], corner[0], corner[1], frame)
            + take_block(visiting, reach_ids[1], corner[2], corner[3], frame)
        )
        weights = coefficients[position]
        probe_now = jnp.einsum("k,kcxy->cxy", weights, probes_wide, precision=lax.Precision.HIGHEST)
        grad_obj, grad_probe = position_terms(
            obj_patch[0],
            obj_patch[1],
            probe_now[0],
            probe_now[1],
            amplitudes[position].astype(jnp.float32),
            1.0,
            forward,
            backward,
        )
        grad_tiles = add_block(grad_tiles, reach_ids[0], corner[0], corner[1], 0.5 * grad_obj)
        grad_tiles = add_block(grad_tiles, reach_ids[1], corner[2], corner[3], 0.5 * grad_obj)
        eigen_acc = eigen_acc + weights[:, None, None, None] * grad_probe[None]
        coef_row = (
            jnp.einsum("kcxy,cxy->k", probes_wide, grad_probe, precision=lax.Precision.HIGHEST)
            / frame
        )
        coef_rows = lax.dynamic_update_slice(coef_rows, coef_row[None], (position, jnp.int32(0)))
        return (grad_tiles, eigen_acc, coef_rows)

    start = (
        jnp.zeros((REACH, 2, tile_side, tile_side), jnp.float32),
        jnp.zeros(eigenprobes.shape, jnp.float32),
        jnp.zeros(coefficients.shape, jnp.float32),
    )
    grad_tiles, eigen_acc, coef_rows = lax.fori_loop(jnp.int32(0), alive_count, visit, start)
    returned = grad_tiles[REACH - 1]
    for section in range(REACH - 2, -1, -1):
        returned = from_behind(returned, "blk", 1) + grad_tiles[section]
    summed = lax.psum_scatter(returned, "probe", scatter_dimension=1, tiled=True)
    scale = (pos_dev * blocks * shares) ** (-0.5)
    slab_rows = frame // shares
    eigen_all = lax.psum(eigen_acc, ("blk", "probe")) * scale
    eigen_share = lax.dynamic_slice_in_dim(eigen_all, member * slab_rows, slab_rows, 2)
    return (summed[None], eigen_share, coef_rows)


def solution(mesh):
    in_specs = (
        P(("recon", "blk"), None, None, None),
        P("recon", None, None, None),
        P(("recon", "blk", "probe"), None),
        P(("recon", "blk", "probe"), None),
        P(("recon", "blk", "probe"), None),
        P(("recon", "blk", "probe"), None, None),
        P(("recon", "blk")),
    )
    out_specs = (
        P(("recon", "blk"), None, "probe", None),
        P("recon", None, "probe", None),
        P(("recon", "blk", "probe"), None),
    )
    return jax.shard_map(
        on_device, mesh=mesh, in_specs=in_specs, out_specs=out_specs, check_vma=False
    )
```

profile of v0, /device:TPU:0, one launch (start us, length us, event | category | flops | bytes accessed | tf_op | source)
XLA Modules:
  0.0 921.2 jit_solution(1120983747204220101)
XLA Ops:
  14.7 22.4 %collective-permute-done = bf16[2,512,512]{1,2,0:T(8,128)(2,1)} collective-permute-done((bf16[2,512,512]{1,2,0:T(8,128)(2,1)S(1)}, bf16[2,512,512]{1,2,0:T(8,128)(2,1)}, u32[]{:S(2)}, u32[]{:S(2)}) %collective-permute-start) | collective-permute-done | bytes 1048608 | tf_op jit(solution)/shard_map/ppermute | solution.py:13
  48.6 14.7 %collective-permute-done.1 = bf16[2,512,512]{1,2,0:T(8,128)(2,1)} collective-permute-done((bf16[2,512,512]{1,2,0:T(8,128)(2,1)}, bf16[2,512,512]{1,2,0:T(8,128)(2,1)}, u32[]{:S(2)}, u32[]{:S(2)}) %collective-permute-start.1) | collective-permute-done | bytes 1048608 | tf_op jit(solution)/shard_map/ppermute | solution.py:13
  72.2 650.0 %while.16 = (s32[]{:T(128)}, f32[3,2,512,512]{2,3,1,0:T(8,128)}, f32[6,2,256,256]{3,2,1,0:T(8,128)}, f32[10,6]{1,0:T(8,128)S(1)}, s32[]{:T(128)}, /*index=5*/s32...) while((s32[]{:T(128)}, f32[3,2,512,512]{2,3,1,0:T(8,128)}, ...), condition=%wide.region_1.2_spmd, body=%wide.region_0.1_spmd.sunk | while | flops 563150912 | bytes 45745520 | solution.py:127
  107.6 10.5 %fusion.95 = f32[1,6]{1,0:T(1,128)S(1)} fusion(f32[2,256,256,1]{2,3,1,0:T(1,128)} %copy.47, f32[6,2,256,256]{3,2,1,0:T(8,128)S(1)} %get-tuple-element.429), kind=kOutput, calls=%fused_computation.9.clone.1 | convolution fusion | flops 9437190 | bytes 3670040 | tf_op jit(solution)/shard_map/while/body/kcxy,cxy->k/dot_general | solution.py:116
  172.0 10.5 %fusion.95 = f32[1,6]{1,0:T(1,128)S(1)} fusion(f32[2,256,256,1]{2,3,1,0:T(1,128)} %copy.47, f32[6,2,256,256]{3,2,1,0:T(8,128)S(1)} %get-tuple-element.429), kind=kOutput, calls=%fused_computation.9.clone.1 | convolution fusion | flops 9437190 | bytes 3670040 | tf_op jit(solution)/shard_map/while/body/kcxy,cxy->k/dot_general | solution.py:116
  186.5 6.6 dynamic_update_slice.21
  236.9 10.5 %fusion.95 = f32[1,6]{1,0:T(1,128)S(1)} fusion(f32[2,256,256,1]{2,3,1,0:T(1,128)} %copy.47, f32[6,2,256,256]{3,2,1,0:T(8,128)S(1)} %get-tuple-element.429), kind=kOutput, calls=%fused_computation.9.clone.1 | convolution fusion | flops 9437190 | bytes 3670040 | tf_op jit(solution)/shard_map/while/body/kcxy,cxy->k/dot_general | solution.py:116
  302.0 10.5 %fusion.95 = f32[1,6]{1,0:T(1,128)S(1)} fusion(f32[2,256,256,1]{2,3,1,0:T(1,128)} %copy.47, f32[6,2,256,256]{3,2,1,0:T(8,128)S(1)} %get-tuple-element.429), kind=kOutput, calls=%fused_computation.9.clone.1 | convolution fusion | flops 9437190 | bytes 3670040 | tf_op jit(solution)/shard_map/while/body/kcxy,cxy->k/dot_general | solution.py:116
  366.7 10.5 %fusion.95 = f32[1,6]{1,0:T(1,128)S(1)} fusion(f32[2,256,256,1]{2,3,1,0:T(1,128)} %copy.47, f32[6,2,256,256]{3,2,1,0:T(8,128)S(1)} %get-tuple-element.429), kind=kOutput, calls=%fused_computation.9.clone.1 | convolution fusion | flops 9437190 | bytes 3670040 | tf_op jit(solution)/shard_map/while/body/kcxy,cxy->k/dot_general | solution.py:116
  381.2 6.6 dynamic_update_slice.21
  390.0 6.7 dynamic_update_slice.22
  432.1 10.5 %fusion.95 = f32[1,6]{1,0:T(1,128)S(1)} fusion(f32[2,256,256,1]{2,3,1,0:T(1,128)} %copy.47, f32[6,2,256,256]{3,2,1,0:T(8,128)S(1)} %get-tuple-element.429), kind=kOutput, calls=%fused_computation.9.clone.1 | convolution fusion | flops 9437190 | bytes 3670040 | tf_op jit(solution)/shard_map/while/body/kcxy,cxy->k/dot_general | solution.py:116
  446.6 6.7 dynamic_update_slice.21
  455.5 6.7 dynamic_update_slice.22
  497.6 10.5 %fusion.95 = f32[1,6]{1,0:T(1,128)S(1)} fusion(f32[2,256,256,1]{2,3,1,0:T(1,128)} %copy.47, f32[6,2,256,256]{3,2,1,0:T(8,128)S(1)} %get-tuple-element.429), kind=kOutput, calls=%fused_computation.9.clone.1 | convolution fusion | flops 9437190 | bytes 3670040 | tf_op jit(solution)/shard_map/while/body/kcxy,cxy->k/dot_general | solution.py:116
  562.4 10.5 %fusion.95 = f32[1,6]{1,0:T(1,128)S(1)} fusion(f32[2,256,256,1]{2,3,1,0:T(1,128)} %copy.47, f32[6,2,256,256]{3,2,1,0:T(8,128)S(1)} %get-tuple-element.429), kind=kOutput, calls=%fused_computation.9.clone.1 | convolution fusion | flops 9437190 | bytes 3670040 | tf_op jit(solution)/shard_map/while/body/kcxy,cxy->k/dot_general | solution.py:116
  576.9 6.7 dynamic_update_slice.21
  627.6 10.5 %fusion.95 = f32[1,6]{1,0:T(1,128)S(1)} fusion(f32[2,256,256,1]{2,3,1,0:T(1,128)} %copy.47, f32[6,2,256,256]{3,2,1,0:T(8,128)S(1)} %get-tuple-element.429), kind=kOutput, calls=%fused_computation.9.clone.1 | convolution fusion | flops 9437190 | bytes 3670040 | tf_op jit(solution)/shard_map/while/body/kcxy,cxy->k/dot_general | solution.py:116
  692.2 10.5 %fusion.95 = f32[1,6]{1,0:T(1,128)S(1)} fusion(f32[2,256,256,1]{2,3,1,0:T(1,128)} %copy.47, f32[6,2,256,256]{3,2,1,0:T(8,128)S(1)} %get-tuple-element.429), kind=kOutput, calls=%fused_computation.9.clone.1 | convolution fusion | flops 9437190 | bytes 3670040 | tf_op jit(solution)/shard_map/while/body/kcxy,cxy->k/dot_general | solution.py:116
  715.5 6.7 dynamic_update_slice.22
  722.2 6.6 copy.16
  730.6 46.3 %collective-permute-done.2 = f32[2,512,512]{2,1,0:T(8,128)S(1)} collective-permute-done((f32[2,512,512]{2,1,0:T(8,128)S(1)}, f32[2,512,512]{2,1,0:T(8,128)S(1)}, u32[]{:S(2)}, u32[]{:S(2)}) %collective-permute-start.2) | collective-permute-done | bytes 2097184 | tf_op jit(solution)/shard_map/ppermute | solution.py:13
  780.4 69.4 %collective-permute-done.3 = f32[2,512,512]{2,1,0:T(8,128)S(1)} collective-permute-done((f32[2,512,512]{2,1,0:T(8,128)}, f32[2,512,512]{2,1,0:T(8,128)S(1)}, u32[]{:S(2)}, u32[]{:S(2)}) %collective-permute-start.3) | collective-permute-done | bytes 2097184 | tf_op jit(solution)/shard_map/ppermute | solution.py:13
  853.9 57.8 %all-reduce.2.cloned.1.call-done = f32[6,2,256,256]{3,2,1,0:T(8,128)} async-done(((f32[6,2,256,256]{3,2,1,0:T(8,128)}), f32[6,2,256,256]{3,2,1,0:T(8,128)}) %all-reduce.2.cloned.1.call-update) | async-done | bytes 3145744 | tf_op jit(solution)/shard_map/psum | solution.py:134
  (404 shorter events, 424.6 us)
Async XLA Ops:
  8.0 903.7 %all-reduce.2.cloned.1.call-start = ((), (), s32[]{:S(2)}) async-start(), calls=%async_computation.2 | async-start | bytes 6291456 | tf_op jit(solution)/shard_map/psum | solution.py:134
  9.5 33.4 %copy-start.5 = (bf16[1,2,512,512]{2,3,1,0:T(8,128)(2,1)}, bf16[1,2,512,512]{2,3,1,0:T(8,128)(2,1)S(1)}, u32[]{:S(2)}) copy-start(bf16[1,2,512,512]{2,3,1,0:T(8,128)(2,1)S(1)} %copy.12) | copy-start | bytes 3145732
  9.6 27.5 %collective-permute-start = (bf16[2,512,512]{1,2,0:T(8,128)(2,1)S(1)}, bf16[2,512,512]{1,2,0:T(8,128)(2,1)}, u32[]{:S(2)}, u32[]{:S(2)}) collective-permute-start(bf16[2,512,512]{1,2,0:T(8,128)(2,1)S(1)} %bitcast.212), channel_id=1, source_target_pairs={{0,12},{4,0},{8,4},{12,8},{1,13},{5,1},{9,5},{13,9},{2,14},{6,2},{... | collective-permute-start | bytes 3145736 | tf_op jit(solution)/shard_map/ppermute | solution.py:13
  37.1 26.2 %collective-permute-start.1 = (bf16[2,512,512]{1,2,0:T(8,128)(2,1)}, bf16[2,512,512]{1,2,0:T(8,128)(2,1)}, u32[]{:S(2)}, u32[]{:S(2)}) collective-permute-start(bf16[2,512,512]{1,2,0:T(8,128)(2,1)} %collective-permute-done), channel_id=1, source_target_pairs={{0,12},{4,0},{8,4},{12,8},{1,13},{5,1},{9,5},{13,9},{2,14},{6,2},{... | collective-permute-start | bytes 3145736 | tf_op jit(solution)/shard_map/ppermute | solution.py:13
  43.7 19.7 %copy-start.6 = (bf16[1,2,512,512]{2,3,1,0:T(8,128)(2,1)S(1)}, bf16[1,2,512,512]{2,3,1,0:T(8,128)(2,1)}, u32[]{:S(2)}) copy-start(bf16[1,2,512,512]{2,3,1,0:T(8,128)(2,1)} %copy-done.5) | copy-start | bytes 3145732
  68.8 3.4 copy-start.7
  95.6 2.8 copy-start.4
  95.6 3.2 copy-start.3
  160.1 2.8 copy-start.4
  160.1 3.2 copy-start.3
  225.0 2.8 copy-start.4
  225.0 3.2 copy-start.3
  290.1 3.2 copy-start.3
  354.7 3.2 copy-start.3
  420.2 2.8 copy-start.4
  420.2 3.2 copy-start.3
  485.7 3.2 copy-start.3
  550.5 3.2 copy-start.3
  615.7 2.8 copy-start.4
  615.7 3.2 copy-start.3
  680.3 3.2 copy-start.3
  730.6 46.4 %collective-permute-start.2 = (f32[2,512,512]{2,1,0:T(8,128)S(1)}, f32[2,512,512]{2,1,0:T(8,128)S(1)}, u32[]{:S(2)}, u32[]{:S(2)}) collective-permute-start(f32[2,512,512]{2,1,0:T(8,128)S(1)} %slice_bitcast_fusion.14), channel_id=1, source_target_pairs={{0,4},{4,8},{8,12},{12,0},{1,5},{5,9},{9,13},{13,1},{2,6},{6,10},{... | collective-permute-start | bytes 6291464 | tf_op jit(solution)/shard_map/ppermute | solution.py:13
  780.3 69.5 %collective-permute-start.3 = (f32[2,512,512]{2,1,0:T(8,128)}, f32[2,512,512]{2,1,0:T(8,128)S(1)}, u32[]{:S(2)}, u32[]{:S(2)}) collective-permute-start(f32[2,512,512]{2,1,0:T(8,128)} %fusion.39), channel_id=1, source_target_pairs={{0,4},{4,8},{8,12},{12,0},{1,5},{5,9},{9,13},{13,1},{2,6},{6,10},{... | collective-permute-start | bytes 6291464 | tf_op jit(solution)/shard_map/ppermute | solution.py:13
  780.3 133.4 %reduce-scatter.2.cloned.1.call-start = ((), (), s32[]{:S(2)}) async-start(), calls=%async_computation.1 | async-start | bytes 2621440 | tf_op jit(solution)/shard_map/reduce_scatter | solution.py:131
  (35 other events, 44.6 us)
Sparse Core Ops, SparseCore 0:
  780.5 131.1 all-reduce.1
Sparse Core Ops, SparseCore 1:
  853.3 34.4 reduce-scatter.1
where the time goes:
time: 928 us; the launch traced here: 921 us
  local copies, waits for them, and re-layouts  237 us (26%)
  waiting for transfers between devices  211 us (23%)
  matrix products  187 us (20%)
  other arithmetic  150 us (16%)
  loops' own time  112 us (12%)
  between operations  16.2 us (2%)
  starting transfers between devices  9.63 us (1%)
    ppermute x4, waiting for transfers between devices, from_behind(): lax.ppermute(array, axis, [(i, (i + by) % peers) for i in range(peers)])  153 us
    dynamic_update_slice x20, local copies, waits for them, and re-layouts, add_block(): return lax.dynamic_update_slice(target, present + piece[None], start_at)  129 us
    another operation x1, loops' own time, on_device(): lax.fori_loop(jnp.int32(0), alive_count, visit, start)  112 us
    dot_general x10, matrix products, visit(): jnp.einsum('kcxy,cxy->k', probes_wide, grad_probe, precision=lax.Precisio...  105 us
    dot_general x10, matrix products, visit(): jnp.einsum('k,kcxy->cxy', weights, probes_wide, precision=lax.Precision.H...  58.9 us
    psum x1, waiting for transfers between devices, on_device(): eigen_all = lax.psum(eigen_acc, ('blk', 'probe')) * scale  57.8 us
    add x20, other arithmetic, add_block(): return lax.dynamic_update_slice(target, present + piece[None], start_at)  43.2 us
    add x10, other arithmetic, visit(): eigen_acc = eigen_acc + weights[:, None, None, None] * grad_probe[None]  40.2 us
  transfers between devices with their start and end apart: 6, of which 5 were waited for; matrix products, arithmetic and copies ran while one was open for 1% of the time, Pallas kernels for 0%

commit v1 on v0

v1 whole, which is shorter than its diff:
```python
import functools
import math

import jax
import jax.numpy as jnp
import ml_dtypes
import numpy as np
from jax import lax
from jax.experimental import pallas as pl
from jax.experimental.pallas import tpu as pltpu
from jax.sharding import PartitionSpec as P

REACH = 3
LANES = 128
STRIP = 16
KRON = 32
VMEM = pltpu.MemorySpace.VMEM
SMEM = pltpu.MemorySpace.SMEM
VMEM_LIMIT = 56 * 1024 * 1024


def tables(frame):
    indices = np.arange(frame)
    angle = (indices[:, None] * indices[None, :] % frame) * (2.0 * math.pi / frame)
    cos_part = np.cos(angle) / math.sqrt(frame)
    sin_part = -np.sin(angle) / math.sqrt(frame)
    forward = np.block([[cos_part, sin_part], [-sin_part, cos_part]])
    forward = forward.astype(np.float32).astype(ml_dtypes.bfloat16)
    return jnp.asarray(forward), jnp.asarray(np.ascontiguousarray(forward.T))


def shift(array, axis, by):
    peers = lax.axis_size(axis)
    return lax.ppermute(array, axis, [(i, (i + by) % peers) for i in range(peers)])


def swap(array, axis, bit):
    peers = lax.axis_size(axis)
    return lax.ppermute(array, axis, [(i, i ^ bit) for i in range(peers)])


def synth_kernel(coef, eig, out):
    modes = eig.shape[0]
    pos_dev = out.shape[0]
    wide = [[eig[k, c].astype(jnp.float32) for k in range(modes)] for c in range(2)]
    for j in range(pos_dev):
        for c in range(2):
            total = coef[j, 0] * wide[c][0]
            for k in range(1, modes):
                total += coef[j, k] * wide[c][k]
            out[j, c] = total


def synth(coefficients, eigenprobes):
    modes, _, frame, _ = eigenprobes.shape
    pos_dev = coefficients.shape[0]
    return pl.pallas_call(
        synth_kernel,
        grid=(frame // STRIP,),
        in_specs=[
            pl.BlockSpec(memory_space=SMEM),
            pl.BlockSpec((modes, 2, STRIP, frame), lambda i: (0, 0, i, 0)),
        ],
        out_specs=pl.BlockSpec((pos_dev, 2, STRIP, frame), lambda i: (0, 0, i, 0)),
        out_shape=jax.ShapeDtypeStruct((pos_dev, 2, frame, frame), jnp.float32),
        name="probe_synthesis",
    )(coefficients, eigenprobes)


def position_kernel(offs, info, *refs):
    pieces = refs[: 1 + 2 * len(offs)]
    (fwd, bwd, probe, amps, keep, send, dprobe, obj, acc, ex, mid, far, patch) = refs[len(pieces):]
    j = pl.program_id(0)
    pos_dev = pl.num_programs(0)
    frame = probe.shape[2]
    side = pieces[0].shape[2]
    blocks = side // LANES
    shares = len(offs)
    slab = side // shares
    alive = info[0, 6]
    member = info[0, 7]

    @pl.when(j == 0)
    def _():
        for section in range(REACH):
            for i in range(1 if section == 0 else shares):
                if section == 0:
                    piece, start, rows = pieces[0], 0, side
                else:
                    piece = pieces[1 + (section - 1) * shares + i]
                    start, rows = pl.multiple_of((member ^ offs[i]) * slab, slab), slab
                for c in range(2):
                    for b in range(blocks):
                        obj[section, c, b, pl.ds(start, rows), :] = piece[
                            c, :, b * LANES:(b + 1) * LANES
                        ].astype(jnp.float32)
        acc[...] = jnp.zeros_like(acc)

    @pl.when(j >= alive)
    def _():
        dprobe[...] = jnp.zeros_like(dprobe)

    @pl.when(j < alive)
    def _():
        lane = lax.broadcasted_iota(jnp.int32, (STRIP, LANES), 1)
        where = []
        for m in range(2):
            row, col = info[j, 2 + 2 * m], info[j, 3 + 2 * m]
            where.append((info[j, m], row, col // LANES, col % LANES))
        strips = range(frame // STRIP)
        for i in strips:
            rows = slice(i * STRIP, (i + 1) * STRIP)
            parts = []
            for c in range(2):
                total = None
                for section, row, cb, s in where:
                    back_by = (LANES - s) % LANES
                    keep_lane = lane < LANES - s
                    rolled = [
                        pltpu.roll(obj[section, c, cb + b, pl.ds(row + i * STRIP, STRIP), :], back_by, 1)
                        for b in range(3)
                    ]
                    block = [jnp.where(keep_lane, rolled[b], rolled[b + 1]) for b in range(2)]
                    total = block if total is None else [x + y for x, y in zip(total, block)]
                parts.append([0.5 * x for x in total])
            for b in range(2):
                cols = slice(b * LANES, (b + 1) * LANES)
                o_re, o_im = parts[0][b], parts[1][b]
                p_re, p_im = probe[0, 0, rows, cols], probe[0, 1, rows, cols]
                patch[0, rows, cols] = o_re
                patch[1, rows, cols] = o_im
                ex[rows, b * LANES:(b + 1) * LANES] = (p_re * o_re - p_im * o_im).astype(jnp.bfloat16)
                ex[rows, frame + b * LANES:frame + (b + 1) * LANES] = (
                    p_re * o_im + p_im * o_re
                ).astype(jnp.bfloat16)

        def transform(table, table_t):
            half = jnp.dot(ex[...], table[...], preferred_element_type=jnp.float32)
            mid[:frame] = half[:, :frame].astype(jnp.bfloat16)
            mid[frame:] = half[:, frame:].astype(jnp.bfloat16)
            far[...] = jnp.dot(table_t[...], mid[...], preferred_element_type=jnp.float32)

        transform(fwd, bwd)
        for i in strips:
            rows = slice(i * STRIP, (i + 1) * STRIP)
            lower = slice(frame + i * STRIP, frame + (i + 1) * STRIP)
            f_re, f_im = far[rows], far[lower]
            factor = 1.0 - amps[0, rows].astype(jnp.float32) * lax.rsqrt(f_re * f_re + f_im * f_im + 1.0)
            ex[rows, :frame] = (f_re * factor).astype(jnp.bfloat16)
            ex[rows, frame:] = (f_im * factor).astype(jnp.bfloat16)
        transform(bwd, fwd)
        for i in strips:
            rows = slice(i * STRIP, (i + 1) * STRIP)
            lower = slice(frame + i * STRIP, frame + (i + 1) * STRIP)
            grads = [[], []]
            for b in range(2):
                cols = slice(b * LANES, (b + 1) * LANES)
                b_re, b_im = far[rows, cols], far[lower, cols]
                o_re, o_im = patch[0, rows, cols], patch[1, rows, cols]
                p_re, p_im = probe[0, 0, rows, cols], probe[0, 1, rows, cols]
                dprobe[0, 0, rows, cols] = (o_re * b_re + o_im * b_im).astype(jnp.bfloat16)
                dprobe[0, 1, rows, cols] = (o_re * b_im - o_im * b_re).astype(jnp.bfloat16)
                grads[0].append(0.5 * (p_re * b_re + p_im * b_im))
                grads[1].append(0.5 * (p_re * b_im - p_im * b_re))
            for section, row, cb, s in where:
                inside = lane >= s
                for c in range(2):
                    low = pltpu.roll(grads[c][0], s, 1)
                    high = pltpu.roll(grads[c][1], s, 1)
                    for b, value in enumerate(
                        (
                            jnp.where(inside, low, 0.0),
                            jnp.where(inside, high, low),
                            jnp.where(inside, 0.0, high),
                        )
                    ):
                        at = (section, c, cb + b, pl.ds(row + i * STRIP, STRIP), slice(None))
                        acc[at] = acc[at] + value

    @pl.when(j == pos_dev - 1)
    def _():
        core = member % 2
        for section in range(REACH):
            for h in range(shares // 2):
                mine = pl.multiple_of((2 * h + core) * slab, slab)
                other = pl.multiple_of((2 * h + 1 - core) * slab, slab)
                for c in range(2):
                    for b in range(blocks):
                        cols = slice(b * LANES, (b + 1) * LANES)
                        keep[section, h, c, :, cols] = acc[section, c, b, pl.ds(mine, slab), :]
                        send[section, h, c, :, cols] = acc[section, c, b, pl.ds(other, slab), :].astype(
                            jnp.bfloat16
                        )


def positions(offs, info, pieces, fwd, bwd, probe, amps):
    pos_dev, _, frame, _ = probe.shape
    side = pieces[0].shape[2]
    shares = len(offs)
    slab = side // shares
    blocks = side // LANES
    whole = pl.BlockSpec(memory_space=VMEM)
    per_pos = lambda j, info: (j, 0, 0, 0)
    half_shape = (REACH, shares // 2, 2, slab, side)
    return pl.pallas_call(
        functools.partial(position_kernel, offs),
        grid_spec=pltpu.PrefetchScalarGridSpec(
            num_scalar_prefetch=1,
            grid=(pos_dev,),
            in_specs=[whole] * (len(pieces) + 2)
            + [
                pl.BlockSpec((1, 2, frame, frame), per_pos),
                pl.BlockSpec((1, frame, frame), lambda j, info: (j, 0, 0)),
            ],
            out_specs=[whole, whole, pl.BlockSpec((1, 2, frame, frame), per_pos)],
            scratch_shapes=[
                pltpu.VMEM((REACH, 2, blocks + 1, side, LANES), jnp.float32),
                pltpu.VMEM((REACH, 2, blocks + 1, side, LANES), jnp.float32),
                pltpu.VMEM((frame, 2 * frame), jnp.bfloat16),
                pltpu.VMEM((2 * frame, frame), jnp.bfloat16),
                pltpu.VMEM((2 * frame, frame), jnp.float32),
                pltpu.VMEM((2, frame, frame), jnp.float32),
            ],
        ),
        out_shape=[
            jax.ShapeDtypeStruct(half_shape, jnp.float32),
            jax.ShapeDtypeStruct(half_shape, jnp.bfloat16),
            jax.ShapeDtypeStruct((pos_dev, 2, frame, frame), jnp.bfloat16),
        ],
        compiler_params=pltpu.CompilerParams(vmem_limit_bytes=VMEM_LIMIT),
        name="positions",
    )(info, *pieces, fwd, bwd, probe, amps)


def eigen_kernel(scale, weights, dprobe, eig, out, cross):
    modes = eig.shape[0]
    pos_dev = dprobe.shape[0]
    frame = eig.shape[3]
    width = pos_dev * KRON

    @pl.when(pl.program_id(0) == 0)
    def _():
        cross[...] = jnp.zeros_like(cross)

    for c in range(2):
        d = dprobe[:, c].reshape(width, frame)
        e = eig[:, c].reshape(modes * KRON, frame)
        grad = jnp.dot(weights[0], d, preferred_element_type=jnp.float32)
        grad += jnp.dot(weights[1], d, preferred_element_type=jnp.float32)
        out[:, c] = (scale * grad).reshape(modes, KRON, frame)
        cross[...] += lax.dot_general(d, e, (((1,), (1,)), ((), ())), preferred_element_type=jnp.float32)


def eigen_terms(scale, weights, dprobe, eigenprobes):
    modes, _, frame, _ = eigenprobes.shape
    pos_dev = dprobe.shape[0]
    return pl.pallas_call(
        functools.partial(eigen_kernel, scale),
        grid=(frame // KRON,),
        in_specs=[
            pl.BlockSpec(memory_space=VMEM),
            pl.BlockSpec((pos_dev, 2, KRON, frame), lambda i: (0, 0, i, 0)),
            pl.BlockSpec((modes, 2, KRON, frame), lambda i: (0, 0, i, 0)),
        ],
        out_specs=[
            pl.BlockSpec((modes, 2, KRON, frame), lambda i: (0, 0, i, 0)),
            pl.BlockSpec((pos_dev * KRON, modes * KRON), lambda i: (0, 0)),
        ],
        out_shape=[
            jax.ShapeDtypeStruct((modes, 2, frame, frame), jnp.float32),
            jax.ShapeDtypeStruct((pos_dev * KRON, modes * KRON), jnp.float32),
        ],
        compiler_params=pltpu.CompilerParams(vmem_limit_bytes=VMEM_LIMIT),
        name="eigen_terms",
    )(weights, dprobe, eigenprobes)


def halve(keep, send, member, shares):
    total = keep + swap(send, "probe", 1).astype(jnp.float32)
    rest = member // 2
    bit = 2
    while bit < shares:
        pairs = total.reshape((total.shape[0] // 2, 2) + total.shape[1:])
        mine = rest % 2
        keep = lax.dynamic_index_in_dim(pairs, mine, 1, False)
        send = lax.dynamic_index_in_dim(pairs, 1 - mine, 1, False).astype(jnp.bfloat16)
        total = keep + swap(send, "probe", bit).astype(jnp.float32)
        rest = rest // 2
        bit *= 2
    return total[0]


def on_device(tiles, eigenprobes, coefficients, tile_list, offsets, amplitudes, group_counts):
    modes, _, frame, _ = eigenprobes.shape
    side = tiles.shape[2]
    pos_dev = coefficients.shape[0]
    blocks = lax.axis_size("blk")
    shares = lax.axis_size("probe")
    my_block = lax.axis_index("blk")
    member = lax.axis_index("probe")
    slab = side // shares
    bits = [1 << i for i in range(shares.bit_length() - 1)]
    forward, backward = tables(frame)

    moving = lax.dynamic_slice_in_dim(tiles[0], member * slab, slab, 1)
    pieces = [tiles[0]]
    offs = [0]
    for bit in reversed(bits):
        offs = offs + [o ^ bit for o in offs]
    for section in range(1, REACH):
        moving = shift(moving, "blk", -1)
        held = [moving]
        for bit in reversed(bits):
            held = held + [swap(piece, "probe", bit) for piece in held]
        pieces += held

    alive = jnp.clip(group_counts[0] - member * pos_dev, 0, pos_dev)
    info = jnp.concatenate(
        [
            (tile_list - my_block) % blocks,
            offsets,
            jnp.broadcast_to(alive, (pos_dev, 1)).astype(jnp.int32),
            jnp.broadcast_to(member, (pos_dev, 1)).astype(jnp.int32),
        ],
        1,
    )
    eye = jnp.eye(KRON, dtype=jnp.float32)
    spread = (coefficients.T[:, None, :, None] * eye[None, :, None, :]).reshape(
        modes * KRON, pos_dev * KRON
    )
    spread_high = spread.astype(jnp.bfloat16)
    weights = jnp.stack([spread_high, (spread - spread_high.astype(jnp.float32)).astype(jnp.bfloat16)])

    probe = synth(coefficients, eigenprobes)
    keep, send, dprobe = positions(offs, info, pieces, forward, backward, probe, amplitudes)

    returned = None
    for section in range(REACH - 1, -1, -1):
        mine = halve(keep[section], send[section], member, shares)
        if returned is None:
            returned = mine
        else:
            returned = shift(returned.astype(jnp.bfloat16), "blk", 1).astype(jnp.float32) + mine

    scale = (pos_dev * blocks * shares) ** (-0.5)
    eigen, cross = eigen_terms(scale, weights, dprobe, eigenprobes)
    slabs = eigen.reshape(modes, 2, shares // 2, 2, frame // shares, frame)
    core = member % 2
    eigen_keep = jnp.moveaxis(lax.dynamic_index_in_dim(slabs, core, 3, False), 2, 0)
    eigen_send = jnp.moveaxis(lax.dynamic_index_in_dim(slabs, 1 - core, 3, False), 2, 0).astype(jnp.bfloat16)
    eigen_mine = halve(eigen_keep, eigen_send, member, shares)
    eigen_share = lax.psum(eigen_mine, "blk")
    coef_rows = jnp.einsum("jrkr->jk", cross.reshape(pos_dev, KRON, modes, KRON)) / frame
    return (returned[None], eigen_share, coef_rows)


def solution(mesh):
    in_specs = (
        P(("recon", "blk"), None, None, None),
        P("recon", None, None, None),
        P(("recon", "blk", "probe"), None),
        P(("recon", "blk", "probe"), None),
        P(("recon", "blk", "probe"), None),
        P(("recon", "blk", "probe"), None, None),
        P(("recon", "blk")),
    )
    out_specs = (
        P(("recon", "blk"), None, "probe", None),
        P("recon", None, "probe", None),
        P(("recon", "blk", "probe"), None),
    )
    return jax.shard_map(
        on_device, mesh=mesh, in_specs=in_specs, out_specs=out_specs, check_vma=False
    )
```

time: 928 us -> 173 us (0.19)
  local copies, waits for them, and re-layouts: 237 us -> 14.1 us
  matrix products: 187 us -> 0 us
  waiting for transfers between devices: 211 us -> 67.9 us
  other arithmetic: 150 us -> 12 us
  loops' own time: 112 us -> 0 us
  Pallas kernels: 0 us -> 46.6 us
    dot_general x60 -> x0, matrix products: 187 us -> none  [the longest x10 105 us: visit(): jnp.einsum('kcxy,cxy->k', probes_wide, grad_probe, precision=lax.Precisio...]
    dynamic_update_slice x30 -> x0, local copies, waits for them, and re-layouts: 130 us -> none  [the longest x20 129 us: add_block(): return lax.dynamic_update_slice(target, present + piece[None], start_at)]
    another operation x1 -> x0, loops' own time: 112 us -> none  [on_device(): lax.fori_loop(jnp.int32(0), alive_count, visit, start)]
    ppermute x4 -> x18, waiting for transfers between devices: 153 us -> 43.3 us  [the longest x14 22.5 us: swap(): return lax.ppermute(array, axis, [(i, i ^ bit) for i in range(peers)])]
    add x32 -> x2, other arithmetic: 90.2 us -> 4.4 us  [halve(): total = keep + swap(send, 'probe', 1).astype(jnp.float32)]
    pallas_call x0 -> x3, Pallas kernels: none -> 46.6 us  [the longest x1 27.5 us: positions(): pl.pallas_call(functools.partial(position_kernel, offs), grid_spec=pltpu....]
    another operation x20 -> x0, local copies, waits for them, and re-layouts: 39.7 us -> none  [position_terms(): jnp.stack([obj_re * back_re + obj_im * back_im, obj_re * back_im - obj_im...]
    psum x1, waiting for transfers between devices: 57.8 us -> 24.6 us  [on_device(): eigen_share = lax.psum(eigen_mine, 'blk')]
  transfers between devices with their start and end apart: 6 -> 19, of which waited for: 5 -> 10; matrix products, arithmetic and copies ran while one was open for 1% -> 12% of each run, Pallas kernels for 0% -> 11%
where the time goes in v1:
time: 173 us; the launch traced here: 172 us
  waiting for transfers between devices  67.9 us (39%)
  Pallas kernels  46.6 us (27%)
  starting transfers between devices  16.4 us (9%)
  between operations  14.9 us (9%)
  local copies, waits for them, and re-layouts  14.1 us (8%)
  other arithmetic  12 us (7%)
    pallas_call x1, Pallas kernels, positions(): pl.pallas_call(functools.partial(position_kernel, offs), grid_spec=pltpu....  27.5 us
    psum x1, waiting for transfers between devices, on_device(): eigen_share = lax.psum(eigen_mine, 'blk')  24.6 us
    ppermute x14, waiting for transfers between devices, swap(): return lax.ppermute(array, axis, [(i, i ^ bit) for i in range(peers)])  22.5 us
    ppermute x4, waiting for transfers between devices, shift(): lax.ppermute(array, axis, [(i, (i + by) % peers) for i in range(peers)])  20.8 us
    pallas_call x1, Pallas kernels, synth(): pl.pallas_call(synth_kernel, grid=(frame // STRIP,), in_specs=[pl.BlockSp...  10.8 us
    ppermute x4, starting transfers between devices, shift(): lax.ppermute(array, axis, [(i, (i + by) % peers) for i in range(peers)])  9.39 us
    pallas_call x1, Pallas kernels, eigen_terms(): pl.pallas_call(functools.partial(eigen_kernel, scale), grid=(frame // KRO...  8.24 us
    ppermute x14, starting transfers between devices, swap(): return lax.ppermute(array, axis, [(i, i ^ bit) for i in range(peers)])  6.94 us
  transfers between devices with their start and end apart: 19, of which 10 were waited for; matrix products, arithmetic and copies ran while one was open for 12% of the time, Pallas kernels for 11%

profile of v1, /device:TPU:0, one launch (start us, length us, event | category | flops | bytes accessed | tf_op | source)
XLA Modules:
  0.0 171.9 jit_solution(7459531441468280907)
XLA Ops:
  8.2 5.1 %collective-permute-start = (bf16[2,128,512]{2,1,0:T(8,128)(2,1)S(1)}, bf16[2,128,512]{2,1,0:T(8,128)(2,1)S(1)}, u32[]{:S(2)}, u32[]{:S(2)}) collective-permute-start(bf16[2,128,512]{2,1,0:T(8,128)(2,1)S(1)} %dynamic-slice_bitcast_fusion), channel_id=1, source_target_pairs={{0,12},{4,0},{8,4},{12,8},{1,13},{5,1},{9,5},{13,9},{2,14},{6,2},{... | collective-permute-start | bytes 786440 | tf_op jit(solution)/shard_map/ppermute | solution.py:34
  13.3 5.6 %collective-permute-done.refs_1_ = bf16[2,128,512]{2,1,0:T(8,128)(2,1)S(1)} collective-permute-done((bf16[2,128,512]{2,1,0:T(8,128)(2,1)S(1)}, bf16[2,128,512]{2,1,0:T(8,128)(2,1)S(1)}, u32[]{:S(2)}, u32[]{:S(2)}) %collective-permute-start) | collective-permute-done | bytes 262176 | tf_op jit(solution)/shard_map/ppermute | solution.py:34
  18.9 4.3 %collective-permute-start.4 = (bf16[2,128,512]{2,1,0:T(8,128)(2,1)S(1)}, bf16[2,128,512]{2,1,0:T(8,128)(2,1)S(1)}, u32[]{:S(2)}, u32[]{:S(2)}) collective-permute-start(bf16[2,128,512]{2,1,0:T(8,128)(2,1)S(1)} %collective-permute-done.refs_1_), channel_id=1, source_target_pairs={{0,12},{4,0},{8,4},{12,8},{1,13},{5,1},{9,5},{13,9},{2,14},{6,2},{... | collective-permute-start | bytes 786440 | tf_op jit(solution)/shard_map/ppermute | solution.py:34
  23.9 1.5 collective-permute-start.1
  25.5 2.4 %collective-permute-done.4.refs_5_ = bf16[2,128,512]{2,1,0:T(8,128)(2,1)S(1)} collective-permute-done((bf16[2,128,512]{2,1,0:T(8,128)(2,1)S(1)}, bf16[2,128,512]{2,1,0:T(8,128)(2,1)S(1)}, u32[]{:S(2)}, u32[]{:S(2)}) %collective-permute-start.4) | collective-permute-done | bytes 262176 | tf_op jit(solution)/shard_map/ppermute | solution.py:34
  27.9 1.5 collective-permute-start.5
  33.2 3.3 %collective-permute-done.5.refs_6_ = bf16[2,128,512]{2,1,0:T(8,128)(2,1)S(1)} collective-permute-done((bf16[2,128,512]{2,1,0:T(8,128)(2,1)S(1)}, bf16[2,128,512]{2,1,0:T(8,128)(2,1)S(1)}, u32[]{:S(2)}, u32[]{:S(2)}) %collective-permute-start.5) | collective-permute-done | bytes 262176 | tf_op jit(solution)/shard_map/ppermute | solution.py:39
  38.4 10.8 %probe_synthesis.1.refs_11_ = f32[10,2,256,256]{3,2,1,0:T(8,128)} custom-call(f32[10,6]{1,0:T(8,128)} %copy.27.coef, bf16[6,2,256,256]{3,2,1,0:T(8,128)(2,1)} %eig.3), custom_call_target="tpu_custom_call" | custom-call | tf_op jit(solution)/shard_map/probe_synthesis/pallas_call | solution.py:57
  50.2 27.5 %positions.1 = (f32[3,2,2,128,512]{4,3,2,1,0:T(8,128)}, bf16[3,2,2,128,512]{4,3,2,1,0:T(8,128)(2,1)}, bf16[10,2,256,256]{3,2,1,0:T(8,128)(2,1)}) custom-call(s32[10,8]{1,0:T(8,128)} %add_add_fusion.info, bf16[2,512,512]{2,1,0:T(8,128)(2,1)} %bitcast.47, bf16[2,128,512]{2,1,0:T(8,128)(2,1)} %copy-done.2, bf16[2,128,512]{2,1,0:T(8,128)(2,1)} %copy-done.4, ...), custom_call_target="tpu_custom_call" | custom-call | tf_op jit(solution)/shard_map/positions/pallas_call | solution.py:205
  77.8 1.5 slice_bitcast_fusion.2
  81.1 8.2 %eigen_terms.1 = (f32[6,2,256,256]{3,2,1,0:T(8,128)}, f32[320,192]{1,0:T(8,128)}) custom-call(bf16[2,192,320]{2,1,0:T(8,128)(2,1)} %pad_maximum_fusion.weights, bf16[10,2,256,256]{3,2,1,0:T(8,128)(2,1)} %get-tuple-element.10.dprobe, bf16[6,2,256,256]{3,2,1,0:T(8,128)(2,1)} %eig.3), custom_call_target="tpu_custom_call" | custom-call | tf_op jit(solution)/shard_map/eigen_terms/pallas_call | solution.py:257
  89.3 2.5 %fusion = bf16[2,6,2,64,256]{4,3,2,1,0:T(8,128)(2,1)} fusion(f32[6,2,2,2,64,256]{5,4,3,2,1,0:T(8,128)} %bitcast.45, s32[]{:T(128)S(6)} %select_n.65), kind=kLoop, calls=%fused_computation.6 | loop fusion | bytes 1572868 | tf_op jit(solution)/shard_map/convert_element_type | solution.py:350
  92.1 3.0 %bitcast_add_fusion.3 = (f32[2,2,128,512]{3,2,1,0:T(8,128)S(1)}, f32[2,2,128,512]{3,2,1,0:T(8,128)S(1)}, f32[2,2,128,512]{3,2,1,0:T(8,128)S(1)}) fusion(bf16[2,2,128,512]{3,2,1,0:T(8,128)(2,1)} %collective-permute-done.8, f32[3,2,2,128,512]{4,3,2,1,0:T(8,128)} %get-tuple-element.8, bf16[2,2,128,512]{3,2,1,0:T(8,128)(2,1)} %collective-permute-done.14, ...), kind=kLoop, calls=%fused_computation.5 | loop fusion | flops 1572864 | bytes 7864320 | tf_op jit(solution)/shard_map/add | solution.py:279
  95.4 1.4 bitcast_add_fusion
  96.9 2.0 %collective-permute-start.17 = (bf16[1,6,2,64,256]{4,3,2,1,0:T(8,128)(2,1)S(1)}, bf16[1,6,2,64,256]{4,3,2,1,0:T(8,128)(2,1)S(1)}, u32[]{:S(2)}, u32[]{:S(2)}) collective-permute-start(bf16[1,6,2,64,256]{4,3,2,1,0:T(8,128)(2,1)S(1)} %dynamic-slice_convert_fusion), channel_id=1, source_target_pairs={{0,2},{1,3},{2,0},{3,1},{4,6},{5,7},{6,4},{7,5},{8,10},{9,11},{10,... | collective-permute-start | bytes 1179656 | tf_op jit(solution)/shard_map/ppermute | solution.py:39
  99.7 4.7 %collective-permute-done.9 = bf16[1,2,128,512]{3,2,1,0:T(8,128)(2,1)S(1)} collective-permute-done((bf16[1,2,128,512]{3,2,1,0:T(8,128)(2,1)S(1)}, bf16[1,2,128,512]{3,2,1,0:T(8,128)(2,1)S(1)}, u32[]{:S(2)}, u32[]{:S(2)}) %collective-permute-start.9) | collective-permute-done | bytes 262176 | tf_op jit(solution)/shard_map/ppermute | solution.py:39
  106.0 6.8 %collective-permute-done.17 = bf16[1,6,2,64,256]{4,3,2,1,0:T(8,128)(2,1)S(1)} collective-permute-done((bf16[1,6,2,64,256]{4,3,2,1,0:T(8,128)(2,1)S(1)}, bf16[1,6,2,64,256]{4,3,2,1,0:T(8,128)(2,1)S(1)}, u32[]{:S(2)}, u32[]{:S(2)}) %collective-permute-start.17) | collective-permute-done | bytes 393248 | tf_op jit(solution)/shard_map/ppermute | solution.py:39
  113.9 4.7 %collective-permute-done.12 = bf16[1,2,128,512]{3,2,1,0:T(8,128)(2,1)} collective-permute-done((bf16[1,2,128,512]{3,2,1,0:T(8,128)(2,1)}, bf16[1,2,128,512]{3,2,1,0:T(8,128)(2,1)}, u32[]{:S(2)}, u32[]{:S(2)}) %collective-permute-start.12) | collective-permute-done | bytes 262176 | tf_op jit(solution)/shard_map/ppermute | solution.py:39
  118.6 1.9 %fusion.2 = bf16[2,128,512]{2,1,0:T(8,128)(2,1)} fusion(bf16[1,2,128,512]{3,2,1,0:T(8,128)(2,1)} %collective-permute-done.12, f32[2,2,128,512]{3,2,1,0:T(8,128)S(1)} %get-tuple-element.20, s32[]{:T(128)S(6)} %select_n.61, bf16[2,128,512]{2,1,0:T(8,128)(2,1)} %collective-permute-done.10), kind=kLoop, calls=%fused_computation.13 | loop fusion | flops 655360 | bytes 1310724 | tf_op jit(solution)/shard_map/convert_element_type | solution.py:343
  121.5 2.2 %collective-permute-done.15 = bf16[1,2,128,512]{3,2,1,0:T(8,128)(2,1)} collective-permute-done((bf16[1,2,128,512]{3,2,1,0:T(8,128)(2,1)}, bf16[1,2,128,512]{3,2,1,0:T(8,128)(2,1)}, u32[]{:S(2)}, u32[]{:S(2)}) %collective-permute-start.15) | collective-permute-done | bytes 262176 | tf_op jit(solution)/shard_map/ppermute | solution.py:39
  123.7 12.8 %collective-permute-done.13 = bf16[2,128,512]{2,1,0:T(8,128)(2,1)S(1)} collective-permute-done((bf16[2,128,512]{2,1,0:T(8,128)(2,1)}, bf16[2,128,512]{2,1,0:T(8,128)(2,1)S(1)}, u32[]{:S(2)}, u32[]{:S(2)}) %collective-permute-start.13) | collective-permute-done | bytes 262176 | tf_op jit(solution)/shard_map/ppermute | solution.py:34
  136.6 1.8 %fusion.1 = f32[1,2,128,512]{3,2,1,0:T(8,128)} fusion(bf16[1,2,128,512]{3,2,1,0:T(8,128)(2,1)} %collective-permute-done.15, f32[2,2,128,512]{3,2,1,0:T(8,128)S(1)} %get-tuple-element.19, s32[]{:T(128)S(6)} %select_n.61, bf16[2,128,512]{2,1,0:T(8,128)(2,1)S(1)} %collective-permute-done.13), kind=kLoop, calls=%fused_computation.11 | loop fusion | flops 524288 | bytes 1572868 | tf_op jit(solution)/shard_map/broadcast_in_dim | solution.py:354
  138.4 24.6 %all-reduce.2.cloned.1.call-done = f32[6,2,64,256]{3,2,1,0:T(8,128)} async-done(((f32[6,2,64,256]{3,2,1,0:T(8,128)}), f32[6,2,64,256]{3,2,1,0:T(8,128)}) %all-reduce.2.cloned.1.call-update) | async-done | bytes 786448 | tf_op jit(solution)/shard_map/psum | solution.py:352
  163.0 2.1 %copy.41 = f32[6,2,64,256]{3,2,1,0:T(8,128)} copy(f32[6,2,64,256]{3,2,1,0:T(8,128)} %all-reduce.2.cloned.1.call-done) | data formatting | bytes 1572864
  (71 shorter events, 14.7 us)
Async XLA Ops:
  7.2 30.1 %copy-start.9 = (f32[10,6]{0,1:T(8,128)S(1)}, f32[10,6]{0,1:T(8,128)}, u32[]{:S(2)}) copy-start(f32[10,6]{0,1:T(8,128)} %param.11) | copy-start | bytes 724
  7.2 155.8 %all-reduce.2.cloned.1.call-start = ((), (), s32[]{:S(2)}) async-start(), calls=%async_computation | async-start | bytes 1572864 | tf_op jit(solution)/shard_map/psum | solution.py:352
  8.2 10.7 %collective-permute-start = (bf16[2,128,512]{2,1,0:T(8,128)(2,1)S(1)}, bf16[2,128,512]{2,1,0:T(8,128)(2,1)S(1)}, u32[]{:S(2)}, u32[]{:S(2)}) collective-permute-start(bf16[2,128,512]{2,1,0:T(8,128)(2,1)S(1)} %dynamic-slice_bitcast_fusion), channel_id=1, source_target_pairs={{0,12},{4,0},{8,4},{12,8},{1,13},{5,1},{9,5},{13,9},{2,14},{6,2},{... | collective-permute-start | bytes 786440 | tf_op jit(solution)/shard_map/ppermute | solution.py:34
  18.9 19.5 %copy-start.2 = (bf16[2,128,512]{2,1,0:T(8,128)(2,1)}, bf16[2,128,512]{2,1,0:T(8,128)(2,1)S(1)}, u32[]{:S(2)}) copy-start(bf16[2,128,512]{2,1,0:T(8,128)(2,1)S(1)} %collective-permute-done.refs_1_) | copy-start | bytes 786436
  18.9 9.0 %collective-permute-start.4 = (bf16[2,128,512]{2,1,0:T(8,128)(2,1)S(1)}, bf16[2,128,512]{2,1,0:T(8,128)(2,1)S(1)}, u32[]{:S(2)}, u32[]{:S(2)}) collective-permute-start(bf16[2,128,512]{2,1,0:T(8,128)(2,1)S(1)} %collective-permute-done.refs_1_), channel_id=1, source_target_pairs={{0,12},{4,0},{8,4},{12,8},{1,13},{5,1},{9,5},{13,9},{2,14},{6,2},{... | collective-permute-start | bytes 786440 | tf_op jit(solution)/shard_map/ppermute | solution.py:34
  23.9 9.3 %collective-permute-start.1 = (bf16[2,128,512]{2,1,0:T(8,128)(2,1)S(1)}, bf16[2,128,512]{2,1,0:T(8,128)(2,1)S(1)}, u32[]{:S(2)}, u32[]{:S(2)}) collective-permute-start(bf16[2,128,512]{2,1,0:T(8,128)(2,1)S(1)} %collective-permute-done.refs_1_), channel_id=1, source_target_pairs={{0,2},{1,3},{2,0},{3,1},{4,6},{5,7},{6,4},{7,5},{8,10},{9,11},{10,... | collective-permute-start | bytes 786440 | tf_op jit(solution)/shard_map/ppermute | solution.py:39
  27.8 10.6 %copy-start.3 = (bf16[2,128,512]{2,1,0:T(8,128)(2,1)}, bf16[2,128,512]{2,1,0:T(8,128)(2,1)S(1)}, u32[]{:S(2)}) copy-start(bf16[2,128,512]{2,1,0:T(8,128)(2,1)S(1)} %collective-permute-done.4.refs_5_) | copy-start | bytes 786436
  27.9 8.7 %collective-permute-start.5 = (bf16[2,128,512]{2,1,0:T(8,128)(2,1)S(1)}, bf16[2,128,512]{2,1,0:T(8,128)(2,1)S(1)}, u32[]{:S(2)}, u32[]{:S(2)}) collective-permute-start(bf16[2,128,512]{2,1,0:T(8,128)(2,1)S(1)} %collective-permute-done.4.refs_5_), channel_id=1, source_target_pairs={{0,2},{1,3},{2,0},{3,1},{4,6},{5,7},{6,4},{7,5},{8,10},{9,11},{10,... | collective-permute-start | bytes 786440 | tf_op jit(solution)/shard_map/ppermute | solution.py:39
  31.9 17.4 %collective-permute-start.2 = (bf16[2,128,512]{2,1,0:T(8,128)(2,1)S(1)}, bf16[2,128,512]{2,1,0:T(8,128)(2,1)S(1)}, u32[]{:S(2)}, u32[]{:S(2)}) collective-permute-start(bf16[2,128,512]{2,1,0:T(8,128)(2,1)S(1)} %collective-permute-done.refs_1_), channel_id=1, source_target_pairs={{0,1},{1,0},{2,3},{3,2},{4,5},{5,4},{6,7},{7,6},{8,9},{9,8},{10,11... | collective-permute-start | bytes 786440 | tf_op jit(solution)/shard_map/ppermute | solution.py:39
  31.9 17.4 %collective-permute-start.6 = (bf16[2,128,512]{2,1,0:T(8,128)(2,1)S(1)}, bf16[2,128,512]{2,1,0:T(8,128)(2,1)S(1)}, u32[]{:S(2)}, u32[]{:S(2)}) collective-permute-start(bf16[2,128,512]{2,1,0:T(8,128)(2,1)S(1)} %collective-permute-done.4.refs_5_), channel_id=1, source_target_pairs={{0,1},{1,0},{2,3},{3,2},{4,5},{5,4},{6,7},{7,6},{8,9},{9,8},{10,11... | collective-permute-start | bytes 786440 | tf_op jit(solution)/shard_map/ppermute | solution.py:39
  33.2 16.0 %copy-start.4 = (bf16[2,128,512]{2,1,0:T(8,128)(2,1)}, bf16[2,128,512]{2,1,0:T(8,128)(2,1)S(1)}, u32[]{:S(2)}) copy-start(bf16[2,128,512]{2,1,0:T(8,128)(2,1)S(1)} %collective-permute-done.1.refs_2_) | copy-start | bytes 786436
  33.2 16.1 %collective-permute-start.3 = (bf16[2,128,512]{2,1,0:T(8,128)(2,1)S(1)}, bf16[2,128,512]{2,1,0:T(8,128)(2,1)S(1)}, u32[]{:S(2)}, u32[]{:S(2)}) collective-permute-start(bf16[2,128,512]{2,1,0:T(8,128)(2,1)S(1)} %collective-permute-done.1.refs_2_), channel_id=1, source_target_pairs={{0,1},{1,0},{2,3},{3,2},{4,5},{5,4},{6,7},{7,6},{8,9},{9,8},{10,11... | collective-permute-start | bytes 786440 | tf_op jit(solution)/shard_map/ppermute | solution.py:39
  36.5 12.8 %copy-start.5 = (bf16[2,128,512]{2,1,0:T(8,128)(2,1)}, bf16[2,128,512]{2,1,0:T(8,128)(2,1)S(1)}, u32[]{:S(2)}) copy-start(bf16[2,128,512]{2,1,0:T(8,128)(2,1)S(1)} %collective-permute-done.5.refs_6_) | copy-start | bytes 786436
  36.5 12.9 %collective-permute-start.7 = (bf16[2,128,512]{2,1,0:T(8,128)(2,1)S(1)}, bf16[2,128,512]{2,1,0:T(8,128)(2,1)}, u32[]{:S(2)}, u32[]{:S(2)}) collective-permute-start(bf16[2,128,512]{2,1,0:T(8,128)(2,1)S(1)} %collective-permute-done.5.refs_6_), channel_id=1, source_target_pairs={{0,1},{1,0},{2,3},{3,2},{4,5},{5,4},{6,7},{7,6},{8,9},{9,8},{10,11... | collective-permute-start | bytes 786440 | tf_op jit(solution)/shard_map/ppermute | solution.py:39
  79.3 12.8 %collective-permute-start.11 = (bf16[2,2,128,512]{3,2,1,0:T(8,128)(2,1)S(1)}, bf16[2,2,128,512]{3,2,1,0:T(8,128)(2,1)}, u32[]{:S(2)}, u32[]{:S(2)}) collective-permute-start(bf16[2,2,128,512]{3,2,1,0:T(8,128)(2,1)S(1)} %get-tuple-element.23), channel_id=1, source_target_pairs={{0,1},{1,0},{2,3},{3,2},{4,5},{5,4},{6,7},{7,6},{8,9},{9,8},{10,11... | collective-permute-start | bytes 1572872 | tf_op jit(solution)/shard_map/ppermute | solution.py:39
  79.8 12.3 %collective-permute-start.14 = (bf16[2,2,128,512]{3,2,1,0:T(8,128)(2,1)S(1)}, bf16[2,2,128,512]{3,2,1,0:T(8,128)(2,1)}, u32[]{:S(2)}, u32[]{:S(2)}) collective-permute-start(bf16[2,2,128,512]{3,2,1,0:T(8,128)(2,1)S(1)} %get-tuple-element.22), channel_id=1, source_target_pairs={{0,1},{1,0},{2,3},{3,2},{4,5},{5,4},{6,7},{7,6},{8,9},{9,8},{10,11... | collective-permute-start | bytes 1572872 | tf_op jit(solution)/shard_map/ppermute | solution.py:39
  79.9 12.3 %collective-permute-start.8 = (bf16[2,2,128,512]{3,2,1,0:T(8,128)(2,1)S(1)}, bf16[2,2,128,512]{3,2,1,0:T(8,128)(2,1)}, u32[]{:S(2)}, u32[]{:S(2)}) collective-permute-start(bf16[2,2,128,512]{3,2,1,0:T(8,128)(2,1)S(1)} %get-tuple-element.21), channel_id=1, source_target_pairs={{0,1},{1,0},{2,3},{3,2},{4,5},{5,4},{6,7},{7,6},{8,9},{9,8},{10,11... | collective-permute-start | bytes 1572872 | tf_op jit(solution)/shard_map/ppermute | solution.py:39
  91.8 3.6 %collective-permute-start.16 = (bf16[2,6,2,64,256]{4,3,2,1,0:T(8,128)(2,1)}, bf16[2,6,2,64,256]{4,3,2,1,0:T(8,128)(2,1)}, u32[]{:S(2)}, u32[]{:S(2)}) collective-permute-start(bf16[2,6,2,64,256]{4,3,2,1,0:T(8,128)(2,1)} %fusion), channel_id=1, source_target_pairs={{0,1},{1,0},{2,3},{3,2},{4,5},{5,4},{6,7},{7,6},{8,9},{9,8},{10,11... | collective-permute-start | bytes 2359304 | tf_op jit(solution)/shard_map/ppermute | solution.py:39
  95.2 9.2 %collective-permute-start.9 = (bf16[1,2,128,512]{3,2,1,0:T(8,128)(2,1)S(1)}, bf16[1,2,128,512]{3,2,1,0:T(8,128)(2,1)S(1)}, u32[]{:S(2)}, u32[]{:S(2)}) collective-permute-start(bf16[1,2,128,512]{3,2,1,0:T(8,128)(2,1)S(1)} %dynamic-slice_convert_fusion.3), channel_id=1, source_target_pairs={{0,2},{1,3},{2,0},{3,1},{4,6},{5,7},{6,4},{7,5},{8,10},{9,11},{10,... | collective-permute-start | bytes 786440 | tf_op jit(solution)/shard_map/ppermute | solution.py:39
  96.9 16.0 %collective-permute-start.17 = (bf16[1,6,2,64,256]{4,3,2,1,0:T(8,128)(2,1)S(1)}, bf16[1,6,2,64,256]{4,3,2,1,0:T(8,128)(2,1)S(1)}, u32[]{:S(2)}, u32[]{:S(2)}) collective-permute-start(bf16[1,6,2,64,256]{4,3,2,1,0:T(8,128)(2,1)S(1)} %dynamic-slice_convert_fusion), channel_id=1, source_target_pairs={{0,2},{1,3},{2,0},{3,1},{4,6},{5,7},{6,4},{7,5},{8,10},{9,11},{10,... | collective-permute-start | bytes 1179656 | tf_op jit(solution)/shard_map/ppermute | solution.py:39
  99.6 19.0 %collective-permute-start.12 = (bf16[1,2,128,512]{3,2,1,0:T(8,128)(2,1)}, bf16[1,2,128,512]{3,2,1,0:T(8,128)(2,1)}, u32[]{:S(2)}, u32[]{:S(2)}) collective-permute-start(bf16[1,2,128,512]{3,2,1,0:T(8,128)(2,1)} %dynamic-slice_convert_fusion.2), channel_id=1, source_target_pairs={{0,2},{1,3},{2,0},{3,1},{4,6},{5,7},{6,4},{7,5},{8,10},{9,11},{10,... | collective-permute-start | bytes 786440 | tf_op jit(solution)/shard_map/ppermute | solution.py:39
  105.2 13.4 %collective-permute-start.10 = (bf16[2,128,512]{2,1,0:T(8,128)(2,1)}, bf16[2,128,512]{2,1,0:T(8,128)(2,1)}, u32[]{:S(2)}, u32[]{:S(2)}) collective-permute-start(bf16[2,128,512]{2,1,0:T(8,128)(2,1)} %fusion.3), channel_id=1, source_target_pairs={{0,4},{4,8},{8,12},{12,0},{1,5},{5,9},{9,13},{13,1},{2,6},{6,10},{... | collective-permute-start | bytes 786440 | tf_op jit(solution)/shard_map/ppermute | solution.py:34
  105.9 17.8 %collective-permute-start.15 = (bf16[1,2,128,512]{3,2,1,0:T(8,128)(2,1)}, bf16[1,2,128,512]{3,2,1,0:T(8,128)(2,1)}, u32[]{:S(2)}, u32[]{:S(2)}) collective-permute-start(bf16[1,2,128,512]{3,2,1,0:T(8,128)(2,1)} %dynamic-slice_convert_fusion.1), channel_id=1, source_target_pairs={{0,2},{1,3},{2,0},{3,1},{4,6},{5,7},{6,4},{7,5},{8,10},{9,11},{10,... | collective-permute-start | bytes 786440 | tf_op jit(solution)/shard_map/ppermute | solution.py:39
  120.4 16.1 %collective-permute-start.13 = (bf16[2,128,512]{2,1,0:T(8,128)(2,1)}, bf16[2,128,512]{2,1,0:T(8,128)(2,1)S(1)}, u32[]{:S(2)}, u32[]{:S(2)}) collective-permute-start(bf16[2,128,512]{2,1,0:T(8,128)(2,1)} %fusion.2), channel_id=1, source_target_pairs={{0,4},{4,8},{8,12},{12,0},{1,5},{5,9},{9,13},{13,1},{2,6},{6,10},{... | collective-permute-start | bytes 786440 | tf_op jit(solution)/shard_map/ppermute | solution.py:34
  (5 other events, 8.2 us)
Sparse Core Ops, SparseCore 0:
  114.0 48.9 all-reduce.1

commit v2 on v0

v2 whole, which is shorter than its diff:
```python
import functools
import math

import jax
import jax.numpy as jnp
import ml_dtypes
import numpy as np
from jax import lax
from jax.experimental import pallas as pl
from jax.experimental.pallas import tpu as pltpu
from jax.sharding import PartitionSpec as P

REACH = 3
LANES = 128
STRIP = 16
VMEM = pltpu.MemorySpace.VMEM
SMEM = pltpu.MemorySpace.SMEM
VMEM_LIMIT = 36 * 1024 * 1024


def tables(frame):
    indices = np.arange(frame)
    angle = (indices[:, None] * indices[None, :] % frame) * (2.0 * math.pi / frame)
    cos_part = np.cos(angle) / math.sqrt(frame)
    sin_part = -np.sin(angle) / math.sqrt(frame)
    forward = np.block([[cos_part, sin_part], [-sin_part, cos_part]])
    forward = forward.astype(np.float32).astype(ml_dtypes.bfloat16)
    return jnp.asarray(np.stack([forward, forward.T]))


def shift(array, axis, by):
    peers = lax.axis_size(axis)
    return lax.ppermute(array, axis, [(i, (i + by) % peers) for i in range(peers)])


def swap(array, axis, bit):
    peers = lax.axis_size(axis)
    return lax.ppermute(array, axis, [(i, i ^ bit) for i in range(peers)])


def slabs_of(member, h):
    pair, core = member >> 1, member & 1
    mine = 2 * (pair ^ h) + core
    return mine, mine ^ 1


def turned(groups, peers):
    return groups // peers if groups % peers == 0 else 0


def coordinates(tile_list, offsets, group_counts, pos_dev):
    blocks = lax.axis_size("blk")
    my_block, member = lax.axis_index("blk"), lax.axis_index("probe")
    alive = jnp.clip(group_counts[0] - member * pos_dev, 0, pos_dev)

    def place(j, m):
        section = lax.rem(tile_list[m, j] - my_block + blocks, blocks)
        return section, offsets[2 * m, j], offsets[2 * m + 1, j]

    return my_block, member, alive, place


def one_hot(shape, axis):
    return (
        lax.broadcasted_iota(jnp.int32, shape, axis) // STRIP == lax.broadcasted_iota(jnp.int32, shape, 1 - axis)
    ).astype(jnp.float32)


def diagonals(array):
    row = lax.broadcasted_iota(jnp.int32, array.shape, 0)
    col = lax.broadcasted_iota(jnp.int32, array.shape, 1)
    return jnp.where(row % STRIP == col % STRIP, array, 0.0)


def exact(left, right):
    return jnp.dot(left, right, precision=lax.Precision.HIGHEST, preferred_element_type=jnp.float32)


def two_terms(array):
    high = array.astype(jnp.bfloat16)
    return high, (array - high.astype(jnp.float32)).astype(jnp.bfloat16)


def position_kernel(offs, scale, tile_list, offsets, group_counts, *refs):
    shares = len(offs)
    pieces = refs[: 1 + (REACH - 1) * shares]
    tables_in, amps_in, eig, coef_in = refs[len(pieces):len(pieces) + 4]
    eigen_send, eigen_keep, grads_out, coef = refs[len(pieces) + 4:len(pieces) + 8]
    (staged, table, probe, amps, obj, ex, mid, far, patch, d_high, d_low, eigen, out_eigen, cross,
     weights, weights_t, piece_sem, table_sem, amps_sem, grad_sem, out_sem) = refs[len(pieces) + 8:]
    pos_dev, _, frame, _ = probe.shape
    modes = eig.shape[0]
    side = staged.shape[2]
    blocks = side // LANES
    slab = side // shares
    my_block, member, alive, place = coordinates(tile_list, offsets, group_counts, pos_dev)
    strips = range(frame // STRIP)

    copies = [pltpu.make_async_copy(pieces[0], staged.at[0], piece_sem.at[0])]
    for section in range(1, REACH):
        for i in range(shares):
            start = pl.multiple_of((member ^ offs[i]) * slab, slab)
            at = 1 + (section - 1) * shares + i
            copies.append(
                pltpu.make_async_copy(
                    pieces[at], staged.at[section, :, pl.ds(start, slab), :], piece_sem.at[at]
                )
            )
    table_copy = pltpu.make_async_copy(tables_in, table, table_sem)
    amps_copy = pltpu.make_async_copy(amps_in, amps, amps_sem)
    for copy in copies + [table_copy, amps_copy]:
        copy.start()

    by_position = (pos_dev * STRIP, pos_dev)
    by_mode = (modes * STRIP, modes)
    tall_t = exact(exact(one_hot(by_mode, 0), coef_in[...]), one_hot(by_position[::-1], 1))
    high, low = two_terms(diagonals(tall_t))
    weights_t[...] = jnp.concatenate([high, low], 0)
    spread = lax.dot_general(
        one_hot(by_position, 0), coef_in[...], (((1,), (1,)), ((), ())),
        precision=lax.Precision.HIGHEST, preferred_element_type=jnp.float32,
    )
    high, low = two_terms(diagonals(exact(spread, one_hot(by_mode[::-1], 1))))
    weights[...] = jnp.concatenate([high, low], 1)

    def synth(i, carry):
        rows = pl.ds(pl.multiple_of(i * STRIP, STRIP), STRIP)
        for c in range(2):
            e = eig[:, c, rows, :].reshape(modes * STRIP, frame)
            made = jnp.dot(
                weights[...], jnp.concatenate([e, e], 0), preferred_element_type=jnp.float32
            )
            probe[:, c, rows, :] = made.reshape(pos_dev, STRIP, frame)
        return carry

    lax.fori_loop(0, frame // STRIP, synth, 0, unroll=4)
    for copy in copies:
        copy.wait()

    def widen(i, carry):
        rows = pl.ds(pl.multiple_of(i * LANES, LANES), LANES)
        for section in range(REACH):
            for c in range(2):
                for b in range(blocks):
                    obj[section, c, b, rows, :] = staged[
                        section, c, rows, b * LANES:(b + 1) * LANES
                    ].astype(jnp.float32)
        return carry

    lax.fori_loop(0, side // LANES, widen, 0)
    table_copy.wait()
    amps_copy.wait()

    lane = lax.broadcasted_iota(jnp.int32, (STRIP, LANES), 1)

    def enter(j, slot):
        where = []
        for m in range(2):
            section, row, col = place(j, m)
            s = col % LANES
            where.append((section, row, col // LANES, (LANES - s) % LANES, lane < LANES - s))
        for i in strips:
            rows = slice(i * STRIP, (i + 1) * STRIP)
            parts = []
            for c in range(2):
                total = None
                for section, row, cb, back_by, keep_lane in where:
                    rolled = [
                        pltpu.roll(obj[section, c, cb + b, pl.ds(row + i * STRIP, STRIP), :], back_by, 1)
                        for b in range(3)
                    ]
                    block = [jnp.where(keep_lane, rolled[b], rolled[b + 1]) for b in range(2)]
                    total = block if total is None else [x + y for x, y in zip(total, block)]
                parts.append([0.5 * x for x in total])
            for b in range(2):
                cols = slice(b * LANES, (b + 1) * LANES)
                o_re, o_im = parts[0][b], parts[1][b]
                p_re, p_im = probe[j, 0, rows, cols], probe[j, 1, rows, cols]
                patch[slot, 0, rows, cols] = o_re
                patch[slot, 1, rows, cols] = o_im
                ex[slot, rows, b * LANES:(b + 1) * LANES] = (p_re * o_re - p_im * o_im).astype(jnp.bfloat16)
                ex[slot, rows, frame + b * LANES:frame + (b + 1) * LANES] = (
                    p_re * o_im + p_im * o_re
                ).astype(jnp.bfloat16)

    def transform(slot, way):
        half = jnp.dot(ex[slot], table[way], preferred_element_type=jnp.float32)
        mid[slot, :frame] = half[:, :frame].astype(jnp.bfloat16)
        mid[slot, frame:] = half[:, frame:].astype(jnp.bfloat16)
        far[slot] = jnp.dot(table[1 - way], mid[slot], preferred_element_type=jnp.float32)

    def residual(j, slot, living):
        for i in strips:
            rows = slice(i * STRIP, (i + 1) * STRIP)
            lower = slice(frame + i * STRIP, frame + (i + 1) * STRIP)
            f_re, f_im = far[slot, rows], far[slot, lower]
            factor = 1.0 - amps[j, rows].astype(jnp.float32) * lax.rsqrt(f_re * f_re + f_im * f_im + 1.0)
            if living is not None:
                factor = factor * living
            ex[slot, rows, :frame] = (f_re * factor).astype(jnp.bfloat16)
            ex[slot, rows, frame:] = (f_im * factor).astype(jnp.bfloat16)

    def leave(j, slot):
        for i in strips:
            rows = slice(i * STRIP, (i + 1) * STRIP)
            lower = slice(frame + i * STRIP, frame + (i + 1) * STRIP)
            b_re, b_im = far[slot, rows], far[slot, lower]
            o_re, o_im = patch[slot, 0, rows], patch[slot, 1, rows]
            p_re, p_im = probe[j, 0, rows], probe[j, 1, rows]
            for c, d in enumerate((o_re * b_re + o_im * b_im, o_re * b_im - o_im * b_re)):
                high = d.astype(jnp.bfloat16)
                d_high[j, c, rows] = high
                d_low[j, c, rows] = (d - high.astype(jnp.float32)).astype(jnp.bfloat16)
            probe[j, 0, rows] = 0.5 * (p_re * b_re + p_im * b_im)
            probe[j, 1, rows] = 0.5 * (p_re * b_im - p_im * b_re)

    def grad_copy(j):
        return pltpu.make_async_copy(probe.at[j], grads_out.at[j], grad_sem.at[j])

    def visit(pair, carry):
        first, second = 2 * pair, 2 * pair + 1
        enter(first, 0)
        transform(0, 0)
        enter(second, 1)
        transform(1, 0)
        residual(first, 0, None)
        transform(0, 1)
        residual(second, 1, jnp.where(second < alive, 1.0, 0.0))
        transform(1, 1)
        leave(first, 0)
        leave(second, 1)
        grad_copy(first).start()
        grad_copy(second).start()
        return carry

    pairs = (alive + 1) // 2
    lax.fori_loop(0, pairs, visit, 0)

    def skip(j, carry):
        d_high[j] = jnp.zeros((2, frame, frame), jnp.bfloat16)
        d_low[j] = jnp.zeros((2, frame, frame), jnp.bfloat16)
        return carry

    lax.fori_loop(2 * pairs, pos_dev, skip, 0)

    cross[...] = jnp.zeros_like(cross)
    rows_q = frame // shares
    groups = 2 * modes
    turn = my_block * turned(groups, lax.axis_size("blk"))

    def eigen_strip(i, carry):
        rows = pl.ds(pl.multiple_of(i * STRIP, STRIP), STRIP)
        q = i // (rows_q // STRIP)
        inner = pl.ds(pl.multiple_of(i % (rows_q // STRIP) * STRIP, STRIP), STRIP)
        for c in range(2):
            high = d_high[:, c, rows, :].reshape(pos_dev * STRIP, frame)
            low = d_low[:, c, rows, :].reshape(pos_dev * STRIP, frame)
            e = eig[:, c, rows, :].reshape(modes * STRIP, frame)
            both = jnp.dot(weights_t[...], high, preferred_element_type=jnp.float32)
            rest = jnp.dot(weights_t[:modes * STRIP], low, preferred_element_type=jnp.float32)
            grad = (both[:modes * STRIP] + both[modes * STRIP:] + rest) * scale
            for k in range(modes):
                group = lax.rem(2 * k + c + groups - turn, groups)
                eigen[q, group, inner, :] = grad[k * STRIP:(k + 1) * STRIP]
            cross[...] += lax.dot_general(
                high, e, (((1,), (1,)), ((), ())), preferred_element_type=jnp.float32
            )
        return carry

    lax.fori_loop(0, frame // STRIP, eigen_strip, 0, unroll=4)
    pending = []

    def start(source, target):
        copy = pltpu.make_async_copy(source, target, out_sem.at[len(pending)])
        copy.start()
        pending.append(copy)

    for h in range(shares // 2):
        mine, other = slabs_of(member, h)
        out_eigen[h] = eigen[other].astype(jnp.bfloat16)
        start(eigen.at[mine], eigen_keep.at[h])
    start(out_eigen, eigen_send)

    total = exact(one_hot(by_position[::-1], 1), diagonals(cross[...]))
    coef[...] = lax.dot_general(
        one_hot(by_mode[::-1], 1), total, (((1,), (1,)), ((), ())),
        precision=lax.Precision.HIGHEST, preferred_element_type=jnp.float32,
    ) * (1.0 / frame)

    def drain(j, carry):
        grad_copy(j).wait()
        return carry

    lax.fori_loop(0, 2 * pairs, drain, 0)
    for copy in pending:
        copy.wait()


def positions(offs, scale, indices, pieces, table, amps, eigenprobes, coefficients):
    modes, _, frame, _ = eigenprobes.shape
    pos_dev = amps.shape[0]
    side = pieces[0].shape[2]
    shares = len(offs)
    blocks = side // LANES
    smem = pl.BlockSpec(memory_space=SMEM)
    whole = pl.BlockSpec(memory_space=VMEM)
    anywhere = pl.BlockSpec(memory_space=pl.ANY)
    eigen_half = (shares // 2, 2 * modes, frame // shares, frame)
    grads = (pos_dev, 2, frame, frame)
    return pl.pallas_call(
        functools.partial(position_kernel, offs, scale),
        in_specs=[smem] * 3 + [anywhere] * (len(pieces) + 2) + [whole] * 2,
        out_specs=[anywhere] * 3 + [whole],
        scratch_shapes=[
            pltpu.VMEM((REACH, 2, side, side), jnp.bfloat16),
            pltpu.VMEM(table.shape, jnp.bfloat16),
            pltpu.VMEM(grads, jnp.float32),
            pltpu.VMEM(amps.shape, jnp.bfloat16),
            pltpu.VMEM((REACH, 2, blocks + 1, side, LANES), jnp.float32),
            pltpu.VMEM((2, frame, 2 * frame), jnp.bfloat16),
            pltpu.VMEM((2, 2 * frame, frame), jnp.bfloat16),
            pltpu.VMEM((2, 2 * frame, frame), jnp.float32),
            pltpu.VMEM((2, 2, frame, frame), jnp.float32),
            pltpu.VMEM(grads, jnp.bfloat16),
            pltpu.VMEM(grads, jnp.bfloat16),
            pltpu.VMEM((shares, 2 * modes, frame // shares, frame), jnp.float32),
            pltpu.VMEM(eigen_half, jnp.bfloat16),
            pltpu.VMEM((pos_dev * STRIP, modes * STRIP), jnp.float32),
            pltpu.VMEM((pos_dev * STRIP, 2 * modes * STRIP), jnp.bfloat16),
            pltpu.VMEM((2 * modes * STRIP, pos_dev * STRIP), jnp.bfloat16),
            pltpu.SemaphoreType.DMA((len(pieces),)),
            pltpu.SemaphoreType.DMA,
            pltpu.SemaphoreType.DMA,
            pltpu.SemaphoreType.DMA((pos_dev,)),
            pltpu.SemaphoreType.DMA((shares // 2 + 1,)),
        ],
        out_shape=[
            jax.ShapeDtypeStruct(eigen_half, jnp.bfloat16),
            jax.ShapeDtypeStruct(eigen_half, jnp.float32),
            jax.ShapeDtypeStruct(grads, jnp.float32),
            jax.ShapeDtypeStruct((modes, pos_dev), jnp.float32),
        ],
        compiler_params=pltpu.CompilerParams(vmem_limit_bytes=VMEM_LIMIT),
        name="positions",
    )(*indices, *pieces, table, amps, eigenprobes, coefficients.T)


def scatter_kernel(shares, tile_list, offsets, group_counts, grads_in, *refs):
    send, keep = refs[:REACH], refs[REACH:2 * REACH]
    grads, acc, out_send, grad_sem, out_sem = refs[2 * REACH:]
    pos_dev, _, frame, _ = grads.shape
    blocks, side = acc.shape[2] - 1, acc.shape[3]
    slab = side // shares
    _, member, alive, place = coordinates(tile_list, offsets, group_counts, pos_dev)

    def grad_copy(j):
        return pltpu.make_async_copy(grads_in.at[j], grads.at[j], grad_sem.at[j])

    def begin(j, carry):
        grad_copy(j).start()
        return carry

    lax.fori_loop(0, alive, begin, 0)

    def clear(i, carry):
        rows = pl.ds(pl.multiple_of(i * LANES, LANES), LANES)
        for section in range(REACH):
            for c in range(2):
                for b in range(blocks + 1):
                    acc[section, c, b, rows, :] = jnp.zeros((LANES, LANES), jnp.float32)
        return carry

    lax.fori_loop(0, side // LANES, clear, 0)
    lane = lax.broadcasted_iota(jnp.int32, (STRIP, LANES), 1)

    def add(j, carry):
        grad_copy(j).wait()
        for m in range(2):
            section, row, col = place(j, m)
            cb, s = col // LANES, col % LANES
            inside = lane >= s
            for i in range(frame // STRIP):
                for c in range(2):
                    low, high = (
                        pltpu.roll(grads[j, c, i * STRIP:(i + 1) * STRIP, b * LANES:(b + 1) * LANES], s, 1)
                        for b in range(2)
                    )
                    for b, value in enumerate(
                        (
                            jnp.where(inside, low, 0.0),
                            jnp.where(inside, high, low),
                            jnp.where(inside, 0.0, high),
                        )
                    ):
                        at = (section, c, cb + b, pl.ds(row + i * STRIP, STRIP), slice(None))
                        acc[at] = acc[at] + value
        return carry

    lax.fori_loop(0, alive, add, 0)
    pending = []

    def start(source, target):
        copy = pltpu.make_async_copy(source, target, out_sem.at[len(pending)])
        copy.start()
        pending.append(copy)

    for section in range(REACH - 1, -1, -1):
        for h in range(shares // 2):
            mine, other = (pl.multiple_of(at * slab, slab) for at in slabs_of(member, h))
            start(acc.at[section, :, pl.ds(0, blocks), pl.ds(mine, slab), :], keep[section].at[h])
            for c in range(2):
                for b in range(blocks):
                    out_send[section, h, c, b] = acc[section, c, b, pl.ds(other, slab), :].astype(jnp.bfloat16)
        start(out_send.at[section], send[section])
    for copy in pending:
        copy.wait()


def scatter(shares, side, indices, grads):
    blocks = side // LANES
    anywhere = pl.BlockSpec(memory_space=pl.ANY)
    half = (shares // 2, 2, blocks, side // shares, LANES)
    return pl.pallas_call(
        functools.partial(scatter_kernel, shares),
        in_specs=[pl.BlockSpec(memory_space=SMEM)] * 3 + [anywhere],
        out_specs=[anywhere] * (2 * REACH),
        scratch_shapes=[
            pltpu.VMEM(grads.shape, jnp.float32),
            pltpu.VMEM((REACH, 2, blocks + 1, side, LANES), jnp.float32),
            pltpu.VMEM((REACH,) + half, jnp.bfloat16),
            pltpu.SemaphoreType.DMA((grads.shape[0],)),
            pltpu.SemaphoreType.DMA((REACH * (shares // 2 + 1),)),
        ],
        out_shape=[jax.ShapeDtypeStruct(half, jnp.bfloat16)] * REACH
        + [jax.ShapeDtypeStruct(half, jnp.float32)] * REACH,
        compiler_params=pltpu.CompilerParams(vmem_limit_bytes=20 * 1024 * 1024),
        cost_estimate=pl.CostEstimate(flops=1 << 24, bytes_accessed=16 << 20, transcendentals=0),
        name="scatter",
    )(*indices, grads)


def after(array, *others):
    return lax.optimization_barrier((array,) + others)[0]


def halve(keep, send, before_core=(), before_cross=()):
    arrived = swap(after(send, *before_core), "probe", 1)
    terms = [keep, after(arrived, *before_cross)]
    bit = 2
    leaving = send
    while keep.shape[0] * 2 > bit:
        pick = lambda term, which: term.reshape((term.shape[0] // 2, 2) + term.shape[1:])[:, which]
        sending = sum(pick(term, 1).astype(jnp.float32) for term in terms).astype(jnp.bfloat16)
        if bit == 2:
            leaving = sending
        arrived = swap(sending, "probe", bit)
        terms = [pick(term, 0) for term in terms] + [arrived]
        bit *= 2
    return sum(term[0].astype(jnp.float32) for term in terms), leaving, arrived


def place_kernel(me, *refs):
    pieces, out = refs[:-1], refs[-1]
    peers = len(pieces)
    for by, piece in enumerate(pieces):
        out[(me[0] + peers - by) % peers] = piece[...].astype(jnp.float32)


def sum_over(axis, value, turned):
    peers = lax.axis_size(axis)
    me = lax.axis_index(axis)
    rows = value.shape[0] // peers

    def chunk(by):
        if turned:
            return value[by * rows:(by + 1) * rows]
        return lax.dynamic_slice_in_dim(value, (me + by) % peers * rows, rows, 0)

    total = chunk(0)
    for by in range(1, peers):
        total += shift(chunk(by).astype(jnp.bfloat16), axis, by).astype(jnp.float32)
    total = total.astype(jnp.bfloat16)
    return [total] + [shift(total, axis, by) for by in range(1, peers)]


def place(axis, held):
    peers, (rows, lanes) = len(held), held[0].shape
    return pl.pallas_call(
        place_kernel,
        in_specs=[pl.BlockSpec(memory_space=SMEM)] + [pl.BlockSpec(memory_space=VMEM)] * peers,
        out_specs=pl.BlockSpec(memory_space=VMEM),
        out_shape=jax.ShapeDtypeStruct((peers, rows, lanes), jnp.float32),
        compiler_params=pltpu.CompilerParams(vmem_limit_bytes=8 * 1024 * 1024),
        name="place",
    )(lax.axis_index(axis).reshape(1).astype(jnp.int32), *held)


def finish_kernel(first, second, out):
    blocks = first.shape[1]
    for c in range(2):
        for b in range(blocks):
            out[c, :, b * LANES:(b + 1) * LANES] = first[c, b] + second[c, b].astype(jnp.float32)


def finish(first, second):
    _, blocks, slab, lanes = first.shape
    return pl.pallas_call(
        finish_kernel,
        in_specs=[pl.BlockSpec(memory_space=VMEM)] * 2,
        out_specs=pl.BlockSpec(memory_space=VMEM),
        out_shape=jax.ShapeDtypeStruct((2, slab, blocks * lanes), jnp.float32),
        compiler_params=pltpu.CompilerParams(vmem_limit_bytes=8 * 1024 * 1024),
        name="finish",
    )(first, second)


def on_device(tiles, eigenprobes, coefficients, tile_list, offsets, amplitudes, group_counts):
    modes, _, frame, _ = eigenprobes.shape
    side = tiles.shape[2]
    pos_dev = coefficients.shape[0]
    blocks = lax.axis_size("blk")
    shares = lax.axis_size("probe")
    member = lax.axis_index("probe")
    slab = side // shares
    bits = [1 << i for i in range(shares.bit_length() - 1)]
    table = tables(frame)

    own = lax.dynamic_slice_in_dim(tiles[0], member * slab, slab, 1)
    pieces = [tiles[0]]
    offs = [0]
    for bit in reversed(bits):
        offs = offs + [o ^ bit for o in offs]
    moving = own
    for section in range(1, REACH):
        moving = shift(moving, "blk", -1)
        held = [moving]
        for bit in reversed(bits):
            held = held + [swap(piece, "probe", bit) for piece in held]
        pieces += held

    indices = (tile_list.T, offsets.T, group_counts)
    scale = (pos_dev * blocks * shares) ** (-0.5)
    eigen_send, eigen_keep, grads, coef_rows = positions(
        tuple(offs), scale, indices, pieces, table, amplitudes, eigenprobes, coefficients
    )

    eigen, leaving, crossed = halve(eigen_keep, eigen_send)
    out = scatter(shares, side, indices, after(grads, leaving))
    send, keep = out[:REACH], out[REACH:]
    last = REACH - 1
    mine, leaving, crossed = halve(keep[last], send[last], before_core=(crossed,))
    eigen = after(eigen, leaving)
    held = sum_over("blk", eigen.reshape(-1, frame), turned(2 * modes, blocks) > 0)
    moving = mine.astype(jnp.bfloat16)
    gate = moving
    for section in range(last - 1, -1, -1):
        mine, _, _ = halve(keep[section], send[section], before_cross=(gate,))
        gate = arrived = shift(moving, "blk", 1)
        if section > 0:
            moving = (arrived.astype(jnp.float32) + mine).astype(jnp.bfloat16)
    eigen_share = place("blk", [after(held[0], moving)] + held[1:])
    eigen_share = eigen_share.reshape(modes, 2, frame // shares, frame)
    summed = finish(mine, arrived)
    return (summed[None], eigen_share, coef_rows.T)


def solution(mesh):
    in_specs = (
        P(("recon", "blk"), None, None, None),
        P("recon", None, None, None),
        P(("recon", "blk", "probe"), None),
        P(("recon", "blk", "probe"), None),
        P(("recon", "blk", "probe"), None),
        P(("recon", "blk", "probe"), None, None),
        P(("recon", "blk")),
    )
    out_specs = (
        P(("recon", "blk"), None, "probe", None),
        P("recon", None, "probe", None),
        P(("recon", "blk", "probe"), None),
    )
    return jax.shard_map(
        on_device, mesh=mesh, in_specs=in_specs, out_specs=out_specs, check_vma=False
    )
```

time: 928 us -> 111 us (0.12)
  local copies, waits for them, and re-layouts: 237 us -> 11.7 us
  matrix products: 187 us -> 0 us
  waiting for transfers between devices: 211 us -> 35.2 us
  other arithmetic: 150 us -> 3.87 us
  loops' own time: 112 us -> 0 us
  Pallas kernels: 0 us -> 28.5 us
  starting transfers between devices: 9.63 us -> 29.4 us
  between operations: 16.2 us -> 1.51 us
    dot_general x60 -> x0, matrix products: 187 us -> none  [the longest x10 105 us: visit(): jnp.einsum('kcxy,cxy->k', probes_wide, grad_probe, precision=lax.Precisio...]
    dynamic_update_slice x30 -> x0, local copies, waits for them, and re-layouts: 130 us -> none  [the longest x20 129 us: add_block(): return lax.dynamic_update_slice(target, present + piece[None], start_at)]
    ppermute x4 -> x24, waiting for transfers between devices: 153 us -> 35.2 us  [the longest x10 20.6 us: shift(): lax.ppermute(array, axis, [(i, (i + by) % peers) for i in range(peers)])]
    another operation x1 -> x0, loops' own time: 112 us -> none  [on_device(): lax.fori_loop(jnp.int32(0), alive_count, visit, start)]
    add x32 -> x2, other arithmetic: 90.2 us -> 1.19 us  [halve(): sum((term[0].astype(jnp.float32) for term in terms))]
    psum x1 -> x0, waiting for transfers between devices: 57.8 us -> none  [on_device(): eigen_all = lax.psum(eigen_acc, ('blk', 'probe')) * scale]
    another operation x20 -> x0, local copies, waits for them, and re-layouts: 39.7 us -> none  [position_terms(): jnp.stack([obj_re * back_re + obj_im * back_im, obj_re * back_im - obj_im...]
    pallas_call x0 -> x4, Pallas kernels: none -> 28.5 us  [the longest x1 20.4 us: positions(): pl.pallas_call(functools.partial(position_kernel, offs, scale), in_specs=...]
  transfers between devices with their start and end apart: 6 -> 24, of which waited for: 5 -> 14; matrix products, arithmetic and copies ran while one was open for 1% -> 3% of each run, Pallas kernels for 0% -> 7%
where the time goes in v2:
time: 111 us; the launch traced here: 110 us
  waiting for transfers between devices  35.2 us (32%)
  starting transfers between devices  29.4 us (26%)
  Pallas kernels  28.5 us (26%)
  local copies, waits for them, and re-layouts  11.7 us (11%)
  other arithmetic  3.87 us (3%)
  between operations  1.51 us (1%)
    ppermute x10, starting transfers between devices, shift(): lax.ppermute(array, axis, [(i, (i + by) % peers) for i in range(peers)])  21.8 us
    ppermute x10, waiting for transfers between devices, shift(): lax.ppermute(array, axis, [(i, (i + by) % peers) for i in range(peers)])  20.6 us
    pallas_call x1, Pallas kernels, positions(): pl.pallas_call(functools.partial(position_kernel, offs, scale), in_specs=...  20.4 us
    ppermute x14, waiting for transfers between devices, swap(): return lax.ppermute(array, axis, [(i, i ^ bit) for i in range(peers)])  14.6 us
    unnamed x26, local copies, waits for them, and re-layouts  10.6 us
    ppermute x14, starting transfers between devices, swap(): return lax.ppermute(array, axis, [(i, i ^ bit) for i in range(peers)])  7.61 us
    pallas_call x1, Pallas kernels, scatter(): pl.pallas_call(functools.partial(scatter_kernel, shares), in_specs=[pl.Bl...  6.31 us
  transfers between devices with their start and end apart: 24, of which 14 were waited for; matrix products, arithmetic and copies ran while one was open for 3% of the time, Pallas kernels for 7%

profile of v2, /device:TPU:0, one launch (start us, length us, event | category | flops | bytes accessed | tf_op | source)
XLA Modules:
  0.0 110.2 jit_solution(2349864775063543186)
XLA Ops:
  1.6 5.1 %collective-permute-start = (bf16[2,128,512]{2,1,0:T(8,128)(2,1)S(1)}, bf16[2,128,512]{2,1,0:T(8,128)(2,1)S(1)}, u32[]{:S(2)}, u32[]{:S(2)}) collective-permute-start(bf16[2,128,512]{2,1,0:T(8,128)(2,1)S(1)} %dynamic-slice_bitcast_fusion), channel_id=1, source_target_pairs={{0,12},{4,0},{8,4},{12,8},{1,13},{5,1},{9,5},{13,9},{2,14},{6,2},{... | collective-permute-start | bytes 786440 | tf_op jit(solution)/shard_map/ppermute | solution.py:33
  6.7 5.6 %collective-permute-done.refs_1_ = bf16[2,128,512]{2,1,0:T(8,128)(2,1)S(1)} collective-permute-done((bf16[2,128,512]{2,1,0:T(8,128)(2,1)S(1)}, bf16[2,128,512]{2,1,0:T(8,128)(2,1)S(1)}, u32[]{:S(2)}, u32[]{:S(2)}) %collective-permute-start) | collective-permute-done | bytes 262176 | tf_op jit(solution)/shard_map/ppermute | solution.py:33
  12.3 4.3 %collective-permute-start.4 = (bf16[2,128,512]{2,1,0:T(8,128)(2,1)S(1)}, bf16[2,128,512]{2,1,0:T(8,128)(2,1)S(1)}, u32[]{:S(2)}, u32[]{:S(2)}) collective-permute-start(bf16[2,128,512]{2,1,0:T(8,128)(2,1)S(1)} %collective-permute-done.refs_1_), channel_id=1, source_target_pairs={{0,12},{4,0},{8,4},{12,8},{1,13},{5,1},{9,5},{13,9},{2,14},{6,2},{... | collective-permute-start | bytes 786440 | tf_op jit(solution)/shard_map/ppermute | solution.py:33
  16.6 1.5 %collective-permute-start.1 = (bf16[2,128,512]{2,1,0:T(8,128)(2,1)S(1)}, bf16[2,128,512]{2,1,0:T(8,128)(2,1)S(1)}, u32[]{:S(2)}, u32[]{:S(2)}) collective-permute-start(bf16[2,128,512]{2,1,0:T(8,128)(2,1)S(1)} %collective-permute-done.refs_1_), channel_id=1, source_target_pairs={{0,2},{1,3},{2,0},{3,1},{4,6},{5,7},{6,4},{7,5},{8,10},{9,11},{10,... | collective-permute-start | bytes 786440 | tf_op jit(solution)/shard_map/ppermute | solution.py:38
  18.1 3.2 %collective-permute-done.4.refs_5_ = bf16[2,128,512]{2,1,0:T(8,128)(2,1)S(1)} collective-permute-done((bf16[2,128,512]{2,1,0:T(8,128)(2,1)S(1)}, bf16[2,128,512]{2,1,0:T(8,128)(2,1)S(1)}, u32[]{:S(2)}, u32[]{:S(2)}) %collective-permute-start.4) | collective-permute-done | bytes 262176 | tf_op jit(solution)/shard_map/ppermute | solution.py:33
  21.3 1.5 %collective-permute-start.5 = (bf16[2,128,512]{2,1,0:T(8,128)(2,1)S(1)}, bf16[2,128,512]{2,1,0:T(8,128)(2,1)S(1)}, u32[]{:S(2)}, u32[]{:S(2)}) collective-permute-start(bf16[2,128,512]{2,1,0:T(8,128)(2,1)S(1)} %collective-permute-done.4.refs_5_), channel_id=1, source_target_pairs={{0,2},{1,3},{2,0},{3,1},{4,6},{5,7},{6,4},{7,5},{8,10},{9,11},{10,... | collective-permute-start | bytes 786440 | tf_op jit(solution)/shard_map/ppermute | solution.py:38
  23.3 1.7 %collective-permute-done.1.refs_2_ = bf16[2,128,512]{2,1,0:T(8,128)(2,1)S(1)} collective-permute-done((bf16[2,128,512]{2,1,0:T(8,128)(2,1)S(1)}, bf16[2,128,512]{2,1,0:T(8,128)(2,1)S(1)}, u32[]{:S(2)}, u32[]{:S(2)}) %collective-permute-start.1) | collective-permute-done | bytes 262176 | tf_op jit(solution)/shard_map/ppermute | solution.py:38
  25.0 4.1 %collective-permute-done.5.refs_6_ = bf16[2,128,512]{2,1,0:T(8,128)(2,1)S(1)} collective-permute-done((bf16[2,128,512]{2,1,0:T(8,128)(2,1)S(1)}, bf16[2,128,512]{2,1,0:T(8,128)(2,1)S(1)}, u32[]{:S(2)}, u32[]{:S(2)}) %collective-permute-start.5) | collective-permute-done | bytes 262176 | tf_op jit(solution)/shard_map/ppermute | solution.py:38
  31.8 1.4 %copy-done.1 = bf16[6,2,256,256]{3,2,1,0:T(8,128)(2,1)S(1)} copy-done((bf16[6,2,256,256]{3,2,1,0:T(8,128)(2,1)S(1)}, bf16[6,2,256,256]{3,2,1,0:T(8,128)(2,1)}, u32[]{:S(2)}) %copy-start.1) | copy-done | bytes 1572888
  33.2 1.3 %copy-done.2 = bf16[10,256,256]{2,1,0:T(8,128)(2,1)S(1)} copy-done((bf16[10,256,256]{2,1,0:T(8,128)(2,1)S(1)}, bf16[10,256,256]{2,1,0:T(8,128)(2,1)}, u32[]{:S(2)}) %copy-start.2) | copy-done | bytes 1310744
  37.8 20.4 %positions.1 = (bf16[2,12,64,256]{3,2,1,0:T(8,128)(2,1)S(1)}, f32[2,12,64,256]{3,2,1,0:T(8,128)S(1)}, f32[10,2,256,256]{3,2,1,0:T(8,128)S(1)}, f32[6,10]{1,0:T(8,128)}) custom-call(s32[2,10]{1,0:T(2,128)S(1)} %bitcast.83, s32[4,10]{1,0:T(4,128)S(1)} %bitcast.80, s32[1]{0:T(128)S(6)} %copy.11.group_counts, bf16[2,512,512]{2,1,0:T(8,128)(2,1)S(1)} %bitcast.71, ...), custom_call_target="tpu_custom_call" | custom-call | tf_op jit(solution)/shard_map/positions/pallas_call | solution.py:310
  58.3 2.3 %collective-permute-done.8 = bf16[2,12,64,256]{3,2,1,0:T(8,128)(2,1)S(1)} collective-permute-done((bf16[2,12,64,256]{3,2,1,0:T(8,128)(2,1)S(1)}, bf16[2,12,64,256]{3,2,1,0:T(8,128)(2,1)S(1)}, u32[]{:S(2)}, u32[]{:S(2)}) %collective-permute-start.8) | collective-permute-done | bytes 786464 | tf_op jit(solution)/shard_map/ppermute | solution.py:38
  61.4 6.3 %scatter.1 = (bf16[2,2,4,128,128]{4,3,2,1,0:T(8,128)(2,1)S(1)}, bf16[2,2,4,128,128]{4,3,2,1,0:T(8,128)(2,1)S(1)}, bf16[2,2,4,128,128]{4,3,2,1,0:T(8,128)(2,1)}, ...) custom-call(s32[2,10]{1,0:T(2,128)S(1)} %bitcast.84, ...), custom_call_target="tpu_custom_call" | custom-call | flops 16777216 | bytes 16777216 | tf_op jit(solution)/shard_map/scatter/pallas_call | solution.py:423
  70.5 1.4 %collective-permute-done.10 = bf16[1,12,64,256]{3,2,1,0:T(8,128)(2,1)S(1)} collective-permute-done((bf16[1,12,64,256]{3,2,1,0:T(8,128)(2,1)S(1)}, bf16[1,12,64,256]{3,2,1,0:T(8,128)(2,1)S(1)}, u32[]{:S(2)}, u32[]{:S(2)}) %collective-permute-start.10) | collective-permute-done | bytes 393248 | tf_op jit(solution)/shard_map/ppermute | solution.py:38
  72.4 2.1 %collective-permute-done.11 = bf16[2,2,4,128,128]{4,3,2,1,0:T(8,128)(2,1)} collective-permute-done((bf16[2,2,4,128,128]{4,3,2,1,0:T(8,128)(2,1)}, bf16[2,2,4,128,128]{4,3,2,1,0:T(8,128)(2,1)}, u32[]{:S(2)}, u32[]{:S(2)}) %collective-permute-start.11) | collective-permute-done | bytes 524320 | tf_op jit(solution)/shard_map/ppermute | solution.py:38
  77.4 4.6 %collective-permute-start.19 = (bf16[192,256]{1,0:T(8,128)(2,1)S(1)}, bf16[192,256]{1,0:T(8,128)(2,1)S(1)}, u32[]{:S(2)}, u32[]{:S(2)}) collective-permute-start(bf16[192,256]{1,0:T(8,128)(2,1)S(1)} %bitcast.94), channel_id=1, source_target_pairs={{0,8},{4,12},{8,0},{12,4},{1,9},{5,13},{9,1},{13,5},{2,10},{6,14},... | collective-permute-start | bytes 294920 | tf_op jit(solution)/shard_map/ppermute | solution.py:33
  82.0 2.2 %collective-permute-done.12 = bf16[1,2,4,128,128]{4,3,2,1,0:T(8,128)(2,1)S(1)} collective-permute-done((bf16[1,2,4,128,128]{4,3,2,1,0:T(8,128)(2,1)S(1)}, bf16[1,2,4,128,128]{4,3,2,1,0:T(8,128)(2,1)S(1)}, u32[]{:S(2)}, u32[]{:S(2)}) %collective-permute-start.12) | collective-permute-done | bytes 262176 | tf_op jit(solution)/shard_map/ppermute | solution.py:38
  84.1 2.8 %collective-permute-start.20 = (bf16[192,256]{1,0:T(8,128)(2,1)S(1)}, bf16[192,256]{1,0:T(8,128)(2,1)S(1)}, u32[]{:S(2)}, u32[]{:S(2)}) collective-permute-start(bf16[192,256]{1,0:T(8,128)(2,1)S(1)} %bitcast.93), channel_id=1, source_target_pairs={{0,12},{4,0},{8,4},{12,8},{1,13},{5,1},{9,5},{13,9},{2,14},{6,2},{... | collective-permute-start | bytes 294920 | tf_op jit(solution)/shard_map/ppermute | solution.py:33
  88.2 1.6 %collective-permute-start.16 = (bf16[1,2,4,128,128]{4,3,2,1,0:T(8,128)(2,1)S(1)}, bf16[1,2,4,128,128]{4,3,2,1,0:T(8,128)(2,1)S(1)}, u32[]{:S(2)}, u32[]{:S(2)}) collective-permute-start(bf16[1,2,4,128,128]{4,3,2,1,0:T(8,128)(2,1)S(1)} %fusion.18), channel_id=1, source_target_pairs={{0,2},{1,3},{2,0},{3,1},{4,6},{5,7},{6,4},{7,5},{8,10},{9,11},{10,... | collective-permute-start | bytes 786440 | tf_op jit(solution)/shard_map/ppermute | solution.py:38
  91.3 3.8 %collective-permute-start.22 = (bf16[192,256]{1,0:T(8,128)(2,1)S(1)}, bf16[192,256]{1,0:T(8,128)(2,1)S(1)}, u32[]{:S(2)}, u32[]{:S(2)}) collective-permute-start(bf16[192,256]{1,0:T(8,128)(2,1)S(1)} %fusion.21.refs_0_), channel_id=1, source_target_pairs={{0,8},{4,12},{8,0},{12,4},{1,9},{5,13},{9,1},{13,5},{2,10},{6,14},... | collective-permute-start | bytes 294920 | tf_op jit(solution)/shard_map/ppermute | solution.py:33
  95.0 4.2 %collective-permute-done.13 = bf16[2,4,128,128]{3,2,1,0:T(8,128)(2,1)S(1)} collective-permute-done((bf16[2,4,128,128]{3,2,1,0:T(8,128)(2,1)S(1)}, bf16[2,4,128,128]{3,2,1,0:T(8,128)(2,1)S(1)}, u32[]{:S(2)}, u32[]{:S(2)}) %collective-permute-start.13) | collective-permute-done | bytes 262176 | tf_op jit(solution)/shard_map/ppermute | solution.py:33
  99.3 1.6 %collective-permute-start.14 = (bf16[1,2,4,128,128]{4,3,2,1,0:T(8,128)(2,1)S(1)}, bf16[1,2,4,128,128]{4,3,2,1,0:T(8,128)(2,1)S(1)}, u32[]{:S(2)}, u32[]{:S(2)}) collective-permute-start(bf16[1,2,4,128,128]{4,3,2,1,0:T(8,128)(2,1)S(1)} %fusion.17), channel_id=1, source_target_pairs={{0,2},{1,3},{2,0},{3,1},{4,6},{5,7},{6,4},{7,5},{8,10},{9,11},{10,... | collective-permute-start | bytes 786440 | tf_op jit(solution)/shard_map/ppermute | solution.py:38
  101.4 5.0 %collective-permute-done.22.refs_2_ = bf16[192,256]{1,0:T(8,128)(2,1)S(1)} collective-permute-done((bf16[192,256]{1,0:T(8,128)(2,1)S(1)}, bf16[192,256]{1,0:T(8,128)(2,1)S(1)}, u32[]{:S(2)}, u32[]{:S(2)}) %collective-permute-start.22) | collective-permute-done | bytes 98336 | tf_op jit(solution)/shard_map/ppermute | solution.py:33
  107.4 1.9 %collective-permute-done.17.second = bf16[2,4,128,128]{3,2,1,0:T(8,128)(2,1)S(1)} collective-permute-done((bf16[2,4,128,128]{3,2,1,0:T(8,128)(2,1)S(1)}, bf16[2,4,128,128]{3,2,1,0:T(8,128)(2,1)S(1)}, u32[]{:S(2)}, u32[]{:S(2)}) %collective-permute-start.17) | collective-permute-done | bytes 262176 | tf_op jit(solution)/shard_map/ppermute | solution.py:33
  (67 shorter events, 18.9 us)
Async XLA Ops:
  1.6 10.7 %collective-permute-start = (bf16[2,128,512]{2,1,0:T(8,128)(2,1)S(1)}, bf16[2,128,512]{2,1,0:T(8,128)(2,1)S(1)}, u32[]{:S(2)}, u32[]{:S(2)}) collective-permute-start(bf16[2,128,512]{2,1,0:T(8,128)(2,1)S(1)} %dynamic-slice_bitcast_fusion), channel_id=1, source_target_pairs={{0,12},{4,0},{8,4},{12,8},{1,13},{5,1},{9,5},{13,9},{2,14},{6,2},{... | collective-permute-start | bytes 786440 | tf_op jit(solution)/shard_map/ppermute | solution.py:33
  12.3 9.0 %collective-permute-start.4 = (bf16[2,128,512]{2,1,0:T(8,128)(2,1)S(1)}, bf16[2,128,512]{2,1,0:T(8,128)(2,1)S(1)}, u32[]{:S(2)}, u32[]{:S(2)}) collective-permute-start(bf16[2,128,512]{2,1,0:T(8,128)(2,1)S(1)} %collective-permute-done.refs_1_), channel_id=1, source_target_pairs={{0,12},{4,0},{8,4},{12,8},{1,13},{5,1},{9,5},{13,9},{2,14},{6,2},{... | collective-permute-start | bytes 786440 | tf_op jit(solution)/shard_map/ppermute | solution.py:33
  16.6 8.4 %collective-permute-start.1 = (bf16[2,128,512]{2,1,0:T(8,128)(2,1)S(1)}, bf16[2,128,512]{2,1,0:T(8,128)(2,1)S(1)}, u32[]{:S(2)}, u32[]{:S(2)}) collective-permute-start(bf16[2,128,512]{2,1,0:T(8,128)(2,1)S(1)} %collective-permute-done.refs_1_), channel_id=1, source_target_pairs={{0,2},{1,3},{2,0},{3,1},{4,6},{5,7},{6,4},{7,5},{8,10},{9,11},{10,... | collective-permute-start | bytes 786440 | tf_op jit(solution)/shard_map/ppermute | solution.py:38
  21.3 7.8 %collective-permute-start.5 = (bf16[2,128,512]{2,1,0:T(8,128)(2,1)S(1)}, bf16[2,128,512]{2,1,0:T(8,128)(2,1)S(1)}, u32[]{:S(2)}, u32[]{:S(2)}) collective-permute-start(bf16[2,128,512]{2,1,0:T(8,128)(2,1)S(1)} %collective-permute-done.4.refs_5_), channel_id=1, source_target_pairs={{0,2},{1,3},{2,0},{3,1},{4,6},{5,7},{6,4},{7,5},{8,10},{9,11},{10,... | collective-permute-start | bytes 786440 | tf_op jit(solution)/shard_map/ppermute | solution.py:38
  22.7 7.0 %collective-permute-start.2 = (bf16[2,128,512]{2,1,0:T(8,128)(2,1)S(1)}, bf16[2,128,512]{2,1,0:T(8,128)(2,1)S(1)}, u32[]{:S(2)}, u32[]{:S(2)}) collective-permute-start(bf16[2,128,512]{2,1,0:T(8,128)(2,1)S(1)} %collective-permute-done.refs_1_), channel_id=1, source_target_pairs={{0,1},{1,0},{2,3},{3,2},{4,5},{5,4},{6,7},{7,6},{8,9},{9,8},{10,11... | collective-permute-start | bytes 786440 | tf_op jit(solution)/shard_map/ppermute | solution.py:38
  22.7 7.0 %collective-permute-start.6 = (bf16[2,128,512]{2,1,0:T(8,128)(2,1)S(1)}, bf16[2,128,512]{2,1,0:T(8,128)(2,1)S(1)}, u32[]{:S(2)}, u32[]{:S(2)}) collective-permute-start(bf16[2,128,512]{2,1,0:T(8,128)(2,1)S(1)} %collective-permute-done.4.refs_5_), channel_id=1, source_target_pairs={{0,1},{1,0},{2,3},{3,2},{4,5},{5,4},{6,7},{7,6},{8,9},{9,8},{10,11... | collective-permute-start | bytes 786440 | tf_op jit(solution)/shard_map/ppermute | solution.py:38
  25.0 4.8 %collective-permute-start.3 = (bf16[2,128,512]{2,1,0:T(8,128)(2,1)S(1)}, bf16[2,128,512]{2,1,0:T(8,128)(2,1)S(1)}, u32[]{:S(2)}, u32[]{:S(2)}) collective-permute-start(bf16[2,128,512]{2,1,0:T(8,128)(2,1)S(1)} %collective-permute-done.1.refs_2_), channel_id=1, source_target_pairs={{0,1},{1,0},{2,3},{3,2},{4,5},{5,4},{6,7},{7,6},{8,9},{9,8},{10,11... | collective-permute-start | bytes 786440 | tf_op jit(solution)/shard_map/ppermute | solution.py:38
  29.1 1.5 %collective-permute-start.7 = (bf16[2,128,512]{2,1,0:T(8,128)(2,1)S(1)}, bf16[2,128,512]{2,1,0:T(8,128)(2,1)S(1)}, u32[]{:S(2)}, u32[]{:S(2)}) collective-permute-start(bf16[2,128,512]{2,1,0:T(8,128)(2,1)S(1)} %collective-permute-done.5.refs_6_), channel_id=1, source_target_pairs={{0,1},{1,0},{2,3},{3,2},{4,5},{5,4},{6,7},{7,6},{8,9},{9,8},{10,11... | collective-permute-start | bytes 786440 | tf_op jit(solution)/shard_map/ppermute | solution.py:38
  58.2 2.4 %collective-permute-start.8 = (bf16[2,12,64,256]{3,2,1,0:T(8,128)(2,1)S(1)}, bf16[2,12,64,256]{3,2,1,0:T(8,128)(2,1)S(1)}, u32[]{:S(2)}, u32[]{:S(2)}) collective-permute-start(bf16[2,12,64,256]{3,2,1,0:T(8,128)(2,1)S(1)} %get-tuple-element.21), channel_id=1, source_target_pairs={{0,1},{1,0},{2,3},{3,2},{4,5},{5,4},{6,7},{7,6},{8,9},{9,8},{10,11... | collective-permute-start | bytes 2359304 | tf_op jit(solution)/shard_map/ppermute | solution.py:38
  60.7 11.2 %collective-permute-start.10 = (bf16[1,12,64,256]{3,2,1,0:T(8,128)(2,1)S(1)}, bf16[1,12,64,256]{3,2,1,0:T(8,128)(2,1)S(1)}, u32[]{:S(2)}, u32[]{:S(2)}) collective-permute-start(bf16[1,12,64,256]{3,2,1,0:T(8,128)(2,1)S(1)} %fusion.15), channel_id=1, source_target_pairs={{0,2},{1,3},{2,0},{3,1},{4,6},{5,7},{6,4},{7,5},{8,10},{9,11},{10,... | collective-permute-start | bytes 1179656 | tf_op jit(solution)/shard_map/ppermute | solution.py:38
  71.9 2.6 %collective-permute-start.11 = (bf16[2,2,4,128,128]{4,3,2,1,0:T(8,128)(2,1)}, bf16[2,2,4,128,128]{4,3,2,1,0:T(8,128)(2,1)}, u32[]{:S(2)}, u32[]{:S(2)}) collective-permute-start(bf16[2,2,4,128,128]{4,3,2,1,0:T(8,128)(2,1)} %get-tuple-element.27), channel_id=1, source_target_pairs={{0,1},{1,0},{2,3},{3,2},{4,5},{5,4},{6,7},{7,6},{8,9},{9,8},{10,11... | collective-permute-start | bytes 1572872 | tf_op jit(solution)/shard_map/ppermute | solution.py:38
  71.9 16.1 %collective-permute-start.15 = (bf16[2,2,4,128,128]{4,3,2,1,0:T(8,128)(2,1)}, bf16[2,2,4,128,128]{4,3,2,1,0:T(8,128)(2,1)S(1)}, u32[]{:S(2)}, u32[]{:S(2)}) collective-permute-start(bf16[2,2,4,128,128]{4,3,2,1,0:T(8,128)(2,1)} %copy-done.11), channel_id=1, source_target_pairs={{0,1},{1,0},{2,3},{3,2},{4,5},{5,4},{6,7},{7,6},{8,9},{9,8},{10,11... | collective-permute-start | bytes 1572872 | tf_op jit(solution)/shard_map/ppermute | solution.py:38
  72.4 22.6 %collective-permute-start.9 = (bf16[2,2,4,128,128]{4,3,2,1,0:T(8,128)(2,1)S(1)}, bf16[2,2,4,128,128]{4,3,2,1,0:T(8,128)(2,1)S(1)}, u32[]{:S(2)}, u32[]{:S(2)}) collective-permute-start(bf16[2,2,4,128,128]{4,3,2,1,0:T(8,128)(2,1)S(1)} %get-tuple-element.24), channel_id=1, source_target_pairs={{0,1},{1,0},{2,3},{3,2},{4,5},{5,4},{6,7},{7,6},{8,9},{9,8},{10,11... | collective-permute-start | bytes 1572872 | tf_op jit(solution)/shard_map/ppermute | solution.py:38
  75.7 8.4 %collective-permute-start.12 = (bf16[1,2,4,128,128]{4,3,2,1,0:T(8,128)(2,1)S(1)}, bf16[1,2,4,128,128]{4,3,2,1,0:T(8,128)(2,1)S(1)}, u32[]{:S(2)}, u32[]{:S(2)}) collective-permute-start(bf16[1,2,4,128,128]{4,3,2,1,0:T(8,128)(2,1)S(1)} %fusion.16), channel_id=1, source_target_pairs={{0,2},{1,3},{2,0},{3,1},{4,6},{5,7},{6,4},{7,5},{8,10},{9,11},{10,... | collective-permute-start | bytes 786440 | tf_op jit(solution)/shard_map/ppermute | solution.py:38
  77.3 10.9 %collective-permute-start.18 = (bf16[192,256]{1,0:T(8,128)(2,1)S(1)}, bf16[192,256]{1,0:T(8,128)(2,1)S(1)}, u32[]{:S(2)}, u32[]{:S(2)}) collective-permute-start(bf16[192,256]{1,0:T(8,128)(2,1)S(1)} %bitcast.95), channel_id=1, source_target_pairs={{0,4},{4,8},{8,12},{12,0},{1,5},{5,9},{9,13},{13,1},{2,6},{6,10},{... | collective-permute-start | bytes 294920 | tf_op jit(solution)/shard_map/ppermute | solution.py:33
  77.4 12.4 %collective-permute-start.19 = (bf16[192,256]{1,0:T(8,128)(2,1)S(1)}, bf16[192,256]{1,0:T(8,128)(2,1)S(1)}, u32[]{:S(2)}, u32[]{:S(2)}) collective-permute-start(bf16[192,256]{1,0:T(8,128)(2,1)S(1)} %bitcast.94), channel_id=1, source_target_pairs={{0,8},{4,12},{8,0},{12,4},{1,9},{5,13},{9,1},{13,5},{2,10},{6,14},... | collective-permute-start | bytes 294920 | tf_op jit(solution)/shard_map/ppermute | solution.py:33
  84.1 6.0 %collective-permute-start.20 = (bf16[192,256]{1,0:T(8,128)(2,1)S(1)}, bf16[192,256]{1,0:T(8,128)(2,1)S(1)}, u32[]{:S(2)}, u32[]{:S(2)}) collective-permute-start(bf16[192,256]{1,0:T(8,128)(2,1)S(1)} %bitcast.93), channel_id=1, source_target_pairs={{0,12},{4,0},{8,4},{12,8},{1,13},{5,1},{9,5},{13,9},{2,14},{6,2},{... | collective-permute-start | bytes 294920 | tf_op jit(solution)/shard_map/ppermute | solution.py:33
  88.0 11.2 %collective-permute-start.13 = (bf16[2,4,128,128]{3,2,1,0:T(8,128)(2,1)S(1)}, bf16[2,4,128,128]{3,2,1,0:T(8,128)(2,1)S(1)}, u32[]{:S(2)}, u32[]{:S(2)}) collective-permute-start(bf16[2,4,128,128]{3,2,1,0:T(8,128)(2,1)S(1)} %fusion.12), channel_id=1, source_target_pairs={{0,4},{4,8},{8,12},{12,0},{1,5},{5,9},{9,13},{13,1},{2,6},{6,10},{... | collective-permute-start | bytes 786440 | tf_op jit(solution)/shard_map/ppermute | solution.py:33
  88.2 12.7 %collective-permute-start.16 = (bf16[1,2,4,128,128]{4,3,2,1,0:T(8,128)(2,1)S(1)}, bf16[1,2,4,128,128]{4,3,2,1,0:T(8,128)(2,1)S(1)}, u32[]{:S(2)}, u32[]{:S(2)}) collective-permute-start(bf16[1,2,4,128,128]{4,3,2,1,0:T(8,128)(2,1)S(1)} %fusion.18), channel_id=1, source_target_pairs={{0,2},{1,3},{2,0},{3,1},{4,6},{5,7},{6,4},{7,5},{8,10},{9,11},{10,... | collective-permute-start | bytes 786440 | tf_op jit(solution)/shard_map/ppermute | solution.py:38
  90.2 11.2 %collective-permute-start.21 = (bf16[192,256]{1,0:T(8,128)(2,1)S(1)}, bf16[192,256]{1,0:T(8,128)(2,1)S(1)}, u32[]{:S(2)}, u32[]{:S(2)}) collective-permute-start(bf16[192,256]{1,0:T(8,128)(2,1)S(1)} %fusion.21.refs_0_), channel_id=1, source_target_pairs={{0,4},{4,8},{8,12},{12,0},{1,5},{5,9},{9,13},{13,1},{2,6},{6,10},{... | collective-permute-start | bytes 294920 | tf_op jit(solution)/shard_map/ppermute | solution.py:33
  91.3 15.1 %collective-permute-start.22 = (bf16[192,256]{1,0:T(8,128)(2,1)S(1)}, bf16[192,256]{1,0:T(8,128)(2,1)S(1)}, u32[]{:S(2)}, u32[]{:S(2)}) collective-permute-start(bf16[192,256]{1,0:T(8,128)(2,1)S(1)} %fusion.21.refs_0_), channel_id=1, source_target_pairs={{0,8},{4,12},{8,0},{12,4},{1,9},{5,13},{9,1},{13,5},{2,10},{6,14},... | collective-permute-start | bytes 294920 | tf_op jit(solution)/shard_map/ppermute | solution.py:33
  95.0 11.4 %collective-permute-start.23 = (bf16[192,256]{1,0:T(8,128)(2,1)S(1)}, bf16[192,256]{1,0:T(8,128)(2,1)S(1)}, u32[]{:S(2)}, u32[]{:S(2)}) collective-permute-start(bf16[192,256]{1,0:T(8,128)(2,1)S(1)} %fusion.21.refs_0_), channel_id=1, source_target_pairs={{0,12},{4,0},{8,4},{12,8},{1,13},{5,1},{9,5},{13,9},{2,14},{6,2},{... | collective-permute-start | bytes 294920 | tf_op jit(solution)/shard_map/ppermute | solution.py:33
  99.3 8.0 %collective-permute-start.14 = (bf16[1,2,4,128,128]{4,3,2,1,0:T(8,128)(2,1)S(1)}, bf16[1,2,4,128,128]{4,3,2,1,0:T(8,128)(2,1)S(1)}, u32[]{:S(2)}, u32[]{:S(2)}) collective-permute-start(bf16[1,2,4,128,128]{4,3,2,1,0:T(8,128)(2,1)S(1)} %fusion.17), channel_id=1, source_target_pairs={{0,2},{1,3},{2,0},{3,1},{4,6},{5,7},{6,4},{7,5},{8,10},{9,11},{10,... | collective-permute-start | bytes 786440 | tf_op jit(solution)/shard_map/ppermute | solution.py:38
  101.0 8.3 %collective-permute-start.17 = (bf16[2,4,128,128]{3,2,1,0:T(8,128)(2,1)S(1)}, bf16[2,4,128,128]{3,2,1,0:T(8,128)(2,1)S(1)}, u32[]{:S(2)}, u32[]{:S(2)}) collective-permute-start(bf16[2,4,128,128]{3,2,1,0:T(8,128)(2,1)S(1)} %fusion.7), channel_id=1, source_target_pairs={{0,4},{4,8},{8,12},{12,0},{1,5},{5,9},{9,13},{13,1},{2,6},{6,10},{... | collective-permute-start | bytes 786440 | tf_op jit(solution)/shard_map/ppermute | solution.py:33
  (13 other events, 31.5 us)

commit v3 on v2

--- a/solution.py
+++ b/solution.py
@@ -44,7 +44,7 @@
     return mine, mine ^ 1
 
 
-def turned(groups, peers):
+def share_of(groups, peers):
     return groups // peers if groups % peers == 0 else 0
 
 
@@ -81,13 +81,39 @@
     return high, (array - high.astype(jnp.float32)).astype(jnp.bfloat16)
 
 
+def stage_kernel(*refs):
+    count = len(refs) // 2
+    sem = refs[-1]
+    copies = [
+        pltpu.make_async_copy(source, target, sem.at[i])
+        for i, (source, target) in enumerate(zip(refs[:count], refs[count:2 * count]))
+    ]
+    for copy in copies:
+        copy.start()
+    for copy in copies:
+        copy.wait()
+
+
+def stage(*arrays):
+    anywhere = pl.BlockSpec(memory_space=pl.ANY)
+    return pl.pallas_call(
+        stage_kernel,
+        in_specs=[anywhere] * len(arrays),
+        out_specs=[anywhere] * len(arrays),
+        scratch_shapes=[pltpu.SemaphoreType.DMA((len(arrays),))],
+        out_shape=[jax.ShapeDtypeStruct(x.shape, x.dtype) for x in arrays],
+        compiler_params=pltpu.CompilerParams(vmem_limit_bytes=1024 * 1024),
+        name="stage",
+    )(*arrays)
+
+
 def position_kernel(offs, scale, tile_list, offsets, group_counts, *refs):
     shares = len(offs)
     pieces = refs[: 1 + (REACH - 1) * shares]
-    tables_in, amps_in, eig, coef_in = refs[len(pieces):len(pieces) + 4]
+    eig_in, amps_in, tables_in, coef_in = refs[len(pieces):len(pieces) + 4]
     eigen_send, eigen_keep, grads_out, coef = refs[len(pieces) + 4:len(pieces) + 8]
-    (staged, table, probe, amps, obj, ex, mid, far, patch, d_high, d_low, eigen, out_eigen, cross,
-     weights, weights_t, piece_sem, table_sem, amps_sem, grad_sem, out_sem) = refs[len(pieces) + 8:]
+    (staged, table, probe, amps, eig, obj, ex, mid, far, patch, d_high, d_low, eigen, out_eigen, cross,
+     weights, weights_t, piece_sem, table_sem, amps_sem, eig_sem, grad_sem, out_sem) = refs[len(pieces) + 8:]
     pos_dev, _, frame, _ = probe.shape
     modes = eig.shape[0]
     side = staged.shape[2]
@@ -108,7 +134,8 @@
             )
     table_copy = pltpu.make_async_copy(tables_in, table, table_sem)
     amps_copy = pltpu.make_async_copy(amps_in, amps, amps_sem)
-    for copy in copies + [table_copy, amps_copy]:
+    eig_copy = pltpu.make_async_copy(eig_in, eig, eig_sem)
+    for copy in [eig_copy] + copies + [table_copy, amps_copy]:
         copy.start()
 
     by_position = (pos_dev * STRIP, pos_dev)
@@ -122,6 +149,7 @@
     )
     high, low = two_terms(diagonals(exact(spread, one_hot(by_mode[::-1], 1))))
     weights[...] = jnp.concatenate([high, low], 1)
+    eig_copy.wait()
 
     def synth(i, carry):
         rows = pl.ds(pl.multiple_of(i * STRIP, STRIP), STRIP)
@@ -246,7 +274,7 @@
     cross[...] = jnp.zeros_like(cross)
     rows_q = frame // shares
     groups = 2 * modes
-    turn = my_block * turned(groups, lax.axis_size("blk"))
+    share = share_of(groups, lax.axis_size("blk"))
 
     def eigen_strip(i, carry):
         rows = pl.ds(pl.multiple_of(i * STRIP, STRIP), STRIP)
@@ -260,7 +288,9 @@
             rest = jnp.dot(weights_t[:modes * STRIP], low, preferred_element_type=jnp.float32)
             grad = (both[:modes * STRIP] + both[modes * STRIP:] + rest) * scale
             for k in range(modes):
-                group = lax.rem(2 * k + c + groups - turn, groups)
+                group = 2 * k + c
+                if share:
+                    group = (group // share ^ my_block) * share + group % share
                 eigen[q, group, inner, :] = grad[k * STRIP:(k + 1) * STRIP]
             cross[...] += lax.dot_general(
                 high, e, (((1,), (1,)), ((), ())), preferred_element_type=jnp.float32
@@ -296,7 +326,7 @@
         copy.wait()
 
 
-def positions(offs, scale, indices, pieces, table, amps, eigenprobes, coefficients):
+def positions(offs, scale, indices, pieces, eigenprobes, amps, table, coef_t):
     modes, _, frame, _ = eigenprobes.shape
     pos_dev = amps.shape[0]
     side = pieces[0].shape[2]
@@ -309,13 +339,14 @@
     grads = (pos_dev, 2, frame, frame)
     return pl.pallas_call(
         functools.partial(position_kernel, offs, scale),
-        in_specs=[smem] * 3 + [anywhere] * (len(pieces) + 2) + [whole] * 2,
+        in_specs=[smem] * 3 + [anywhere] * (len(pieces) + 3) + [whole],
         out_specs=[anywhere] * 3 + [whole],
         scratch_shapes=[
             pltpu.VMEM((REACH, 2, side, side), jnp.bfloat16),
             pltpu.VMEM(table.shape, jnp.bfloat16),
             pltpu.VMEM(grads, jnp.float32),
             pltpu.VMEM(amps.shape, jnp.bfloat16),
+            pltpu.VMEM(eigenprobes.shape, jnp.bfloat16),
             pltpu.VMEM((REACH, 2, blocks + 1, side, LANES), jnp.float32),
             pltpu.VMEM((2, frame, 2 * frame), jnp.bfloat16),
             pltpu.VMEM((2, 2 * frame, frame), jnp.bfloat16),
@@ -331,6 +362,7 @@
             pltpu.SemaphoreType.DMA((len(pieces),)),
             pltpu.SemaphoreType.DMA,
             pltpu.SemaphoreType.DMA,
+            pltpu.SemaphoreType.DMA,
             pltpu.SemaphoreType.DMA((pos_dev,)),
             pltpu.SemaphoreType.DMA((shares // 2 + 1,)),
         ],
@@ -342,7 +374,7 @@
         ],
         compiler_params=pltpu.CompilerParams(vmem_limit_bytes=VMEM_LIMIT),
         name="positions",
-    )(*indices, *pieces, table, amps, eigenprobes, coefficients.T)
+    )(*indices, *pieces, eigenprobes, amps, table, coef_t)
 
 
 def scatter_kernel(shares, tile_list, offsets, group_counts, grads_in, *refs):
@@ -443,6 +475,10 @@
     return lax.optimization_barrier((array,) + others)[0]
 
 
+def after_all(arrays, *others):
+    return lax.optimization_barrier(tuple(arrays) + others)[:len(arrays)]
+
+
 def halve(keep, send, before_core=(), before_cross=()):
     arrived = swap(after(send, *before_core), "probe", 1)
     terms = [keep, after(arrived, *before_cross)]
@@ -459,40 +495,62 @@
     return sum(term[0].astype(jnp.float32) for term in terms), leaving, arrived
 
 
-def place_kernel(me, *refs):
+def next_tiles(own, axis):
+    peers = lax.axis_size(axis)
+    near = lax.ppermute(own, axis, [(i, i - 1) for i in range(1, peers)])
+    around = lax.ppermute(own, axis, [(0, peers - 1)])
+    far_around = lax.ppermute(own, axis, [(0, peers - 2), (1, peers - 1)])
+    far = lax.ppermute(near, axis, [(i, i - 1) for i in range(1, peers - 1)])
+    return near + around, far + far_around
+
+
+def scatter_rows(axis, value):
+    me = lax.axis_index(axis)
+    total = lax.dynamic_index_in_dim(value, me, 0, False)
+    sent = []
+    for i in range(1, lax.axis_size(axis)):
+        sent.append(lax.dynamic_index_in_dim(value, me ^ i, 0, False).astype(jnp.bfloat16))
+        total += swap(sent[-1], axis, i).astype(jnp.float32)
+    return total.astype(jnp.bfloat16), sent
+
+
+def scatter_sum(axis, value):
+    terms = [value]
+    sent = []
+    bit = 1
+    while bit < lax.axis_size(axis):
+        pick = lambda term, which: term.reshape((term.shape[0] // 2, 2) + term.shape[1:])[:, which]
+        sent.append(sum(pick(term, 1).astype(jnp.float32) for term in terms).astype(jnp.bfloat16))
+        terms = [pick(term, 0) for term in terms] + [swap(sent[-1], axis, bit)]
+        bit *= 2
+    return sum(term[0].astype(jnp.float32) for term in terms).astype(jnp.bfloat16), sent
+
+
+def gather_shares(axis, total):
+    held = {0: total}
+    bit = lax.axis_size(axis) // 2
+    while bit:
+        held.update({i ^ bit: swap(piece, axis, bit) for i, piece in held.items()})
+        bit //= 2
+    return [held[i] for i in range(lax.axis_size(axis))]
+
+
+def place_kernel(axis, *refs):
     pieces, out = refs[:-1], refs[-1]
-    peers = len(pieces)
-    for by, piece in enumerate(pieces):
-        out[(me[0] + peers - by) % peers] = piece[...].astype(jnp.float32)
-
-
-def sum_over(axis, value, turned):
-    peers = lax.axis_size(axis)
     me = lax.axis_index(axis)
-    rows = value.shape[0] // peers
-
-    def chunk(by):
-        if turned:
-            return value[by * rows:(by + 1) * rows]
-        return lax.dynamic_slice_in_dim(value, (me + by) % peers * rows, rows, 0)
-
-    total = chunk(0)
-    for by in range(1, peers):
-        total += shift(chunk(by).astype(jnp.bfloat16), axis, by).astype(jnp.float32)
-    total = total.astype(jnp.bfloat16)
-    return [total] + [shift(total, axis, by) for by in range(1, peers)]
+    for i, piece in enumerate(pieces):
+        out[me ^ i] = piece[...].astype(jnp.float32)
 
 
 def place(axis, held):
-    peers, (rows, lanes) = len(held), held[0].shape
     return pl.pallas_call(
-        place_kernel,
-        in_specs=[pl.BlockSpec(memory_space=SMEM)] + [pl.BlockSpec(memory_space=VMEM)] * peers,
+        functools.partial(place_kernel, axis),
+        in_specs=[pl.BlockSpec(memory_space=VMEM)] * len(held),
         out_specs=pl.BlockSpec(memory_space=VMEM),
-        out_shape=jax.ShapeDtypeStruct((peers, rows, lanes), jnp.float32),
+        out_shape=jax.ShapeDtypeStruct((len(held),) + held[0].shape, jnp.float32),
         compiler_params=pltpu.CompilerParams(vmem_limit_bytes=8 * 1024 * 1024),
         name="place",
-    )(lax.axis_index(axis).reshape(1).astype(jnp.int32), *held)
+    )(*held)
 
 
 def finish_kernel(first, second, out):
@@ -523,43 +581,52 @@
     member = lax.axis_index("probe")
     slab = side // shares
     bits = [1 << i for i in range(shares.bit_length() - 1)]
-    table = tables(frame)
-
-    own = lax.dynamic_slice_in_dim(tiles[0], member * slab, slab, 1)
-    pieces = [tiles[0]]
+
     offs = [0]
     for bit in reversed(bits):
         offs = offs + [o ^ bit for o in offs]
-    moving = own
-    for section in range(1, REACH):
-        moving = shift(moving, "blk", -1)
-        held = [moving]
-        for bit in reversed(bits):
-            held = held + [swap(piece, "probe", bit) for piece in held]
-        pieces += held
-
-    indices = (tile_list.T, offsets.T, group_counts)
+    quarter = lax.dynamic_slice_in_dim(tiles[0], member * slab, slab, 1)
+    near, far = next_tiles(quarter, "blk")
+    held = [[near], [far]]
+    eig, amps = stage(*after_all((eigenprobes, amplitudes), near))
+    held[1][0] = after(held[1][0], eig)
+    table, tile, coef_t, lists, corners = stage(
+        *after_all((tables(frame), tiles[0], coefficients.T, tile_list.T, offsets.T), held[1][0])
+    )
+    for bit in reversed(bits):
+        for part in held:
+            arrived = [swap(piece, "probe", bit) for piece in part]
+            if bit > 1:
+                arrived[0] = after(arrived[0], eig if part is held[0] else table)
+            part += arrived
+
+    indices = (lists, corners, group_counts)
     scale = (pos_dev * blocks * shares) ** (-0.5)
     eigen_send, eigen_keep, grads, coef_rows = positions(
-        tuple(offs), scale, indices, pieces, table, amplitudes, eigenprobes, coefficients
+        tuple(offs), scale, indices, [tile] + held[0] + held[1], eig, amps, table, coef_t
     )
 
     eigen, leaving, crossed = halve(eigen_keep, eigen_send)
     out = scatter(shares, side, indices, after(grads, leaving))
     send, keep = out[:REACH], out[REACH:]
     last = REACH - 1
-    mine, leaving, crossed = halve(keep[last], send[last], before_core=(crossed,))
-    eigen = after(eigen, leaving)
-    held = sum_over("blk", eigen.reshape(-1, frame), turned(2 * modes, blocks) > 0)
-    moving = mine.astype(jnp.bfloat16)
-    gate = moving
+    share = share_of(2 * modes, blocks)
+    if share:
+        total, sent = scatter_sum("blk", eigen.reshape((blocks, share) + eigen.shape[1:]))
+    else:
+        total, sent = scatter_rows("blk", eigen.reshape(blocks, -1, frame))
+    mine, leaving, _ = halve(keep[last], send[last], before_core=(crossed,), before_cross=sent[:1])
+    moving = after(mine.astype(jnp.bfloat16), *sent[1:])
     for section in range(last - 1, -1, -1):
-        mine, _, _ = halve(keep[section], send[section], before_cross=(gate,))
-        gate = arrived = shift(moving, "blk", 1)
+        mine, leaving, _ = halve(keep[section], send[section], before_cross=(moving,))
+        if section == last - 1:
+            total = after(total, leaving)
+        arrived = shift(moving, "blk", 1)
         if section > 0:
             moving = (arrived.astype(jnp.float32) + mine).astype(jnp.bfloat16)
-    eigen_share = place("blk", [after(held[0], moving)] + held[1:])
-    eigen_share = eigen_share.reshape(modes, 2, frame // shares, frame)
+    shares_of_eigen = gather_shares("blk", total)
+    shares_of_eigen[0] = after(shares_of_eigen[0], leaving)
+    eigen_share = place("blk", shares_of_eigen).reshape(modes, 2, frame // shares, frame)
     summed = finish(mine, arrived)
     return (summed[None], eigen_share, coef_rows.T)
 

time: 111 us -> 114 us (1.027)
  waiting for transfers between devices: 35.2 us -> 44.7 us
  local copies, waits for them, and re-layouts: 11.7 us -> 2.56 us
  starting transfers between devices: 29.4 us -> 35.8 us
  other arithmetic: 3.87 us -> 0.96 us
    ppermute x10 -> x2, starting transfers between devices: 21.8 us -> 3.7 us  [shift(): lax.ppermute(array, axis, [(i, (i + by) % peers) for i in range(peers)])]
    ppermute x14 -> x19, waiting for transfers between devices: 14.6 us -> 30.4 us  [swap(): return lax.ppermute(array, axis, [(i, i ^ bit) for i in range(peers)])]
    ppermute x14 -> x19, starting transfers between devices: 7.61 us -> 20.2 us  [swap(): return lax.ppermute(array, axis, [(i, i ^ bit) for i in range(peers)])]
    ppermute x0 -> x4, starting transfers between devices: none -> 11.9 us  [the longest x1 8.05 us: next_tiles(): around = lax.ppermute(own, axis, [(0, peers - 1)])]
    ppermute x10 -> x2, waiting for transfers between devices: 20.6 us -> 8.95 us  [shift(): lax.ppermute(array, axis, [(i, (i + by) % peers) for i in range(peers)])]
    unnamed x26 -> x14, local copies, waits for them, and re-layouts: 10.6 us -> 1.43 us
    ppermute x0 -> x4, waiting for transfers between devices: none -> 5.36 us  [the longest x1 3.59 us: next_tiles(): around = lax.ppermute(own, axis, [(0, peers - 1)])]
    convert_element_type x4 -> x3, other arithmetic: 1.41 us -> 0.17 us  [halve(): sum((pick(term, 1).astype(jnp.float32) for term in terms))]
  transfers between devices with their start and end apart: 24 -> 25, of which waited for: 14 -> 16; matrix products, arithmetic and copies ran while one was open for 3% -> 1% of each run, Pallas kernels for 7% -> 6%
where the time goes in v3:
time: 114 us
  waiting for transfers between devices  44.7 us (39%)
  starting transfers between devices  35.8 us (31%)
  Pallas kernels  28.6 us (25%)
  local copies, waits for them, and re-layouts  2.56 us (2%)
  between operations  1.55 us (1%)
    ppermute x19, waiting for transfers between devices, swap(): return lax.ppermute(array, axis, [(i, i ^ bit) for i in range(peers)])  30.4 us
    pallas_call x1, Pallas kernels, positions(): pl.pallas_call(functools.partial(position_kernel, offs, scale), in_specs=...  20.5 us
    ppermute x19, starting transfers between devices, swap(): return lax.ppermute(array, axis, [(i, i ^ bit) for i in range(peers)])  20.2 us
    ppermute x2, waiting for transfers between devices, shift(): lax.ppermute(array, axis, [(i, (i + by) % peers) for i in range(peers)])  8.95 us
    ppermute x1, starting transfers between devices, next_tiles(): around = lax.ppermute(own, axis, [(0, peers - 1)])  8.05 us
    pallas_call x1, Pallas kernels, scatter(): pl.pallas_call(functools.partial(scatter_kernel, shares), in_specs=[pl.Bl...  5.91 us
    ppermute x2, starting transfers between devices, shift(): lax.ppermute(array, axis, [(i, (i + by) % peers) for i in range(peers)])  3.7 us
    ppermute x1, waiting for transfers between devices, next_tiles(): around = lax.ppermute(own, axis, [(0, peers - 1)])  3.59 us
  transfers between devices with their start and end apart: 25, of which 16 were waited for; matrix products, arithmetic and copies ran while one was open for 1% of the time, Pallas kernels for 6%

profile of v3, /device:TPU:0, one launch (start us, length us, event | category | flops | bytes accessed | tf_op | source)
XLA Modules:
  0.0 114.2 jit_solution(2866638232055974641)
XLA Ops:
  1.7 1.3 %collective-permute-start = (bf16[2,128,512]{2,1,0:T(8,128)(2,1)S(1)}, bf16[2,128,512]{2,1,0:T(8,128)(2,1)S(1)}, u32[]{:S(2)}, u32[]{:S(2)}) collective-permute-start(bf16[2,128,512]{2,1,0:T(8,128)(2,1)S(1)} %dynamic-slice_bitcast_fusion), channel_id=1, source_target_pairs={{4,0},{8,4},{12,8},{5,1},{9,5},{13,9},{6,2},{10,6},{14,10},{7,3},{... | collective-permute-start | bytes 786440 | tf_op jit(solution)/shard_map/ppermute | solution.py:500
  3.0 8.0 %collective-permute-start.3 = (bf16[2,128,512]{2,1,0:T(8,128)(2,1)S(1)}, bf16[2,128,512]{2,1,0:T(8,128)(2,1)S(1)}, u32[]{:S(2)}, u32[]{:S(2)}) collective-permute-start(bf16[2,128,512]{2,1,0:T(8,128)(2,1)S(1)} %dynamic-slice_bitcast_fusion), channel_id=1, source_target_pairs={{0,12},{1,13},{2,14},{3,15},{16,28},{17,29},{18,30},{19,31}} | collective-permute-start | bytes 786440 | tf_op jit(solution)/shard_map/ppermute | solution.py:501
  11.1 1.3 %collective-permute-start.2 = (bf16[2,128,512]{2,1,0:T(8,128)(2,1)S(1)}, bf16[2,128,512]{2,1,0:T(8,128)(2,1)S(1)}, u32[]{:S(2)}, u32[]{:S(2)}) collective-permute-start(bf16[2,128,512]{2,1,0:T(8,128)(2,1)S(1)} %dynamic-slice_bitcast_fusion), channel_id=1, source_target_pairs={{0,8},{4,12},{1,9},{5,13},{2,10},{6,14},{3,11},{7,15},{16,24},{20,... | collective-permute-start | bytes 786440 | tf_op jit(solution)/shard_map/ppermute | solution.py:502
  14.2 3.6 %collective-permute-done.3 = bf16[2,128,512]{2,1,0:T(8,128)(2,1)S(1)} collective-permute-done((bf16[2,128,512]{2,1,0:T(8,128)(2,1)S(1)}, bf16[2,128,512]{2,1,0:T(8,128)(2,1)S(1)}, u32[]{:S(2)}, u32[]{:S(2)}) %collective-permute-start.3) | collective-permute-done | bytes 262176 | tf_op jit(solution)/shard_map/ppermute | solution.py:501
  17.9 1.6 %collective-permute-start.4 = (bf16[2,128,512]{2,1,0:T(8,128)(2,1)S(1)}, bf16[2,128,512]{2,1,0:T(8,128)(2,1)S(1)}, u32[]{:S(2)}, u32[]{:S(2)}) collective-permute-start(bf16[2,128,512]{2,1,0:T(8,128)(2,1)S(1)} %add.121.refs_1_), channel_id=1, source_target_pairs={{0,2},{1,3},{2,0},{3,1},{4,6},{5,7},{6,4},{7,5},{8,10},{9,11},{10,... | collective-permute-start | bytes 786440 | tf_op jit(solution)/shard_map/ppermute | solution.py:38
  19.5 1.4 %copy-done.1 = bf16[6,2,256,256]{3,2,1,0:T(8,128)(2,1)S(1)} copy-done((bf16[6,2,256,256]{3,2,1,0:T(8,128)(2,1)S(1)}, bf16[6,2,256,256]{3,2,1,0:T(8,128)(2,1)}, u32[]{:S(2)}) %copy-start.1) | copy-done | bytes 1572888
  22.4 1.4 %collective-permute-start.7 = (bf16[2,128,512]{2,1,0:T(8,128)(2,1)S(1)}, bf16[2,128,512]{2,1,0:T(8,128)(2,1)S(1)}, u32[]{:S(2)}, u32[]{:S(2)}) collective-permute-start(bf16[2,128,512]{2,1,0:T(8,128)(2,1)S(1)} %add.120.refs_5_), channel_id=1, source_target_pairs={{0,2},{1,3},{2,0},{3,1},{4,6},{5,7},{6,4},{7,5},{8,10},{9,11},{10,... | collective-permute-start | bytes 786440 | tf_op jit(solution)/shard_map/ppermute | solution.py:38
  25.5 4.5 %collective-permute-done.7.refs_6_ = bf16[2,128,512]{2,1,0:T(8,128)(2,1)S(1)} collective-permute-done((bf16[2,128,512]{2,1,0:T(8,128)(2,1)S(1)}, bf16[2,128,512]{2,1,0:T(8,128)(2,1)S(1)}, u32[]{:S(2)}, u32[]{:S(2)}) %collective-permute-start.7) | collective-permute-done | bytes 262176 | tf_op jit(solution)/shard_map/ppermute | solution.py:38
  31.5 20.5 %positions.1 = (bf16[2,12,64,256]{3,2,1,0:T(8,128)(2,1)S(1)}, f32[2,12,64,256]{3,2,1,0:T(8,128)S(1)}, f32[10,2,256,256]{3,2,1,0:T(8,128)S(1)}, f32[6,10]{1,0:T(8,128)}) custom-call(s32[2,10]{1,0:T(2,128)S(1)} %get-tuple-element.47.tile_list, s32[4,10]{1,0:T(4,128)S(1)} %get-tuple-element.48.offsets, s32[1]{0:T(128)S(6)} %copy.15.group_counts, ...), custom_call_target="tpu_custom_call" | custom-call | tf_op jit(solution)/shard_map/positions/pallas_call | solution.py:340
  52.1 2.3 %collective-permute-done.10 = bf16[2,12,64,256]{3,2,1,0:T(8,128)(2,1)S(1)} collective-permute-done((bf16[2,12,64,256]{3,2,1,0:T(8,128)(2,1)S(1)}, bf16[2,12,64,256]{3,2,1,0:T(8,128)(2,1)S(1)}, u32[]{:S(2)}, u32[]{:S(2)}) %collective-permute-start.10) | collective-permute-done | bytes 786464 | tf_op jit(solution)/shard_map/ppermute | solution.py:38
  54.7 5.9 %scatter.1 = (bf16[2,2,4,128,128]{4,3,2,1,0:T(8,128)(2,1)S(1)}, bf16[2,2,4,128,128]{4,3,2,1,0:T(8,128)(2,1)S(1)}, bf16[2,2,4,128,128]{4,3,2,1,0:T(8,128)(2,1)S(1...) custom-call(s32[2,10]{1,0:T(2,128)S(1)} %get-tuple-element.47.tile_lis, ...), custom_call_target="tpu_custom_call" | custom-call | flops 16777216 | bytes 16777216 | tf_op jit(solution)/shard_map/scatter/pallas_call | solution.py:455
  60.6 5.2 %collective-permute-done.12 = bf16[1,12,64,256]{3,2,1,0:T(8,128)(2,1)S(1)} collective-permute-done((bf16[1,12,64,256]{3,2,1,0:T(8,128)(2,1)S(1)}, bf16[1,12,64,256]{3,2,1,0:T(8,128)(2,1)S(1)}, u32[]{:S(2)}, u32[]{:S(2)}) %collective-permute-start.12) | collective-permute-done | bytes 393248 | tf_op jit(solution)/shard_map/ppermute | solution.py:38
  66.4 7.5 %collective-permute-start.15 = (bf16[2,3,64,256]{3,2,1,0:T(8,128)(2,1)S(1)}, bf16[2,3,64,256]{3,2,1,0:T(8,128)(2,1)S(1)}, u32[]{:S(2)}, u32[]{:S(2)}) collective-permute-start(bf16[2,3,64,256]{3,2,1,0:T(8,128)(2,1)S(1)} %fusion.17), channel_id=1, source_target_pairs={{0,4},{4,0},{8,12},{12,8},{1,5},{5,1},{9,13},{13,9},{2,6},{6,2},{1... | collective-permute-start | bytes 589832 | tf_op jit(solution)/shard_map/ppermute | solution.py:38
  74.4 4.6 %collective-permute-done.15 = bf16[2,3,64,256]{3,2,1,0:T(8,128)(2,1)S(1)} collective-permute-done((bf16[2,3,64,256]{3,2,1,0:T(8,128)(2,1)S(1)}, bf16[2,3,64,256]{3,2,1,0:T(8,128)(2,1)S(1)}, u32[]{:S(2)}, u32[]{:S(2)}) %collective-permute-start.15) | collective-permute-done | bytes 196640 | tf_op jit(solution)/shard_map/ppermute | solution.py:38
  79.0 3.0 %collective-permute-done.14 = bf16[1,2,4,128,128]{4,3,2,1,0:T(8,128)(2,1)S(1)} collective-permute-done((bf16[1,2,4,128,128]{4,3,2,1,0:T(8,128)(2,1)S(1)}, bf16[1,2,4,128,128]{4,3,2,1,0:T(8,128)(2,1)S(1)}, u32[]{:S(2)}, u32[]{:S(2)}) %collective-permute-start.14) | collective-permute-done | bytes 262176 | tf_op jit(solution)/shard_map/ppermute | solution.py:38
  82.1 1.7 %collective-permute-start.16 = (bf16[2,4,128,128]{3,2,1,0:T(8,128)(2,1)S(1)}, bf16[2,4,128,128]{3,2,1,0:T(8,128)(2,1)S(1)}, u32[]{:S(2)}, u32[]{:S(2)}) collective-permute-start(bf16[2,4,128,128]{3,2,1,0:T(8,128)(2,1)S(1)} %fusion.10), channel_id=1, source_target_pairs={{0,4},{4,8},{8,12},{12,0},{1,5},{5,9},{9,13},{13,1},{2,6},{6,10},{... | collective-permute-start | bytes 786440 | tf_op jit(solution)/shard_map/ppermute | solution.py:33
  84.2 4.6 %collective-permute-start.21 = (bf16[1,3,64,256]{3,2,1,0:T(8,128)(2,1)S(1)}, bf16[1,3,64,256]{3,2,1,0:T(8,128)(2,1)S(1)}, u32[]{:S(2)}, u32[]{:S(2)}) collective-permute-start(bf16[1,3,64,256]{3,2,1,0:T(8,128)(2,1)S(1)} %fusion.22), channel_id=1, source_target_pairs={{0,8},{4,12},{8,0},{12,4},{1,9},{5,13},{9,1},{13,5},{2,10},{6,14},... | collective-permute-start | bytes 294920 | tf_op jit(solution)/shard_map/ppermute | solution.py:38
  88.8 4.7 %collective-permute-done.16 = bf16[2,4,128,128]{3,2,1,0:T(8,128)(2,1)S(1)} collective-permute-done((bf16[2,4,128,128]{3,2,1,0:T(8,128)(2,1)S(1)}, bf16[2,4,128,128]{3,2,1,0:T(8,128)(2,1)S(1)}, u32[]{:S(2)}, u32[]{:S(2)}) %collective-permute-start.16) | collective-permute-done | bytes 262176 | tf_op jit(solution)/shard_map/ppermute | solution.py:33
  93.7 1.6 %collective-permute-start.19 = (bf16[1,2,4,128,128]{4,3,2,1,0:T(8,128)(2,1)S(1)}, bf16[1,2,4,128,128]{4,3,2,1,0:T(8,128)(2,1)S(1)}, u32[]{:S(2)}, u32[]{:S(2)}) collective-permute-start(bf16[1,2,4,128,128]{4,3,2,1,0:T(8,128)(2,1)S(1)} %fusion.16), channel_id=1, source_target_pairs={{0,2},{1,3},{2,0},{3,1},{4,6},{5,7},{6,4},{7,5},{8,10},{9,11},{10,... | collective-permute-start | bytes 786440 | tf_op jit(solution)/shard_map/ppermute | solution.py:38
  95.3 1.3 %collective-permute-done.21 = bf16[1,3,64,256]{3,2,1,0:T(8,128)(2,1)S(1)} collective-permute-done((bf16[1,3,64,256]{3,2,1,0:T(8,128)(2,1)S(1)}, bf16[1,3,64,256]{3,2,1,0:T(8,128)(2,1)S(1)}, u32[]{:S(2)}, u32[]{:S(2)}) %collective-permute-start.21) | collective-permute-done | bytes 98336 | tf_op jit(solution)/shard_map/ppermute | solution.py:38
  98.3 4.5 %collective-permute-done.23.refs_2_ = bf16[3,64,256]{2,1,0:T(8,128)(2,1)S(1)} collective-permute-done((bf16[3,64,256]{2,1,0:T(8,128)(2,1)S(1)}, bf16[3,64,256]{2,1,0:T(8,128)(2,1)S(1)}, u32[]{:S(2)}, u32[]{:S(2)}) %collective-permute-start.23) | collective-permute-done | bytes 98336 | tf_op jit(solution)/shard_map/ppermute | solution.py:38
  102.8 2.0 %collective-permute-start.20 = (bf16[2,4,128,128]{3,2,1,0:T(8,128)(2,1)S(1)}, bf16[2,4,128,128]{3,2,1,0:T(8,128)(2,1)S(1)}, u32[]{:S(2)}, u32[]{:S(2)}) collective-permute-start(bf16[2,4,128,128]{3,2,1,0:T(8,128)(2,1)S(1)} %fusion.6), channel_id=1, source_target_pairs={{0,4},{4,8},{8,12},{12,0},{1,5},{5,9},{9,13},{13,1},{2,6},{6,10},{... | collective-permute-start | bytes 786440 | tf_op jit(solution)/shard_map/ppermute | solution.py:33
  104.9 3.3 %collective-permute-done.24.refs_3_ = bf16[3,64,256]{2,1,0:T(8,128)(2,1)S(1)} collective-permute-done((bf16[3,64,256]{2,1,0:T(8,128)(2,1)S(1)}, bf16[3,64,256]{2,1,0:T(8,128)(2,1)S(1)}, u32[]{:S(2)}, u32[]{:S(2)}) %collective-permute-start.24) | collective-permute-done | bytes 98336 | tf_op jit(solution)/shard_map/ppermute | solution.py:38
  109.2 4.2 %collective-permute-done.20.second = bf16[2,4,128,128]{3,2,1,0:T(8,128)(2,1)S(1)} collective-permute-done((bf16[2,4,128,128]{3,2,1,0:T(8,128)(2,1)S(1)}, bf16[2,4,128,128]{3,2,1,0:T(8,128)(2,1)S(1)}, u32[]{:S(2)}, u32[]{:S(2)}) %collective-permute-start.20) | collective-permute-done | bytes 262176 | tf_op jit(solution)/shard_map/ppermute | solution.py:33
  (61 shorter events, 12.8 us)
Async XLA Ops:
  1.7 11.2 %collective-permute-start = (bf16[2,128,512]{2,1,0:T(8,128)(2,1)S(1)}, bf16[2,128,512]{2,1,0:T(8,128)(2,1)S(1)}, u32[]{:S(2)}, u32[]{:S(2)}) collective-permute-start(bf16[2,128,512]{2,1,0:T(8,128)(2,1)S(1)} %dynamic-slice_bitcast_fusion), channel_id=1, source_target_pairs={{4,0},{8,4},{12,8},{5,1},{9,5},{13,9},{6,2},{10,6},{14,10},{7,3},{... | collective-permute-start | bytes 786440 | tf_op jit(solution)/shard_map/ppermute | solution.py:500
  3.0 14.8 %collective-permute-start.3 = (bf16[2,128,512]{2,1,0:T(8,128)(2,1)S(1)}, bf16[2,128,512]{2,1,0:T(8,128)(2,1)S(1)}, u32[]{:S(2)}, u32[]{:S(2)}) collective-permute-start(bf16[2,128,512]{2,1,0:T(8,128)(2,1)S(1)} %dynamic-slice_bitcast_fusion), channel_id=1, source_target_pairs={{0,12},{1,13},{2,14},{3,15},{16,28},{17,29},{18,30},{19,31}} | collective-permute-start | bytes 786440 | tf_op jit(solution)/shard_map/ppermute | solution.py:501
  11.1 10.9 %collective-permute-start.2 = (bf16[2,128,512]{2,1,0:T(8,128)(2,1)S(1)}, bf16[2,128,512]{2,1,0:T(8,128)(2,1)S(1)}, u32[]{:S(2)}, u32[]{:S(2)}) collective-permute-start(bf16[2,128,512]{2,1,0:T(8,128)(2,1)S(1)} %dynamic-slice_bitcast_fusion), channel_id=1, source_target_pairs={{0,8},{4,12},{1,9},{5,13},{2,10},{6,14},{3,11},{7,15},{16,24},{20,... | collective-permute-start | bytes 786440 | tf_op jit(solution)/shard_map/ppermute | solution.py:502
  13.0 9.4 %collective-permute-start.1 = (bf16[2,128,512]{2,1,0:T(8,128)(2,1)S(1)}, bf16[2,128,512]{2,1,0:T(8,128)(2,1)S(1)}, u32[]{:S(2)}, u32[]{:S(2)}) collective-permute-start(bf16[2,128,512]{2,1,0:T(8,128)(2,1)S(1)} %collective-permute-done), channel_id=1, source_target_pairs={{4,0},{8,4},{5,1},{9,5},{6,2},{10,6},{7,3},{11,7},{20,16},{24,20},... | collective-permute-start | bytes 786440 | tf_op jit(solution)/shard_map/ppermute | solution.py:503
  17.9 7.3 %collective-permute-start.4 = (bf16[2,128,512]{2,1,0:T(8,128)(2,1)S(1)}, bf16[2,128,512]{2,1,0:T(8,128)(2,1)S(1)}, u32[]{:S(2)}, u32[]{:S(2)}) collective-permute-start(bf16[2,128,512]{2,1,0:T(8,128)(2,1)S(1)} %add.121.refs_1_), channel_id=1, source_target_pairs={{0,2},{1,3},{2,0},{3,1},{4,6},{5,7},{6,4},{7,5},{8,10},{9,11},{10,... | collective-permute-start | bytes 786440 | tf_op jit(solution)/shard_map/ppermute | solution.py:38
  22.4 7.6 %collective-permute-start.7 = (bf16[2,128,512]{2,1,0:T(8,128)(2,1)S(1)}, bf16[2,128,512]{2,1,0:T(8,128)(2,1)S(1)}, u32[]{:S(2)}, u32[]{:S(2)}) collective-permute-start(bf16[2,128,512]{2,1,0:T(8,128)(2,1)S(1)} %add.120.refs_5_), channel_id=1, source_target_pairs={{0,2},{1,3},{2,0},{3,1},{4,6},{5,7},{6,4},{7,5},{8,10},{9,11},{10,... | collective-permute-start | bytes 786440 | tf_op jit(solution)/shard_map/ppermute | solution.py:38
  23.8 6.8 %collective-permute-start.5 = (bf16[2,128,512]{2,1,0:T(8,128)(2,1)S(1)}, bf16[2,128,512]{2,1,0:T(8,128)(2,1)S(1)}, u32[]{:S(2)}, u32[]{:S(2)}) collective-permute-start(bf16[2,128,512]{2,1,0:T(8,128)(2,1)S(1)} %add.121.refs_1_), channel_id=1, source_target_pairs={{0,1},{1,0},{2,3},{3,2},{4,5},{5,4},{6,7},{7,6},{8,9},{9,8},{10,11... | collective-permute-start | bytes 786440 | tf_op jit(solution)/shard_map/ppermute | solution.py:38
  23.8 6.8 %collective-permute-start.8 = (bf16[2,128,512]{2,1,0:T(8,128)(2,1)S(1)}, bf16[2,128,512]{2,1,0:T(8,128)(2,1)S(1)}, u32[]{:S(2)}, u32[]{:S(2)}) collective-permute-start(bf16[2,128,512]{2,1,0:T(8,128)(2,1)S(1)} %add.120.refs_5_), channel_id=1, source_target_pairs={{0,1},{1,0},{2,3},{3,2},{4,5},{5,4},{6,7},{7,6},{8,9},{9,8},{10,11... | collective-permute-start | bytes 786440 | tf_op jit(solution)/shard_map/ppermute | solution.py:38
  25.2 5.4 %collective-permute-start.6 = (bf16[2,128,512]{2,1,0:T(8,128)(2,1)S(1)}, bf16[2,128,512]{2,1,0:T(8,128)(2,1)S(1)}, u32[]{:S(2)}, u32[]{:S(2)}) collective-permute-start(bf16[2,128,512]{2,1,0:T(8,128)(2,1)S(1)} %collective-permute-done.4.refs_2_), channel_id=1, source_target_pairs={{0,1},{1,0},{2,3},{3,2},{4,5},{5,4},{6,7},{7,6},{8,9},{9,8},{10,11... | collective-permute-start | bytes 786440 | tf_op jit(solution)/shard_map/ppermute | solution.py:38
  52.0 2.4 %collective-permute-start.10 = (bf16[2,12,64,256]{3,2,1,0:T(8,128)(2,1)S(1)}, bf16[2,12,64,256]{3,2,1,0:T(8,128)(2,1)S(1)}, u32[]{:S(2)}, u32[]{:S(2)}) collective-permute-start(bf16[2,12,64,256]{3,2,1,0:T(8,128)(2,1)S(1)} %get-tuple-element.57), channel_id=1, source_target_pairs={{0,1},{1,0},{2,3},{3,2},{4,5},{5,4},{6,7},{7,6},{8,9},{9,8},{10,11... | collective-permute-start | bytes 2359304 | tf_op jit(solution)/shard_map/ppermute | solution.py:38
  54.6 11.2 %collective-permute-start.12 = (bf16[1,12,64,256]{3,2,1,0:T(8,128)(2,1)S(1)}, bf16[1,12,64,256]{3,2,1,0:T(8,128)(2,1)S(1)}, u32[]{:S(2)}, u32[]{:S(2)}) collective-permute-start(bf16[1,12,64,256]{3,2,1,0:T(8,128)(2,1)S(1)} %get-tuple-element.74), channel_id=1, source_target_pairs={{0,2},{1,3},{2,0},{3,1},{4,6},{5,7},{6,4},{7,5},{8,10},{9,11},{10,... | collective-permute-start | bytes 1179656 | tf_op jit(solution)/shard_map/ppermute | solution.py:38
  65.8 8.1 %collective-permute-start.13 = (bf16[2,2,4,128,128]{4,3,2,1,0:T(8,128)(2,1)S(1)}, bf16[2,2,4,128,128]{4,3,2,1,0:T(8,128)(2,1)S(1)}, u32[]{:S(2)}, u32[]{:S(2)}) collective-permute-start(bf16[2,2,4,128,128]{4,3,2,1,0:T(8,128)(2,1)S(1)} %get-tuple-element.63), channel_id=1, source_target_pairs={{0,1},{1,0},{2,3},{3,2},{4,5},{5,4},{6,7},{7,6},{8,9},{9,8},{10,11... | collective-permute-start | bytes 1572872 | tf_op jit(solution)/shard_map/ppermute | solution.py:38
  65.8 18.0 %collective-permute-start.17 = (bf16[2,2,4,128,128]{4,3,2,1,0:T(8,128)(2,1)S(1)}, bf16[2,2,4,128,128]{4,3,2,1,0:T(8,128)(2,1)S(1)}, u32[]{:S(2)}, u32[]{:S(2)}) collective-permute-start(bf16[2,2,4,128,128]{4,3,2,1,0:T(8,128)(2,1)S(1)} %get-tuple-element.67), channel_id=1, source_target_pairs={{0,1},{1,0},{2,3},{3,2},{4,5},{5,4},{6,7},{7,6},{8,9},{9,8},{10,11... | collective-permute-start | bytes 1572872 | tf_op jit(solution)/shard_map/ppermute | solution.py:38
  66.4 12.6 %collective-permute-start.15 = (bf16[2,3,64,256]{3,2,1,0:T(8,128)(2,1)S(1)}, bf16[2,3,64,256]{3,2,1,0:T(8,128)(2,1)S(1)}, u32[]{:S(2)}, u32[]{:S(2)}) collective-permute-start(bf16[2,3,64,256]{3,2,1,0:T(8,128)(2,1)S(1)} %fusion.17), channel_id=1, source_target_pairs={{0,4},{4,0},{8,12},{12,8},{1,5},{5,1},{9,13},{13,9},{2,6},{6,2},{1... | collective-permute-start | bytes 589832 | tf_op jit(solution)/shard_map/ppermute | solution.py:38
  74.0 8.0 %collective-permute-start.14 = (bf16[1,2,4,128,128]{4,3,2,1,0:T(8,128)(2,1)S(1)}, bf16[1,2,4,128,128]{4,3,2,1,0:T(8,128)(2,1)S(1)}, u32[]{:S(2)}, u32[]{:S(2)}) collective-permute-start(bf16[1,2,4,128,128]{4,3,2,1,0:T(8,128)(2,1)S(1)} %fusion.14), channel_id=1, source_target_pairs={{0,2},{1,3},{2,0},{3,1},{4,6},{5,7},{6,4},{7,5},{8,10},{9,11},{10,... | collective-permute-start | bytes 786440 | tf_op jit(solution)/shard_map/ppermute | solution.py:38
  82.1 11.4 %collective-permute-start.16 = (bf16[2,4,128,128]{3,2,1,0:T(8,128)(2,1)S(1)}, bf16[2,4,128,128]{3,2,1,0:T(8,128)(2,1)S(1)}, u32[]{:S(2)}, u32[]{:S(2)}) collective-permute-start(bf16[2,4,128,128]{3,2,1,0:T(8,128)(2,1)S(1)} %fusion.10), channel_id=1, source_target_pairs={{0,4},{4,8},{8,12},{12,0},{1,5},{5,9},{9,13},{13,1},{2,6},{6,10},{... | collective-permute-start | bytes 786440 | tf_op jit(solution)/shard_map/ppermute | solution.py:33
  83.8 9.7 %collective-permute-start.18 = (bf16[1,2,4,128,128]{4,3,2,1,0:T(8,128)(2,1)S(1)}, bf16[1,2,4,128,128]{4,3,2,1,0:T(8,128)(2,1)S(1)}, u32[]{:S(2)}, u32[]{:S(2)}) collective-permute-start(bf16[1,2,4,128,128]{4,3,2,1,0:T(8,128)(2,1)S(1)} %fusion.15), channel_id=1, source_target_pairs={{0,2},{1,3},{2,0},{3,1},{4,6},{5,7},{6,4},{7,5},{8,10},{9,11},{10,... | collective-permute-start | bytes 786440 | tf_op jit(solution)/shard_map/ppermute | solution.py:38
  84.2 9.4 %collective-permute-start.11 = (bf16[2,2,4,128,128]{4,3,2,1,0:T(8,128)(2,1)S(1)}, bf16[2,2,4,128,128]{4,3,2,1,0:T(8,128)(2,1)S(1)}, u32[]{:S(2)}, u32[]{:S(2)}) collective-permute-start(bf16[2,2,4,128,128]{4,3,2,1,0:T(8,128)(2,1)S(1)} %get-tuple-element.60), channel_id=1, source_target_pairs={{0,1},{1,0},{2,3},{3,2},{4,5},{5,4},{6,7},{7,6},{8,9},{9,8},{10,11... | collective-permute-start | bytes 1572872 | tf_op jit(solution)/shard_map/ppermute | solution.py:38
  84.2 12.4 %collective-permute-start.21 = (bf16[1,3,64,256]{3,2,1,0:T(8,128)(2,1)S(1)}, bf16[1,3,64,256]{3,2,1,0:T(8,128)(2,1)S(1)}, u32[]{:S(2)}, u32[]{:S(2)}) collective-permute-start(bf16[1,3,64,256]{3,2,1,0:T(8,128)(2,1)S(1)} %fusion.22), channel_id=1, source_target_pairs={{0,8},{4,12},{8,0},{12,4},{1,9},{5,13},{9,1},{13,5},{2,10},{6,14},... | collective-permute-start | bytes 294920 | tf_op jit(solution)/shard_map/ppermute | solution.py:38
  93.7 15.4 %collective-permute-start.19 = (bf16[1,2,4,128,128]{4,3,2,1,0:T(8,128)(2,1)S(1)}, bf16[1,2,4,128,128]{4,3,2,1,0:T(8,128)(2,1)S(1)}, u32[]{:S(2)}, u32[]{:S(2)}) collective-permute-start(bf16[1,2,4,128,128]{4,3,2,1,0:T(8,128)(2,1)S(1)} %fusion.16), channel_id=1, source_target_pairs={{0,2},{1,3},{2,0},{3,1},{4,6},{5,7},{6,4},{7,5},{8,10},{9,11},{10,... | collective-permute-start | bytes 786440 | tf_op jit(solution)/shard_map/ppermute | solution.py:38
  96.6 6.2 %collective-permute-start.23 = (bf16[3,64,256]{2,1,0:T(8,128)(2,1)S(1)}, bf16[3,64,256]{2,1,0:T(8,128)(2,1)S(1)}, u32[]{:S(2)}, u32[]{:S(2)}) collective-permute-start(bf16[3,64,256]{2,1,0:T(8,128)(2,1)S(1)} %fusion.20.refs_0_), channel_id=1, source_target_pairs={{0,8},{4,12},{8,0},{12,4},{1,9},{5,13},{9,1},{13,5},{2,10},{6,14},... | collective-permute-start | bytes 294920 | tf_op jit(solution)/shard_map/ppermute | solution.py:38
  97.6 7.3 %collective-permute-start.22 = (bf16[3,64,256]{2,1,0:T(8,128)(2,1)S(1)}, bf16[3,64,256]{2,1,0:T(8,128)(2,1)S(1)}, u32[]{:S(2)}, u32[]{:S(2)}) collective-permute-start(bf16[3,64,256]{2,1,0:T(8,128)(2,1)S(1)} %fusion.20.refs_0_), channel_id=1, source_target_pairs={{0,4},{4,0},{8,12},{12,8},{1,5},{5,1},{9,13},{13,9},{2,6},{6,2},{1... | collective-permute-start | bytes 294920 | tf_op jit(solution)/shard_map/ppermute | solution.py:38
  102.8 5.3 %collective-permute-start.24 = (bf16[3,64,256]{2,1,0:T(8,128)(2,1)S(1)}, bf16[3,64,256]{2,1,0:T(8,128)(2,1)S(1)}, u32[]{:S(2)}, u32[]{:S(2)}) collective-permute-start(bf16[3,64,256]{2,1,0:T(8,128)(2,1)S(1)} %collective-permute-done.23.refs_2_), channel_id=1, source_target_pairs={{0,4},{4,0},{8,12},{12,8},{1,5},{5,1},{9,13},{13,9},{2,6},{6,2},{1... | collective-permute-start | bytes 294920 | tf_op jit(solution)/shard_map/ppermute | solution.py:38
  102.8 10.5 %collective-permute-start.20 = (bf16[2,4,128,128]{3,2,1,0:T(8,128)(2,1)S(1)}, bf16[2,4,128,128]{3,2,1,0:T(8,128)(2,1)S(1)}, u32[]{:S(2)}, u32[]{:S(2)}) collective-permute-start(bf16[2,4,128,128]{3,2,1,0:T(8,128)(2,1)S(1)} %fusion.6), channel_id=1, source_target_pairs={{0,4},{4,8},{8,12},{12,0},{1,5},{5,9},{9,13},{13,1},{2,6},{6,10},{... | collective-permute-start | bytes 786440 | tf_op jit(solution)/shard_map/ppermute | solution.py:33
  (8 other events, 46.5 us)

commit v4 on v3

--- a/solution.py
+++ b/solution.py
@@ -42,6 +42,10 @@
     pair, core = member >> 1, member & 1
     mine = 2 * (pair ^ h) + core
     return mine, mine ^ 1
+
+
+def far_first(shares):
+    return [*range(1, shares // 2, 2), *range(0, shares // 2, 2)]
 
 
 def share_of(groups, peers):
@@ -111,9 +115,10 @@
     shares = len(offs)
     pieces = refs[: 1 + (REACH - 1) * shares]
     eig_in, amps_in, tables_in, coef_in = refs[len(pieces):len(pieces) + 4]
-    eigen_send, eigen_keep, grads_out, coef = refs[len(pieces) + 4:len(pieces) + 8]
+    eigen_send, eigen_keep = refs[len(pieces) + 4:len(pieces) + 6], refs[len(pieces) + 6:len(pieces) + 8]
+    grads_out, coef = refs[len(pieces) + 8:len(pieces) + 10]
     (staged, table, probe, amps, eig, obj, ex, mid, far, patch, d_high, d_low, eigen, out_eigen, cross,
-     weights, weights_t, piece_sem, table_sem, amps_sem, eig_sem, grad_sem, out_sem) = refs[len(pieces) + 8:]
+     weights, weights_t, piece_sem, table_sem, amps_sem, eig_sem, grad_sem, out_sem) = refs[len(pieces) + 10:]
     pos_dev, _, frame, _ = probe.shape
     modes = eig.shape[0]
     side = staged.shape[2]
@@ -305,11 +310,11 @@
         copy.start()
         pending.append(copy)
 
-    for h in range(shares // 2):
+    for h in far_first(shares):
         mine, other = slabs_of(member, h)
         out_eigen[h] = eigen[other].astype(jnp.bfloat16)
-        start(eigen.at[mine], eigen_keep.at[h])
-    start(out_eigen, eigen_send)
+        start(out_eigen.at[h], eigen_send[h % 2].at[h // 2])
+        start(eigen.at[mine], eigen_keep[h % 2].at[h // 2])
 
     total = exact(one_hot(by_position[::-1], 1), diagonals(cross[...]))
     coef[...] = lax.dot_general(
@@ -336,11 +341,12 @@
     whole = pl.BlockSpec(memory_space=VMEM)
     anywhere = pl.BlockSpec(memory_space=pl.ANY)
     eigen_half = (shares // 2, 2 * modes, frame // shares, frame)
+    eigen_part = (shares // 4,) + eigen_half[1:]
     grads = (pos_dev, 2, frame, frame)
     return pl.pallas_call(
         functools.partial(position_kernel, offs, scale),
         in_specs=[smem] * 3 + [anywhere] * (len(pieces) + 3) + [whole],
-        out_specs=[anywhere] * 3 + [whole],
+        out_specs=[anywhere] * 5 + [whole],
         scratch_shapes=[
             pltpu.VMEM((REACH, 2, side, side), jnp.bfloat16),
             pltpu.VMEM(table.shape, jnp.bfloat16),
@@ -364,11 +370,13 @@
             pltpu.SemaphoreType.DMA,
             pltpu.SemaphoreType.DMA,
             pltpu.SemaphoreType.DMA((pos_dev,)),
-            pltpu.SemaphoreType.DMA((shares // 2 + 1,)),
+            pltpu.SemaphoreType.DMA((shares,)),
         ],
         out_shape=[
-            jax.ShapeDtypeStruct(eigen_half, jnp.bfloat16),
-            jax.ShapeDtypeStruct(eigen_half, jnp.float32),
+            jax.ShapeDtypeStruct(eigen_part, jnp.bfloat16),
+            jax.ShapeDtypeStruct(eigen_part, jnp.bfloat16),
+            jax.ShapeDtypeStruct(eigen_part, jnp.float32),
+            jax.ShapeDtypeStruct(eigen_part, jnp.float32),
             jax.ShapeDtypeStruct(grads, jnp.float32),
             jax.ShapeDtypeStruct((modes, pos_dev), jnp.float32),
         ],
@@ -378,8 +386,8 @@
 
 
 def scatter_kernel(shares, tile_list, offsets, group_counts, grads_in, *refs):
-    send, keep = refs[:REACH], refs[REACH:2 * REACH]
-    grads, acc, out_send, grad_sem, out_sem = refs[2 * REACH:]
+    send, keep = refs[:2 * REACH], refs[2 * REACH:4 * REACH]
+    grads, acc, out_send, grad_sem, out_sem = refs[4 * REACH:]
     pos_dev, _, frame, _ = grads.shape
     blocks, side = acc.shape[2] - 1, acc.shape[3]
     slab = side // shares
@@ -437,13 +445,16 @@
         pending.append(copy)
 
     for section in range(REACH - 1, -1, -1):
-        for h in range(shares // 2):
+        for h in far_first(shares):
             mine, other = (pl.multiple_of(at * slab, slab) for at in slabs_of(member, h))
-            start(acc.at[section, :, pl.ds(0, blocks), pl.ds(mine, slab), :], keep[section].at[h])
+            start(
+                acc.at[section, :, pl.ds(0, blocks), pl.ds(mine, slab), :],
+                keep[2 * section + h % 2].at[h // 2],
+            )
             for c in range(2):
                 for b in range(blocks):
                     out_send[section, h, c, b] = acc[section, c, b, pl.ds(other, slab), :].astype(jnp.bfloat16)
-        start(out_send.at[section], send[section])
+            start(out_send.at[section, h], send[2 * section + h % 2].at[h // 2])
     for copy in pending:
         copy.wait()
 
@@ -452,19 +463,20 @@
     blocks = side // LANES
     anywhere = pl.BlockSpec(memory_space=pl.ANY)
     half = (shares // 2, 2, blocks, side // shares, LANES)
+    part = (shares // 4,) + half[1:]
     return pl.pallas_call(
         functools.partial(scatter_kernel, shares),
         in_specs=[pl.BlockSpec(memory_space=SMEM)] * 3 + [anywhere],
-        out_specs=[anywhere] * (2 * REACH),
+        out_specs=[anywhere] * (4 * REACH),
         scratch_shapes=[
             pltpu.VMEM(grads.shape, jnp.float32),
             pltpu.VMEM((REACH, 2, blocks + 1, side, LANES), jnp.float32),
             pltpu.VMEM((REACH,) + half, jnp.bfloat16),
             pltpu.SemaphoreType.DMA((grads.shape[0],)),
-            pltpu.SemaphoreType.DMA((REACH * (shares // 2 + 1),)),
+            pltpu.SemaphoreType.DMA((REACH * shares,)),
         ],
-        out_shape=[jax.ShapeDtypeStruct(half, jnp.bfloat16)] * REACH
-        + [jax.ShapeDtypeStruct(half, jnp.float32)] * REACH,
+        out_shape=[jax.ShapeDtypeStruct(part, jnp.bfloat16)] * (2 * REACH)
+        + [jax.ShapeDtypeStruct(part, jnp.float32)] * (2 * REACH),
         compiler_params=pltpu.CompilerParams(vmem_limit_bytes=20 * 1024 * 1024),
         cost_estimate=pl.CostEstimate(flops=1 << 24, bytes_accessed=16 << 20, transcendentals=0),
         name="scatter",
@@ -480,28 +492,19 @@
 
 
 def halve(keep, send, before_core=(), before_cross=()):
-    arrived = swap(after(send, *before_core), "probe", 1)
-    terms = [keep, after(arrived, *before_cross)]
+    far = [keep[1], after(swap(after(send[1], *before_core), "probe", 1), *before_cross)]
+    terms = [keep[0], swap(send[0], "probe", 1)]
+    leaving = None
     bit = 2
-    leaving = send
-    while keep.shape[0] * 2 > bit:
+    while True:
+        sending = sum(term.astype(jnp.float32) for term in far).astype(jnp.bfloat16)
+        leaving = sending if leaving is None else leaving
+        terms.append(swap(sending, "probe", bit))
+        if terms[0].shape[0] == 1:
+            return sum(term[0].astype(jnp.float32) for term in terms), leaving, terms[-1]
         pick = lambda term, which: term.reshape((term.shape[0] // 2, 2) + term.shape[1:])[:, which]
-        sending = sum(pick(term, 1).astype(jnp.float32) for term in terms).astype(jnp.bfloat16)
-        if bit == 2:
-            leaving = sending
-        arrived = swap(sending, "probe", bit)
-        terms = [pick(term, 0) for term in terms] + [arrived]
+        far, terms = [pick(term, 1) for term in terms], [pick(term, 0) for term in terms]
         bit *= 2
-    return sum(term[0].astype(jnp.float32) for term in terms), leaving, arrived
-
-
-def next_tiles(own, axis):
-    peers = lax.axis_size(axis)
-    near = lax.ppermute(own, axis, [(i, i - 1) for i in range(1, peers)])
-    around = lax.ppermute(own, axis, [(0, peers - 1)])
-    far_around = lax.ppermute(own, axis, [(0, peers - 2), (1, peers - 1)])
-    far = lax.ppermute(near, axis, [(i, i - 1) for i in range(1, peers - 1)])
-    return near + around, far + far_around
 
 
 def scatter_rows(axis, value):
@@ -526,11 +529,13 @@
     return sum(term[0].astype(jnp.float32) for term in terms).astype(jnp.bfloat16), sent
 
 
-def gather_shares(axis, total):
+def gather_shares(axis, total, *others):
     held = {0: total}
     bit = lax.axis_size(axis) // 2
     while bit:
         held.update({i ^ bit: swap(piece, axis, bit) for i, piece in held.items()})
+        if others:
+            held[bit], others = after(held[bit], *others), ()
         bit //= 2
     return [held[i] for i in range(lax.axis_size(axis))]
 
@@ -586,8 +591,8 @@
     for bit in reversed(bits):
         offs = offs + [o ^ bit for o in offs]
     quarter = lax.dynamic_slice_in_dim(tiles[0], member * slab, slab, 1)
-    near, far = next_tiles(quarter, "blk")
-    held = [[near], [far]]
+    near = shift(quarter, "blk", -1)
+    held = [[near], [shift(near, "blk", -1)]]
     eig, amps = stage(*after_all((eigenprobes, amplitudes), near))
     held[1][0] = after(held[1][0], eig)
     table, tile, coef_t, lists, corners = stage(
@@ -602,31 +607,29 @@
 
     indices = (lists, corners, group_counts)
     scale = (pos_dev * blocks * shares) ** (-0.5)
-    eigen_send, eigen_keep, grads, coef_rows = positions(
+    out = positions(
         tuple(offs), scale, indices, [tile] + held[0] + held[1], eig, amps, table, coef_t
     )
+    eigen_send, eigen_keep, grads, coef_rows = out[:2], out[2:4], out[4], out[5]
 
     eigen, leaving, crossed = halve(eigen_keep, eigen_send)
     out = scatter(shares, side, indices, after(grads, leaving))
-    send, keep = out[:REACH], out[REACH:]
+    send, keep = ([out[at + 2 * i:at + 2 * i + 2] for i in range(REACH)] for at in (0, 2 * REACH))
     last = REACH - 1
     share = share_of(2 * modes, blocks)
     if share:
         total, sent = scatter_sum("blk", eigen.reshape((blocks, share) + eigen.shape[1:]))
     else:
         total, sent = scatter_rows("blk", eigen.reshape(blocks, -1, frame))
-    mine, leaving, _ = halve(keep[last], send[last], before_core=(crossed,), before_cross=sent[:1])
-    moving = after(mine.astype(jnp.bfloat16), *sent[1:])
+    mine, _, _ = halve(keep[last], send[last], before_core=(crossed,))
+    moving = after(mine.astype(jnp.bfloat16), *sent[:1])
     for section in range(last - 1, -1, -1):
-        mine, leaving, _ = halve(keep[section], send[section], before_cross=(moving,))
-        if section == last - 1:
-            total = after(total, leaving)
+        mine, _, _ = halve(keep[section], send[section], before_cross=(moving,))
         arrived = shift(moving, "blk", 1)
         if section > 0:
             moving = (arrived.astype(jnp.float32) + mine).astype(jnp.bfloat16)
-    shares_of_eigen = gather_shares("blk", total)
-    shares_of_eigen[0] = after(shares_of_eigen[0], leaving)
-    eigen_share = place("blk", shares_of_eigen).reshape(modes, 2, frame // shares, frame)
+    eigen_share = place("blk", gather_shares("blk", total, arrived))
+    eigen_share = eigen_share.reshape(modes, 2, frame // shares, frame)
     summed = finish(mine, arrived)
     return (summed[None], eigen_share, coef_rows.T)
 

time: 114 us -> 108 us (0.947)
  starting transfers between devices: 35.8 us -> 23 us
  waiting for transfers between devices: 44.7 us -> 49.8 us
  local copies, waits for them, and re-layouts: 2.56 us -> 3.78 us
    ppermute x4 -> x0, starting transfers between devices: 11.9 us -> none  [the longest x1 8.05 us: next_tiles(): around = lax.ppermute(own, axis, [(0, peers - 1)])]
    ppermute x19 -> x23, waiting for transfers between devices: 30.4 us -> 41.2 us  [swap(): return lax.ppermute(array, axis, [(i, i ^ bit) for i in range(peers)])]
    ppermute x19 -> x23, starting transfers between devices: 20.2 us -> 13.5 us  [swap(): return lax.ppermute(array, axis, [(i, i ^ bit) for i in range(peers)])]
    ppermute x2 -> x4, starting transfers between devices: 3.7 us -> 9.5 us  [shift(): lax.ppermute(array, axis, [(i, (i + by) % peers) for i in range(peers)])]
    ppermute x4 -> x0, waiting for transfers between devices: 5.36 us -> none  [the longest x1 3.59 us: next_tiles(): around = lax.ppermute(own, axis, [(0, peers - 1)])]
    unnamed x14, local copies, waits for them, and re-layouts: 1.43 us -> 2.75 us
    ppermute x2 -> x4, waiting for transfers between devices: 8.95 us -> 8.61 us  [shift(): lax.ppermute(array, axis, [(i, (i + by) % peers) for i in range(peers)])]
  transfers between devices with their start and end apart: 25 -> 27, of which waited for: 16 -> 16; matrix products, arithmetic and copies ran while one was open for 1% -> 1% of each run, Pallas kernels for 6% -> 7%
where the time goes in v4:
time: 108 us
  waiting for transfers between devices  49.8 us (46%)
  Pallas kernels  29 us (27%)
  starting transfers between devices  23 us (21%)
  local copies, waits for them, and re-layouts  3.78 us (4%)
  between operations  1.58 us (1%)
    ppermute x23, waiting for transfers between devices, swap(): return lax.ppermute(array, axis, [(i, i ^ bit) for i in range(peers)])  41.2 us
    pallas_call x1, Pallas kernels, positions(): pl.pallas_call(functools.partial(position_kernel, offs, scale), in_specs=...  20.9 us
    ppermute x23, starting transfers between devices, swap(): return lax.ppermute(array, axis, [(i, i ^ bit) for i in range(peers)])  13.5 us
    ppermute x4, starting transfers between devices, shift(): lax.ppermute(array, axis, [(i, (i + by) % peers) for i in range(peers)])  9.5 us
    ppermute x4, waiting for transfers between devices, shift(): lax.ppermute(array, axis, [(i, (i + by) % peers) for i in range(peers)])  8.61 us
    pallas_call x1, Pallas kernels, scatter(): pl.pallas_call(functools.partial(scatter_kernel, shares), in_specs=[pl.Bl...  5.96 us
    unnamed x14, local copies, waits for them, and re-layouts  2.75 us
  transfers between devices with their start and end apart: 27, of which 16 were waited for; matrix products, arithmetic and copies ran while one was open for 1% of the time, Pallas kernels for 7%

profile of v4, /device:TPU:0, one launch (start us, length us, event | category | flops | bytes accessed | tf_op | source)
XLA Modules:
  0.0 108.0 jit_solution(13855966911521692945)
XLA Ops:
  1.7 5.1 %collective-permute-start = (bf16[2,128,512]{2,1,0:T(8,128)(2,1)S(1)}, bf16[2,128,512]{2,1,0:T(8,128)(2,1)S(1)}, u32[]{:S(2)}, u32[]{:S(2)}) collective-permute-start(bf16[2,128,512]{2,1,0:T(8,128)(2,1)S(1)} %dynamic-slice_bitcast_fusion), channel_id=1, source_target_pairs={{0,12},{4,0},{8,4},{12,8},{1,13},{5,1},{9,5},{13,9},{2,14},{6,2},{... | collective-permute-start | bytes 786440 | tf_op jit(solution)/shard_map/ppermute | solution.py:33
  6.8 5.6 %collective-permute-done.refs_1_ = bf16[2,128,512]{2,1,0:T(8,128)(2,1)S(1)} collective-permute-done((bf16[2,128,512]{2,1,0:T(8,128)(2,1)S(1)}, bf16[2,128,512]{2,1,0:T(8,128)(2,1)S(1)}, u32[]{:S(2)}, u32[]{:S(2)}) %collective-permute-start) | collective-permute-done | bytes 262176 | tf_op jit(solution)/shard_map/ppermute | solution.py:33
  12.3 4.3 %collective-permute-start.1 = (bf16[2,128,512]{2,1,0:T(8,128)(2,1)S(1)}, bf16[2,128,512]{2,1,0:T(8,128)(2,1)S(1)}, u32[]{:S(2)}, u32[]{:S(2)}) collective-permute-start(bf16[2,128,512]{2,1,0:T(8,128)(2,1)S(1)} %collective-permute-done.refs_1_), channel_id=1, source_target_pairs={{0,12},{4,0},{8,4},{12,8},{1,13},{5,1},{9,5},{13,9},{2,14},{6,2},{... | collective-permute-start | bytes 786440 | tf_op jit(solution)/shard_map/ppermute | solution.py:33
  16.6 1.5 %collective-permute-start.2 = (bf16[2,128,512]{2,1,0:T(8,128)(2,1)S(1)}, bf16[2,128,512]{2,1,0:T(8,128)(2,1)S(1)}, u32[]{:S(2)}, u32[]{:S(2)}) collective-permute-start(bf16[2,128,512]{2,1,0:T(8,128)(2,1)S(1)} %collective-permute-done.refs_1_), channel_id=1, source_target_pairs={{0,2},{1,3},{2,0},{3,1},{4,6},{5,7},{6,4},{7,5},{8,10},{9,11},{10,... | collective-permute-start | bytes 786440 | tf_op jit(solution)/shard_map/ppermute | solution.py:38
  18.1 1.4 %copy-done.1 = bf16[6,2,256,256]{3,2,1,0:T(8,128)(2,1)S(1)} copy-done((bf16[6,2,256,256]{3,2,1,0:T(8,128)(2,1)S(1)}, bf16[6,2,256,256]{3,2,1,0:T(8,128)(2,1)}, u32[]{:S(2)}) %copy-start.1) | copy-done | bytes 1572888
  19.5 1.3 %copy-done.2 = bf16[10,256,256]{2,1,0:T(8,128)(2,1)S(1)} copy-done((bf16[10,256,256]{2,1,0:T(8,128)(2,1)S(1)}, bf16[10,256,256]{2,1,0:T(8,128)(2,1)}, u32[]{:S(2)}) %copy-start.2) | copy-done | bytes 1310744
  21.3 1.5 %collective-permute-start.5 = (bf16[2,128,512]{2,1,0:T(8,128)(2,1)S(1)}, bf16[2,128,512]{2,1,0:T(8,128)(2,1)S(1)}, u32[]{:S(2)}, u32[]{:S(2)}) collective-permute-start(bf16[2,128,512]{2,1,0:T(8,128)(2,1)S(1)} %collective-permute-done.1.refs_5_), channel_id=1, source_target_pairs={{0,2},{1,3},{2,0},{3,1},{4,6},{5,7},{6,4},{7,5},{8,10},{9,11},{10,... | collective-permute-start | bytes 786440 | tf_op jit(solution)/shard_map/ppermute | solution.py:38
  23.3 1.5 %collective-permute-done.2.refs_2_ = bf16[2,128,512]{2,1,0:T(8,128)(2,1)S(1)} collective-permute-done((bf16[2,128,512]{2,1,0:T(8,128)(2,1)S(1)}, bf16[2,128,512]{2,1,0:T(8,128)(2,1)S(1)}, u32[]{:S(2)}, u32[]{:S(2)}) %collective-permute-start.2) | collective-permute-done | bytes 262176 | tf_op jit(solution)/shard_map/ppermute | solution.py:38
  25.1 4.1 %collective-permute-done.5.refs_6_ = bf16[2,128,512]{2,1,0:T(8,128)(2,1)S(1)} collective-permute-done((bf16[2,128,512]{2,1,0:T(8,128)(2,1)S(1)}, bf16[2,128,512]{2,1,0:T(8,128)(2,1)S(1)}, u32[]{:S(2)}, u32[]{:S(2)}) %collective-permute-start.5) | collective-permute-done | bytes 262176 | tf_op jit(solution)/shard_map/ppermute | solution.py:38
  30.7 20.9 %positions.1 = (bf16[1,12,64,256]{3,2,1,0:T(8,128)(2,1)S(1)}, bf16[1,12,64,256]{3,2,1,0:T(8,128)(2,1)S(1)}, f32[1,12,64,256]{3,2,1,0:T(8,128)S(1)}, f32[1,12,64,...) custom-call(s32[2,10]{1,0:T(2,128)S(1)} %get-tuple-element.53.tile_list, ...), custom_call_target="tpu_custom_call" | custom-call | tf_op jit(solution)/shard_map/positions/pallas_call | solution.py:346
  51.7 1.6 %collective-permute-done.8 = bf16[1,12,64,256]{3,2,1,0:T(8,128)(2,1)S(1)} collective-permute-done((bf16[1,12,64,256]{3,2,1,0:T(8,128)(2,1)S(1)}, bf16[1,12,64,256]{3,2,1,0:T(8,128)(2,1)S(1)}, u32[]{:S(2)}, u32[]{:S(2)}) %collective-permute-start.8) | collective-permute-done | bytes 393248 | tf_op jit(solution)/shard_map/ppermute | solution.py:38
  53.4 1.5 %collective-permute-start.12 = (bf16[1,12,64,256]{3,2,1,0:T(8,128)(2,1)S(1)}, bf16[1,12,64,256]{3,2,1,0:T(8,128)(2,1)S(1)}, u32[]{:S(2)}, u32[]{:S(2)}) collective-permute-start(bf16[1,12,64,256]{3,2,1,0:T(8,128)(2,1)S(1)} %add_convert_fusion), channel_id=1, source_target_pairs={{0,2},{1,3},{2,0},{3,1},{4,6},{5,7},{6,4},{7,5},{8,10},{9,11},{10,... | collective-permute-start | bytes 1179656 | tf_op jit(solution)/shard_map/ppermute | solution.py:38
  55.0 6.0 %scatter.1 = (bf16[1,2,4,128,128]{4,3,2,1,0:T(8,128)(2,1)S(1)}, bf16[1,2,4,128,128]{4,3,2,1,0:T(8,128)(2,1)S(1)}, bf16[1,2,4,128,128]{4,3,2,1,0:T(8,128)(2,1)S(1...) custom-call(s32[2,10]{1,0:T(2,128)S(1)} %get-tuple-element.53.tile_l, ...), custom_call_target="tpu_custom_call" | custom-call | flops 16777216 | bytes 16777216 | tf_op jit(solution)/shard_map/scatter/pallas_call | solution.py:467
  60.9 3.7 %collective-permute-done.12 = bf16[1,12,64,256]{3,2,1,0:T(8,128)(2,1)S(1)} collective-permute-done((bf16[1,12,64,256]{3,2,1,0:T(8,128)(2,1)S(1)}, bf16[1,12,64,256]{3,2,1,0:T(8,128)(2,1)S(1)}, u32[]{:S(2)}, u32[]{:S(2)}) %collective-permute-start.12) | collective-permute-done | bytes 393248 | tf_op jit(solution)/shard_map/ppermute | solution.py:38
  66.8 1.5 %collective-permute-start.14 = (bf16[1,2,4,128,128]{4,3,2,1,0:T(8,128)(2,1)S(1)}, bf16[1,2,4,128,128]{4,3,2,1,0:T(8,128)(2,1)S(1)}, u32[]{:S(2)}, u32[]{:S(2)}) collective-permute-start(bf16[1,2,4,128,128]{4,3,2,1,0:T(8,128)(2,1)S(1)} %add_convert_fusion.4), channel_id=1, source_target_pairs={{0,2},{1,3},{2,0},{3,1},{4,6},{5,7},{6,4},{7,5},{8,10},{9,11},{10,... | collective-permute-start | bytes 786440 | tf_op jit(solution)/shard_map/ppermute | solution.py:38
  68.5 6.6 %collective-permute-done.14 = bf16[1,2,4,128,128]{4,3,2,1,0:T(8,128)(2,1)S(1)} collective-permute-done((bf16[1,2,4,128,128]{4,3,2,1,0:T(8,128)(2,1)S(1)}, bf16[1,2,4,128,128]{4,3,2,1,0:T(8,128)(2,1)S(1)}, u32[]{:S(2)}, u32[]{:S(2)}) %collective-permute-start.14) | collective-permute-done | bytes 262176 | tf_op jit(solution)/shard_map/ppermute | solution.py:38
  75.4 1.6 %collective-permute-start.19 = (bf16[1,2,4,128,128]{4,3,2,1,0:T(8,128)(2,1)S(1)}, bf16[1,2,4,128,128]{4,3,2,1,0:T(8,128)(2,1)S(1)}, u32[]{:S(2)}, u32[]{:S(2)}) collective-permute-start(bf16[1,2,4,128,128]{4,3,2,1,0:T(8,128)(2,1)S(1)} %add_convert_fusion.2), channel_id=1, source_target_pairs={{0,2},{1,3},{2,0},{3,1},{4,6},{5,7},{6,4},{7,5},{8,10},{9,11},{10,... | collective-permute-start | bytes 786440 | tf_op jit(solution)/shard_map/ppermute | solution.py:38
  77.1 2.2 %collective-permute-start.23 = (bf16[1,3,64,256]{3,2,1,0:T(8,128)(2,1)S(1)}, bf16[1,3,64,256]{3,2,1,0:T(8,128)(2,1)S(1)}, u32[]{:S(2)}, u32[]{:S(2)}) collective-permute-start(bf16[1,3,64,256]{3,2,1,0:T(8,128)(2,1)S(1)} %fusion.7), channel_id=1, source_target_pairs={{0,8},{4,12},{8,0},{12,4},{1,9},{5,13},{9,1},{13,5},{2,10},{6,14},... | collective-permute-start | bytes 294920 | tf_op jit(solution)/shard_map/ppermute | solution.py:38
  79.3 3.6 %collective-permute-done.19 = bf16[1,2,4,128,128]{4,3,2,1,0:T(8,128)(2,1)S(1)} collective-permute-done((bf16[1,2,4,128,128]{4,3,2,1,0:T(8,128)(2,1)S(1)}, bf16[1,2,4,128,128]{4,3,2,1,0:T(8,128)(2,1)S(1)}, u32[]{:S(2)}, u32[]{:S(2)}) %collective-permute-start.19) | collective-permute-done | bytes 262176 | tf_op jit(solution)/shard_map/ppermute | solution.py:38
  82.9 2.8 %collective-permute-done.16 = bf16[2,4,128,128]{3,2,1,0:T(8,128)(2,1)S(1)} collective-permute-done((bf16[2,4,128,128]{3,2,1,0:T(8,128)(2,1)S(1)}, bf16[2,4,128,128]{3,2,1,0:T(8,128)(2,1)S(1)}, u32[]{:S(2)}, u32[]{:S(2)}) %collective-permute-start.16) | collective-permute-done | bytes 262176 | tf_op jit(solution)/shard_map/ppermute | solution.py:33
  86.0 1.6 %collective-permute-start.20 = (bf16[1,2,4,128,128]{4,3,2,1,0:T(8,128)(2,1)S(1)}, bf16[1,2,4,128,128]{4,3,2,1,0:T(8,128)(2,1)S(1)}, u32[]{:S(2)}, u32[]{:S(2)}) collective-permute-start(bf16[1,2,4,128,128]{4,3,2,1,0:T(8,128)(2,1)S(1)} %add_convert_fusion.1), channel_id=1, source_target_pairs={{0,2},{1,3},{2,0},{3,1},{4,6},{5,7},{6,4},{7,5},{8,10},{9,11},{10,... | collective-permute-start | bytes 786440 | tf_op jit(solution)/shard_map/ppermute | solution.py:38
  87.6 8.9 %collective-permute-done.23 = bf16[1,3,64,256]{3,2,1,0:T(8,128)(2,1)S(1)} collective-permute-done((bf16[1,3,64,256]{3,2,1,0:T(8,128)(2,1)S(1)}, bf16[1,3,64,256]{3,2,1,0:T(8,128)(2,1)S(1)}, u32[]{:S(2)}, u32[]{:S(2)}) %collective-permute-start.23) | collective-permute-done | bytes 98336 | tf_op jit(solution)/shard_map/ppermute | solution.py:38
  96.7 5.7 %collective-permute-done.25.refs_2_ = bf16[3,64,256]{2,1,0:T(8,128)(2,1)S(1)} collective-permute-done((bf16[3,64,256]{2,1,0:T(8,128)(2,1)S(1)}, bf16[3,64,256]{2,1,0:T(8,128)(2,1)S(1)}, u32[]{:S(2)}, u32[]{:S(2)}) %collective-permute-start.25) | collective-permute-done | bytes 98336 | tf_op jit(solution)/shard_map/ppermute | solution.py:38
  103.6 3.4 %collective-permute-done.26.refs_3_ = bf16[3,64,256]{2,1,0:T(8,128)(2,1)S(1)} collective-permute-done((bf16[3,64,256]{2,1,0:T(8,128)(2,1)S(1)}, bf16[3,64,256]{2,1,0:T(8,128)(2,1)S(1)}, u32[]{:S(2)}, u32[]{:S(2)}) %collective-permute-start.26) | collective-permute-done | bytes 98336 | tf_op jit(solution)/shard_map/ppermute | solution.py:38
  (63 shorter events, 8.6 us)
Async XLA Ops:
  1.7 10.7 %collective-permute-start = (bf16[2,128,512]{2,1,0:T(8,128)(2,1)S(1)}, bf16[2,128,512]{2,1,0:T(8,128)(2,1)S(1)}, u32[]{:S(2)}, u32[]{:S(2)}) collective-permute-start(bf16[2,128,512]{2,1,0:T(8,128)(2,1)S(1)} %dynamic-slice_bitcast_fusion), channel_id=1, source_target_pairs={{0,12},{4,0},{8,4},{12,8},{1,13},{5,1},{9,5},{13,9},{2,14},{6,2},{... | collective-permute-start | bytes 786440 | tf_op jit(solution)/shard_map/ppermute | solution.py:33
  12.3 9.0 %collective-permute-start.1 = (bf16[2,128,512]{2,1,0:T(8,128)(2,1)S(1)}, bf16[2,128,512]{2,1,0:T(8,128)(2,1)S(1)}, u32[]{:S(2)}, u32[]{:S(2)}) collective-permute-start(bf16[2,128,512]{2,1,0:T(8,128)(2,1)S(1)} %collective-permute-done.refs_1_), channel_id=1, source_target_pairs={{0,12},{4,0},{8,4},{12,8},{1,13},{5,1},{9,5},{13,9},{2,14},{6,2},{... | collective-permute-start | bytes 786440 | tf_op jit(solution)/shard_map/ppermute | solution.py:33
  16.6 8.2 %collective-permute-start.2 = (bf16[2,128,512]{2,1,0:T(8,128)(2,1)S(1)}, bf16[2,128,512]{2,1,0:T(8,128)(2,1)S(1)}, u32[]{:S(2)}, u32[]{:S(2)}) collective-permute-start(bf16[2,128,512]{2,1,0:T(8,128)(2,1)S(1)} %collective-permute-done.refs_1_), channel_id=1, source_target_pairs={{0,2},{1,3},{2,0},{3,1},{4,6},{5,7},{6,4},{7,5},{8,10},{9,11},{10,... | collective-permute-start | bytes 786440 | tf_op jit(solution)/shard_map/ppermute | solution.py:38
  21.3 7.8 %collective-permute-start.5 = (bf16[2,128,512]{2,1,0:T(8,128)(2,1)S(1)}, bf16[2,128,512]{2,1,0:T(8,128)(2,1)S(1)}, u32[]{:S(2)}, u32[]{:S(2)}) collective-permute-start(bf16[2,128,512]{2,1,0:T(8,128)(2,1)S(1)} %collective-permute-done.1.refs_5_), channel_id=1, source_target_pairs={{0,2},{1,3},{2,0},{3,1},{4,6},{5,7},{6,4},{7,5},{8,10},{9,11},{10,... | collective-permute-start | bytes 786440 | tf_op jit(solution)/shard_map/ppermute | solution.py:38
  22.8 7.0 %collective-permute-start.3 = (bf16[2,128,512]{2,1,0:T(8,128)(2,1)S(1)}, bf16[2,128,512]{2,1,0:T(8,128)(2,1)S(1)}, u32[]{:S(2)}, u32[]{:S(2)}) collective-permute-start(bf16[2,128,512]{2,1,0:T(8,128)(2,1)S(1)} %collective-permute-done.refs_1_), channel_id=1, source_target_pairs={{0,1},{1,0},{2,3},{3,2},{4,5},{5,4},{6,7},{7,6},{8,9},{9,8},{10,11... | collective-permute-start | bytes 786440 | tf_op jit(solution)/shard_map/ppermute | solution.py:38
  22.8 7.0 %collective-permute-start.6 = (bf16[2,128,512]{2,1,0:T(8,128)(2,1)S(1)}, bf16[2,128,512]{2,1,0:T(8,128)(2,1)S(1)}, u32[]{:S(2)}, u32[]{:S(2)}) collective-permute-start(bf16[2,128,512]{2,1,0:T(8,128)(2,1)S(1)} %collective-permute-done.1.refs_5_), channel_id=1, source_target_pairs={{0,1},{1,0},{2,3},{3,2},{4,5},{5,4},{6,7},{7,6},{8,9},{9,8},{10,11... | collective-permute-start | bytes 786440 | tf_op jit(solution)/shard_map/ppermute | solution.py:38
  24.8 5.0 %collective-permute-start.4 = (bf16[2,128,512]{2,1,0:T(8,128)(2,1)S(1)}, bf16[2,128,512]{2,1,0:T(8,128)(2,1)S(1)}, u32[]{:S(2)}, u32[]{:S(2)}) collective-permute-start(bf16[2,128,512]{2,1,0:T(8,128)(2,1)S(1)} %collective-permute-done.2.refs_2_), channel_id=1, source_target_pairs={{0,1},{1,0},{2,3},{3,2},{4,5},{5,4},{6,7},{7,6},{8,9},{9,8},{10,11... | collective-permute-start | bytes 786440 | tf_op jit(solution)/shard_map/ppermute | solution.py:38
  53.4 11.2 %collective-permute-start.12 = (bf16[1,12,64,256]{3,2,1,0:T(8,128)(2,1)S(1)}, bf16[1,12,64,256]{3,2,1,0:T(8,128)(2,1)S(1)}, u32[]{:S(2)}, u32[]{:S(2)}) collective-permute-start(bf16[1,12,64,256]{3,2,1,0:T(8,128)(2,1)S(1)} %add_convert_fusion), channel_id=1, source_target_pairs={{0,2},{1,3},{2,0},{3,1},{4,6},{5,7},{6,4},{7,5},{8,10},{9,11},{10,... | collective-permute-start | bytes 1179656 | tf_op jit(solution)/shard_map/ppermute | solution.py:38
  64.7 2.1 %collective-permute-start.15 = (bf16[1,12,64,256]{3,2,1,0:T(8,128)(2,1)S(1)}, bf16[1,12,64,256]{3,2,1,0:T(8,128)(2,1)S(1)}, u32[]{:S(2)}, u32[]{:S(2)}) collective-permute-start(bf16[1,12,64,256]{3,2,1,0:T(8,128)(2,1)S(1)} %get-tuple-element.75), channel_id=1, source_target_pairs={{0,1},{1,0},{2,3},{3,2},{4,5},{5,4},{6,7},{7,6},{8,9},{9,8},{10,11... | collective-permute-start | bytes 1179656 | tf_op jit(solution)/shard_map/ppermute | solution.py:38
  65.2 37.2 %collective-permute-start.9 = (bf16[1,2,4,128,128]{4,3,2,1,0:T(8,128)(2,1)S(1)}, bf16[1,2,4,128,128]{4,3,2,1,0:T(8,128)(2,1)S(1)}, u32[]{:S(2)}, u32[]{:S(2)}) collective-permute-start(bf16[1,2,4,128,128]{4,3,2,1,0:T(8,128)(2,1)S(1)} %get-tuple-element.66), channel_id=1, source_target_pairs={{0,1},{1,0},{2,3},{3,2},{4,5},{5,4},{6,7},{7,6},{8,9},{9,8},{10,11... | collective-permute-start | bytes 786440 | tf_op jit(solution)/shard_map/ppermute | solution.py:38
  65.2 3.2 %collective-permute-start.11 = (bf16[1,2,4,128,128]{4,3,2,1,0:T(8,128)(2,1)S(1)}, bf16[1,2,4,128,128]{4,3,2,1,0:T(8,128)(2,1)S(1)}, u32[]{:S(2)}, u32[]{:S(2)}) collective-permute-start(bf16[1,2,4,128,128]{4,3,2,1,0:T(8,128)(2,1)S(1)} %get-tuple-element.70), channel_id=1, source_target_pairs={{0,1},{1,0},{2,3},{3,2},{4,5},{5,4},{6,7},{7,6},{8,9},{9,8},{10,11... | collective-permute-start | bytes 786440 | tf_op jit(solution)/shard_map/ppermute | solution.py:38
  65.7 11.4 %collective-permute-start.17 = (bf16[1,2,4,128,128]{4,3,2,1,0:T(8,128)(2,1)S(1)}, bf16[1,2,4,128,128]{4,3,2,1,0:T(8,128)(2,1)S(1)}, u32[]{:S(2)}, u32[]{:S(2)}) collective-permute-start(bf16[1,2,4,128,128]{4,3,2,1,0:T(8,128)(2,1)S(1)} %get-tuple-element.78), channel_id=1, source_target_pairs={{0,1},{1,0},{2,3},{3,2},{4,5},{5,4},{6,7},{7,6},{8,9},{9,8},{10,11... | collective-permute-start | bytes 786440 | tf_op jit(solution)/shard_map/ppermute | solution.py:38
  66.2 9.1 %collective-permute-start.18 = (bf16[1,2,4,128,128]{4,3,2,1,0:T(8,128)(2,1)S(1)}, bf16[1,2,4,128,128]{4,3,2,1,0:T(8,128)(2,1)S(1)}, u32[]{:S(2)}, u32[]{:S(2)}) collective-permute-start(bf16[1,2,4,128,128]{4,3,2,1,0:T(8,128)(2,1)S(1)} %get-tuple-element.80), channel_id=1, source_target_pairs={{0,1},{1,0},{2,3},{3,2},{4,5},{5,4},{6,7},{7,6},{8,9},{9,8},{10,11... | collective-permute-start | bytes 786440 | tf_op jit(solution)/shard_map/ppermute | solution.py:38
  66.8 8.3 %collective-permute-start.14 = (bf16[1,2,4,128,128]{4,3,2,1,0:T(8,128)(2,1)S(1)}, bf16[1,2,4,128,128]{4,3,2,1,0:T(8,128)(2,1)S(1)}, u32[]{:S(2)}, u32[]{:S(2)}) collective-permute-start(bf16[1,2,4,128,128]{4,3,2,1,0:T(8,128)(2,1)S(1)} %add_convert_fusion.4), channel_id=1, source_target_pairs={{0,2},{1,3},{2,0},{3,1},{4,6},{5,7},{6,4},{7,5},{8,10},{9,11},{10,... | collective-permute-start | bytes 786440 | tf_op jit(solution)/shard_map/ppermute | solution.py:38
  68.4 8.5 %collective-permute-start.22 = (bf16[2,3,64,256]{3,2,1,0:T(8,128)(2,1)S(1)}, bf16[2,3,64,256]{3,2,1,0:T(8,128)(2,1)S(1)}, u32[]{:S(2)}, u32[]{:S(2)}) collective-permute-start(bf16[2,3,64,256]{3,2,1,0:T(8,128)(2,1)S(1)} %fusion.2), channel_id=1, source_target_pairs={{0,4},{4,0},{8,12},{12,8},{1,5},{5,1},{9,13},{13,9},{2,6},{6,2},{1... | collective-permute-start | bytes 589832 | tf_op jit(solution)/shard_map/ppermute | solution.py:38
  75.2 10.5 %collective-permute-start.16 = (bf16[2,4,128,128]{3,2,1,0:T(8,128)(2,1)S(1)}, bf16[2,4,128,128]{3,2,1,0:T(8,128)(2,1)S(1)}, u32[]{:S(2)}, u32[]{:S(2)}) collective-permute-start(bf16[2,4,128,128]{3,2,1,0:T(8,128)(2,1)S(1)} %fusion.1), channel_id=1, source_target_pairs={{0,4},{4,8},{8,12},{12,0},{1,5},{5,9},{9,13},{13,1},{2,6},{6,10},{... | collective-permute-start | bytes 786440 | tf_op jit(solution)/shard_map/ppermute | solution.py:33
  75.4 7.6 %collective-permute-start.19 = (bf16[1,2,4,128,128]{4,3,2,1,0:T(8,128)(2,1)S(1)}, bf16[1,2,4,128,128]{4,3,2,1,0:T(8,128)(2,1)S(1)}, u32[]{:S(2)}, u32[]{:S(2)}) collective-permute-start(bf16[1,2,4,128,128]{4,3,2,1,0:T(8,128)(2,1)S(1)} %add_convert_fusion.2), channel_id=1, source_target_pairs={{0,2},{1,3},{2,0},{3,1},{4,6},{5,7},{6,4},{7,5},{8,10},{9,11},{10,... | collective-permute-start | bytes 786440 | tf_op jit(solution)/shard_map/ppermute | solution.py:38
  77.0 9.0 %collective-permute-start.10 = (bf16[1,2,4,128,128]{4,3,2,1,0:T(8,128)(2,1)S(1)}, bf16[1,2,4,128,128]{4,3,2,1,0:T(8,128)(2,1)S(1)}, u32[]{:S(2)}, u32[]{:S(2)}) collective-permute-start(bf16[1,2,4,128,128]{4,3,2,1,0:T(8,128)(2,1)S(1)} %get-tuple-element.68), channel_id=1, source_target_pairs={{0,1},{1,0},{2,3},{3,2},{4,5},{5,4},{6,7},{7,6},{8,9},{9,8},{10,11... | collective-permute-start | bytes 786440 | tf_op jit(solution)/shard_map/ppermute | solution.py:38
  77.1 19.4 %collective-permute-start.23 = (bf16[1,3,64,256]{3,2,1,0:T(8,128)(2,1)S(1)}, bf16[1,3,64,256]{3,2,1,0:T(8,128)(2,1)S(1)}, u32[]{:S(2)}, u32[]{:S(2)}) collective-permute-start(bf16[1,3,64,256]{3,2,1,0:T(8,128)(2,1)S(1)} %fusion.7), channel_id=1, source_target_pairs={{0,8},{4,12},{8,0},{12,4},{1,9},{5,13},{9,1},{13,5},{2,10},{6,14},... | collective-permute-start | bytes 294920 | tf_op jit(solution)/shard_map/ppermute | solution.py:38
  85.9 16.5 %collective-permute-start.21 = (bf16[2,4,128,128]{3,2,1,0:T(8,128)(2,1)S(1)}, bf16[2,4,128,128]{3,2,1,0:T(8,128)(2,1)S(1)}, u32[]{:S(2)}, u32[]{:S(2)}) collective-permute-start(bf16[2,4,128,128]{3,2,1,0:T(8,128)(2,1)S(1)} %fusion), channel_id=1, source_target_pairs={{0,4},{4,8},{8,12},{12,0},{1,5},{5,9},{9,13},{13,1},{2,6},{6,10},{... | collective-permute-start | bytes 786440 | tf_op jit(solution)/shard_map/ppermute | solution.py:33
  86.0 16.4 %collective-permute-start.20 = (bf16[1,2,4,128,128]{4,3,2,1,0:T(8,128)(2,1)S(1)}, bf16[1,2,4,128,128]{4,3,2,1,0:T(8,128)(2,1)S(1)}, u32[]{:S(2)}, u32[]{:S(2)}) collective-permute-start(bf16[1,2,4,128,128]{4,3,2,1,0:T(8,128)(2,1)S(1)} %add_convert_fusion.1), channel_id=1, source_target_pairs={{0,2},{1,3},{2,0},{3,1},{4,6},{5,7},{6,4},{7,5},{8,10},{9,11},{10,... | collective-permute-start | bytes 786440 | tf_op jit(solution)/shard_map/ppermute | solution.py:38
  96.6 5.8 %collective-permute-start.25 = (bf16[3,64,256]{2,1,0:T(8,128)(2,1)S(1)}, bf16[3,64,256]{2,1,0:T(8,128)(2,1)S(1)}, u32[]{:S(2)}, u32[]{:S(2)}) collective-permute-start(bf16[3,64,256]{2,1,0:T(8,128)(2,1)S(1)} %fusion.6.refs_0_), channel_id=1, source_target_pairs={{0,8},{4,12},{8,0},{12,4},{1,9},{5,13},{9,1},{13,5},{2,10},{6,14},... | collective-permute-start | bytes 294920 | tf_op jit(solution)/shard_map/ppermute | solution.py:38
  96.6 6.9 %collective-permute-start.24 = (bf16[3,64,256]{2,1,0:T(8,128)(2,1)S(1)}, bf16[3,64,256]{2,1,0:T(8,128)(2,1)S(1)}, u32[]{:S(2)}, u32[]{:S(2)}) collective-permute-start(bf16[3,64,256]{2,1,0:T(8,128)(2,1)S(1)} %fusion.6.refs_0_), channel_id=1, source_target_pairs={{0,4},{4,0},{8,12},{12,8},{1,5},{5,1},{9,13},{13,9},{2,6},{6,2},{1... | collective-permute-start | bytes 294920 | tf_op jit(solution)/shard_map/ppermute | solution.py:38
  102.4 4.6 %collective-permute-start.26 = (bf16[3,64,256]{2,1,0:T(8,128)(2,1)S(1)}, bf16[3,64,256]{2,1,0:T(8,128)(2,1)S(1)}, u32[]{:S(2)}, u32[]{:S(2)}) collective-permute-start(bf16[3,64,256]{2,1,0:T(8,128)(2,1)S(1)} %collective-permute-done.25.refs_2_), channel_id=1, source_target_pairs={{0,4},{4,0},{8,12},{12,8},{1,5},{5,1},{9,13},{13,9},{2,6},{6,2},{1... | collective-permute-start | bytes 294920 | tf_op jit(solution)/shard_map/ppermute | solution.py:38
  (10 other events, 107.3 us)

commit v5 on v4

--- a/solution.py
+++ b/solution.py
@@ -507,37 +507,14 @@
         bit *= 2
 
 
-def scatter_rows(axis, value):
+def scatter_sum(axis, value, relative):
     me = lax.axis_index(axis)
-    total = lax.dynamic_index_in_dim(value, me, 0, False)
-    sent = []
-    for i in range(1, lax.axis_size(axis)):
-        sent.append(lax.dynamic_index_in_dim(value, me ^ i, 0, False).astype(jnp.bfloat16))
-        total += swap(sent[-1], axis, i).astype(jnp.float32)
+    share = (lambda i: value[i]) if relative else (lambda i: lax.dynamic_index_in_dim(value, me ^ i, 0, False))
+    total = share(0)
+    sent = [share(i).astype(jnp.bfloat16) for i in range(1, lax.axis_size(axis))]
+    for i, sending in enumerate(sent, 1):
+        total += swap(sending, axis, i).astype(jnp.float32)
     return total.astype(jnp.bfloat16), sent
-
-
-def scatter_sum(axis, value):
-    terms = [value]
-    sent = []
-    bit = 1
-    while bit < lax.axis_size(axis):
-        pick = lambda term, which: term.reshape((term.shape[0] // 2, 2) + term.shape[1:])[:, which]
-        sent.append(sum(pick(term, 1).astype(jnp.float32) for term in terms).astype(jnp.bfloat16))
-        terms = [pick(term, 0) for term in terms] + [swap(sent[-1], axis, bit)]
-        bit *= 2
-    return sum(term[0].astype(jnp.float32) for term in terms).astype(jnp.bfloat16), sent
-
-
-def gather_shares(axis, total, *others):
-    held = {0: total}
-    bit = lax.axis_size(axis) // 2
-    while bit:
-        held.update({i ^ bit: swap(piece, axis, bit) for i, piece in held.items()})
-        if others:
-            held[bit], others = after(held[bit], *others), ()
-        bit //= 2
-    return [held[i] for i in range(lax.axis_size(axis))]
 
 
 def place_kernel(axis, *refs):
@@ -616,19 +593,19 @@
     out = scatter(shares, side, indices, after(grads, leaving))
     send, keep = ([out[at + 2 * i:at + 2 * i + 2] for i in range(REACH)] for at in (0, 2 * REACH))
     last = REACH - 1
-    share = share_of(2 * modes, blocks)
-    if share:
-        total, sent = scatter_sum("blk", eigen.reshape((blocks, share) + eigen.shape[1:]))
-    else:
-        total, sent = scatter_rows("blk", eigen.reshape(blocks, -1, frame))
-    mine, _, _ = halve(keep[last], send[last], before_core=(crossed,))
-    moving = after(mine.astype(jnp.bfloat16), *sent[:1])
+    relative = share_of(2 * modes, blocks) > 0
+    total, sent = scatter_sum("blk", eigen.reshape(blocks, -1, frame), relative)
+    mine, leaving, _ = halve(keep[last], send[last], before_cross=sent)
+    moving = after(mine.astype(jnp.bfloat16), total)
     for section in range(last - 1, -1, -1):
-        mine, _, _ = halve(keep[section], send[section], before_cross=(moving,))
+        mine, leaving, _ = halve(keep[section], send[section], before_cross=(moving,))
+        if section == last - 1:
+            total = after(total, leaving)
         arrived = shift(moving, "blk", 1)
         if section > 0:
             moving = (arrived.astype(jnp.float32) + mine).astype(jnp.bfloat16)
-    eigen_share = place("blk", gather_shares("blk", total, arrived))
+    gathered = [swap(total, "blk", i) for i in range(1, blocks)]
+    eigen_share = place("blk", [after(total, arrived)] + gathered)
     eigen_share = eigen_share.reshape(modes, 2, frame // shares, frame)
     summed = finish(mine, arrived)
     return (summed[None], eigen_share, coef_rows.T)

time: 108 us -> 106 us (0.981)
  waiting for transfers between devices: 49.8 us -> 42.4 us
  starting transfers between devices: 23 us -> 28 us
    ppermute x23 -> x24, waiting for transfers between devices: 41.2 us -> 25.2 us  [swap(): return lax.ppermute(array, axis, [(i, i ^ bit) for i in range(peers)])]
    ppermute x4, waiting for transfers between devices: 8.61 us -> 17.1 us  [shift(): lax.ppermute(array, axis, [(i, (i + by) % peers) for i in range(peers)])]
    ppermute x23 -> x24, starting transfers between devices: 13.5 us -> 17.2 us  [swap(): return lax.ppermute(array, axis, [(i, i ^ bit) for i in range(peers)])]
    ppermute x4, starting transfers between devices: 9.5 us -> 10.7 us  [shift(): lax.ppermute(array, axis, [(i, (i + by) % peers) for i in range(peers)])]
  transfers between devices with their start and end apart: 27 -> 28, of which waited for: 16 -> 15; matrix products, arithmetic and copies ran while one was open for 1% -> 1% of each run, Pallas kernels for 7% -> 7%
where the time goes in v5:
time: 106 us
  waiting for transfers between devices  42.4 us (40%)
  Pallas kernels  29 us (27%)
  starting transfers between devices  28 us (26%)
  local copies, waits for them, and re-layouts  3.77 us (4%)
  between operations  1.53 us (1%)
    ppermute x24, waiting for transfers between devices, swap(): return lax.ppermute(array, axis, [(i, i ^ bit) for i in range(peers)])  25.2 us
    pallas_call x1, Pallas kernels, positions(): pl.pallas_call(functools.partial(position_kernel, offs, scale), in_specs=...  20.9 us
    ppermute x24, starting transfers between devices, swap(): return lax.ppermute(array, axis, [(i, i ^ bit) for i in range(peers)])  17.2 us
    ppermute x4, waiting for transfers between devices, shift(): lax.ppermute(array, axis, [(i, (i + by) % peers) for i in range(peers)])  17.1 us
    ppermute x4, starting transfers between devices, shift(): lax.ppermute(array, axis, [(i, (i + by) % peers) for i in range(peers)])  10.7 us
    pallas_call x1, Pallas kernels, scatter(): pl.pallas_call(functools.partial(scatter_kernel, shares), in_specs=[pl.Bl...  5.96 us
    unnamed x14, local copies, waits for them, and re-layouts  2.75 us
  transfers between devices with their start and end apart: 28, of which 15 were waited for; matrix products, arithmetic and copies ran while one was open for 1% of the time, Pallas kernels for 7%

profile of v5, /device:TPU:0, one launch (start us, length us, event | category | flops | bytes accessed | tf_op | source)
XLA Modules:
  0.0 105.5 jit_solution(10987741663215368453)
XLA Ops:
  1.7 5.1 %collective-permute-start = (bf16[2,128,512]{2,1,0:T(8,128)(2,1)S(1)}, bf16[2,128,512]{2,1,0:T(8,128)(2,1)S(1)}, u32[]{:S(2)}, u32[]{:S(2)}) collective-permute-start(bf16[2,128,512]{2,1,0:T(8,128)(2,1)S(1)} %dynamic-slice_bitcast_fusion), channel_id=1, source_target_pairs={{0,12},{4,0},{8,4},{12,8},{1,13},{5,1},{9,5},{13,9},{2,14},{6,2},{... | collective-permute-start | bytes 786440 | tf_op jit(solution)/shard_map/ppermute | solution.py:33
  6.8 5.6 %collective-permute-done.refs_1_ = bf16[2,128,512]{2,1,0:T(8,128)(2,1)S(1)} collective-permute-done((bf16[2,128,512]{2,1,0:T(8,128)(2,1)S(1)}, bf16[2,128,512]{2,1,0:T(8,128)(2,1)S(1)}, u32[]{:S(2)}, u32[]{:S(2)}) %collective-permute-start) | collective-permute-done | bytes 262176 | tf_op jit(solution)/shard_map/ppermute | solution.py:33
  12.3 4.3 %collective-permute-start.1 = (bf16[2,128,512]{2,1,0:T(8,128)(2,1)S(1)}, bf16[2,128,512]{2,1,0:T(8,128)(2,1)S(1)}, u32[]{:S(2)}, u32[]{:S(2)}) collective-permute-start(bf16[2,128,512]{2,1,0:T(8,128)(2,1)S(1)} %collective-permute-done.refs_1_), channel_id=1, source_target_pairs={{0,12},{4,0},{8,4},{12,8},{1,13},{5,1},{9,5},{13,9},{2,14},{6,2},{... | collective-permute-start | bytes 786440 | tf_op jit(solution)/shard_map/ppermute | solution.py:33
  16.6 1.5 %collective-permute-start.2 = (bf16[2,128,512]{2,1,0:T(8,128)(2,1)S(1)}, bf16[2,128,512]{2,1,0:T(8,128)(2,1)S(1)}, u32[]{:S(2)}, u32[]{:S(2)}) collective-permute-start(bf16[2,128,512]{2,1,0:T(8,128)(2,1)S(1)} %collective-permute-done.refs_1_), channel_id=1, source_target_pairs={{0,2},{1,3},{2,0},{3,1},{4,6},{5,7},{6,4},{7,5},{8,10},{9,11},{10,... | collective-permute-start | bytes 786440 | tf_op jit(solution)/shard_map/ppermute | solution.py:38
  18.1 1.4 %copy-done.1 = bf16[6,2,256,256]{3,2,1,0:T(8,128)(2,1)S(1)} copy-done((bf16[6,2,256,256]{3,2,1,0:T(8,128)(2,1)S(1)}, bf16[6,2,256,256]{3,2,1,0:T(8,128)(2,1)}, u32[]{:S(2)}) %copy-start.1) | copy-done | bytes 1572888
  19.5 1.3 %copy-done.2 = bf16[10,256,256]{2,1,0:T(8,128)(2,1)S(1)} copy-done((bf16[10,256,256]{2,1,0:T(8,128)(2,1)S(1)}, bf16[10,256,256]{2,1,0:T(8,128)(2,1)}, u32[]{:S(2)}) %copy-start.2) | copy-done | bytes 1310744
  21.3 1.5 %collective-permute-start.5 = (bf16[2,128,512]{2,1,0:T(8,128)(2,1)S(1)}, bf16[2,128,512]{2,1,0:T(8,128)(2,1)S(1)}, u32[]{:S(2)}, u32[]{:S(2)}) collective-permute-start(bf16[2,128,512]{2,1,0:T(8,128)(2,1)S(1)} %collective-permute-done.1.refs_5_), channel_id=1, source_target_pairs={{0,2},{1,3},{2,0},{3,1},{4,6},{5,7},{6,4},{7,5},{8,10},{9,11},{10,... | collective-permute-start | bytes 786440 | tf_op jit(solution)/shard_map/ppermute | solution.py:38
  23.3 1.5 %collective-permute-done.2.refs_2_ = bf16[2,128,512]{2,1,0:T(8,128)(2,1)S(1)} collective-permute-done((bf16[2,128,512]{2,1,0:T(8,128)(2,1)S(1)}, bf16[2,128,512]{2,1,0:T(8,128)(2,1)S(1)}, u32[]{:S(2)}, u32[]{:S(2)}) %collective-permute-start.2) | collective-permute-done | bytes 262176 | tf_op jit(solution)/shard_map/ppermute | solution.py:38
  25.1 4.1 %collective-permute-done.5.refs_6_ = bf16[2,128,512]{2,1,0:T(8,128)(2,1)S(1)} collective-permute-done((bf16[2,128,512]{2,1,0:T(8,128)(2,1)S(1)}, bf16[2,128,512]{2,1,0:T(8,128)(2,1)S(1)}, u32[]{:S(2)}, u32[]{:S(2)}) %collective-permute-start.5) | collective-permute-done | bytes 262176 | tf_op jit(solution)/shard_map/ppermute | solution.py:38
  30.7 20.9 %positions.1 = (bf16[1,12,64,256]{3,2,1,0:T(8,128)(2,1)S(1)}, bf16[1,12,64,256]{3,2,1,0:T(8,128)(2,1)S(1)}, f32[1,12,64,256]{3,2,1,0:T(8,128)S(1)}, f32[1,12,64,...) custom-call(s32[2,10]{1,0:T(2,128)S(1)} %get-tuple-element.54.tile_list, ...), custom_call_target="tpu_custom_call" | custom-call | tf_op jit(solution)/shard_map/positions/pallas_call | solution.py:346
  52.1 1.2 %collective-permute-done.8 = bf16[1,12,64,256]{3,2,1,0:T(8,128)(2,1)S(1)} collective-permute-done((bf16[1,12,64,256]{3,2,1,0:T(8,128)(2,1)S(1)}, bf16[1,12,64,256]{3,2,1,0:T(8,128)(2,1)S(1)}, u32[]{:S(2)}, u32[]{:S(2)}) %collective-permute-start.8) | collective-permute-done | bytes 393248 | tf_op jit(solution)/shard_map/ppermute | solution.py:38
  53.5 6.0 %scatter.1 = (bf16[1,2,4,128,128]{4,3,2,1,0:T(8,128)(2,1)S(1)}, bf16[1,2,4,128,128]{4,3,2,1,0:T(8,128)(2,1)S(1)}, bf16[1,2,4,128,128]{4,3,2,1,0:T(8,128)(2,1)S(1...) custom-call(s32[2,10]{1,0:T(2,128)S(1)} %get-tuple-element.54.tile_l, ...), custom_call_target="tpu_custom_call" | custom-call | flops 16777216 | bytes 16777216 | tf_op jit(solution)/shard_map/scatter/pallas_call | solution.py:467
  60.1 4.6 %collective-permute-done.14 = bf16[1,12,64,256]{3,2,1,0:T(8,128)(2,1)S(1)} collective-permute-done((bf16[1,12,64,256]{3,2,1,0:T(8,128)(2,1)S(1)}, bf16[1,12,64,256]{3,2,1,0:T(8,128)(2,1)S(1)}, u32[]{:S(2)}, u32[]{:S(2)}) %collective-permute-start.14) | collective-permute-done | bytes 393248 | tf_op jit(solution)/shard_map/ppermute | solution.py:38
  64.9 2.9 %collective-permute-start.18 = (bf16[192,256]{1,0:T(8,128)(2,1)S(1)}, bf16[192,256]{1,0:T(8,128)(2,1)S(1)}, u32[]{:S(2)}, u32[]{:S(2)}) collective-permute-start(bf16[192,256]{1,0:T(8,128)(2,1)S(1)} %bitcast.35), channel_id=1, source_target_pairs={{0,12},{4,8},{8,4},{12,0},{1,13},{5,9},{9,5},{13,1},{2,14},{6,10},... | collective-permute-start | bytes 294920 | tf_op jit(solution)/shard_map/ppermute | solution.py:38
  68.5 1.4 %collective-permute-start.15 = (bf16[1,2,4,128,128]{4,3,2,1,0:T(8,128)(2,1)S(1)}, bf16[1,2,4,128,128]{4,3,2,1,0:T(8,128)(2,1)S(1)}, u32[]{:S(2)}, u32[]{:S(2)}) collective-permute-start(bf16[1,2,4,128,128]{4,3,2,1,0:T(8,128)(2,1)S(1)} %add_convert_fusion.4), channel_id=1, source_target_pairs={{0,2},{1,3},{2,0},{3,1},{4,6},{5,7},{6,4},{7,5},{8,10},{9,11},{10,... | collective-permute-start | bytes 786440 | tf_op jit(solution)/shard_map/ppermute | solution.py:38
  69.9 4.5 %collective-permute-done.17 = bf16[192,256]{1,0:T(8,128)(2,1)S(1)} collective-permute-done((bf16[192,256]{1,0:T(8,128)(2,1)S(1)}, bf16[192,256]{1,0:T(8,128)(2,1)S(1)}, u32[]{:S(2)}, u32[]{:S(2)}) %collective-permute-start.17) | collective-permute-done | bytes 98336 | tf_op jit(solution)/shard_map/ppermute | solution.py:38
  76.4 1.3 %collective-permute-start.22 = (bf16[1,2,4,128,128]{4,3,2,1,0:T(8,128)(2,1)S(1)}, bf16[1,2,4,128,128]{4,3,2,1,0:T(8,128)(2,1)S(1)}, u32[]{:S(2)}, u32[]{:S(2)}) collective-permute-start(bf16[1,2,4,128,128]{4,3,2,1,0:T(8,128)(2,1)S(1)} %add_convert_fusion.2), channel_id=1, source_target_pairs={{0,2},{1,3},{2,0},{3,1},{4,6},{5,7},{6,4},{7,5},{8,10},{9,11},{10,... | collective-permute-start | bytes 786440 | tf_op jit(solution)/shard_map/ppermute | solution.py:38
  77.6 1.3 %collective-permute-start.19 = (bf16[2,4,128,128]{3,2,1,0:T(8,128)(2,1)S(1)}, bf16[2,4,128,128]{3,2,1,0:T(8,128)(2,1)S(1)}, u32[]{:S(2)}, u32[]{:S(2)}) collective-permute-start(bf16[2,4,128,128]{3,2,1,0:T(8,128)(2,1)S(1)} %fusion.1), channel_id=1, source_target_pairs={{0,4},{4,8},{8,12},{12,0},{1,5},{5,9},{9,13},{13,1},{2,6},{6,10},{... | collective-permute-start | bytes 786440 | tf_op jit(solution)/shard_map/ppermute | solution.py:33
  79.5 5.3 %collective-permute-done.22 = bf16[1,2,4,128,128]{4,3,2,1,0:T(8,128)(2,1)S(1)} collective-permute-done((bf16[1,2,4,128,128]{4,3,2,1,0:T(8,128)(2,1)S(1)}, bf16[1,2,4,128,128]{4,3,2,1,0:T(8,128)(2,1)S(1)}, u32[]{:S(2)}, u32[]{:S(2)}) %collective-permute-start.22) | collective-permute-done | bytes 262176 | tf_op jit(solution)/shard_map/ppermute | solution.py:38
  84.8 2.7 %collective-permute-done.19 = bf16[2,4,128,128]{3,2,1,0:T(8,128)(2,1)S(1)} collective-permute-done((bf16[2,4,128,128]{3,2,1,0:T(8,128)(2,1)S(1)}, bf16[2,4,128,128]{3,2,1,0:T(8,128)(2,1)S(1)}, u32[]{:S(2)}, u32[]{:S(2)}) %collective-permute-start.19) | collective-permute-done | bytes 262176 | tf_op jit(solution)/shard_map/ppermute | solution.py:33
  88.6 1.6 %collective-permute-start.26 = (bf16[192,256]{1,0:T(8,128)(2,1)S(1)}, bf16[192,256]{1,0:T(8,128)(2,1)S(1)}, u32[]{:S(2)}, u32[]{:S(2)}) collective-permute-start(bf16[192,256]{1,0:T(8,128)(2,1)S(1)} %fusion.4.refs_0_), channel_id=1, source_target_pairs={{0,8},{4,12},{8,0},{12,4},{1,9},{5,13},{9,1},{13,5},{2,10},{6,14},... | collective-permute-start | bytes 294920 | tf_op jit(solution)/shard_map/ppermute | solution.py:38
  90.3 2.7 %collective-permute-start.25 = (bf16[192,256]{1,0:T(8,128)(2,1)S(1)}, bf16[192,256]{1,0:T(8,128)(2,1)S(1)}, u32[]{:S(2)}, u32[]{:S(2)}) collective-permute-start(bf16[192,256]{1,0:T(8,128)(2,1)S(1)} %fusion.4.refs_0_), channel_id=1, source_target_pairs={{0,4},{4,0},{8,12},{12,8},{1,5},{5,1},{9,13},{13,9},{2,6},{6,2},{1... | collective-permute-start | bytes 294920 | tf_op jit(solution)/shard_map/ppermute | solution.py:38
  93.0 2.0 %collective-permute-done.23 = bf16[1,2,4,128,128]{4,3,2,1,0:T(8,128)(2,1)S(1)} collective-permute-done((bf16[1,2,4,128,128]{4,3,2,1,0:T(8,128)(2,1)S(1)}, bf16[1,2,4,128,128]{4,3,2,1,0:T(8,128)(2,1)S(1)}, u32[]{:S(2)}, u32[]{:S(2)}) %collective-permute-start.23) | collective-permute-done | bytes 262176 | tf_op jit(solution)/shard_map/ppermute | solution.py:38
  95.1 8.6 %collective-permute-done.24.second = bf16[2,4,128,128]{3,2,1,0:T(8,128)(2,1)S(1)} collective-permute-done((bf16[2,4,128,128]{3,2,1,0:T(8,128)(2,1)S(1)}, bf16[2,4,128,128]{3,2,1,0:T(8,128)(2,1)S(1)}, u32[]{:S(2)}, u32[]{:S(2)}) %collective-permute-start.24) | collective-permute-done | bytes 262176 | tf_op jit(solution)/shard_map/ppermute | solution.py:33
  (64 shorter events, 10.8 us)
Async XLA Ops:
  1.7 10.7 %collective-permute-start = (bf16[2,128,512]{2,1,0:T(8,128)(2,1)S(1)}, bf16[2,128,512]{2,1,0:T(8,128)(2,1)S(1)}, u32[]{:S(2)}, u32[]{:S(2)}) collective-permute-start(bf16[2,128,512]{2,1,0:T(8,128)(2,1)S(1)} %dynamic-slice_bitcast_fusion), channel_id=1, source_target_pairs={{0,12},{4,0},{8,4},{12,8},{1,13},{5,1},{9,5},{13,9},{2,14},{6,2},{... | collective-permute-start | bytes 786440 | tf_op jit(solution)/shard_map/ppermute | solution.py:33
  12.3 9.0 %collective-permute-start.1 = (bf16[2,128,512]{2,1,0:T(8,128)(2,1)S(1)}, bf16[2,128,512]{2,1,0:T(8,128)(2,1)S(1)}, u32[]{:S(2)}, u32[]{:S(2)}) collective-permute-start(bf16[2,128,512]{2,1,0:T(8,128)(2,1)S(1)} %collective-permute-done.refs_1_), channel_id=1, source_target_pairs={{0,12},{4,0},{8,4},{12,8},{1,13},{5,1},{9,5},{13,9},{2,14},{6,2},{... | collective-permute-start | bytes 786440 | tf_op jit(solution)/shard_map/ppermute | solution.py:33
  16.6 8.2 %collective-permute-start.2 = (bf16[2,128,512]{2,1,0:T(8,128)(2,1)S(1)}, bf16[2,128,512]{2,1,0:T(8,128)(2,1)S(1)}, u32[]{:S(2)}, u32[]{:S(2)}) collective-permute-start(bf16[2,128,512]{2,1,0:T(8,128)(2,1)S(1)} %collective-permute-done.refs_1_), channel_id=1, source_target_pairs={{0,2},{1,3},{2,0},{3,1},{4,6},{5,7},{6,4},{7,5},{8,10},{9,11},{10,... | collective-permute-start | bytes 786440 | tf_op jit(solution)/shard_map/ppermute | solution.py:38
  21.3 7.8 %collective-permute-start.5 = (bf16[2,128,512]{2,1,0:T(8,128)(2,1)S(1)}, bf16[2,128,512]{2,1,0:T(8,128)(2,1)S(1)}, u32[]{:S(2)}, u32[]{:S(2)}) collective-permute-start(bf16[2,128,512]{2,1,0:T(8,128)(2,1)S(1)} %collective-permute-done.1.refs_5_), channel_id=1, source_target_pairs={{0,2},{1,3},{2,0},{3,1},{4,6},{5,7},{6,4},{7,5},{8,10},{9,11},{10,... | collective-permute-start | bytes 786440 | tf_op jit(solution)/shard_map/ppermute | solution.py:38
  22.8 7.0 %collective-permute-start.3 = (bf16[2,128,512]{2,1,0:T(8,128)(2,1)S(1)}, bf16[2,128,512]{2,1,0:T(8,128)(2,1)S(1)}, u32[]{:S(2)}, u32[]{:S(2)}) collective-permute-start(bf16[2,128,512]{2,1,0:T(8,128)(2,1)S(1)} %collective-permute-done.refs_1_), channel_id=1, source_target_pairs={{0,1},{1,0},{2,3},{3,2},{4,5},{5,4},{6,7},{7,6},{8,9},{9,8},{10,11... | collective-permute-start | bytes 786440 | tf_op jit(solution)/shard_map/ppermute | solution.py:38
  22.8 7.0 %collective-permute-start.6 = (bf16[2,128,512]{2,1,0:T(8,128)(2,1)S(1)}, bf16[2,128,512]{2,1,0:T(8,128)(2,1)S(1)}, u32[]{:S(2)}, u32[]{:S(2)}) collective-permute-start(bf16[2,128,512]{2,1,0:T(8,128)(2,1)S(1)} %collective-permute-done.1.refs_5_), channel_id=1, source_target_pairs={{0,1},{1,0},{2,3},{3,2},{4,5},{5,4},{6,7},{7,6},{8,9},{9,8},{10,11... | collective-permute-start | bytes 786440 | tf_op jit(solution)/shard_map/ppermute | solution.py:38
  51.6 8.5 %collective-permute-start.13 = (bf16[1,12,64,256]{3,2,1,0:T(8,128)(2,1)S(1)}, bf16[1,12,64,256]{3,2,1,0:T(8,128)(2,1)S(1)}, u32[]{:S(2)}, u32[]{:S(2)}) collective-permute-start(bf16[1,12,64,256]{3,2,1,0:T(8,128)(2,1)S(1)} %get-tuple-element.75), channel_id=1, source_target_pairs={{0,1},{1,0},{2,3},{3,2},{4,5},{5,4},{6,7},{7,6},{8,9},{9,8},{10,11... | collective-permute-start | bytes 1179656 | tf_op jit(solution)/shard_map/ppermute | solution.py:38
  53.4 11.2 %collective-permute-start.14 = (bf16[1,12,64,256]{3,2,1,0:T(8,128)(2,1)S(1)}, bf16[1,12,64,256]{3,2,1,0:T(8,128)(2,1)S(1)}, u32[]{:S(2)}, u32[]{:S(2)}) collective-permute-start(bf16[1,12,64,256]{3,2,1,0:T(8,128)(2,1)S(1)} %add_convert_fusion), channel_id=1, source_target_pairs={{0,2},{1,3},{2,0},{3,1},{4,6},{5,7},{6,4},{7,5},{8,10},{9,11},{10,... | collective-permute-start | bytes 1179656 | tf_op jit(solution)/shard_map/ppermute | solution.py:38
  59.5 15.7 %collective-permute-start.11 = (bf16[1,2,4,128,128]{4,3,2,1,0:T(8,128)(2,1)S(1)}, bf16[1,2,4,128,128]{4,3,2,1,0:T(8,128)(2,1)S(1)}, u32[]{:S(2)}, u32[]{:S(2)}) collective-permute-start(bf16[1,2,4,128,128]{4,3,2,1,0:T(8,128)(2,1)S(1)} %get-tuple-element.71), channel_id=1, source_target_pairs={{0,1},{1,0},{2,3},{3,2},{4,5},{5,4},{6,7},{7,6},{8,9},{9,8},{10,11... | collective-permute-start | bytes 786440 | tf_op jit(solution)/shard_map/ppermute | solution.py:38
  59.6 8.8 %collective-permute-start.12 = (bf16[1,2,4,128,128]{4,3,2,1,0:T(8,128)(2,1)S(1)}, bf16[1,2,4,128,128]{4,3,2,1,0:T(8,128)(2,1)S(1)}, u32[]{:S(2)}, u32[]{:S(2)}) collective-permute-start(bf16[1,2,4,128,128]{4,3,2,1,0:T(8,128)(2,1)S(1)} %get-tuple-element.73), channel_id=1, source_target_pairs={{0,1},{1,0},{2,3},{3,2},{4,5},{5,4},{6,7},{7,6},{8,9},{9,8},{10,11... | collective-permute-start | bytes 786440 | tf_op jit(solution)/shard_map/ppermute | solution.py:38
  64.8 9.5 %collective-permute-start.17 = (bf16[192,256]{1,0:T(8,128)(2,1)S(1)}, bf16[192,256]{1,0:T(8,128)(2,1)S(1)}, u32[]{:S(2)}, u32[]{:S(2)}) collective-permute-start(bf16[192,256]{1,0:T(8,128)(2,1)S(1)} %bitcast.36), channel_id=1, source_target_pairs={{0,8},{4,12},{8,0},{12,4},{1,9},{5,13},{9,1},{13,5},{2,10},{6,14},... | collective-permute-start | bytes 294920 | tf_op jit(solution)/shard_map/ppermute | solution.py:38
  64.9 9.5 %collective-permute-start.18 = (bf16[192,256]{1,0:T(8,128)(2,1)S(1)}, bf16[192,256]{1,0:T(8,128)(2,1)S(1)}, u32[]{:S(2)}, u32[]{:S(2)}) collective-permute-start(bf16[192,256]{1,0:T(8,128)(2,1)S(1)} %bitcast.35), channel_id=1, source_target_pairs={{0,12},{4,8},{8,4},{12,0},{1,13},{5,9},{9,5},{13,1},{2,14},{6,10},... | collective-permute-start | bytes 294920 | tf_op jit(solution)/shard_map/ppermute | solution.py:38
  67.8 7.3 %collective-permute-start.16 = (bf16[192,256]{1,0:T(8,128)(2,1)S(1)}, bf16[192,256]{1,0:T(8,128)(2,1)S(1)}, u32[]{:S(2)}, u32[]{:S(2)}) collective-permute-start(bf16[192,256]{1,0:T(8,128)(2,1)S(1)} %bitcast.34), channel_id=1, source_target_pairs={{0,4},{4,0},{8,12},{12,8},{1,5},{5,1},{9,13},{13,9},{2,6},{6,2},{1... | collective-permute-start | bytes 294920 | tf_op jit(solution)/shard_map/ppermute | solution.py:38
  68.5 7.0 %collective-permute-start.15 = (bf16[1,2,4,128,128]{4,3,2,1,0:T(8,128)(2,1)S(1)}, bf16[1,2,4,128,128]{4,3,2,1,0:T(8,128)(2,1)S(1)}, u32[]{:S(2)}, u32[]{:S(2)}) collective-permute-start(bf16[1,2,4,128,128]{4,3,2,1,0:T(8,128)(2,1)S(1)} %add_convert_fusion.4), channel_id=1, source_target_pairs={{0,2},{1,3},{2,0},{3,1},{4,6},{5,7},{6,4},{7,5},{8,10},{9,11},{10,... | collective-permute-start | bytes 786440 | tf_op jit(solution)/shard_map/ppermute | solution.py:38
  74.4 5.1 %collective-permute-start.20 = (bf16[1,2,4,128,128]{4,3,2,1,0:T(8,128)(2,1)S(1)}, bf16[1,2,4,128,128]{4,3,2,1,0:T(8,128)(2,1)S(1)}, u32[]{:S(2)}, u32[]{:S(2)}) collective-permute-start(bf16[1,2,4,128,128]{4,3,2,1,0:T(8,128)(2,1)S(1)} %get-tuple-element.79), channel_id=1, source_target_pairs={{0,1},{1,0},{2,3},{3,2},{4,5},{5,4},{6,7},{7,6},{8,9},{9,8},{10,11... | collective-permute-start | bytes 786440 | tf_op jit(solution)/shard_map/ppermute | solution.py:38
  76.4 8.4 %collective-permute-start.22 = (bf16[1,2,4,128,128]{4,3,2,1,0:T(8,128)(2,1)S(1)}, bf16[1,2,4,128,128]{4,3,2,1,0:T(8,128)(2,1)S(1)}, u32[]{:S(2)}, u32[]{:S(2)}) collective-permute-start(bf16[1,2,4,128,128]{4,3,2,1,0:T(8,128)(2,1)S(1)} %add_convert_fusion.2), channel_id=1, source_target_pairs={{0,2},{1,3},{2,0},{3,1},{4,6},{5,7},{6,4},{7,5},{8,10},{9,11},{10,... | collective-permute-start | bytes 786440 | tf_op jit(solution)/shard_map/ppermute | solution.py:38
  77.6 9.9 %collective-permute-start.19 = (bf16[2,4,128,128]{3,2,1,0:T(8,128)(2,1)S(1)}, bf16[2,4,128,128]{3,2,1,0:T(8,128)(2,1)S(1)}, u32[]{:S(2)}, u32[]{:S(2)}) collective-permute-start(bf16[2,4,128,128]{3,2,1,0:T(8,128)(2,1)S(1)} %fusion.1), channel_id=1, source_target_pairs={{0,4},{4,8},{8,12},{12,0},{1,5},{5,9},{9,13},{13,1},{2,6},{6,10},{... | collective-permute-start | bytes 786440 | tf_op jit(solution)/shard_map/ppermute | solution.py:33
  79.0 14.0 %collective-permute-start.9 = (bf16[1,2,4,128,128]{4,3,2,1,0:T(8,128)(2,1)S(1)}, bf16[1,2,4,128,128]{4,3,2,1,0:T(8,128)(2,1)S(1)}, u32[]{:S(2)}, u32[]{:S(2)}) collective-permute-start(bf16[1,2,4,128,128]{4,3,2,1,0:T(8,128)(2,1)S(1)} %get-tuple-element.67), channel_id=1, source_target_pairs={{0,1},{1,0},{2,3},{3,2},{4,5},{5,4},{6,7},{7,6},{8,9},{9,8},{10,11... | collective-permute-start | bytes 786440 | tf_op jit(solution)/shard_map/ppermute | solution.py:38
  79.0 8.7 %collective-permute-start.10 = (bf16[1,2,4,128,128]{4,3,2,1,0:T(8,128)(2,1)S(1)}, bf16[1,2,4,128,128]{4,3,2,1,0:T(8,128)(2,1)S(1)}, u32[]{:S(2)}, u32[]{:S(2)}) collective-permute-start(bf16[1,2,4,128,128]{4,3,2,1,0:T(8,128)(2,1)S(1)} %get-tuple-element.69), channel_id=1, source_target_pairs={{0,1},{1,0},{2,3},{3,2},{4,5},{5,4},{6,7},{7,6},{8,9},{9,8},{10,11... | collective-permute-start | bytes 786440 | tf_op jit(solution)/shard_map/ppermute | solution.py:38
  87.7 7.3 %collective-permute-start.23 = (bf16[1,2,4,128,128]{4,3,2,1,0:T(8,128)(2,1)S(1)}, bf16[1,2,4,128,128]{4,3,2,1,0:T(8,128)(2,1)S(1)}, u32[]{:S(2)}, u32[]{:S(2)}) collective-permute-start(bf16[1,2,4,128,128]{4,3,2,1,0:T(8,128)(2,1)S(1)} %add_convert_fusion.1), channel_id=1, source_target_pairs={{0,2},{1,3},{2,0},{3,1},{4,6},{5,7},{6,4},{7,5},{8,10},{9,11},{10,... | collective-permute-start | bytes 786440 | tf_op jit(solution)/shard_map/ppermute | solution.py:38
  88.6 16.0 %collective-permute-start.27 = (bf16[192,256]{1,0:T(8,128)(2,1)S(1)}, bf16[192,256]{1,0:T(8,128)(2,1)S(1)}, u32[]{:S(2)}, u32[]{:S(2)}) collective-permute-start(bf16[192,256]{1,0:T(8,128)(2,1)S(1)} %fusion.4.refs_0_), channel_id=1, source_target_pairs={{0,12},{4,8},{8,4},{12,0},{1,13},{5,9},{9,5},{13,1},{2,14},{6,10},... | collective-permute-start | bytes 294920 | tf_op jit(solution)/shard_map/ppermute | solution.py:38
  88.6 16.0 %collective-permute-start.26 = (bf16[192,256]{1,0:T(8,128)(2,1)S(1)}, bf16[192,256]{1,0:T(8,128)(2,1)S(1)}, u32[]{:S(2)}, u32[]{:S(2)}) collective-permute-start(bf16[192,256]{1,0:T(8,128)(2,1)S(1)} %fusion.4.refs_0_), channel_id=1, source_target_pairs={{0,8},{4,12},{8,0},{12,4},{1,9},{5,13},{9,1},{13,5},{2,10},{6,14},... | collective-permute-start | bytes 294920 | tf_op jit(solution)/shard_map/ppermute | solution.py:38
  90.3 14.3 %collective-permute-start.25 = (bf16[192,256]{1,0:T(8,128)(2,1)S(1)}, bf16[192,256]{1,0:T(8,128)(2,1)S(1)}, u32[]{:S(2)}, u32[]{:S(2)}) collective-permute-start(bf16[192,256]{1,0:T(8,128)(2,1)S(1)} %fusion.4.refs_0_), channel_id=1, source_target_pairs={{0,4},{4,0},{8,12},{12,8},{1,5},{5,1},{9,13},{13,9},{2,6},{6,2},{1... | collective-permute-start | bytes 294920 | tf_op jit(solution)/shard_map/ppermute | solution.py:38
  93.0 10.7 %collective-permute-start.24 = (bf16[2,4,128,128]{3,2,1,0:T(8,128)(2,1)S(1)}, bf16[2,4,128,128]{3,2,1,0:T(8,128)(2,1)S(1)}, u32[]{:S(2)}, u32[]{:S(2)}) collective-permute-start(bf16[2,4,128,128]{3,2,1,0:T(8,128)(2,1)S(1)} %fusion), channel_id=1, source_target_pairs={{0,4},{4,8},{8,12},{12,0},{1,5},{5,9},{9,13},{13,1},{2,6},{6,10},{... | collective-permute-start | bytes 786440 | tf_op jit(solution)/shard_map/ppermute | solution.py:33
  (11 other events, 112.7 us)

commit v6 on v5

--- a/solution.py
+++ b/solution.py
@@ -483,6 +483,13 @@
     )(*indices, grads)
 
 
+def from_next(array, axis):
+    last = lax.axis_size(axis) - 1
+    around = lax.ppermute(array, axis, [(0, last)])
+    short = lax.ppermute(array, axis, [(i, i - 1) for i in range(1, last + 1)])
+    return short + around
+
+
 def after(array, *others):
     return lax.optimization_barrier((array,) + others)[0]
 
@@ -568,8 +575,8 @@
     for bit in reversed(bits):
         offs = offs + [o ^ bit for o in offs]
     quarter = lax.dynamic_slice_in_dim(tiles[0], member * slab, slab, 1)
-    near = shift(quarter, "blk", -1)
-    held = [[near], [shift(near, "blk", -1)]]
+    near = from_next(quarter, "blk")
+    held = [[near], [from_next(near, "blk")]]
     eig, amps = stage(*after_all((eigenprobes, amplitudes), near))
     held[1][0] = after(held[1][0], eig)
     table, tile, coef_t, lists, corners = stage(
@@ -597,14 +604,13 @@
     total, sent = scatter_sum("blk", eigen.reshape(blocks, -1, frame), relative)
     mine, leaving, _ = halve(keep[last], send[last], before_cross=sent)
     moving = after(mine.astype(jnp.bfloat16), total)
+    gathered = [swap(total, "blk", i) for i in range(1, blocks)]
     for section in range(last - 1, -1, -1):
-        mine, leaving, _ = halve(keep[section], send[section], before_cross=(moving,))
-        if section == last - 1:
-            total = after(total, leaving)
+        gate = [moving] + (gathered if section == 0 else [])
+        mine, _, _ = halve(keep[section], send[section], before_cross=gate)
         arrived = shift(moving, "blk", 1)
         if section > 0:
             moving = (arrived.astype(jnp.float32) + mine).astype(jnp.bfloat16)
-    gathered = [swap(total, "blk", i) for i in range(1, blocks)]
     eigen_share = place("blk", [after(total, arrived)] + gathered)
     eigen_share = eigen_share.reshape(modes, 2, frame // shares, frame)
     summed = finish(mine, arrived)

time: 106 us -> 119 us (1.12)
  waiting for transfers between devices: 42.4 us -> 53.6 us
  starting transfers between devices: 28 us -> 30.6 us
  local copies, waits for them, and re-layouts: 3.77 us -> 2.55 us
    ppermute x4 -> x2, waiting for transfers between devices: 17.1 us -> 2.3 us  [shift(): lax.ppermute(array, axis, [(i, (i + by) % peers) for i in range(peers)])]
    ppermute x24, waiting for transfers between devices: 25.2 us -> 38.7 us  [swap(): return lax.ppermute(array, axis, [(i, i ^ bit) for i in range(peers)])]
    ppermute x0 -> x4, waiting for transfers between devices: none -> 12.7 us  [the longest x2 8.26 us: from_next(): short = lax.ppermute(array, axis, [(i, i - 1) for i in range(1, last + 1)])]
    ppermute x0 -> x4, starting transfers between devices: none -> 11.8 us  [the longest x2 9.18 us: from_next(): around = lax.ppermute(array, axis, [(0, last)])]
    ppermute x4 -> x2, starting transfers between devices: 10.7 us -> 3.82 us  [shift(): lax.ppermute(array, axis, [(i, (i + by) % peers) for i in range(peers)])]
    ppermute x24, starting transfers between devices: 17.2 us -> 15 us  [swap(): return lax.ppermute(array, axis, [(i, i ^ bit) for i in range(peers)])]
    unnamed x14, local copies, waits for them, and re-layouts: 2.75 us -> 1.43 us
  transfers between devices with their start and end apart: 28 -> 30, of which waited for: 15 -> 15; matrix products, arithmetic and copies ran while one was open for 1% -> 1% of each run, Pallas kernels for 7% -> 5%
where the time goes in v6:
time: 119 us; the launch traced here: 118 us
  waiting for transfers between devices  53.6 us (45%)
  starting transfers between devices  30.6 us (26%)
  Pallas kernels  29 us (24%)
  local copies, waits for them, and re-layouts  2.55 us (2%)
  between operations  1.56 us (1%)
    ppermute x24, waiting for transfers between devices, swap(): return lax.ppermute(array, axis, [(i, i ^ bit) for i in range(peers)])  38.7 us
    pallas_call x1, Pallas kernels, positions(): pl.pallas_call(functools.partial(position_kernel, offs, scale), in_specs=...  20.8 us
    ppermute x24, starting transfers between devices, swap(): return lax.ppermute(array, axis, [(i, i ^ bit) for i in range(peers)])  15 us
    ppermute x2, starting transfers between devices, from_next(): around = lax.ppermute(array, axis, [(0, last)])  9.18 us
    ppermute x2, waiting for transfers between devices, from_next(): short = lax.ppermute(array, axis, [(i, i - 1) for i in range(1, last + 1)])  8.26 us
    pallas_call x1, Pallas kernels, scatter(): pl.pallas_call(functools.partial(scatter_kernel, shares), in_specs=[pl.Bl...  5.93 us
    ppermute x2, waiting for transfers between devices, from_next(): around = lax.ppermute(array, axis, [(0, last)])  4.4 us
    ppermute x2, starting transfers between devices, shift(): lax.ppermute(array, axis, [(i, (i + by) % peers) for i in range(peers)])  3.82 us
  transfers between devices with their start and end apart: 30, of which 15 were waited for; matrix products, arithmetic and copies ran while one was open for 1% of the time, Pallas kernels for 5%

profile of v6, /device:TPU:0, one launch (start us, length us, event | category | flops | bytes accessed | tf_op | source)
XLA Modules:
  0.0 118.3 jit_solution(12434769211929377182)
XLA Ops:
  1.7 7.0 %collective-permute-start.1 = (bf16[2,128,512]{2,1,0:T(8,128)(2,1)S(1)}, bf16[2,128,512]{2,1,0:T(8,128)(2,1)S(1)}, u32[]{:S(2)}, u32[]{:S(2)}) collective-permute-start(bf16[2,128,512]{2,1,0:T(8,128)(2,1)S(1)} %dynamic-slice_bitcast_fusion), channel_id=1, source_target_pairs={{0,12},{1,13},{2,14},{3,15},{16,28},{17,29},{18,30},{19,31}} | collective-permute-start | bytes 786440 | tf_op jit(solution)/shard_map/ppermute | solution.py:488
  8.7 1.3 %collective-permute-start = (bf16[2,128,512]{2,1,0:T(8,128)(2,1)S(1)}, bf16[2,128,512]{2,1,0:T(8,128)(2,1)S(1)}, u32[]{:S(2)}, u32[]{:S(2)}) collective-permute-start(bf16[2,128,512]{2,1,0:T(8,128)(2,1)S(1)} %dynamic-slice_bitcast_fusion), channel_id=1, source_target_pairs={{4,0},{8,4},{12,8},{5,1},{9,5},{13,9},{6,2},{10,6},{14,10},{7,3},{... | collective-permute-start | bytes 786440 | tf_op jit(solution)/shard_map/ppermute | solution.py:489
  10.0 4.2 %collective-permute-done.1 = bf16[2,128,512]{2,1,0:T(8,128)(2,1)S(1)} collective-permute-done((bf16[2,128,512]{2,1,0:T(8,128)(2,1)S(1)}, bf16[2,128,512]{2,1,0:T(8,128)(2,1)S(1)}, u32[]{:S(2)}, u32[]{:S(2)}) %collective-permute-start.1) | collective-permute-done | bytes 262176 | tf_op jit(solution)/shard_map/ppermute | solution.py:488
  14.2 4.1 %collective-permute-done = bf16[2,128,512]{2,1,0:T(8,128)(2,1)S(1)} collective-permute-done((bf16[2,128,512]{2,1,0:T(8,128)(2,1)S(1)}, bf16[2,128,512]{2,1,0:T(8,128)(2,1)S(1)}, u32[]{:S(2)}, u32[]{:S(2)}) %collective-permute-start) | collective-permute-done | bytes 262176 | tf_op jit(solution)/shard_map/ppermute | solution.py:489
  18.5 2.2 %collective-permute-start.3 = (bf16[2,128,512]{2,1,0:T(8,128)(2,1)S(1)}, bf16[2,128,512]{2,1,0:T(8,128)(2,1)S(1)}, u32[]{:S(2)}, u32[]{:S(2)}) collective-permute-start(bf16[2,128,512]{2,1,0:T(8,128)(2,1)S(1)} %add.69.refs_1_), channel_id=1, source_target_pairs={{0,12},{1,13},{2,14},{3,15},{16,28},{17,29},{18,30},{19,31}} | collective-permute-start | bytes 786440 | tf_op jit(solution)/shard_map/ppermute | solution.py:488
  20.7 1.3 %collective-permute-start.2 = (bf16[2,128,512]{2,1,0:T(8,128)(2,1)S(1)}, bf16[2,128,512]{2,1,0:T(8,128)(2,1)S(1)}, u32[]{:S(2)}, u32[]{:S(2)}) collective-permute-start(bf16[2,128,512]{2,1,0:T(8,128)(2,1)S(1)} %add.69.refs_1_), channel_id=1, source_target_pairs={{4,0},{8,4},{12,8},{5,1},{9,5},{13,9},{6,2},{10,6},{14,10},{7,3},{... | collective-permute-start | bytes 786440 | tf_op jit(solution)/shard_map/ppermute | solution.py:489
  22.0 1.6 %collective-permute-start.4 = (bf16[2,128,512]{2,1,0:T(8,128)(2,1)S(1)}, bf16[2,128,512]{2,1,0:T(8,128)(2,1)S(1)}, u32[]{:S(2)}, u32[]{:S(2)}) collective-permute-start(bf16[2,128,512]{2,1,0:T(8,128)(2,1)S(1)} %add.69.refs_1_), channel_id=1, source_target_pairs={{0,2},{1,3},{2,0},{3,1},{4,6},{5,7},{6,4},{7,5},{8,10},{9,11},{10,... | collective-permute-start | bytes 786440 | tf_op jit(solution)/shard_map/ppermute | solution.py:38
  23.5 1.4 %copy-done.1 = bf16[6,2,256,256]{3,2,1,0:T(8,128)(2,1)S(1)} copy-done((bf16[6,2,256,256]{3,2,1,0:T(8,128)(2,1)S(1)}, bf16[6,2,256,256]{3,2,1,0:T(8,128)(2,1)}, u32[]{:S(2)}) %copy-start.1) | copy-done | bytes 1572888
  25.3 4.1 %collective-permute-done.2 = bf16[2,128,512]{2,1,0:T(8,128)(2,1)S(1)} collective-permute-done((bf16[2,128,512]{2,1,0:T(8,128)(2,1)S(1)}, bf16[2,128,512]{2,1,0:T(8,128)(2,1)S(1)}, u32[]{:S(2)}, u32[]{:S(2)}) %collective-permute-start.2) | collective-permute-done | bytes 262176 | tf_op jit(solution)/shard_map/ppermute | solution.py:489
  29.5 1.6 %collective-permute-start.7 = (bf16[2,128,512]{2,1,0:T(8,128)(2,1)S(1)}, bf16[2,128,512]{2,1,0:T(8,128)(2,1)S(1)}, u32[]{:S(2)}, u32[]{:S(2)}) collective-permute-start(bf16[2,128,512]{2,1,0:T(8,128)(2,1)S(1)} %add.70.refs_5_), channel_id=1, source_target_pairs={{0,2},{1,3},{2,0},{3,1},{4,6},{5,7},{6,4},{7,5},{8,10},{9,11},{10,... | collective-permute-start | bytes 786440 | tf_op jit(solution)/shard_map/ppermute | solution.py:38
  31.9 4.1 %collective-permute-done.7.refs_6_ = bf16[2,128,512]{2,1,0:T(8,128)(2,1)S(1)} collective-permute-done((bf16[2,128,512]{2,1,0:T(8,128)(2,1)S(1)}, bf16[2,128,512]{2,1,0:T(8,128)(2,1)S(1)}, u32[]{:S(2)}, u32[]{:S(2)}) %collective-permute-start.7) | collective-permute-done | bytes 262176 | tf_op jit(solution)/shard_map/ppermute | solution.py:38
  37.5 20.8 %positions.1 = (bf16[1,12,64,256]{3,2,1,0:T(8,128)(2,1)S(1)}, bf16[1,12,64,256]{3,2,1,0:T(8,128)(2,1)S(1)}, f32[1,12,64,256]{3,2,1,0:T(8,128)S(1)}, f32[1,12,64,...) custom-call(s32[2,10]{1,0:T(2,128)S(1)} %get-tuple-element.53.tile_list, ...), custom_call_target="tpu_custom_call" | custom-call | tf_op jit(solution)/shard_map/positions/pallas_call | solution.py:346
  60.3 5.9 %scatter.1 = (bf16[1,2,4,128,128]{4,3,2,1,0:T(8,128)(2,1)S(1)}, bf16[1,2,4,128,128]{4,3,2,1,0:T(8,128)(2,1)S(1)}, bf16[1,2,4,128,128]{4,3,2,1,0:T(8,128)(2,1)S(1...) custom-call(s32[2,10]{1,0:T(2,128)S(1)} %get-tuple-element.53.tile_l, ...), custom_call_target="tpu_custom_call" | custom-call | flops 16777216 | bytes 16777216 | tf_op jit(solution)/shard_map/scatter/pallas_call | solution.py:467
  66.8 4.6 %collective-permute-done.16 = bf16[1,12,64,256]{3,2,1,0:T(8,128)(2,1)S(1)} collective-permute-done((bf16[1,12,64,256]{3,2,1,0:T(8,128)(2,1)S(1)}, bf16[1,12,64,256]{3,2,1,0:T(8,128)(2,1)S(1)}, u32[]{:S(2)}, u32[]{:S(2)}) %collective-permute-start.16) | collective-permute-done | bytes 393248 | tf_op jit(solution)/shard_map/ppermute | solution.py:38
  71.7 3.3 %collective-permute-start.20 = (bf16[192,256]{1,0:T(8,128)(2,1)S(1)}, bf16[192,256]{1,0:T(8,128)(2,1)S(1)}, u32[]{:S(2)}, u32[]{:S(2)}) collective-permute-start(bf16[192,256]{1,0:T(8,128)(2,1)S(1)} %bitcast.35), channel_id=1, source_target_pairs={{0,12},{4,8},{8,4},{12,0},{1,13},{5,9},{9,5},{13,1},{2,14},{6,10},... | collective-permute-start | bytes 294920 | tf_op jit(solution)/shard_map/ppermute | solution.py:38
  75.6 5.8 %collective-permute-done.19 = bf16[192,256]{1,0:T(8,128)(2,1)S(1)} collective-permute-done((bf16[192,256]{1,0:T(8,128)(2,1)S(1)}, bf16[192,256]{1,0:T(8,128)(2,1)S(1)}, u32[]{:S(2)}, u32[]{:S(2)}) %collective-permute-start.19) | collective-permute-done | bytes 98336 | tf_op jit(solution)/shard_map/ppermute | solution.py:38
  84.1 1.7 %collective-permute-start.21 = (bf16[2,4,128,128]{3,2,1,0:T(8,128)(2,1)S(1)}, bf16[2,4,128,128]{3,2,1,0:T(8,128)(2,1)S(1)}, u32[]{:S(2)}, u32[]{:S(2)}) collective-permute-start(bf16[2,4,128,128]{3,2,1,0:T(8,128)(2,1)S(1)} %fusion.1), channel_id=1, source_target_pairs={{0,4},{4,8},{8,12},{12,0},{1,5},{5,9},{9,13},{13,1},{2,6},{6,10},{... | collective-permute-start | bytes 786440 | tf_op jit(solution)/shard_map/ppermute | solution.py:33
  86.3 2.1 %collective-permute-start.27 = (bf16[192,256]{1,0:T(8,128)(2,1)S(1)}, bf16[192,256]{1,0:T(8,128)(2,1)S(1)}, u32[]{:S(2)}, u32[]{:S(2)}) collective-permute-start(bf16[192,256]{1,0:T(8,128)(2,1)S(1)} %fusion.4.refs_0_), channel_id=1, source_target_pairs={{0,12},{4,8},{8,4},{12,0},{1,13},{5,9},{9,5},{13,1},{2,14},{6,10},... | collective-permute-start | bytes 294920 | tf_op jit(solution)/shard_map/ppermute | solution.py:38
  88.4 3.4 %collective-permute-done.24 = bf16[1,2,4,128,128]{4,3,2,1,0:T(8,128)(2,1)S(1)} collective-permute-done((bf16[1,2,4,128,128]{4,3,2,1,0:T(8,128)(2,1)S(1)}, bf16[1,2,4,128,128]{4,3,2,1,0:T(8,128)(2,1)S(1)}, u32[]{:S(2)}, u32[]{:S(2)}) %collective-permute-start.24) | collective-permute-done | bytes 262176 | tf_op jit(solution)/shard_map/ppermute | solution.py:38
  92.8 2.3 %collective-permute-done.21 = bf16[2,4,128,128]{3,2,1,0:T(8,128)(2,1)S(1)} collective-permute-done((bf16[2,4,128,128]{3,2,1,0:T(8,128)(2,1)S(1)}, bf16[2,4,128,128]{3,2,1,0:T(8,128)(2,1)S(1)}, u32[]{:S(2)}, u32[]{:S(2)}) %collective-permute-start.21) | collective-permute-done | bytes 262176 | tf_op jit(solution)/shard_map/ppermute | solution.py:33
  95.3 2.1 %collective-permute-start.29 = (bf16[2,4,128,128]{3,2,1,0:T(8,128)(2,1)S(1)}, bf16[2,4,128,128]{3,2,1,0:T(8,128)(2,1)S(1)}, u32[]{:S(2)}, u32[]{:S(2)}) collective-permute-start(bf16[2,4,128,128]{3,2,1,0:T(8,128)(2,1)S(1)} %fusion), channel_id=1, source_target_pairs={{0,4},{4,8},{8,12},{12,0},{1,5},{5,9},{9,13},{13,1},{2,6},{6,10},{... | collective-permute-start | bytes 786440 | tf_op jit(solution)/shard_map/ppermute | solution.py:33
  97.3 10.7 %collective-permute-done.26.refs_2_ = bf16[192,256]{1,0:T(8,128)(2,1)S(1)} collective-permute-done((bf16[192,256]{1,0:T(8,128)(2,1)S(1)}, bf16[192,256]{1,0:T(8,128)(2,1)S(1)}, u32[]{:S(2)}, u32[]{:S(2)}) %collective-permute-start.26) | collective-permute-done | bytes 98336 | tf_op jit(solution)/shard_map/ppermute | solution.py:38
  108.1 1.5 %collective-permute-start.28 = (bf16[1,2,4,128,128]{4,3,2,1,0:T(8,128)(2,1)S(1)}, bf16[1,2,4,128,128]{4,3,2,1,0:T(8,128)(2,1)S(1)}, u32[]{:S(2)}, u32[]{:S(2)}) collective-permute-start(bf16[1,2,4,128,128]{4,3,2,1,0:T(8,128)(2,1)S(1)} %add_convert_fusion.1), channel_id=1, source_target_pairs={{0,2},{1,3},{2,0},{3,1},{4,6},{5,7},{6,4},{7,5},{8,10},{9,11},{10,... | collective-permute-start | bytes 786440 | tf_op jit(solution)/shard_map/ppermute | solution.py:38
  109.5 6.8 %collective-permute-done.28 = bf16[1,2,4,128,128]{4,3,2,1,0:T(8,128)(2,1)S(1)} collective-permute-done((bf16[1,2,4,128,128]{4,3,2,1,0:T(8,128)(2,1)S(1)}, bf16[1,2,4,128,128]{4,3,2,1,0:T(8,128)(2,1)S(1)}, u32[]{:S(2)}, u32[]{:S(2)}) %collective-permute-start.28) | collective-permute-done | bytes 262176 | tf_op jit(solution)/shard_map/ppermute | solution.py:38
  (70 shorter events, 12.8 us)
Async XLA Ops:
  1.7 12.5 %collective-permute-start.1 = (bf16[2,128,512]{2,1,0:T(8,128)(2,1)S(1)}, bf16[2,128,512]{2,1,0:T(8,128)(2,1)S(1)}, u32[]{:S(2)}, u32[]{:S(2)}) collective-permute-start(bf16[2,128,512]{2,1,0:T(8,128)(2,1)S(1)} %dynamic-slice_bitcast_fusion), channel_id=1, source_target_pairs={{0,12},{1,13},{2,14},{3,15},{16,28},{17,29},{18,30},{19,31}} | collective-permute-start | bytes 786440 | tf_op jit(solution)/shard_map/ppermute | solution.py:488
  8.7 9.7 %collective-permute-start = (bf16[2,128,512]{2,1,0:T(8,128)(2,1)S(1)}, bf16[2,128,512]{2,1,0:T(8,128)(2,1)S(1)}, u32[]{:S(2)}, u32[]{:S(2)}) collective-permute-start(bf16[2,128,512]{2,1,0:T(8,128)(2,1)S(1)} %dynamic-slice_bitcast_fusion), channel_id=1, source_target_pairs={{4,0},{8,4},{12,8},{5,1},{9,5},{13,9},{6,2},{10,6},{14,10},{7,3},{... | collective-permute-start | bytes 786440 | tf_op jit(solution)/shard_map/ppermute | solution.py:489
  18.5 6.9 %collective-permute-start.3 = (bf16[2,128,512]{2,1,0:T(8,128)(2,1)S(1)}, bf16[2,128,512]{2,1,0:T(8,128)(2,1)S(1)}, u32[]{:S(2)}, u32[]{:S(2)}) collective-permute-start(bf16[2,128,512]{2,1,0:T(8,128)(2,1)S(1)} %add.69.refs_1_), channel_id=1, source_target_pairs={{0,12},{1,13},{2,14},{3,15},{16,28},{17,29},{18,30},{19,31}} | collective-permute-start | bytes 786440 | tf_op jit(solution)/shard_map/ppermute | solution.py:488
  20.7 8.8 %collective-permute-start.2 = (bf16[2,128,512]{2,1,0:T(8,128)(2,1)S(1)}, bf16[2,128,512]{2,1,0:T(8,128)(2,1)S(1)}, u32[]{:S(2)}, u32[]{:S(2)}) collective-permute-start(bf16[2,128,512]{2,1,0:T(8,128)(2,1)S(1)} %add.69.refs_1_), channel_id=1, source_target_pairs={{4,0},{8,4},{12,8},{5,1},{9,5},{13,9},{6,2},{10,6},{14,10},{7,3},{... | collective-permute-start | bytes 786440 | tf_op jit(solution)/shard_map/ppermute | solution.py:489
  22.0 9.6 %collective-permute-start.4 = (bf16[2,128,512]{2,1,0:T(8,128)(2,1)S(1)}, bf16[2,128,512]{2,1,0:T(8,128)(2,1)S(1)}, u32[]{:S(2)}, u32[]{:S(2)}) collective-permute-start(bf16[2,128,512]{2,1,0:T(8,128)(2,1)S(1)} %add.69.refs_1_), channel_id=1, source_target_pairs={{0,2},{1,3},{2,0},{3,1},{4,6},{5,7},{6,4},{7,5},{8,10},{9,11},{10,... | collective-permute-start | bytes 786440 | tf_op jit(solution)/shard_map/ppermute | solution.py:38
  29.5 6.4 %collective-permute-start.7 = (bf16[2,128,512]{2,1,0:T(8,128)(2,1)S(1)}, bf16[2,128,512]{2,1,0:T(8,128)(2,1)S(1)}, u32[]{:S(2)}, u32[]{:S(2)}) collective-permute-start(bf16[2,128,512]{2,1,0:T(8,128)(2,1)S(1)} %add.70.refs_5_), channel_id=1, source_target_pairs={{0,2},{1,3},{2,0},{3,1},{4,6},{5,7},{6,4},{7,5},{8,10},{9,11},{10,... | collective-permute-start | bytes 786440 | tf_op jit(solution)/shard_map/ppermute | solution.py:38
  31.1 5.5 %collective-permute-start.8 = (bf16[2,128,512]{2,1,0:T(8,128)(2,1)S(1)}, bf16[2,128,512]{2,1,0:T(8,128)(2,1)S(1)}, u32[]{:S(2)}, u32[]{:S(2)}) collective-permute-start(bf16[2,128,512]{2,1,0:T(8,128)(2,1)S(1)} %add.70.refs_5_), channel_id=1, source_target_pairs={{0,1},{1,0},{2,3},{3,2},{4,5},{5,4},{6,7},{7,6},{8,9},{9,8},{10,11... | collective-permute-start | bytes 786440 | tf_op jit(solution)/shard_map/ppermute | solution.py:38
  58.4 8.4 %collective-permute-start.15 = (bf16[1,12,64,256]{3,2,1,0:T(8,128)(2,1)S(1)}, bf16[1,12,64,256]{3,2,1,0:T(8,128)(2,1)S(1)}, u32[]{:S(2)}, u32[]{:S(2)}) collective-permute-start(bf16[1,12,64,256]{3,2,1,0:T(8,128)(2,1)S(1)} %get-tuple-element.74), channel_id=1, source_target_pairs={{0,1},{1,0},{2,3},{3,2},{4,5},{5,4},{6,7},{7,6},{8,9},{9,8},{10,11... | collective-permute-start | bytes 1179656 | tf_op jit(solution)/shard_map/ppermute | solution.py:38
  60.2 11.2 %collective-permute-start.16 = (bf16[1,12,64,256]{3,2,1,0:T(8,128)(2,1)S(1)}, bf16[1,12,64,256]{3,2,1,0:T(8,128)(2,1)S(1)}, u32[]{:S(2)}, u32[]{:S(2)}) collective-permute-start(bf16[1,12,64,256]{3,2,1,0:T(8,128)(2,1)S(1)} %add_convert_fusion), channel_id=1, source_target_pairs={{0,2},{1,3},{2,0},{3,1},{4,6},{5,7},{6,4},{7,5},{8,10},{9,11},{10,... | collective-permute-start | bytes 1179656 | tf_op jit(solution)/shard_map/ppermute | solution.py:38
  66.3 15.7 %collective-permute-start.13 = (bf16[1,2,4,128,128]{4,3,2,1,0:T(8,128)(2,1)S(1)}, bf16[1,2,4,128,128]{4,3,2,1,0:T(8,128)(2,1)S(1)}, u32[]{:S(2)}, u32[]{:S(2)}) collective-permute-start(bf16[1,2,4,128,128]{4,3,2,1,0:T(8,128)(2,1)S(1)} %get-tuple-element.70), channel_id=1, source_target_pairs={{0,1},{1,0},{2,3},{3,2},{4,5},{5,4},{6,7},{7,6},{8,9},{9,8},{10,11... | collective-permute-start | bytes 786440 | tf_op jit(solution)/shard_map/ppermute | solution.py:38
  66.3 8.9 %collective-permute-start.14 = (bf16[1,2,4,128,128]{4,3,2,1,0:T(8,128)(2,1)S(1)}, bf16[1,2,4,128,128]{4,3,2,1,0:T(8,128)(2,1)S(1)}, u32[]{:S(2)}, u32[]{:S(2)}) collective-permute-start(bf16[1,2,4,128,128]{4,3,2,1,0:T(8,128)(2,1)S(1)} %get-tuple-element.72), channel_id=1, source_target_pairs={{0,1},{1,0},{2,3},{3,2},{4,5},{5,4},{6,7},{7,6},{8,9},{9,8},{10,11... | collective-permute-start | bytes 786440 | tf_op jit(solution)/shard_map/ppermute | solution.py:38
  71.6 9.8 %collective-permute-start.19 = (bf16[192,256]{1,0:T(8,128)(2,1)S(1)}, bf16[192,256]{1,0:T(8,128)(2,1)S(1)}, u32[]{:S(2)}, u32[]{:S(2)}) collective-permute-start(bf16[192,256]{1,0:T(8,128)(2,1)S(1)} %bitcast.36), channel_id=1, source_target_pairs={{0,8},{4,12},{8,0},{12,4},{1,9},{5,13},{9,1},{13,5},{2,10},{6,14},... | collective-permute-start | bytes 294920 | tf_op jit(solution)/shard_map/ppermute | solution.py:38
  71.7 9.7 %collective-permute-start.20 = (bf16[192,256]{1,0:T(8,128)(2,1)S(1)}, bf16[192,256]{1,0:T(8,128)(2,1)S(1)}, u32[]{:S(2)}, u32[]{:S(2)}) collective-permute-start(bf16[192,256]{1,0:T(8,128)(2,1)S(1)} %bitcast.35), channel_id=1, source_target_pairs={{0,12},{4,8},{8,4},{12,0},{1,13},{5,9},{9,5},{13,1},{2,14},{6,10},... | collective-permute-start | bytes 294920 | tf_op jit(solution)/shard_map/ppermute | solution.py:38
  75.0 6.9 %collective-permute-start.18 = (bf16[192,256]{1,0:T(8,128)(2,1)S(1)}, bf16[192,256]{1,0:T(8,128)(2,1)S(1)}, u32[]{:S(2)}, u32[]{:S(2)}) collective-permute-start(bf16[192,256]{1,0:T(8,128)(2,1)S(1)} %bitcast.34), channel_id=1, source_target_pairs={{0,4},{4,0},{8,12},{12,8},{1,5},{5,1},{9,13},{13,9},{2,6},{6,2},{1... | collective-permute-start | bytes 294920 | tf_op jit(solution)/shard_map/ppermute | solution.py:38
  75.3 6.9 %collective-permute-start.17 = (bf16[1,2,4,128,128]{4,3,2,1,0:T(8,128)(2,1)S(1)}, bf16[1,2,4,128,128]{4,3,2,1,0:T(8,128)(2,1)S(1)}, u32[]{:S(2)}, u32[]{:S(2)}) collective-permute-start(bf16[1,2,4,128,128]{4,3,2,1,0:T(8,128)(2,1)S(1)} %add_convert_fusion.4), channel_id=1, source_target_pairs={{0,2},{1,3},{2,0},{3,1},{4,6},{5,7},{6,4},{7,5},{8,10},{9,11},{10,... | collective-permute-start | bytes 786440 | tf_op jit(solution)/shard_map/ppermute | solution.py:38
  83.4 8.4 %collective-permute-start.24 = (bf16[1,2,4,128,128]{4,3,2,1,0:T(8,128)(2,1)S(1)}, bf16[1,2,4,128,128]{4,3,2,1,0:T(8,128)(2,1)S(1)}, u32[]{:S(2)}, u32[]{:S(2)}) collective-permute-start(bf16[1,2,4,128,128]{4,3,2,1,0:T(8,128)(2,1)S(1)} %add_convert_fusion.2), channel_id=1, source_target_pairs={{0,2},{1,3},{2,0},{3,1},{4,6},{5,7},{6,4},{7,5},{8,10},{9,11},{10,... | collective-permute-start | bytes 786440 | tf_op jit(solution)/shard_map/ppermute | solution.py:38
  84.1 11.0 %collective-permute-start.21 = (bf16[2,4,128,128]{3,2,1,0:T(8,128)(2,1)S(1)}, bf16[2,4,128,128]{3,2,1,0:T(8,128)(2,1)S(1)}, u32[]{:S(2)}, u32[]{:S(2)}) collective-permute-start(bf16[2,4,128,128]{3,2,1,0:T(8,128)(2,1)S(1)} %fusion.1), channel_id=1, source_target_pairs={{0,4},{4,8},{8,12},{12,0},{1,5},{5,9},{9,13},{13,1},{2,6},{6,10},{... | collective-permute-start | bytes 786440 | tf_op jit(solution)/shard_map/ppermute | solution.py:33
  85.8 23.7 %collective-permute-start.11 = (bf16[1,2,4,128,128]{4,3,2,1,0:T(8,128)(2,1)S(1)}, bf16[1,2,4,128,128]{4,3,2,1,0:T(8,128)(2,1)S(1)}, u32[]{:S(2)}, u32[]{:S(2)}) collective-permute-start(bf16[1,2,4,128,128]{4,3,2,1,0:T(8,128)(2,1)S(1)} %get-tuple-element.66), channel_id=1, source_target_pairs={{0,1},{1,0},{2,3},{3,2},{4,5},{5,4},{6,7},{7,6},{8,9},{9,8},{10,11... | collective-permute-start | bytes 786440 | tf_op jit(solution)/shard_map/ppermute | solution.py:38
  85.8 9.4 %collective-permute-start.12 = (bf16[1,2,4,128,128]{4,3,2,1,0:T(8,128)(2,1)S(1)}, bf16[1,2,4,128,128]{4,3,2,1,0:T(8,128)(2,1)S(1)}, u32[]{:S(2)}, u32[]{:S(2)}) collective-permute-start(bf16[1,2,4,128,128]{4,3,2,1,0:T(8,128)(2,1)S(1)} %get-tuple-element.68), channel_id=1, source_target_pairs={{0,1},{1,0},{2,3},{3,2},{4,5},{5,4},{6,7},{7,6},{8,9},{9,8},{10,11... | collective-permute-start | bytes 786440 | tf_op jit(solution)/shard_map/ppermute | solution.py:38
  86.3 11.0 %collective-permute-start.27 = (bf16[192,256]{1,0:T(8,128)(2,1)S(1)}, bf16[192,256]{1,0:T(8,128)(2,1)S(1)}, u32[]{:S(2)}, u32[]{:S(2)}) collective-permute-start(bf16[192,256]{1,0:T(8,128)(2,1)S(1)} %fusion.4.refs_0_), channel_id=1, source_target_pairs={{0,12},{4,8},{8,4},{12,0},{1,13},{5,9},{9,5},{13,1},{2,14},{6,10},... | collective-permute-start | bytes 294920 | tf_op jit(solution)/shard_map/ppermute | solution.py:38
  91.8 16.2 %collective-permute-start.26 = (bf16[192,256]{1,0:T(8,128)(2,1)S(1)}, bf16[192,256]{1,0:T(8,128)(2,1)S(1)}, u32[]{:S(2)}, u32[]{:S(2)}) collective-permute-start(bf16[192,256]{1,0:T(8,128)(2,1)S(1)} %fusion.4.refs_0_), channel_id=1, source_target_pairs={{0,8},{4,12},{8,0},{12,4},{1,9},{5,13},{9,1},{13,5},{2,10},{6,14},... | collective-permute-start | bytes 294920 | tf_op jit(solution)/shard_map/ppermute | solution.py:38
  95.1 12.9 %collective-permute-start.25 = (bf16[192,256]{1,0:T(8,128)(2,1)S(1)}, bf16[192,256]{1,0:T(8,128)(2,1)S(1)}, u32[]{:S(2)}, u32[]{:S(2)}) collective-permute-start(bf16[192,256]{1,0:T(8,128)(2,1)S(1)} %fusion.4.refs_0_), channel_id=1, source_target_pairs={{0,4},{4,0},{8,12},{12,8},{1,5},{5,1},{9,13},{13,9},{2,6},{6,2},{1... | collective-permute-start | bytes 294920 | tf_op jit(solution)/shard_map/ppermute | solution.py:38
  95.3 14.3 %collective-permute-start.29 = (bf16[2,4,128,128]{3,2,1,0:T(8,128)(2,1)S(1)}, bf16[2,4,128,128]{3,2,1,0:T(8,128)(2,1)S(1)}, u32[]{:S(2)}, u32[]{:S(2)}) collective-permute-start(bf16[2,4,128,128]{3,2,1,0:T(8,128)(2,1)S(1)} %fusion), channel_id=1, source_target_pairs={{0,4},{4,8},{8,12},{12,0},{1,5},{5,9},{9,13},{13,1},{2,6},{6,10},{... | collective-permute-start | bytes 786440 | tf_op jit(solution)/shard_map/ppermute | solution.py:33
  108.1 8.3 %collective-permute-start.28 = (bf16[1,2,4,128,128]{4,3,2,1,0:T(8,128)(2,1)S(1)}, bf16[1,2,4,128,128]{4,3,2,1,0:T(8,128)(2,1)S(1)}, u32[]{:S(2)}, u32[]{:S(2)}) collective-permute-start(bf16[1,2,4,128,128]{4,3,2,1,0:T(8,128)(2,1)S(1)} %add_convert_fusion.1), channel_id=1, source_target_pairs={{0,2},{1,3},{2,0},{3,1},{4,6},{5,7},{6,4},{7,5},{8,10},{9,11},{10,... | collective-permute-start | bytes 786440 | tf_op jit(solution)/shard_map/ppermute | solution.py:38
  (13 other events, 104.7 us)

commit v7 on v5

--- a/solution.py
+++ b/solution.py
@@ -113,7 +113,7 @@
 
 def position_kernel(offs, scale, tile_list, offsets, group_counts, *refs):
     shares = len(offs)
-    pieces = refs[: 1 + (REACH - 1) * shares]
+    pieces = refs[: 1 + 2 * (REACH - 1) * shares]
     eig_in, amps_in, tables_in, coef_in = refs[len(pieces):len(pieces) + 4]
     eigen_send, eigen_keep = refs[len(pieces) + 4:len(pieces) + 6], refs[len(pieces) + 6:len(pieces) + 8]
     grads_out, coef = refs[len(pieces) + 8:len(pieces) + 10]
@@ -131,12 +131,13 @@
     for section in range(1, REACH):
         for i in range(shares):
             start = pl.multiple_of((member ^ offs[i]) * slab, slab)
-            at = 1 + (section - 1) * shares + i
-            copies.append(
-                pltpu.make_async_copy(
-                    pieces[at], staged.at[section, :, pl.ds(start, slab), :], piece_sem.at[at]
+            for c in range(2):
+                at = len(copies)
+                copies.append(
+                    pltpu.make_async_copy(
+                        pieces[at], staged.at[section, c, pl.ds(start, slab), :], piece_sem.at[at]
+                    )
                 )
-            )
     table_copy = pltpu.make_async_copy(tables_in, table, table_sem)
     amps_copy = pltpu.make_async_copy(amps_in, amps, amps_sem)
     eig_copy = pltpu.make_async_copy(eig_in, eig, eig_sem)
@@ -567,25 +568,33 @@
     offs = [0]
     for bit in reversed(bits):
         offs = offs + [o ^ bit for o in offs]
-    quarter = lax.dynamic_slice_in_dim(tiles[0], member * slab, slab, 1)
-    near = shift(quarter, "blk", -1)
-    held = [[near], [shift(near, "blk", -1)]]
-    eig, amps = stage(*after_all((eigenprobes, amplitudes), near))
-    held[1][0] = after(held[1][0], eig)
-    table, tile, coef_t, lists, corners = stage(
-        *after_all((tables(frame), tiles[0], coefficients.T, tile_list.T, offsets.T), held[1][0])
+    (eig,) = stage(eigenprobes)
+    moving = [
+        lax.dynamic_slice(tiles, (0, c, member * slab, 0), (1, 1, slab, side)).reshape(slab, side)
+        for c in range(2)
+    ]
+    held = []
+    for section in range(1, REACH):
+        moving = [shift(part, "blk", -1) for part in moving]
+        if section == 1:
+            moving[0] = after(moving[0], eig)
+        held.append([[part] for part in moving])
+    amps, table, tile, coef_t, lists, corners = stage(
+        *after_all((amplitudes, tables(frame), tiles[0], coefficients.T, tile_list.T, offsets.T), *moving)
     )
     for bit in reversed(bits):
-        for part in held:
-            arrived = [swap(piece, "probe", bit) for piece in part]
-            if bit > 1:
-                arrived[0] = after(arrived[0], eig if part is held[0] else table)
-            part += arrived
+        for section in held:
+            for c, part in enumerate(section):
+                arrived = [swap(piece, "probe", bit) for piece in part]
+                if bit > 1 and c == 1 and section is held[-1]:
+                    arrived[0] = after(arrived[0], table)
+                part += arrived
+    pieces = [tile] + [part[i] for section in held for i in range(shares) for part in section]
 
     indices = (lists, corners, group_counts)
     scale = (pos_dev * blocks * shares) ** (-0.5)
     out = positions(
-        tuple(offs), scale, indices, [tile] + held[0] + held[1], eig, amps, table, coef_t
+        tuple(offs), scale, indices, pieces, eig, amps, table, coef_t
     )
     eigen_send, eigen_keep, grads, coef_rows = out[:2], out[2:4], out[4], out[5]
 
@@ -597,14 +606,15 @@
     total, sent = scatter_sum("blk", eigen.reshape(blocks, -1, frame), relative)
     mine, leaving, _ = halve(keep[last], send[last], before_cross=sent)
     moving = after(mine.astype(jnp.bfloat16), total)
+    gathered = [swap(total, "blk", i) for i in range(1, blocks)]
+    gate = moving
     for section in range(last - 1, -1, -1):
-        mine, leaving, _ = halve(keep[section], send[section], before_cross=(moving,))
-        if section == last - 1:
-            total = after(total, leaving)
+        mine, _, gate = halve(keep[section], send[section], before_cross=(gate,))
         arrived = shift(moving, "blk", 1)
         if section > 0:
             moving = (arrived.astype(jnp.float32) + mine).astype(jnp.bfloat16)
-    gathered = [swap(total, "blk", i) for i in range(1, blocks)]
+        if section == 1:
+            moving = after(moving, *gathered)
     eigen_share = place("blk", [after(total, arrived)] + gathered)
     eigen_share = eigen_share.reshape(modes, 2, frame // shares, frame)
     summed = finish(mine, arrived)

time: 106 us -> 112 us (1.057)
  starting transfers between devices: 28 us -> 35.6 us
  waiting for transfers between devices: 42.4 us -> 38.5 us
  Pallas kernels: 29 us -> 31.8 us
    ppermute x24 -> x30, starting transfers between devices: 17.2 us -> 24.3 us  [swap(): return lax.ppermute(array, axis, [(i, i ^ bit) for i in range(peers)])]
    pallas_call x1, Pallas kernels: 20.9 us -> 23.8 us  [positions(): pl.pallas_call(functools.partial(position_kernel, offs, scale), in_specs=...]
    ppermute x24 -> x30, waiting for transfers between devices: 25.2 us -> 22.4 us  [swap(): return lax.ppermute(array, axis, [(i, i ^ bit) for i in range(peers)])]
    ppermute x4 -> x6, waiting for transfers between devices: 17.1 us -> 16 us  [shift(): lax.ppermute(array, axis, [(i, (i + by) % peers) for i in range(peers)])]
    ppermute x4 -> x6, starting transfers between devices: 10.7 us -> 11.3 us  [shift(): lax.ppermute(array, axis, [(i, (i + by) % peers) for i in range(peers)])]
  transfers between devices with their start and end apart: 28 -> 36, of which waited for: 15 -> 16; matrix products, arithmetic and copies ran while one was open for 1% -> 1% of each run, Pallas kernels for 7% -> 6%
where the time goes in v7:
time: 112 us
  waiting for transfers between devices  38.5 us (34%)
  starting transfers between devices  35.6 us (32%)
  Pallas kernels  31.8 us (28%)
  local copies, waits for them, and re-layouts  3.67 us (3%)
  between operations  1.5 us (1%)
    ppermute x30, starting transfers between devices, swap(): return lax.ppermute(array, axis, [(i, i ^ bit) for i in range(peers)])  24.3 us
    pallas_call x1, Pallas kernels, positions(): pl.pallas_call(functools.partial(position_kernel, offs, scale), in_specs=...  23.8 us
    ppermute x30, waiting for transfers between devices, swap(): return lax.ppermute(array, axis, [(i, i ^ bit) for i in range(peers)])  22.4 us
    ppermute x6, waiting for transfers between devices, shift(): lax.ppermute(array, axis, [(i, (i + by) % peers) for i in range(peers)])  16 us
    ppermute x6, starting transfers between devices, shift(): lax.ppermute(array, axis, [(i, (i + by) % peers) for i in range(peers)])  11.3 us
    pallas_call x1, Pallas kernels, scatter(): pl.pallas_call(functools.partial(scatter_kernel, shares), in_specs=[pl.Bl...  5.86 us
    unnamed x14, local copies, waits for them, and re-layouts  2.65 us
  transfers between devices with their start and end apart: 36, of which 16 were waited for; matrix products, arithmetic and copies ran while one was open for 1% of the time, Pallas kernels for 6%

profile of v7, /device:TPU:0, one launch (start us, length us, event | category | flops | bytes accessed | tf_op | source)
XLA Modules:
  0.0 111.9 jit_solution(15973752403032097349)
XLA Ops:
  1.6 5.1 %collective-permute-start.2 = (bf16[128,512]{1,0:T(8,128)(2,1)S(1)}, bf16[128,512]{1,0:T(8,128)(2,1)S(1)}, u32[]{:S(2)}, u32[]{:S(2)}) collective-permute-start(bf16[128,512]{1,0:T(8,128)(2,1)S(1)} %get-tuple-element.83), channel_id=1, source_target_pairs={{0,12},{4,0},{8,4},{12,8},{1,13},{5,1},{9,5},{13,9},{2,14},{6,2},{... | collective-permute-start | bytes 393224 | tf_op jit(solution)/shard_map/ppermute | solution.py:33
  7.2 3.4 %collective-permute-done.2.refs_2_ = bf16[128,512]{1,0:T(8,128)(2,1)S(1)} collective-permute-done((bf16[128,512]{1,0:T(8,128)(2,1)S(1)}, bf16[128,512]{1,0:T(8,128)(2,1)S(1)}, u32[]{:S(2)}, u32[]{:S(2)}) %collective-permute-start.2) | collective-permute-done | bytes 131104 | tf_op jit(solution)/shard_map/ppermute | solution.py:33
  10.6 4.3 %collective-permute-start.3 = (bf16[128,512]{1,0:T(8,128)(2,1)S(1)}, bf16[128,512]{1,0:T(8,128)(2,1)S(1)}, u32[]{:S(2)}, u32[]{:S(2)}) collective-permute-start(bf16[128,512]{1,0:T(8,128)(2,1)S(1)} %collective-permute-done.2.refs_2_), channel_id=1, source_target_pairs={{0,12},{4,0},{8,4},{12,8},{1,13},{5,1},{9,5},{13,9},{2,14},{6,2},{... | collective-permute-start | bytes 393224 | tf_op jit(solution)/shard_map/ppermute | solution.py:33
  14.9 1.4 %copy-done.1 = bf16[6,2,256,256]{3,2,1,0:T(8,128)(2,1)S(1)} copy-done((bf16[6,2,256,256]{3,2,1,0:T(8,128)(2,1)S(1)}, bf16[6,2,256,256]{3,2,1,0:T(8,128)(2,1)}, u32[]{:S(2)}) %copy-start.1) | copy-done | bytes 1572888
  16.5 1.6 %collective-permute-start.5 = (bf16[128,512]{1,0:T(8,128)(2,1)S(1)}, bf16[128,512]{1,0:T(8,128)(2,1)S(1)}, u32[]{:S(2)}, u32[]{:S(2)}) collective-permute-start(bf16[128,512]{1,0:T(8,128)(2,1)S(1)} %collective-permute-done.2.refs_2_), channel_id=1, source_target_pairs={{0,2},{1,3},{2,0},{3,1},{4,6},{5,7},{6,4},{7,5},{8,10},{9,11},{10,... | collective-permute-start | bytes 393224 | tf_op jit(solution)/shard_map/ppermute | solution.py:38
  18.1 2.1 %collective-permute-start.11 = (bf16[128,512]{1,0:T(8,128)(2,1)S(1)}, bf16[128,512]{1,0:T(8,128)(2,1)S(1)}, u32[]{:S(2)}, u32[]{:S(2)}) collective-permute-start(bf16[128,512]{1,0:T(8,128)(2,1)S(1)} %collective-permute-done.3.refs_10_), channel_id=1, source_target_pairs={{0,2},{1,3},{2,0},{3,1},{4,6},{5,7},{6,4},{7,5},{8,10},{9,11},{10,... | collective-permute-start | bytes 393224 | tf_op jit(solution)/shard_map/ppermute | solution.py:38
  24.1 1.2 %copy-done.3 = bf16[2,512,512]{2,1,0:T(8,128)(2,1)S(1)} copy-done((bf16[2,512,512]{2,1,0:T(8,128)(2,1)S(1)}, bf16[2,512,512]{2,1,0:T(8,128)(2,1)}, u32[]{:S(2)}) %copy-start.3) | copy-done | bytes 1048600
  27.5 1.4 %collective-permute-done.10.refs_11_ = bf16[128,512]{1,0:T(8,128)(2,1)S(1)} collective-permute-done((bf16[128,512]{1,0:T(8,128)(2,1)S(1)}, bf16[128,512]{1,0:T(8,128)(2,1)S(1)}, u32[]{:S(2)}, u32[]{:S(2)}) %collective-permute-start.10) | collective-permute-done | bytes 131104 | tf_op jit(solution)/shard_map/ppermute | solution.py:38
  30.5 23.8 %positions.1 = (bf16[1,12,64,256]{3,2,1,0:T(8,128)(2,1)S(1)}, bf16[1,12,64,256]{3,2,1,0:T(8,128)(2,1)S(1)}, f32[1,12,64,256]{3,2,1,0:T(8,128)S(1)}, f32[1,12,64,...) custom-call(s32[2,10]{1,0:T(2,128)S(1)} %get-tuple-element.49.tile_list, ...), custom_call_target="tpu_custom_call" | custom-call | tf_op jit(solution)/shard_map/positions/pallas_call | solution.py:347
  54.8 1.2 %collective-permute-done.16 = bf16[1,12,64,256]{3,2,1,0:T(8,128)(2,1)S(1)} collective-permute-done((bf16[1,12,64,256]{3,2,1,0:T(8,128)(2,1)S(1)}, bf16[1,12,64,256]{3,2,1,0:T(8,128)(2,1)S(1)}, u32[]{:S(2)}, u32[]{:S(2)}) %collective-permute-start.16) | collective-permute-done | bytes 393248 | tf_op jit(solution)/shard_map/ppermute | solution.py:38
  56.1 1.8 %collective-permute-start.23 = (bf16[1,12,64,256]{3,2,1,0:T(8,128)(2,1)S(1)}, bf16[1,12,64,256]{3,2,1,0:T(8,128)(2,1)S(1)}, u32[]{:S(2)}, u32[]{:S(2)}) collective-permute-start(bf16[1,12,64,256]{3,2,1,0:T(8,128)(2,1)S(1)} %add_convert_fusion), channel_id=1, source_target_pairs={{0,2},{1,3},{2,0},{3,1},{4,6},{5,7},{6,4},{7,5},{8,10},{9,11},{10,... | collective-permute-start | bytes 1179656 | tf_op jit(solution)/shard_map/ppermute | solution.py:38
  57.9 5.9 %scatter.1 = (bf16[1,2,4,128,128]{4,3,2,1,0:T(8,128)(2,1)S(1)}, bf16[1,2,4,128,128]{4,3,2,1,0:T(8,128)(2,1)S(1)}, bf16[1,2,4,128,128]{4,3,2,1,0:T(8,128)(2,1)S(1...) custom-call(s32[2,10]{1,0:T(2,128)S(1)} %get-tuple-element.49.tile_l, ...), custom_call_target="tpu_custom_call" | custom-call | flops 16777216 | bytes 16777216 | tf_op jit(solution)/shard_map/scatter/pallas_call | solution.py:468
  64.3 3.2 %collective-permute-done.23 = bf16[1,12,64,256]{3,2,1,0:T(8,128)(2,1)S(1)} collective-permute-done((bf16[1,12,64,256]{3,2,1,0:T(8,128)(2,1)S(1)}, bf16[1,12,64,256]{3,2,1,0:T(8,128)(2,1)S(1)}, u32[]{:S(2)}, u32[]{:S(2)}) %collective-permute-start.23) | collective-permute-done | bytes 393248 | tf_op jit(solution)/shard_map/ppermute | solution.py:38
  68.7 3.4 %collective-permute-start.27 = (bf16[192,256]{1,0:T(8,128)(2,1)S(1)}, bf16[192,256]{1,0:T(8,128)(2,1)S(1)}, u32[]{:S(2)}, u32[]{:S(2)}) collective-permute-start(bf16[192,256]{1,0:T(8,128)(2,1)S(1)} %bitcast.37), channel_id=1, source_target_pairs={{0,12},{4,8},{8,4},{12,0},{1,13},{5,9},{9,5},{13,1},{2,14},{6,10},... | collective-permute-start | bytes 294920 | tf_op jit(solution)/shard_map/ppermute | solution.py:38
  72.7 1.6 %collective-permute-start.24 = (bf16[1,2,4,128,128]{4,3,2,1,0:T(8,128)(2,1)S(1)}, bf16[1,2,4,128,128]{4,3,2,1,0:T(8,128)(2,1)S(1)}, u32[]{:S(2)}, u32[]{:S(2)}) collective-permute-start(bf16[1,2,4,128,128]{4,3,2,1,0:T(8,128)(2,1)S(1)} %add_convert_fusion.4), channel_id=1, source_target_pairs={{0,2},{1,3},{2,0},{3,1},{4,6},{5,7},{6,4},{7,5},{8,10},{9,11},{10,... | collective-permute-start | bytes 786440 | tf_op jit(solution)/shard_map/ppermute | solution.py:38
  74.3 4.1 %collective-permute-done.26 = bf16[192,256]{1,0:T(8,128)(2,1)S(1)} collective-permute-done((bf16[192,256]{1,0:T(8,128)(2,1)S(1)}, bf16[192,256]{1,0:T(8,128)(2,1)S(1)}, u32[]{:S(2)}, u32[]{:S(2)}) %collective-permute-start.26) | collective-permute-done | bytes 98336 | tf_op jit(solution)/shard_map/ppermute | solution.py:38
  80.1 1.5 %collective-permute-start.28 = (bf16[1,2,4,128,128]{4,3,2,1,0:T(8,128)(2,1)S(1)}, bf16[1,2,4,128,128]{4,3,2,1,0:T(8,128)(2,1)S(1)}, u32[]{:S(2)}, u32[]{:S(2)}) collective-permute-start(bf16[1,2,4,128,128]{4,3,2,1,0:T(8,128)(2,1)S(1)} %add_convert_fusion.2), channel_id=1, source_target_pairs={{0,2},{1,3},{2,0},{3,1},{4,6},{5,7},{6,4},{7,5},{8,10},{9,11},{10,... | collective-permute-start | bytes 786440 | tf_op jit(solution)/shard_map/ppermute | solution.py:38
  81.6 1.4 %collective-permute-start.30 = (bf16[2,4,128,128]{3,2,1,0:T(8,128)(2,1)S(1)}, bf16[2,4,128,128]{3,2,1,0:T(8,128)(2,1)S(1)}, u32[]{:S(2)}, u32[]{:S(2)}) collective-permute-start(bf16[2,4,128,128]{3,2,1,0:T(8,128)(2,1)S(1)} %fusion.1), channel_id=1, source_target_pairs={{0,4},{4,8},{8,12},{12,0},{1,5},{5,9},{9,13},{13,1},{2,6},{6,10},{... | collective-permute-start | bytes 786440 | tf_op jit(solution)/shard_map/ppermute | solution.py:33
  83.6 2.4 %collective-permute-start.34 = (bf16[192,256]{1,0:T(8,128)(2,1)S(1)}, bf16[192,256]{1,0:T(8,128)(2,1)S(1)}, u32[]{:S(2)}, u32[]{:S(2)}) collective-permute-start(bf16[192,256]{1,0:T(8,128)(2,1)S(1)} %fusion.4.refs_0_), channel_id=1, source_target_pairs={{0,12},{4,8},{8,4},{12,0},{1,13},{5,9},{9,5},{13,1},{2,14},{6,10},... | collective-permute-start | bytes 294920 | tf_op jit(solution)/shard_map/ppermute | solution.py:38
  86.0 2.4 %collective-permute-done.28 = bf16[1,2,4,128,128]{4,3,2,1,0:T(8,128)(2,1)S(1)} collective-permute-done((bf16[1,2,4,128,128]{4,3,2,1,0:T(8,128)(2,1)S(1)}, bf16[1,2,4,128,128]{4,3,2,1,0:T(8,128)(2,1)S(1)}, u32[]{:S(2)}, u32[]{:S(2)}) %collective-permute-start.28) | collective-permute-done | bytes 262176 | tf_op jit(solution)/shard_map/ppermute | solution.py:38
  88.4 1.2 %collective-permute-start.33 = (bf16[192,256]{1,0:T(8,128)(2,1)S(1)}, bf16[192,256]{1,0:T(8,128)(2,1)S(1)}, u32[]{:S(2)}, u32[]{:S(2)}) collective-permute-start(bf16[192,256]{1,0:T(8,128)(2,1)S(1)} %fusion.4.refs_0_), channel_id=1, source_target_pairs={{0,8},{4,12},{8,0},{12,4},{1,9},{5,13},{9,1},{13,5},{2,10},{6,14},... | collective-permute-start | bytes 294920 | tf_op jit(solution)/shard_map/ppermute | solution.py:38
  89.6 3.1 %collective-permute-done.30 = bf16[2,4,128,128]{3,2,1,0:T(8,128)(2,1)S(1)} collective-permute-done((bf16[2,4,128,128]{3,2,1,0:T(8,128)(2,1)S(1)}, bf16[2,4,128,128]{3,2,1,0:T(8,128)(2,1)S(1)}, u32[]{:S(2)}, u32[]{:S(2)}) %collective-permute-start.30) | collective-permute-done | bytes 262176 | tf_op jit(solution)/shard_map/ppermute | solution.py:33
  94.9 5.1 %collective-permute-done.33.refs_2_ = bf16[192,256]{1,0:T(8,128)(2,1)S(1)} collective-permute-done((bf16[192,256]{1,0:T(8,128)(2,1)S(1)}, bf16[192,256]{1,0:T(8,128)(2,1)S(1)}, u32[]{:S(2)}, u32[]{:S(2)}) %collective-permute-start.33) | collective-permute-done | bytes 98336 | tf_op jit(solution)/shard_map/ppermute | solution.py:38
  100.5 9.5 %collective-permute-done.35.second = bf16[2,4,128,128]{3,2,1,0:T(8,128)(2,1)S(1)} collective-permute-done((bf16[2,4,128,128]{3,2,1,0:T(8,128)(2,1)S(1)}, bf16[2,4,128,128]{3,2,1,0:T(8,128)(2,1)S(1)}, u32[]{:S(2)}, u32[]{:S(2)}) %collective-permute-start.35) | collective-permute-done | bytes 262176 | tf_op jit(solution)/shard_map/ppermute | solution.py:33
  (80 shorter events, 18.3 us)
Async XLA Ops:
  1.6 9.0 %collective-permute-start.2 = (bf16[128,512]{1,0:T(8,128)(2,1)S(1)}, bf16[128,512]{1,0:T(8,128)(2,1)S(1)}, u32[]{:S(2)}, u32[]{:S(2)}) collective-permute-start(bf16[128,512]{1,0:T(8,128)(2,1)S(1)} %get-tuple-element.83), channel_id=1, source_target_pairs={{0,12},{4,0},{8,4},{12,8},{1,13},{5,1},{9,5},{13,9},{2,14},{6,2},{... | collective-permute-start | bytes 393224 | tf_op jit(solution)/shard_map/ppermute | solution.py:33
  6.7 9.7 %collective-permute-start = (bf16[128,512]{1,0:T(8,128)(2,1)S(1)}, bf16[128,512]{1,0:T(8,128)(2,1)S(1)}, u32[]{:S(2)}, u32[]{:S(2)}) collective-permute-start(bf16[128,512]{1,0:T(8,128)(2,1)S(1)} %get-tuple-element.84), channel_id=1, source_target_pairs={{0,12},{4,0},{8,4},{12,8},{1,13},{5,1},{9,5},{13,9},{2,14},{6,2},{... | collective-permute-start | bytes 393224 | tf_op jit(solution)/shard_map/ppermute | solution.py:33
  10.6 7.4 %collective-permute-start.3 = (bf16[128,512]{1,0:T(8,128)(2,1)S(1)}, bf16[128,512]{1,0:T(8,128)(2,1)S(1)}, u32[]{:S(2)}, u32[]{:S(2)}) collective-permute-start(bf16[128,512]{1,0:T(8,128)(2,1)S(1)} %collective-permute-done.2.refs_2_), channel_id=1, source_target_pairs={{0,12},{4,0},{8,4},{12,8},{1,13},{5,1},{9,5},{13,9},{2,14},{6,2},{... | collective-permute-start | bytes 393224 | tf_op jit(solution)/shard_map/ppermute | solution.py:33
  18.1 6.0 %collective-permute-start.11 = (bf16[128,512]{1,0:T(8,128)(2,1)S(1)}, bf16[128,512]{1,0:T(8,128)(2,1)S(1)}, u32[]{:S(2)}, u32[]{:S(2)}) collective-permute-start(bf16[128,512]{1,0:T(8,128)(2,1)S(1)} %collective-permute-done.3.refs_10_), channel_id=1, source_target_pairs={{0,2},{1,3},{2,0},{3,1},{4,6},{5,7},{6,4},{7,5},{8,10},{9,11},{10,... | collective-permute-start | bytes 393224 | tf_op jit(solution)/shard_map/ppermute | solution.py:38
  20.2 6.0 %collective-permute-start.6 = (bf16[128,512]{1,0:T(8,128)(2,1)S(1)}, bf16[128,512]{1,0:T(8,128)(2,1)S(1)}, u32[]{:S(2)}, u32[]{:S(2)}) collective-permute-start(bf16[128,512]{1,0:T(8,128)(2,1)S(1)} %collective-permute-done.refs_1_), channel_id=1, source_target_pairs={{0,1},{1,0},{2,3},{3,2},{4,5},{5,4},{6,7},{7,6},{8,9},{9,8},{10,11... | collective-permute-start | bytes 393224 | tf_op jit(solution)/shard_map/ppermute | solution.py:38
  21.9 5.7 %collective-permute-start.4 = (bf16[128,512]{1,0:T(8,128)(2,1)S(1)}, bf16[128,512]{1,0:T(8,128)(2,1)S(1)}, u32[]{:S(2)}, u32[]{:S(2)}) collective-permute-start(bf16[128,512]{1,0:T(8,128)(2,1)S(1)} %collective-permute-done.refs_1_), channel_id=1, source_target_pairs={{0,2},{1,3},{2,0},{3,1},{4,6},{5,7},{6,4},{7,5},{8,10},{9,11},{10,... | collective-permute-start | bytes 393224 | tf_op jit(solution)/shard_map/ppermute | solution.py:38
  23.0 5.9 %collective-permute-start.10 = (bf16[128,512]{1,0:T(8,128)(2,1)S(1)}, bf16[128,512]{1,0:T(8,128)(2,1)S(1)}, u32[]{:S(2)}, u32[]{:S(2)}) collective-permute-start(bf16[128,512]{1,0:T(8,128)(2,1)S(1)} %collective-permute-done.1.refs_9_), channel_id=1, source_target_pairs={{0,2},{1,3},{2,0},{3,1},{4,6},{5,7},{6,4},{7,5},{8,10},{9,11},{10,... | collective-permute-start | bytes 393224 | tf_op jit(solution)/shard_map/ppermute | solution.py:38
  54.7 9.7 %collective-permute-start.22 = (bf16[1,12,64,256]{3,2,1,0:T(8,128)(2,1)S(1)}, bf16[1,12,64,256]{3,2,1,0:T(8,128)(2,1)S(1)}, u32[]{:S(2)}, u32[]{:S(2)}) collective-permute-start(bf16[1,12,64,256]{3,2,1,0:T(8,128)(2,1)S(1)} %get-tuple-element.71), channel_id=1, source_target_pairs={{0,1},{1,0},{2,3},{3,2},{4,5},{5,4},{6,7},{7,6},{8,9},{9,8},{10,11... | collective-permute-start | bytes 1179656 | tf_op jit(solution)/shard_map/ppermute | solution.py:38
  56.1 11.4 %collective-permute-start.23 = (bf16[1,12,64,256]{3,2,1,0:T(8,128)(2,1)S(1)}, bf16[1,12,64,256]{3,2,1,0:T(8,128)(2,1)S(1)}, u32[]{:S(2)}, u32[]{:S(2)}) collective-permute-start(bf16[1,12,64,256]{3,2,1,0:T(8,128)(2,1)S(1)} %add_convert_fusion), channel_id=1, source_target_pairs={{0,2},{1,3},{2,0},{3,1},{4,6},{5,7},{6,4},{7,5},{8,10},{9,11},{10,... | collective-permute-start | bytes 1179656 | tf_op jit(solution)/shard_map/ppermute | solution.py:38
  63.8 15.2 %collective-permute-start.20 = (bf16[1,2,4,128,128]{4,3,2,1,0:T(8,128)(2,1)S(1)}, bf16[1,2,4,128,128]{4,3,2,1,0:T(8,128)(2,1)S(1)}, u32[]{:S(2)}, u32[]{:S(2)}) collective-permute-start(bf16[1,2,4,128,128]{4,3,2,1,0:T(8,128)(2,1)S(1)} %get-tuple-element.67), channel_id=1, source_target_pairs={{0,1},{1,0},{2,3},{3,2},{4,5},{5,4},{6,7},{7,6},{8,9},{9,8},{10,11... | collective-permute-start | bytes 786440 | tf_op jit(solution)/shard_map/ppermute | solution.py:38
  63.9 8.8 %collective-permute-start.21 = (bf16[1,2,4,128,128]{4,3,2,1,0:T(8,128)(2,1)S(1)}, bf16[1,2,4,128,128]{4,3,2,1,0:T(8,128)(2,1)S(1)}, u32[]{:S(2)}, u32[]{:S(2)}) collective-permute-start(bf16[1,2,4,128,128]{4,3,2,1,0:T(8,128)(2,1)S(1)} %get-tuple-element.69), channel_id=1, source_target_pairs={{0,1},{1,0},{2,3},{3,2},{4,5},{5,4},{6,7},{7,6},{8,9},{9,8},{10,11... | collective-permute-start | bytes 786440 | tf_op jit(solution)/shard_map/ppermute | solution.py:38
  67.8 10.6 %collective-permute-start.26 = (bf16[192,256]{1,0:T(8,128)(2,1)S(1)}, bf16[192,256]{1,0:T(8,128)(2,1)S(1)}, u32[]{:S(2)}, u32[]{:S(2)}) collective-permute-start(bf16[192,256]{1,0:T(8,128)(2,1)S(1)} %bitcast.38), channel_id=1, source_target_pairs={{0,8},{4,12},{8,0},{12,4},{1,9},{5,13},{9,1},{13,5},{2,10},{6,14},... | collective-permute-start | bytes 294920 | tf_op jit(solution)/shard_map/ppermute | solution.py:38
  68.7 9.7 %collective-permute-start.27 = (bf16[192,256]{1,0:T(8,128)(2,1)S(1)}, bf16[192,256]{1,0:T(8,128)(2,1)S(1)}, u32[]{:S(2)}, u32[]{:S(2)}) collective-permute-start(bf16[192,256]{1,0:T(8,128)(2,1)S(1)} %bitcast.37), channel_id=1, source_target_pairs={{0,12},{4,8},{8,4},{12,0},{1,13},{5,9},{9,5},{13,1},{2,14},{6,10},... | collective-permute-start | bytes 294920 | tf_op jit(solution)/shard_map/ppermute | solution.py:38
  72.1 6.7 %collective-permute-start.25 = (bf16[192,256]{1,0:T(8,128)(2,1)S(1)}, bf16[192,256]{1,0:T(8,128)(2,1)S(1)}, u32[]{:S(2)}, u32[]{:S(2)}) collective-permute-start(bf16[192,256]{1,0:T(8,128)(2,1)S(1)} %bitcast.36), channel_id=1, source_target_pairs={{0,4},{4,0},{8,12},{12,8},{1,5},{5,1},{9,13},{13,9},{2,6},{6,2},{1... | collective-permute-start | bytes 294920 | tf_op jit(solution)/shard_map/ppermute | solution.py:38
  72.7 7.2 %collective-permute-start.24 = (bf16[1,2,4,128,128]{4,3,2,1,0:T(8,128)(2,1)S(1)}, bf16[1,2,4,128,128]{4,3,2,1,0:T(8,128)(2,1)S(1)}, u32[]{:S(2)}, u32[]{:S(2)}) collective-permute-start(bf16[1,2,4,128,128]{4,3,2,1,0:T(8,128)(2,1)S(1)} %add_convert_fusion.4), channel_id=1, source_target_pairs={{0,2},{1,3},{2,0},{3,1},{4,6},{5,7},{6,4},{7,5},{8,10},{9,11},{10,... | collective-permute-start | bytes 786440 | tf_op jit(solution)/shard_map/ppermute | solution.py:38
  80.1 8.3 %collective-permute-start.28 = (bf16[1,2,4,128,128]{4,3,2,1,0:T(8,128)(2,1)S(1)}, bf16[1,2,4,128,128]{4,3,2,1,0:T(8,128)(2,1)S(1)}, u32[]{:S(2)}, u32[]{:S(2)}) collective-permute-start(bf16[1,2,4,128,128]{4,3,2,1,0:T(8,128)(2,1)S(1)} %add_convert_fusion.2), channel_id=1, source_target_pairs={{0,2},{1,3},{2,0},{3,1},{4,6},{5,7},{6,4},{7,5},{8,10},{9,11},{10,... | collective-permute-start | bytes 786440 | tf_op jit(solution)/shard_map/ppermute | solution.py:38
  81.6 11.1 %collective-permute-start.30 = (bf16[2,4,128,128]{3,2,1,0:T(8,128)(2,1)S(1)}, bf16[2,4,128,128]{3,2,1,0:T(8,128)(2,1)S(1)}, u32[]{:S(2)}, u32[]{:S(2)}) collective-permute-start(bf16[2,4,128,128]{3,2,1,0:T(8,128)(2,1)S(1)} %fusion.1), channel_id=1, source_target_pairs={{0,4},{4,8},{8,12},{12,0},{1,5},{5,9},{9,13},{13,1},{2,6},{6,10},{... | collective-permute-start | bytes 786440 | tf_op jit(solution)/shard_map/ppermute | solution.py:33
  83.0 26.9 %collective-permute-start.17 = (bf16[1,2,4,128,128]{4,3,2,1,0:T(8,128)(2,1)S(1)}, bf16[1,2,4,128,128]{4,3,2,1,0:T(8,128)(2,1)S(1)}, u32[]{:S(2)}, u32[]{:S(2)}) collective-permute-start(bf16[1,2,4,128,128]{4,3,2,1,0:T(8,128)(2,1)S(1)} %get-tuple-element.61), channel_id=1, source_target_pairs={{0,1},{1,0},{2,3},{3,2},{4,5},{5,4},{6,7},{7,6},{8,9},{9,8},{10,11... | collective-permute-start | bytes 786440 | tf_op jit(solution)/shard_map/ppermute | solution.py:38
  83.0 10.7 %collective-permute-start.18 = (bf16[1,2,4,128,128]{4,3,2,1,0:T(8,128)(2,1)S(1)}, bf16[1,2,4,128,128]{4,3,2,1,0:T(8,128)(2,1)S(1)}, u32[]{:S(2)}, u32[]{:S(2)}) collective-permute-start(bf16[1,2,4,128,128]{4,3,2,1,0:T(8,128)(2,1)S(1)} %get-tuple-element.63), channel_id=1, source_target_pairs={{0,1},{1,0},{2,3},{3,2},{4,5},{5,4},{6,7},{7,6},{8,9},{9,8},{10,11... | collective-permute-start | bytes 786440 | tf_op jit(solution)/shard_map/ppermute | solution.py:38
  83.6 11.3 %collective-permute-start.34 = (bf16[192,256]{1,0:T(8,128)(2,1)S(1)}, bf16[192,256]{1,0:T(8,128)(2,1)S(1)}, u32[]{:S(2)}, u32[]{:S(2)}) collective-permute-start(bf16[192,256]{1,0:T(8,128)(2,1)S(1)} %fusion.4.refs_0_), channel_id=1, source_target_pairs={{0,12},{4,8},{8,4},{12,0},{1,13},{5,9},{9,5},{13,1},{2,14},{6,10},... | collective-permute-start | bytes 294920 | tf_op jit(solution)/shard_map/ppermute | solution.py:38
  88.4 11.6 %collective-permute-start.33 = (bf16[192,256]{1,0:T(8,128)(2,1)S(1)}, bf16[192,256]{1,0:T(8,128)(2,1)S(1)}, u32[]{:S(2)}, u32[]{:S(2)}) collective-permute-start(bf16[192,256]{1,0:T(8,128)(2,1)S(1)} %fusion.4.refs_0_), channel_id=1, source_target_pairs={{0,8},{4,12},{8,0},{12,4},{1,9},{5,13},{9,1},{13,5},{2,10},{6,14},... | collective-permute-start | bytes 294920 | tf_op jit(solution)/shard_map/ppermute | solution.py:38
  92.7 7.2 %collective-permute-start.32 = (bf16[192,256]{1,0:T(8,128)(2,1)S(1)}, bf16[192,256]{1,0:T(8,128)(2,1)S(1)}, u32[]{:S(2)}, u32[]{:S(2)}) collective-permute-start(bf16[192,256]{1,0:T(8,128)(2,1)S(1)} %fusion.4.refs_0_), channel_id=1, source_target_pairs={{0,4},{4,0},{8,12},{12,8},{1,5},{5,1},{9,13},{13,9},{2,6},{6,2},{1... | collective-permute-start | bytes 294920 | tf_op jit(solution)/shard_map/ppermute | solution.py:38
  99.9 10.0 %collective-permute-start.35 = (bf16[2,4,128,128]{3,2,1,0:T(8,128)(2,1)S(1)}, bf16[2,4,128,128]{3,2,1,0:T(8,128)(2,1)S(1)}, u32[]{:S(2)}, u32[]{:S(2)}) collective-permute-start(bf16[2,4,128,128]{3,2,1,0:T(8,128)(2,1)S(1)} %fusion), channel_id=1, source_target_pairs={{0,4},{4,8},{8,12},{12,0},{1,5},{5,9},{9,13},{13,1},{2,6},{6,10},{... | collective-permute-start | bytes 786440 | tf_op jit(solution)/shard_map/ppermute | solution.py:33
  100.0 10.0 %collective-permute-start.29 = (bf16[1,2,4,128,128]{4,3,2,1,0:T(8,128)(2,1)S(1)}, bf16[1,2,4,128,128]{4,3,2,1,0:T(8,128)(2,1)S(1)}, u32[]{:S(2)}, u32[]{:S(2)}) collective-permute-start(bf16[1,2,4,128,128]{4,3,2,1,0:T(8,128)(2,1)S(1)} %add_convert_fusion.1), channel_id=1, source_target_pairs={{0,2},{1,3},{2,0},{3,1},{4,6},{5,7},{6,4},{7,5},{8,10},{9,11},{10,... | collective-permute-start | bytes 786440 | tf_op jit(solution)/shard_map/ppermute | solution.py:38
  (19 other events, 103.9 us)

commit v8 on v5

--- a/solution.py
+++ b/solution.py
@@ -46,10 +46,6 @@
 
 def far_first(shares):
     return [*range(1, shares // 2, 2), *range(0, shares // 2, 2)]
-
-
-def share_of(groups, peers):
-    return groups // peers if groups % peers == 0 else 0
 
 
 def coordinates(tile_list, offsets, group_counts, pos_dev):
@@ -278,8 +274,6 @@
 
     cross[...] = jnp.zeros_like(cross)
     rows_q = frame // shares
-    groups = 2 * modes
-    share = share_of(groups, lax.axis_size("blk"))
 
     def eigen_strip(i, carry):
         rows = pl.ds(pl.multiple_of(i * STRIP, STRIP), STRIP)
@@ -293,10 +287,7 @@
             rest = jnp.dot(weights_t[:modes * STRIP], low, preferred_element_type=jnp.float32)
             grad = (both[:modes * STRIP] + both[modes * STRIP:] + rest) * scale
             for k in range(modes):
-                group = 2 * k + c
-                if share:
-                    group = (group // share ^ my_block) * share + group % share
-                eigen[q, group, inner, :] = grad[k * STRIP:(k + 1) * STRIP]
+                eigen[q, 2 * k + c, inner, :] = grad[k * STRIP:(k + 1) * STRIP]
             cross[...] += lax.dot_general(
                 high, e, (((1,), (1,)), ((), ())), preferred_element_type=jnp.float32
             )
@@ -507,32 +498,16 @@
         bit *= 2
 
 
-def scatter_sum(axis, value, relative):
-    me = lax.axis_index(axis)
-    share = (lambda i: value[i]) if relative else (lambda i: lax.dynamic_index_in_dim(value, me ^ i, 0, False))
-    total = share(0)
-    sent = [share(i).astype(jnp.bfloat16) for i in range(1, lax.axis_size(axis))]
-    for i, sending in enumerate(sent, 1):
-        total += swap(sending, axis, i).astype(jnp.float32)
-    return total.astype(jnp.bfloat16), sent
-
-
-def place_kernel(axis, *refs):
-    pieces, out = refs[:-1], refs[-1]
-    me = lax.axis_index(axis)
-    for i, piece in enumerate(pieces):
-        out[me ^ i] = piece[...].astype(jnp.float32)
-
-
-def place(axis, held):
-    return pl.pallas_call(
-        functools.partial(place_kernel, axis),
-        in_specs=[pl.BlockSpec(memory_space=VMEM)] * len(held),
-        out_specs=pl.BlockSpec(memory_space=VMEM),
-        out_shape=jax.ShapeDtypeStruct((len(held),) + held[0].shape, jnp.float32),
-        compiler_params=pltpu.CompilerParams(vmem_limit_bytes=8 * 1024 * 1024),
-        name="place",
-    )(*held)
+def sum_over(axis, value):
+    peers = lax.axis_size(axis)
+    shares = lax.all_to_all(value.astype(jnp.bfloat16), axis, 0, 0)
+    total = jnp.sum(shares.astype(jnp.float32), 0).astype(jnp.bfloat16)
+
+    def gather(*others):
+        copies = jnp.broadcast_to(after(total, *others), (peers,) + total.shape)
+        return lax.all_to_all(copies, axis, 0, 0).astype(jnp.float32)
+
+    return total, gather
 
 
 def finish_kernel(first, second, out):
@@ -593,20 +568,16 @@
     out = scatter(shares, side, indices, after(grads, leaving))
     send, keep = ([out[at + 2 * i:at + 2 * i + 2] for i in range(REACH)] for at in (0, 2 * REACH))
     last = REACH - 1
-    relative = share_of(2 * modes, blocks) > 0
-    total, sent = scatter_sum("blk", eigen.reshape(blocks, -1, frame), relative)
-    mine, leaving, _ = halve(keep[last], send[last], before_cross=sent)
+    mine, leaving, _ = halve(keep[last], send[last], before_cross=(crossed,))
+    total, gather = sum_over("blk", after(eigen, leaving).reshape(blocks, -1, frame))
     moving = after(mine.astype(jnp.bfloat16), total)
+    gate = moving
     for section in range(last - 1, -1, -1):
-        mine, leaving, _ = halve(keep[section], send[section], before_cross=(moving,))
-        if section == last - 1:
-            total = after(total, leaving)
+        mine, gate, _ = halve(keep[section], send[section], before_cross=(gate,))
         arrived = shift(moving, "blk", 1)
         if section > 0:
             moving = (arrived.astype(jnp.float32) + mine).astype(jnp.bfloat16)
-    gathered = [swap(total, "blk", i) for i in range(1, blocks)]
-    eigen_share = place("blk", [after(total, arrived)] + gathered)
-    eigen_share = eigen_share.reshape(modes, 2, frame // shares, frame)
+    eigen_share = gather(gate).reshape(modes, 2, frame // shares, frame)
     summed = finish(mine, arrived)
     return (summed[None], eigen_share, coef_rows.T)
 

time: 106 us -> 110 us (1.038)
  other arithmetic: 0.85 us -> 7.79 us
  waiting for transfers between devices: 42.4 us -> 38 us
  starting transfers between devices: 28 us -> 29.2 us
    all_to_all x0 -> x2, starting transfers between devices: none -> 8.69 us  [the longest x1 4.58 us: gather(): return lax.all_to_all(copies, axis, 0, 0).astype(jnp.float32)]
    ppermute x24 -> x18, starting transfers between devices: 17.2 us -> 8.76 us  [swap(): return lax.ppermute(array, axis, [(i, i ^ bit) for i in range(peers)])]
    ppermute x4, waiting for transfers between devices: 17.1 us -> 11.8 us  [shift(): lax.ppermute(array, axis, [(i, (i + by) % peers) for i in range(peers)])]
    convert_element_type x4, other arithmetic: 0.31 us -> 2.9 us  [halve(): sum((term.astype(jnp.float32) for term in far)).astype(jnp.bfloat16)]
    all_to_all x0 -> x2, waiting for transfers between devices: none -> 1.86 us  [the longest x1 1.66 us: sum_over(): shares = lax.all_to_all(value.astype(jnp.bfloat16), axis, 0, 0)]
    ppermute x24 -> x18, waiting for transfers between devices: 25.2 us -> 24.3 us  [swap(): return lax.ppermute(array, axis, [(i, i ^ bit) for i in range(peers)])]
    unnamed x14 -> x18, local copies, waits for them, and re-layouts: 2.75 us -> 2.76 us
  transfers between devices with their start and end apart: 28 -> 24, of which waited for: 15 -> 13; matrix products, arithmetic and copies ran while one was open for 1% -> 6% of each run, Pallas kernels for 7% -> 7%
where the time goes in v8:
time: 110 us; the launch traced here: 109 us
  waiting for transfers between devices  38 us (35%)
  starting transfers between devices  29.2 us (27%)
  Pallas kernels  28 us (25%)
  other arithmetic  7.79 us (7%)
  local copies, waits for them, and re-layouts  4.51 us (4%)
  between operations  1.51 us (1%)
    ppermute x18, waiting for transfers between devices, swap(): return lax.ppermute(array, axis, [(i, i ^ bit) for i in range(peers)])  24.3 us
    pallas_call x1, Pallas kernels, positions(): pl.pallas_call(functools.partial(position_kernel, offs, scale), in_specs=...  20.9 us
    ppermute x4, waiting for transfers between devices, shift(): lax.ppermute(array, axis, [(i, (i + by) % peers) for i in range(peers)])  11.8 us
    ppermute x4, starting transfers between devices, shift(): lax.ppermute(array, axis, [(i, (i + by) % peers) for i in range(peers)])  11.8 us
    ppermute x18, starting transfers between devices, swap(): return lax.ppermute(array, axis, [(i, i ^ bit) for i in range(peers)])  8.76 us
    pallas_call x1, Pallas kernels, scatter(): pl.pallas_call(functools.partial(scatter_kernel, shares), in_specs=[pl.Bl...  5.91 us
    all_to_all x1, starting transfers between devices, gather(): return lax.all_to_all(copies, axis, 0, 0).astype(jnp.float32)  4.58 us
    all_to_all x1, starting transfers between devices, sum_over(): shares = lax.all_to_all(value.astype(jnp.bfloat16), axis, 0, 0)  4.11 us
  transfers between devices with their start and end apart: 24, of which 13 were waited for; matrix products, arithmetic and copies ran while one was open for 6% of the time, Pallas kernels for 7%

profile of v8, /device:TPU:0, one launch (start us, length us, event | category | flops | bytes accessed | tf_op | source)
XLA Modules:
  0.0 109.1 jit_solution(9044727191610774966)
XLA Ops:
  1.7 5.1 %collective-permute-start = (bf16[2,128,512]{2,1,0:T(8,128)(2,1)S(1)}, bf16[2,128,512]{2,1,0:T(8,128)(2,1)S(1)}, u32[]{:S(2)}, u32[]{:S(2)}) collective-permute-start(bf16[2,128,512]{2,1,0:T(8,128)(2,1)S(1)} %dynamic-slice_bitcast_fusion), channel_id=1, source_target_pairs={{0,12},{4,0},{8,4},{12,8},{1,13},{5,1},{9,5},{13,9},{2,14},{6,2},{... | collective-permute-start | bytes 786440 | tf_op jit(solution)/shard_map/ppermute | solution.py:33
  6.8 5.6 %collective-permute-done.refs_1_ = bf16[2,128,512]{2,1,0:T(8,128)(2,1)S(1)} collective-permute-done((bf16[2,128,512]{2,1,0:T(8,128)(2,1)S(1)}, bf16[2,128,512]{2,1,0:T(8,128)(2,1)S(1)}, u32[]{:S(2)}, u32[]{:S(2)}) %collective-permute-start) | collective-permute-done | bytes 262176 | tf_op jit(solution)/shard_map/ppermute | solution.py:33
  12.3 4.3 %collective-permute-start.1 = (bf16[2,128,512]{2,1,0:T(8,128)(2,1)S(1)}, bf16[2,128,512]{2,1,0:T(8,128)(2,1)S(1)}, u32[]{:S(2)}, u32[]{:S(2)}) collective-permute-start(bf16[2,128,512]{2,1,0:T(8,128)(2,1)S(1)} %collective-permute-done.refs_1_), channel_id=1, source_target_pairs={{0,12},{4,0},{8,4},{12,8},{1,13},{5,1},{9,5},{13,9},{2,14},{6,2},{... | collective-permute-start | bytes 786440 | tf_op jit(solution)/shard_map/ppermute | solution.py:33
  16.6 1.5 %collective-permute-start.2 = (bf16[2,128,512]{2,1,0:T(8,128)(2,1)S(1)}, bf16[2,128,512]{2,1,0:T(8,128)(2,1)S(1)}, u32[]{:S(2)}, u32[]{:S(2)}) collective-permute-start(bf16[2,128,512]{2,1,0:T(8,128)(2,1)S(1)} %collective-permute-done.refs_1_), channel_id=1, source_target_pairs={{0,2},{1,3},{2,0},{3,1},{4,6},{5,7},{6,4},{7,5},{8,10},{9,11},{10,... | collective-permute-start | bytes 786440 | tf_op jit(solution)/shard_map/ppermute | solution.py:38
  18.1 1.4 %copy-done.1 = bf16[6,2,256,256]{3,2,1,0:T(8,128)(2,1)S(1)} copy-done((bf16[6,2,256,256]{3,2,1,0:T(8,128)(2,1)S(1)}, bf16[6,2,256,256]{3,2,1,0:T(8,128)(2,1)}, u32[]{:S(2)}) %copy-start.1) | copy-done | bytes 1572888
  19.5 1.3 %copy-done.2 = bf16[10,256,256]{2,1,0:T(8,128)(2,1)S(1)} copy-done((bf16[10,256,256]{2,1,0:T(8,128)(2,1)S(1)}, bf16[10,256,256]{2,1,0:T(8,128)(2,1)}, u32[]{:S(2)}) %copy-start.2) | copy-done | bytes 1310744
  21.3 1.5 %collective-permute-start.5 = (bf16[2,128,512]{2,1,0:T(8,128)(2,1)S(1)}, bf16[2,128,512]{2,1,0:T(8,128)(2,1)S(1)}, u32[]{:S(2)}, u32[]{:S(2)}) collective-permute-start(bf16[2,128,512]{2,1,0:T(8,128)(2,1)S(1)} %collective-permute-done.1.refs_5_), channel_id=1, source_target_pairs={{0,2},{1,3},{2,0},{3,1},{4,6},{5,7},{6,4},{7,5},{8,10},{9,11},{10,... | collective-permute-start | bytes 786440 | tf_op jit(solution)/shard_map/ppermute | solution.py:38
  23.3 1.5 %collective-permute-done.2.refs_2_ = bf16[2,128,512]{2,1,0:T(8,128)(2,1)S(1)} collective-permute-done((bf16[2,128,512]{2,1,0:T(8,128)(2,1)S(1)}, bf16[2,128,512]{2,1,0:T(8,128)(2,1)S(1)}, u32[]{:S(2)}, u32[]{:S(2)}) %collective-permute-start.2) | collective-permute-done | bytes 262176 | tf_op jit(solution)/shard_map/ppermute | solution.py:38
  25.1 4.1 %collective-permute-done.5.refs_6_ = bf16[2,128,512]{2,1,0:T(8,128)(2,1)S(1)} collective-permute-done((bf16[2,128,512]{2,1,0:T(8,128)(2,1)S(1)}, bf16[2,128,512]{2,1,0:T(8,128)(2,1)S(1)}, u32[]{:S(2)}, u32[]{:S(2)}) %collective-permute-start.5) | collective-permute-done | bytes 262176 | tf_op jit(solution)/shard_map/ppermute | solution.py:38
  30.7 20.9 %positions.1 = (bf16[1,12,64,256]{3,2,1,0:T(8,128)(2,1)S(1)}, bf16[1,12,64,256]{3,2,1,0:T(8,128)(2,1)S(1)}, f32[1,12,64,256]{3,2,1,0:T(8,128)S(1)}, f32[1,12,64,...) custom-call(s32[2,10]{1,0:T(2,128)S(1)} %get-tuple-element.54.tile_list, ...), custom_call_target="tpu_custom_call" | custom-call | tf_op jit(solution)/shard_map/positions/pallas_call | solution.py:337
  51.6 1.7 %collective-permute-done.8 = bf16[1,12,64,256]{3,2,1,0:T(8,128)(2,1)S(1)} collective-permute-done((bf16[1,12,64,256]{3,2,1,0:T(8,128)(2,1)S(1)}, bf16[1,12,64,256]{3,2,1,0:T(8,128)(2,1)S(1)}, u32[]{:S(2)}, u32[]{:S(2)}) %collective-permute-start.8) | collective-permute-done | bytes 393248 | tf_op jit(solution)/shard_map/ppermute | solution.py:38
  53.5 5.9 %scatter.1 = (bf16[1,2,4,128,128]{4,3,2,1,0:T(8,128)(2,1)S(1)}, bf16[1,2,4,128,128]{4,3,2,1,0:T(8,128)(2,1)S(1)}, bf16[1,2,4,128,128]{4,3,2,1,0:T(8,128)(2,1)S(1...) custom-call(s32[2,10]{1,0:T(2,128)S(1)} %get-tuple-element.54.tile_l, ...), custom_call_target="tpu_custom_call" | custom-call | flops 16777216 | bytes 16777216 | tf_op jit(solution)/shard_map/scatter/pallas_call | solution.py:458
  61.1 3.6 %collective-permute-done.14 = bf16[1,12,64,256]{3,2,1,0:T(8,128)(2,1)S(1)} collective-permute-done((bf16[1,12,64,256]{3,2,1,0:T(8,128)(2,1)S(1)}, bf16[1,12,64,256]{3,2,1,0:T(8,128)(2,1)S(1)}, u32[]{:S(2)}, u32[]{:S(2)}) %collective-permute-start.14) | collective-permute-done | bytes 393248 | tf_op jit(solution)/shard_map/ppermute | solution.py:38
  66.4 4.1 %all-to-all-start = ((bf16[4,192,256]{2,1,0:T(8,128)(2,1)}), bf16[4,192,256]{2,1,0:T(8,128)(2,1)}, u32[]{:S(2)}, u32[]{:S(2)}) async-start(bf16[4,192,256]{2,1,0:T(8,128)(2,1)} %bitcast.26), calls=%async_computation | async-start | bytes 786432 | tf_op jit(solution)/shard_map/all_to_all | solution.py:503
  70.6 1.4 %collective-permute-start.15 = (bf16[1,2,4,128,128]{4,3,2,1,0:T(8,128)(2,1)}, bf16[1,2,4,128,128]{4,3,2,1,0:T(8,128)(2,1)S(1)}, u32[]{:S(2)}, u32[]{:S(2)}) collective-permute-start(bf16[1,2,4,128,128]{4,3,2,1,0:T(8,128)(2,1)} %add_convert_fusion.4), channel_id=1, source_target_pairs={{0,2},{1,3},{2,0},{3,1},{4,6},{5,7},{6,4},{7,5},{8,10},{9,11},{10,... | collective-permute-start | bytes 786440 | tf_op jit(solution)/shard_map/ppermute | solution.py:38
  72.7 6.8 %collective-permute-done.15 = bf16[1,2,4,128,128]{4,3,2,1,0:T(8,128)(2,1)S(1)} collective-permute-done((bf16[1,2,4,128,128]{4,3,2,1,0:T(8,128)(2,1)}, bf16[1,2,4,128,128]{4,3,2,1,0:T(8,128)(2,1)S(1)}, u32[]{:S(2)}, u32[]{:S(2)}) %collective-permute-start.15) | collective-permute-done | bytes 262176 | tf_op jit(solution)/shard_map/ppermute | solution.py:38
  80.3 1.7 %all-to-all-done = bf16[4,192,256]{2,1,0:T(8,128)(2,1)} async-done(((bf16[4,192,256]{2,1,0:T(8,128)(2,1)}), bf16[4,192,256]{2,1,0:T(8,128)(2,1)}, u32[]{:S(2)}, u32[]{:S(2)}) %all-to-all-start) | async-done | bytes 393248 | tf_op jit(solution)/shard_map/all_to_all | solution.py:503
  82.0 1.1 reduce_sum.12
  84.3 1.6 %collective-permute-start.20 = (bf16[1,2,4,128,128]{4,3,2,1,0:T(8,128)(2,1)S(1)}, bf16[1,2,4,128,128]{4,3,2,1,0:T(8,128)(2,1)S(1)}, u32[]{:S(2)}, u32[]{:S(2)}) collective-permute-start(bf16[1,2,4,128,128]{4,3,2,1,0:T(8,128)(2,1)S(1)} %add_convert_fusion.2), channel_id=1, source_target_pairs={{0,2},{1,3},{2,0},{3,1},{4,6},{5,7},{6,4},{7,5},{8,10},{9,11},{10,... | collective-permute-start | bytes 786440 | tf_op jit(solution)/shard_map/ppermute | solution.py:38
  87.7 4.6 %all-to-all-start.1 = ((bf16[4,192,256]{2,1,0:T(8,128)(2,1)}), bf16[4,192,256]{2,1,0:T(8,128)(2,1)S(1)}, u32[]{:S(2)}, u32[]{:S(2)}) async-start(bf16[4,192,256]{2,1,0:T(8,128)(2,1)} %broadcast_in_dim.7), calls=%async_computation.1 | async-start | bytes 786432 | tf_op jit(solution)/shard_map/all_to_all | solution.py:508
  93.1 1.1 fusion
  94.2 2.1 %collective-permute-start.21 = (bf16[2,4,128,128]{3,2,1,0:T(8,128)(2,1)S(1)}, bf16[2,4,128,128]{3,2,1,0:T(8,128)(2,1)S(1)}, u32[]{:S(2)}, u32[]{:S(2)}) collective-permute-start(bf16[2,4,128,128]{3,2,1,0:T(8,128)(2,1)S(1)} %fusion), channel_id=1, source_target_pairs={{0,4},{4,8},{8,12},{12,0},{1,5},{5,9},{9,13},{13,1},{2,6},{6,10},{... | collective-permute-start | bytes 786440 | tf_op jit(solution)/shard_map/ppermute | solution.py:33
  96.2 4.7 %collective-permute-done.17 = bf16[1,2,4,128,128]{4,3,2,1,0:T(8,128)(2,1)S(1)} collective-permute-done((bf16[1,2,4,128,128]{4,3,2,1,0:T(8,128)(2,1)S(1)}, bf16[1,2,4,128,128]{4,3,2,1,0:T(8,128)(2,1)S(1)}, u32[]{:S(2)}, u32[]{:S(2)}) %collective-permute-start.17) | collective-permute-done | bytes 262176 | tf_op jit(solution)/shard_map/ppermute | solution.py:38
  101.1 6.0 %collective-permute-done.21.second = bf16[2,4,128,128]{3,2,1,0:T(8,128)(2,1)S(1)} collective-permute-done((bf16[2,4,128,128]{3,2,1,0:T(8,128)(2,1)S(1)}, bf16[2,4,128,128]{3,2,1,0:T(8,128)(2,1)S(1)}, u32[]{:S(2)}, u32[]{:S(2)}) %collective-permute-start.21) | collective-permute-done | bytes 262176 | tf_op jit(solution)/shard_map/ppermute | solution.py:33
  (59 shorter events, 14.2 us)
Async XLA Ops:
  1.7 10.7 %collective-permute-start = (bf16[2,128,512]{2,1,0:T(8,128)(2,1)S(1)}, bf16[2,128,512]{2,1,0:T(8,128)(2,1)S(1)}, u32[]{:S(2)}, u32[]{:S(2)}) collective-permute-start(bf16[2,128,512]{2,1,0:T(8,128)(2,1)S(1)} %dynamic-slice_bitcast_fusion), channel_id=1, source_target_pairs={{0,12},{4,0},{8,4},{12,8},{1,13},{5,1},{9,5},{13,9},{2,14},{6,2},{... | collective-permute-start | bytes 786440 | tf_op jit(solution)/shard_map/ppermute | solution.py:33
  12.3 9.0 %collective-permute-start.1 = (bf16[2,128,512]{2,1,0:T(8,128)(2,1)S(1)}, bf16[2,128,512]{2,1,0:T(8,128)(2,1)S(1)}, u32[]{:S(2)}, u32[]{:S(2)}) collective-permute-start(bf16[2,128,512]{2,1,0:T(8,128)(2,1)S(1)} %collective-permute-done.refs_1_), channel_id=1, source_target_pairs={{0,12},{4,0},{8,4},{12,8},{1,13},{5,1},{9,5},{13,9},{2,14},{6,2},{... | collective-permute-start | bytes 786440 | tf_op jit(solution)/shard_map/ppermute | solution.py:33
  16.6 8.2 %collective-permute-start.2 = (bf16[2,128,512]{2,1,0:T(8,128)(2,1)S(1)}, bf16[2,128,512]{2,1,0:T(8,128)(2,1)S(1)}, u32[]{:S(2)}, u32[]{:S(2)}) collective-permute-start(bf16[2,128,512]{2,1,0:T(8,128)(2,1)S(1)} %collective-permute-done.refs_1_), channel_id=1, source_target_pairs={{0,2},{1,3},{2,0},{3,1},{4,6},{5,7},{6,4},{7,5},{8,10},{9,11},{10,... | collective-permute-start | bytes 786440 | tf_op jit(solution)/shard_map/ppermute | solution.py:38
  21.3 7.8 %collective-permute-start.5 = (bf16[2,128,512]{2,1,0:T(8,128)(2,1)S(1)}, bf16[2,128,512]{2,1,0:T(8,128)(2,1)S(1)}, u32[]{:S(2)}, u32[]{:S(2)}) collective-permute-start(bf16[2,128,512]{2,1,0:T(8,128)(2,1)S(1)} %collective-permute-done.1.refs_5_), channel_id=1, source_target_pairs={{0,2},{1,3},{2,0},{3,1},{4,6},{5,7},{6,4},{7,5},{8,10},{9,11},{10,... | collective-permute-start | bytes 786440 | tf_op jit(solution)/shard_map/ppermute | solution.py:38
  22.8 7.0 %collective-permute-start.3 = (bf16[2,128,512]{2,1,0:T(8,128)(2,1)S(1)}, bf16[2,128,512]{2,1,0:T(8,128)(2,1)S(1)}, u32[]{:S(2)}, u32[]{:S(2)}) collective-permute-start(bf16[2,128,512]{2,1,0:T(8,128)(2,1)S(1)} %collective-permute-done.refs_1_), channel_id=1, source_target_pairs={{0,1},{1,0},{2,3},{3,2},{4,5},{5,4},{6,7},{7,6},{8,9},{9,8},{10,11... | collective-permute-start | bytes 786440 | tf_op jit(solution)/shard_map/ppermute | solution.py:38
  22.8 7.0 %collective-permute-start.6 = (bf16[2,128,512]{2,1,0:T(8,128)(2,1)S(1)}, bf16[2,128,512]{2,1,0:T(8,128)(2,1)S(1)}, u32[]{:S(2)}, u32[]{:S(2)}) collective-permute-start(bf16[2,128,512]{2,1,0:T(8,128)(2,1)S(1)} %collective-permute-done.1.refs_5_), channel_id=1, source_target_pairs={{0,1},{1,0},{2,3},{3,2},{4,5},{5,4},{6,7},{7,6},{8,9},{9,8},{10,11... | collective-permute-start | bytes 786440 | tf_op jit(solution)/shard_map/ppermute | solution.py:38
  24.8 5.0 %collective-permute-start.4 = (bf16[2,128,512]{2,1,0:T(8,128)(2,1)S(1)}, bf16[2,128,512]{2,1,0:T(8,128)(2,1)S(1)}, u32[]{:S(2)}, u32[]{:S(2)}) collective-permute-start(bf16[2,128,512]{2,1,0:T(8,128)(2,1)S(1)} %collective-permute-done.2.refs_2_), channel_id=1, source_target_pairs={{0,1},{1,0},{2,3},{3,2},{4,5},{5,4},{6,7},{7,6},{8,9},{9,8},{10,11... | collective-permute-start | bytes 786440 | tf_op jit(solution)/shard_map/ppermute | solution.py:38
  29.1 1.5 %collective-permute-start.7 = (bf16[2,128,512]{2,1,0:T(8,128)(2,1)S(1)}, bf16[2,128,512]{2,1,0:T(8,128)(2,1)S(1)}, u32[]{:S(2)}, u32[]{:S(2)}) collective-permute-start(bf16[2,128,512]{2,1,0:T(8,128)(2,1)S(1)} %collective-permute-done.5.refs_6_), channel_id=1, source_target_pairs={{0,1},{1,0},{2,3},{3,2},{4,5},{5,4},{6,7},{7,6},{8,9},{9,8},{10,11... | collective-permute-start | bytes 786440 | tf_op jit(solution)/shard_map/ppermute | solution.py:38
  51.5 1.8 %collective-permute-start.8 = (bf16[1,12,64,256]{3,2,1,0:T(8,128)(2,1)S(1)}, bf16[1,12,64,256]{3,2,1,0:T(8,128)(2,1)S(1)}, u32[]{:S(2)}, u32[]{:S(2)}) collective-permute-start(bf16[1,12,64,256]{3,2,1,0:T(8,128)(2,1)S(1)} %get-tuple-element.64), channel_id=1, source_target_pairs={{0,1},{1,0},{2,3},{3,2},{4,5},{5,4},{6,7},{7,6},{8,9},{9,8},{10,11... | collective-permute-start | bytes 1179656 | tf_op jit(solution)/shard_map/ppermute | solution.py:38
  53.4 11.2 %collective-permute-start.14 = (bf16[1,12,64,256]{3,2,1,0:T(8,128)(2,1)S(1)}, bf16[1,12,64,256]{3,2,1,0:T(8,128)(2,1)S(1)}, u32[]{:S(2)}, u32[]{:S(2)}) collective-permute-start(bf16[1,12,64,256]{3,2,1,0:T(8,128)(2,1)S(1)} %add_convert_fusion), channel_id=1, source_target_pairs={{0,2},{1,3},{2,0},{3,1},{4,6},{5,7},{6,4},{7,5},{8,10},{9,11},{10,... | collective-permute-start | bytes 1179656 | tf_op jit(solution)/shard_map/ppermute | solution.py:38
  59.5 1.6 %collective-permute-start.13 = (bf16[1,2,4,128,128]{4,3,2,1,0:T(8,128)(2,1)S(1)}, bf16[1,2,4,128,128]{4,3,2,1,0:T(8,128)(2,1)S(1)}, u32[]{:S(2)}, u32[]{:S(2)}) collective-permute-start(bf16[1,2,4,128,128]{4,3,2,1,0:T(8,128)(2,1)S(1)} %get-tuple-element.75), channel_id=1, source_target_pairs={{0,1},{1,0},{2,3},{3,2},{4,5},{5,4},{6,7},{7,6},{8,9},{9,8},{10,11... | collective-permute-start | bytes 786440 | tf_op jit(solution)/shard_map/ppermute | solution.py:38
  59.5 5.9 %collective-permute-start.16 = (bf16[1,12,64,256]{3,2,1,0:T(8,128)(2,1)S(1)}, bf16[1,12,64,256]{3,2,1,0:T(8,128)(2,1)S(1)}, u32[]{:S(2)}, u32[]{:S(2)}) collective-permute-start(bf16[1,12,64,256]{3,2,1,0:T(8,128)(2,1)S(1)} %get-tuple-element.78), channel_id=1, source_target_pairs={{0,1},{1,0},{2,3},{3,2},{4,5},{5,4},{6,7},{7,6},{8,9},{9,8},{10,11... | collective-permute-start | bytes 1179656 | tf_op jit(solution)/shard_map/ppermute | solution.py:38
  66.4 15.6 %all-to-all-start = ((bf16[4,192,256]{2,1,0:T(8,128)(2,1)}), bf16[4,192,256]{2,1,0:T(8,128)(2,1)}, u32[]{:S(2)}, u32[]{:S(2)}) async-start(bf16[4,192,256]{2,1,0:T(8,128)(2,1)} %bitcast.26), calls=%async_computation | async-start | bytes 786432 | tf_op jit(solution)/shard_map/all_to_all | solution.py:503
  70.5 2.2 %collective-permute-start.12 = (bf16[1,2,4,128,128]{4,3,2,1,0:T(8,128)(2,1)}, bf16[1,2,4,128,128]{4,3,2,1,0:T(8,128)(2,1)S(1)}, u32[]{:S(2)}, u32[]{:S(2)}) collective-permute-start(bf16[1,2,4,128,128]{4,3,2,1,0:T(8,128)(2,1)} %copy-done.8), channel_id=1, source_target_pairs={{0,1},{1,0},{2,3},{3,2},{4,5},{5,4},{6,7},{7,6},{8,9},{9,8},{10,11... | collective-permute-start | bytes 786440 | tf_op jit(solution)/shard_map/ppermute | solution.py:38
  70.6 8.9 %collective-permute-start.15 = (bf16[1,2,4,128,128]{4,3,2,1,0:T(8,128)(2,1)}, bf16[1,2,4,128,128]{4,3,2,1,0:T(8,128)(2,1)S(1)}, u32[]{:S(2)}, u32[]{:S(2)}) collective-permute-start(bf16[1,2,4,128,128]{4,3,2,1,0:T(8,128)(2,1)} %add_convert_fusion.4), channel_id=1, source_target_pairs={{0,2},{1,3},{2,0},{3,1},{4,6},{5,7},{6,4},{7,5},{8,10},{9,11},{10,... | collective-permute-start | bytes 786440 | tf_op jit(solution)/shard_map/ppermute | solution.py:38
  71.9 11.4 %collective-permute-start.11 = (bf16[1,2,4,128,128]{4,3,2,1,0:T(8,128)(2,1)}, bf16[1,2,4,128,128]{4,3,2,1,0:T(8,128)(2,1)}, u32[]{:S(2)}, u32[]{:S(2)}) collective-permute-start(bf16[1,2,4,128,128]{4,3,2,1,0:T(8,128)(2,1)} %copy-done.7), channel_id=1, source_target_pairs={{0,1},{1,0},{2,3},{3,2},{4,5},{5,4},{6,7},{7,6},{8,9},{9,8},{10,11... | collective-permute-start | bytes 786440 | tf_op jit(solution)/shard_map/ppermute | solution.py:38
  72.2 13.7 %collective-permute-start.10 = (bf16[1,2,4,128,128]{4,3,2,1,0:T(8,128)(2,1)S(1)}, bf16[1,2,4,128,128]{4,3,2,1,0:T(8,128)(2,1)}, u32[]{:S(2)}, u32[]{:S(2)}) collective-permute-start(bf16[1,2,4,128,128]{4,3,2,1,0:T(8,128)(2,1)S(1)} %get-tuple-element.69), channel_id=1, source_target_pairs={{0,1},{1,0},{2,3},{3,2},{4,5},{5,4},{6,7},{7,6},{8,9},{9,8},{10,11... | collective-permute-start | bytes 786440 | tf_op jit(solution)/shard_map/ppermute | solution.py:38
  72.5 20.6 %collective-permute-start.19 = (bf16[1,2,4,128,128]{4,3,2,1,0:T(8,128)(2,1)S(1)}, bf16[1,2,4,128,128]{4,3,2,1,0:T(8,128)(2,1)}, u32[]{:S(2)}, u32[]{:S(2)}) collective-permute-start(bf16[1,2,4,128,128]{4,3,2,1,0:T(8,128)(2,1)S(1)} %get-tuple-element.84), channel_id=1, source_target_pairs={{0,1},{1,0},{2,3},{3,2},{4,5},{5,4},{6,7},{7,6},{8,9},{9,8},{10,11... | collective-permute-start | bytes 786440 | tf_op jit(solution)/shard_map/ppermute | solution.py:38
  83.0 10.0 %collective-permute-start.18 = (bf16[2,4,128,128]{3,2,1,0:T(8,128)(2,1)}, bf16[2,4,128,128]{3,2,1,0:T(8,128)(2,1)S(1)}, u32[]{:S(2)}, u32[]{:S(2)}) collective-permute-start(bf16[2,4,128,128]{3,2,1,0:T(8,128)(2,1)} %fusion.1), channel_id=1, source_target_pairs={{0,4},{4,8},{8,12},{12,0},{1,5},{5,9},{9,13},{13,1},{2,6},{6,10},{... | collective-permute-start | bytes 786440 | tf_op jit(solution)/shard_map/ppermute | solution.py:33
  84.3 8.7 %collective-permute-start.20 = (bf16[1,2,4,128,128]{4,3,2,1,0:T(8,128)(2,1)S(1)}, bf16[1,2,4,128,128]{4,3,2,1,0:T(8,128)(2,1)S(1)}, u32[]{:S(2)}, u32[]{:S(2)}) collective-permute-start(bf16[1,2,4,128,128]{4,3,2,1,0:T(8,128)(2,1)S(1)} %add_convert_fusion.2), channel_id=1, source_target_pairs={{0,2},{1,3},{2,0},{3,1},{4,6},{5,7},{6,4},{7,5},{8,10},{9,11},{10,... | collective-permute-start | bytes 786440 | tf_op jit(solution)/shard_map/ppermute | solution.py:38
  87.7 20.4 %all-to-all-start.1 = ((bf16[4,192,256]{2,1,0:T(8,128)(2,1)}), bf16[4,192,256]{2,1,0:T(8,128)(2,1)S(1)}, u32[]{:S(2)}, u32[]{:S(2)}) async-start(bf16[4,192,256]{2,1,0:T(8,128)(2,1)} %broadcast_in_dim.7), calls=%async_computation.1 | async-start | bytes 786432 | tf_op jit(solution)/shard_map/all_to_all | solution.py:508
  92.3 4.0 %collective-permute-start.9 = (bf16[1,2,4,128,128]{4,3,2,1,0:T(8,128)(2,1)S(1)}, bf16[1,2,4,128,128]{4,3,2,1,0:T(8,128)(2,1)S(1)}, u32[]{:S(2)}, u32[]{:S(2)}) collective-permute-start(bf16[1,2,4,128,128]{4,3,2,1,0:T(8,128)(2,1)S(1)} %get-tuple-element.67), channel_id=1, source_target_pairs={{0,1},{1,0},{2,3},{3,2},{4,5},{5,4},{6,7},{7,6},{8,9},{9,8},{10,11... | collective-permute-start | bytes 786440 | tf_op jit(solution)/shard_map/ppermute | solution.py:38
  92.3 8.7 %collective-permute-start.17 = (bf16[1,2,4,128,128]{4,3,2,1,0:T(8,128)(2,1)S(1)}, bf16[1,2,4,128,128]{4,3,2,1,0:T(8,128)(2,1)S(1)}, u32[]{:S(2)}, u32[]{:S(2)}) collective-permute-start(bf16[1,2,4,128,128]{4,3,2,1,0:T(8,128)(2,1)S(1)} %add_convert_fusion.1), channel_id=1, source_target_pairs={{0,2},{1,3},{2,0},{3,1},{4,6},{5,7},{6,4},{7,5},{8,10},{9,11},{10,... | collective-permute-start | bytes 786440 | tf_op jit(solution)/shard_map/ppermute | solution.py:38
  94.2 12.9 %collective-permute-start.21 = (bf16[2,4,128,128]{3,2,1,0:T(8,128)(2,1)S(1)}, bf16[2,4,128,128]{3,2,1,0:T(8,128)(2,1)S(1)}, u32[]{:S(2)}, u32[]{:S(2)}) collective-permute-start(bf16[2,4,128,128]{3,2,1,0:T(8,128)(2,1)S(1)} %fusion), channel_id=1, source_target_pairs={{0,4},{4,8},{8,12},{12,0},{1,5},{5,9},{9,13},{13,1},{2,6},{6,10},{... | collective-permute-start | bytes 786440 | tf_op jit(solution)/shard_map/ppermute | solution.py:33
  (9 other events, 116.3 us)

commit v9 on v8

--- a/solution.py
+++ b/solution.py
@@ -498,16 +498,28 @@
         bit *= 2
 
 
-def sum_over(axis, value):
-    peers = lax.axis_size(axis)
-    shares = lax.all_to_all(value.astype(jnp.bfloat16), axis, 0, 0)
-    total = jnp.sum(shares.astype(jnp.float32), 0).astype(jnp.bfloat16)
-
-    def gather(*others):
-        copies = jnp.broadcast_to(after(total, *others), (peers,) + total.shape)
-        return lax.all_to_all(copies, axis, 0, 0).astype(jnp.float32)
-
-    return total, gather
+def add_up_kernel(shares, out):
+    total = shares[0].astype(jnp.float32)
+    for i in range(1, shares.shape[0]):
+        total += shares[i].astype(jnp.float32)
+    total = total.astype(jnp.bfloat16)
+    for i in range(out.shape[0]):
+        out[i] = total
+
+
+def widen_kernel(array, out):
+    out[...] = array[...].astype(jnp.float32)
+
+
+def small_call(kernel, array, kind, name):
+    return pl.pallas_call(
+        kernel,
+        in_specs=[pl.BlockSpec(memory_space=VMEM)],
+        out_specs=pl.BlockSpec(memory_space=VMEM),
+        out_shape=jax.ShapeDtypeStruct(array.shape, kind),
+        compiler_params=pltpu.CompilerParams(vmem_limit_bytes=8 * 1024 * 1024),
+        name=name,
+    )(array)
 
 
 def finish_kernel(first, second, out):
@@ -569,15 +581,21 @@
     send, keep = ([out[at + 2 * i:at + 2 * i + 2] for i in range(REACH)] for at in (0, 2 * REACH))
     last = REACH - 1
     mine, leaving, _ = halve(keep[last], send[last], before_cross=(crossed,))
-    total, gather = sum_over("blk", after(eigen, leaving).reshape(blocks, -1, frame))
-    moving = after(mine.astype(jnp.bfloat16), total)
+    scattered = after(eigen, leaving).reshape(blocks, -1, frame).astype(jnp.bfloat16)
+    scattered = lax.all_to_all(scattered, "blk", 0, 0)
+    moving = mine.astype(jnp.bfloat16)
     gate = moving
     for section in range(last - 1, -1, -1):
-        mine, gate, _ = halve(keep[section], send[section], before_cross=(gate,))
+        mine, _, gate = halve(keep[section], send[section], before_cross=(gate,))
+        if section == last - 1:
+            scattered = after(scattered, gate)
         arrived = shift(moving, "blk", 1)
         if section > 0:
             moving = (arrived.astype(jnp.float32) + mine).astype(jnp.bfloat16)
-    eigen_share = gather(gate).reshape(modes, 2, frame // shares, frame)
+    copies = small_call(add_up_kernel, scattered, jnp.bfloat16, "add_up")
+    gathered = lax.all_to_all(copies, "blk", 0, 0)
+    eigen_share = small_call(widen_kernel, gathered, jnp.float32, "widen")
+    eigen_share = eigen_share.reshape(modes, 2, frame // shares, frame)
     summed = finish(mine, arrived)
     return (summed[None], eigen_share, coef_rows.T)
 

time: 110 us -> 106 us (0.964)
  waiting for transfers between devices: 38 us -> 28.5 us
  starting transfers between devices: 29.2 us -> 34.7 us
  Pallas kernels: 28 us -> 30.3 us
    ppermute x18, starting transfers between devices: 8.76 us -> 15.6 us  [swap(): return lax.ppermute(array, axis, [(i, i ^ bit) for i in range(peers)])]
    ppermute x18, waiting for transfers between devices: 24.3 us -> 17.8 us  [swap(): return lax.ppermute(array, axis, [(i, i ^ bit) for i in range(peers)])]
    all_to_all x2, waiting for transfers between devices: 1.86 us -> 0.01 us  [the longest x1 0.01 us: on_device(): gathered = lax.all_to_all(copies, 'blk', 0, 0)]
    pallas_call x0 -> x2, Pallas kernels: none -> 1.73 us  [small_call(): pl.pallas_call(kernel, in_specs=[pl.BlockSpec(memory_space=VMEM)], out_sp...]
    unnamed x18 -> x14, local copies, waits for them, and re-layouts: 2.76 us -> 2.75 us
  transfers between devices with their start and end apart: 24 -> 24, of which waited for: 13 -> 12; matrix products, arithmetic and copies ran while one was open for 6% -> 6% of each run, Pallas kernels for 7% -> 8%
where the time goes in v9:
time: 106 us
  starting transfers between devices  34.7 us (33%)
  Pallas kernels  30.3 us (29%)
  waiting for transfers between devices  28.5 us (27%)
  other arithmetic  6.92 us (7%)
  local copies, waits for them, and re-layouts  3.73 us (4%)
  between operations  1.48 us (1%)
    pallas_call x1, Pallas kernels, positions(): pl.pallas_call(functools.partial(position_kernel, offs, scale), in_specs=...  20.9 us
    ppermute x18, waiting for transfers between devices, swap(): return lax.ppermute(array, axis, [(i, i ^ bit) for i in range(peers)])  17.8 us
    ppermute x18, starting transfers between devices, swap(): return lax.ppermute(array, axis, [(i, i ^ bit) for i in range(peers)])  15.6 us
    ppermute x4, starting transfers between devices, shift(): lax.ppermute(array, axis, [(i, (i + by) % peers) for i in range(peers)])  11.4 us
    ppermute x4, waiting for transfers between devices, shift(): lax.ppermute(array, axis, [(i, (i + by) % peers) for i in range(peers)])  10.8 us
    pallas_call x1, Pallas kernels, scatter(): pl.pallas_call(functools.partial(scatter_kernel, shares), in_specs=[pl.Bl...  6.39 us
    all_to_all x1, starting transfers between devices, on_device(): gathered = lax.all_to_all(copies, 'blk', 0, 0)  4.24 us
    all_to_all x1, starting transfers between devices, on_device(): scattered = lax.all_to_all(scattered, 'blk', 0, 0)  3.46 us
  transfers between devices with their start and end apart: 24, of which 12 were waited for; matrix products, arithmetic and copies ran while one was open for 6% of the time, Pallas kernels for 8%

profile of v9, /device:TPU:0, one launch (start us, length us, event | category | flops | bytes accessed | tf_op | source)
XLA Modules:
  0.0 105.6 jit_solution(10351112246086923592)
XLA Ops:
  1.7 5.1 %collective-permute-start = (bf16[2,128,512]{2,1,0:T(8,128)(2,1)S(1)}, bf16[2,128,512]{2,1,0:T(8,128)(2,1)S(1)}, u32[]{:S(2)}, u32[]{:S(2)}) collective-permute-start(bf16[2,128,512]{2,1,0:T(8,128)(2,1)S(1)} %dynamic-slice_bitcast_fusion), channel_id=1, source_target_pairs={{0,12},{4,0},{8,4},{12,8},{1,13},{5,1},{9,5},{13,9},{2,14},{6,2},{... | collective-permute-start | bytes 786440 | tf_op jit(solution)/shard_map/ppermute | solution.py:33
  6.8 5.6 %collective-permute-done.refs_1_ = bf16[2,128,512]{2,1,0:T(8,128)(2,1)S(1)} collective-permute-done((bf16[2,128,512]{2,1,0:T(8,128)(2,1)S(1)}, bf16[2,128,512]{2,1,0:T(8,128)(2,1)S(1)}, u32[]{:S(2)}, u32[]{:S(2)}) %collective-permute-start) | collective-permute-done | bytes 262176 | tf_op jit(solution)/shard_map/ppermute | solution.py:33
  12.3 4.3 %collective-permute-start.1 = (bf16[2,128,512]{2,1,0:T(8,128)(2,1)S(1)}, bf16[2,128,512]{2,1,0:T(8,128)(2,1)S(1)}, u32[]{:S(2)}, u32[]{:S(2)}) collective-permute-start(bf16[2,128,512]{2,1,0:T(8,128)(2,1)S(1)} %collective-permute-done.refs_1_), channel_id=1, source_target_pairs={{0,12},{4,0},{8,4},{12,8},{1,13},{5,1},{9,5},{13,9},{2,14},{6,2},{... | collective-permute-start | bytes 786440 | tf_op jit(solution)/shard_map/ppermute | solution.py:33
  16.6 1.5 %collective-permute-start.2 = (bf16[2,128,512]{2,1,0:T(8,128)(2,1)S(1)}, bf16[2,128,512]{2,1,0:T(8,128)(2,1)S(1)}, u32[]{:S(2)}, u32[]{:S(2)}) collective-permute-start(bf16[2,128,512]{2,1,0:T(8,128)(2,1)S(1)} %collective-permute-done.refs_1_), channel_id=1, source_target_pairs={{0,2},{1,3},{2,0},{3,1},{4,6},{5,7},{6,4},{7,5},{8,10},{9,11},{10,... | collective-permute-start | bytes 786440 | tf_op jit(solution)/shard_map/ppermute | solution.py:38
  18.1 1.4 %copy-done.1 = bf16[6,2,256,256]{3,2,1,0:T(8,128)(2,1)S(1)} copy-done((bf16[6,2,256,256]{3,2,1,0:T(8,128)(2,1)S(1)}, bf16[6,2,256,256]{3,2,1,0:T(8,128)(2,1)}, u32[]{:S(2)}) %copy-start.1) | copy-done | bytes 1572888
  19.5 1.3 %copy-done.2 = bf16[10,256,256]{2,1,0:T(8,128)(2,1)S(1)} copy-done((bf16[10,256,256]{2,1,0:T(8,128)(2,1)S(1)}, bf16[10,256,256]{2,1,0:T(8,128)(2,1)}, u32[]{:S(2)}) %copy-start.2) | copy-done | bytes 1310744
  21.3 1.5 %collective-permute-start.5 = (bf16[2,128,512]{2,1,0:T(8,128)(2,1)S(1)}, bf16[2,128,512]{2,1,0:T(8,128)(2,1)S(1)}, u32[]{:S(2)}, u32[]{:S(2)}) collective-permute-start(bf16[2,128,512]{2,1,0:T(8,128)(2,1)S(1)} %collective-permute-done.1.refs_5_), channel_id=1, source_target_pairs={{0,2},{1,3},{2,0},{3,1},{4,6},{5,7},{6,4},{7,5},{8,10},{9,11},{10,... | collective-permute-start | bytes 786440 | tf_op jit(solution)/shard_map/ppermute | solution.py:38
  23.3 1.5 %collective-permute-done.2.refs_2_ = bf16[2,128,512]{2,1,0:T(8,128)(2,1)S(1)} collective-permute-done((bf16[2,128,512]{2,1,0:T(8,128)(2,1)S(1)}, bf16[2,128,512]{2,1,0:T(8,128)(2,1)S(1)}, u32[]{:S(2)}, u32[]{:S(2)}) %collective-permute-start.2) | collective-permute-done | bytes 262176 | tf_op jit(solution)/shard_map/ppermute | solution.py:38
  25.1 4.1 %collective-permute-done.5.refs_6_ = bf16[2,128,512]{2,1,0:T(8,128)(2,1)S(1)} collective-permute-done((bf16[2,128,512]{2,1,0:T(8,128)(2,1)S(1)}, bf16[2,128,512]{2,1,0:T(8,128)(2,1)S(1)}, u32[]{:S(2)}, u32[]{:S(2)}) %collective-permute-start.5) | collective-permute-done | bytes 262176 | tf_op jit(solution)/shard_map/ppermute | solution.py:38
  30.7 20.9 %positions.1 = (bf16[1,12,64,256]{3,2,1,0:T(8,128)(2,1)S(1)}, bf16[1,12,64,256]{3,2,1,0:T(8,128)(2,1)S(1)}, f32[1,12,64,256]{3,2,1,0:T(8,128)S(1)}, f32[1,12,64,...) custom-call(s32[2,10]{1,0:T(2,128)S(1)} %get-tuple-element.53.tile_list, ...), custom_call_target="tpu_custom_call" | custom-call | tf_op jit(solution)/shard_map/positions/pallas_call | solution.py:337
  51.7 1.6 %collective-permute-done.8 = bf16[1,12,64,256]{3,2,1,0:T(8,128)(2,1)S(1)} collective-permute-done((bf16[1,12,64,256]{3,2,1,0:T(8,128)(2,1)S(1)}, bf16[1,12,64,256]{3,2,1,0:T(8,128)(2,1)S(1)}, u32[]{:S(2)}, u32[]{:S(2)}) %collective-permute-start.8) | collective-permute-done | bytes 393248 | tf_op jit(solution)/shard_map/ppermute | solution.py:38
  53.4 1.5 %collective-permute-start.14 = (bf16[1,12,64,256]{3,2,1,0:T(8,128)(2,1)S(1)}, bf16[1,12,64,256]{3,2,1,0:T(8,128)(2,1)S(1)}, u32[]{:S(2)}, u32[]{:S(2)}) collective-permute-start(bf16[1,12,64,256]{3,2,1,0:T(8,128)(2,1)S(1)} %add_convert_fusion), channel_id=1, source_target_pairs={{0,2},{1,3},{2,0},{3,1},{4,6},{5,7},{6,4},{7,5},{8,10},{9,11},{10,... | collective-permute-start | bytes 1179656 | tf_op jit(solution)/shard_map/ppermute | solution.py:38
  55.0 6.4 %scatter.1 = (bf16[1,2,4,128,128]{4,3,2,1,0:T(8,128)(2,1)S(1)}, bf16[1,2,4,128,128]{4,3,2,1,0:T(8,128)(2,1)}, bf16[1,2,4,128,128]{4,3,2,1,0:T(8,128)(2,1)S(1)}, ...) custom-call(s32[2,10]{1,0:T(2,128)S(1)} %get-tuple-element.53.tile_l, ...), custom_call_target="tpu_custom_call" | custom-call | flops 16777216 | bytes 16777216 | tf_op jit(solution)/shard_map/scatter/pallas_call | solution.py:458
  63.1 1.5 %collective-permute-done.14 = bf16[1,12,64,256]{3,2,1,0:T(8,128)(2,1)S(1)} collective-permute-done((bf16[1,12,64,256]{3,2,1,0:T(8,128)(2,1)S(1)}, bf16[1,12,64,256]{3,2,1,0:T(8,128)(2,1)S(1)}, u32[]{:S(2)}, u32[]{:S(2)}) %collective-permute-start.14) | collective-permute-done | bytes 393248 | tf_op jit(solution)/shard_map/ppermute | solution.py:38
  65.4 1.5 %collective-permute-start.15 = (bf16[1,2,4,128,128]{4,3,2,1,0:T(8,128)(2,1)}, bf16[1,2,4,128,128]{4,3,2,1,0:T(8,128)(2,1)}, u32[]{:S(2)}, u32[]{:S(2)}) collective-permute-start(bf16[1,2,4,128,128]{4,3,2,1,0:T(8,128)(2,1)} %add_convert_fusion.4), channel_id=1, source_target_pairs={{0,2},{1,3},{2,0},{3,1},{4,6},{5,7},{6,4},{7,5},{8,10},{9,11},{10,... | collective-permute-start | bytes 786440 | tf_op jit(solution)/shard_map/ppermute | solution.py:38
  67.9 3.5 %all-to-all-start = ((bf16[4,192,256]{2,1,0:T(8,128)(2,1)}), bf16[4,192,256]{2,1,0:T(8,128)(2,1)S(1)}, u32[]{:S(2)}, u32[]{:S(2)}) async-start(bf16[4,192,256]{2,1,0:T(8,128)(2,1)} %bitcast.24), calls=%async_computation | async-start | bytes 786432 | tf_op jit(solution)/shard_map/all_to_all | solution.py:585
  71.4 1.9 %collective-permute-done.15 = bf16[1,2,4,128,128]{4,3,2,1,0:T(8,128)(2,1)} collective-permute-done((bf16[1,2,4,128,128]{4,3,2,1,0:T(8,128)(2,1)}, bf16[1,2,4,128,128]{4,3,2,1,0:T(8,128)(2,1)}, u32[]{:S(2)}, u32[]{:S(2)}) %collective-permute-start.15) | collective-permute-done | bytes 262176 | tf_op jit(solution)/shard_map/ppermute | solution.py:38
  73.3 1.8 %fusion.1 = bf16[2,4,128,128]{3,2,1,0:T(8,128)(2,1)} fusion(bf16[1,2,4,128,128]{4,3,2,1,0:T(8,128)(2,1)} %collective-permute-done.15, f32[1,2,4,128,128]{4,3,2,1,0:T(8,128)S(1)} %get-tuple-element.71, bf16[1,2,4,128,128]{4,3,2,1,0:T(8,128)(2,1)} %collective-permute-done.12), kind=kLoop, calls=%fused_computation.9 | loop fusion | flops 655360 | bytes 1310720 | tf_op jit(solution)/shard_map/convert_element_type | solution.py:586
  76.1 1.5 %collective-permute-start.16 = (bf16[1,2,4,128,128]{4,3,2,1,0:T(8,128)(2,1)S(1)}, bf16[1,2,4,128,128]{4,3,2,1,0:T(8,128)(2,1)S(1)}, u32[]{:S(2)}, u32[]{:S(2)}) collective-permute-start(bf16[1,2,4,128,128]{4,3,2,1,0:T(8,128)(2,1)S(1)} %add_convert_fusion.2), channel_id=1, source_target_pairs={{0,2},{1,3},{2,0},{3,1},{4,6},{5,7},{6,4},{7,5},{8,10},{9,11},{10,... | collective-permute-start | bytes 786440 | tf_op jit(solution)/shard_map/ppermute | solution.py:38
  78.2 4.6 %collective-permute-done.16 = bf16[1,2,4,128,128]{4,3,2,1,0:T(8,128)(2,1)S(1)} collective-permute-done((bf16[1,2,4,128,128]{4,3,2,1,0:T(8,128)(2,1)S(1)}, bf16[1,2,4,128,128]{4,3,2,1,0:T(8,128)(2,1)S(1)}, u32[]{:S(2)}, u32[]{:S(2)}) %collective-permute-start.16) | collective-permute-done | bytes 262176 | tf_op jit(solution)/shard_map/ppermute | solution.py:38
  83.6 4.2 %all-to-all-start.1 = ((bf16[4,192,256]{2,1,0:T(8,128)(2,1)}), bf16[4,192,256]{2,1,0:T(8,128)(2,1)S(1)}, u32[]{:S(2)}, u32[]{:S(2)}) async-start(bf16[4,192,256]{2,1,0:T(8,128)(2,1)} %add_up.1), calls=%async_computation.1 | async-start | bytes 786432 | tf_op jit(solution)/shard_map/all_to_all | solution.py:596
  88.9 5.6 %collective-permute-start.17 = (bf16[1,2,4,128,128]{4,3,2,1,0:T(8,128)(2,1)S(1)}, bf16[1,2,4,128,128]{4,3,2,1,0:T(8,128)(2,1)S(1)}, u32[]{:S(2)}, u32[]{:S(2)}) collective-permute-start(bf16[1,2,4,128,128]{4,3,2,1,0:T(8,128)(2,1)S(1)} %add_convert_fusion.1), channel_id=1, source_target_pairs={{0,2},{1,3},{2,0},{3,1},{4,6},{5,7},{6,4},{7,5},{8,10},{9,11},{10,... | collective-permute-start | bytes 786440 | tf_op jit(solution)/shard_map/ppermute | solution.py:38
  95.6 2.0 %collective-permute-start.20 = (bf16[2,4,128,128]{3,2,1,0:T(8,128)(2,1)S(1)}, bf16[2,4,128,128]{3,2,1,0:T(8,128)(2,1)S(1)}, u32[]{:S(2)}, u32[]{:S(2)}) collective-permute-start(bf16[2,4,128,128]{3,2,1,0:T(8,128)(2,1)S(1)} %fusion), channel_id=1, source_target_pairs={{0,4},{4,8},{8,12},{12,0},{1,5},{5,9},{9,13},{13,1},{2,6},{6,10},{... | collective-permute-start | bytes 786440 | tf_op jit(solution)/shard_map/ppermute | solution.py:33
  98.9 5.0 %collective-permute-done.20.second = bf16[2,4,128,128]{3,2,1,0:T(8,128)(2,1)S(1)} collective-permute-done((bf16[2,4,128,128]{3,2,1,0:T(8,128)(2,1)S(1)}, bf16[2,4,128,128]{3,2,1,0:T(8,128)(2,1)S(1)}, u32[]{:S(2)}, u32[]{:S(2)}) %collective-permute-start.20) | collective-permute-done | bytes 262176 | tf_op jit(solution)/shard_map/ppermute | solution.py:33
  (54 shorter events, 14.3 us)
Async XLA Ops:
  1.7 10.7 %collective-permute-start = (bf16[2,128,512]{2,1,0:T(8,128)(2,1)S(1)}, bf16[2,128,512]{2,1,0:T(8,128)(2,1)S(1)}, u32[]{:S(2)}, u32[]{:S(2)}) collective-permute-start(bf16[2,128,512]{2,1,0:T(8,128)(2,1)S(1)} %dynamic-slice_bitcast_fusion), channel_id=1, source_target_pairs={{0,12},{4,0},{8,4},{12,8},{1,13},{5,1},{9,5},{13,9},{2,14},{6,2},{... | collective-permute-start | bytes 786440 | tf_op jit(solution)/shard_map/ppermute | solution.py:33
  12.3 9.0 %collective-permute-start.1 = (bf16[2,128,512]{2,1,0:T(8,128)(2,1)S(1)}, bf16[2,128,512]{2,1,0:T(8,128)(2,1)S(1)}, u32[]{:S(2)}, u32[]{:S(2)}) collective-permute-start(bf16[2,128,512]{2,1,0:T(8,128)(2,1)S(1)} %collective-permute-done.refs_1_), channel_id=1, source_target_pairs={{0,12},{4,0},{8,4},{12,8},{1,13},{5,1},{9,5},{13,9},{2,14},{6,2},{... | collective-permute-start | bytes 786440 | tf_op jit(solution)/shard_map/ppermute | solution.py:33
  16.6 8.2 %collective-permute-start.2 = (bf16[2,128,512]{2,1,0:T(8,128)(2,1)S(1)}, bf16[2,128,512]{2,1,0:T(8,128)(2,1)S(1)}, u32[]{:S(2)}, u32[]{:S(2)}) collective-permute-start(bf16[2,128,512]{2,1,0:T(8,128)(2,1)S(1)} %collective-permute-done.refs_1_), channel_id=1, source_target_pairs={{0,2},{1,3},{2,0},{3,1},{4,6},{5,7},{6,4},{7,5},{8,10},{9,11},{10,... | collective-permute-start | bytes 786440 | tf_op jit(solution)/shard_map/ppermute | solution.py:38
  21.3 7.8 %collective-permute-start.5 = (bf16[2,128,512]{2,1,0:T(8,128)(2,1)S(1)}, bf16[2,128,512]{2,1,0:T(8,128)(2,1)S(1)}, u32[]{:S(2)}, u32[]{:S(2)}) collective-permute-start(bf16[2,128,512]{2,1,0:T(8,128)(2,1)S(1)} %collective-permute-done.1.refs_5_), channel_id=1, source_target_pairs={{0,2},{1,3},{2,0},{3,1},{4,6},{5,7},{6,4},{7,5},{8,10},{9,11},{10,... | collective-permute-start | bytes 786440 | tf_op jit(solution)/shard_map/ppermute | solution.py:38
  22.8 7.0 %collective-permute-start.3 = (bf16[2,128,512]{2,1,0:T(8,128)(2,1)S(1)}, bf16[2,128,512]{2,1,0:T(8,128)(2,1)S(1)}, u32[]{:S(2)}, u32[]{:S(2)}) collective-permute-start(bf16[2,128,512]{2,1,0:T(8,128)(2,1)S(1)} %collective-permute-done.refs_1_), channel_id=1, source_target_pairs={{0,1},{1,0},{2,3},{3,2},{4,5},{5,4},{6,7},{7,6},{8,9},{9,8},{10,11... | collective-permute-start | bytes 786440 | tf_op jit(solution)/shard_map/ppermute | solution.py:38
  22.8 7.0 %collective-permute-start.6 = (bf16[2,128,512]{2,1,0:T(8,128)(2,1)S(1)}, bf16[2,128,512]{2,1,0:T(8,128)(2,1)S(1)}, u32[]{:S(2)}, u32[]{:S(2)}) collective-permute-start(bf16[2,128,512]{2,1,0:T(8,128)(2,1)S(1)} %collective-permute-done.1.refs_5_), channel_id=1, source_target_pairs={{0,1},{1,0},{2,3},{3,2},{4,5},{5,4},{6,7},{7,6},{8,9},{9,8},{10,11... | collective-permute-start | bytes 786440 | tf_op jit(solution)/shard_map/ppermute | solution.py:38
  24.8 5.0 %collective-permute-start.4 = (bf16[2,128,512]{2,1,0:T(8,128)(2,1)S(1)}, bf16[2,128,512]{2,1,0:T(8,128)(2,1)S(1)}, u32[]{:S(2)}, u32[]{:S(2)}) collective-permute-start(bf16[2,128,512]{2,1,0:T(8,128)(2,1)S(1)} %collective-permute-done.2.refs_2_), channel_id=1, source_target_pairs={{0,1},{1,0},{2,3},{3,2},{4,5},{5,4},{6,7},{7,6},{8,9},{9,8},{10,11... | collective-permute-start | bytes 786440 | tf_op jit(solution)/shard_map/ppermute | solution.py:38
  29.1 1.5 %collective-permute-start.7 = (bf16[2,128,512]{2,1,0:T(8,128)(2,1)S(1)}, bf16[2,128,512]{2,1,0:T(8,128)(2,1)S(1)}, u32[]{:S(2)}, u32[]{:S(2)}) collective-permute-start(bf16[2,128,512]{2,1,0:T(8,128)(2,1)S(1)} %collective-permute-done.5.refs_6_), channel_id=1, source_target_pairs={{0,1},{1,0},{2,3},{3,2},{4,5},{5,4},{6,7},{7,6},{8,9},{9,8},{10,11... | collective-permute-start | bytes 786440 | tf_op jit(solution)/shard_map/ppermute | solution.py:38
  51.5 1.8 %collective-permute-start.8 = (bf16[1,12,64,256]{3,2,1,0:T(8,128)(2,1)S(1)}, bf16[1,12,64,256]{3,2,1,0:T(8,128)(2,1)S(1)}, u32[]{:S(2)}, u32[]{:S(2)}) collective-permute-start(bf16[1,12,64,256]{3,2,1,0:T(8,128)(2,1)S(1)} %get-tuple-element.63), channel_id=1, source_target_pairs={{0,1},{1,0},{2,3},{3,2},{4,5},{5,4},{6,7},{7,6},{8,9},{9,8},{10,11... | collective-permute-start | bytes 1179656 | tf_op jit(solution)/shard_map/ppermute | solution.py:38
  53.4 11.2 %collective-permute-start.14 = (bf16[1,12,64,256]{3,2,1,0:T(8,128)(2,1)S(1)}, bf16[1,12,64,256]{3,2,1,0:T(8,128)(2,1)S(1)}, u32[]{:S(2)}, u32[]{:S(2)}) collective-permute-start(bf16[1,12,64,256]{3,2,1,0:T(8,128)(2,1)S(1)} %add_convert_fusion), channel_id=1, source_target_pairs={{0,2},{1,3},{2,0},{3,1},{4,6},{5,7},{6,4},{7,5},{8,10},{9,11},{10,... | collective-permute-start | bytes 1179656 | tf_op jit(solution)/shard_map/ppermute | solution.py:38
  61.4 1.6 %collective-permute-start.13 = (bf16[1,2,4,128,128]{4,3,2,1,0:T(8,128)(2,1)S(1)}, bf16[1,2,4,128,128]{4,3,2,1,0:T(8,128)(2,1)S(1)}, u32[]{:S(2)}, u32[]{:S(2)}) collective-permute-start(bf16[1,2,4,128,128]{4,3,2,1,0:T(8,128)(2,1)S(1)} %get-tuple-element.74), channel_id=1, source_target_pairs={{0,1},{1,0},{2,3},{3,2},{4,5},{5,4},{6,7},{7,6},{8,9},{9,8},{10,11... | collective-permute-start | bytes 786440 | tf_op jit(solution)/shard_map/ppermute | solution.py:38
  61.5 5.5 %collective-permute-start.21 = (bf16[1,12,64,256]{3,2,1,0:T(8,128)(2,1)S(1)}, bf16[1,12,64,256]{3,2,1,0:T(8,128)(2,1)S(1)}, u32[]{:S(2)}, u32[]{:S(2)}) collective-permute-start(bf16[1,12,64,256]{3,2,1,0:T(8,128)(2,1)S(1)} %get-tuple-element.81), channel_id=1, source_target_pairs={{0,1},{1,0},{2,3},{3,2},{4,5},{5,4},{6,7},{7,6},{8,9},{9,8},{10,11... | collective-permute-start | bytes 1179656 | tf_op jit(solution)/shard_map/ppermute | solution.py:38
  62.0 16.2 %collective-permute-start.10 = (bf16[1,2,4,128,128]{4,3,2,1,0:T(8,128)(2,1)}, bf16[1,2,4,128,128]{4,3,2,1,0:T(8,128)(2,1)}, u32[]{:S(2)}, u32[]{:S(2)}) collective-permute-start(bf16[1,2,4,128,128]{4,3,2,1,0:T(8,128)(2,1)} %get-tuple-element.68), channel_id=1, source_target_pairs={{0,1},{1,0},{2,3},{3,2},{4,5},{5,4},{6,7},{7,6},{8,9},{9,8},{10,11... | collective-permute-start | bytes 786440 | tf_op jit(solution)/shard_map/ppermute | solution.py:38
  62.0 13.1 %collective-permute-start.11 = (bf16[1,2,4,128,128]{4,3,2,1,0:T(8,128)(2,1)}, bf16[1,2,4,128,128]{4,3,2,1,0:T(8,128)(2,1)}, u32[]{:S(2)}, u32[]{:S(2)}) collective-permute-start(bf16[1,2,4,128,128]{4,3,2,1,0:T(8,128)(2,1)} %get-tuple-element.70), channel_id=1, source_target_pairs={{0,1},{1,0},{2,3},{3,2},{4,5},{5,4},{6,7},{7,6},{8,9},{9,8},{10,11... | collective-permute-start | bytes 786440 | tf_op jit(solution)/shard_map/ppermute | solution.py:38
  63.0 8.4 %collective-permute-start.12 = (bf16[1,2,4,128,128]{4,3,2,1,0:T(8,128)(2,1)}, bf16[1,2,4,128,128]{4,3,2,1,0:T(8,128)(2,1)}, u32[]{:S(2)}, u32[]{:S(2)}) collective-permute-start(bf16[1,2,4,128,128]{4,3,2,1,0:T(8,128)(2,1)} %get-tuple-element.72), channel_id=1, source_target_pairs={{0,1},{1,0},{2,3},{3,2},{4,5},{5,4},{6,7},{7,6},{8,9},{9,8},{10,11... | collective-permute-start | bytes 786440 | tf_op jit(solution)/shard_map/ppermute | solution.py:38
  65.4 7.8 %collective-permute-start.15 = (bf16[1,2,4,128,128]{4,3,2,1,0:T(8,128)(2,1)}, bf16[1,2,4,128,128]{4,3,2,1,0:T(8,128)(2,1)}, u32[]{:S(2)}, u32[]{:S(2)}) collective-permute-start(bf16[1,2,4,128,128]{4,3,2,1,0:T(8,128)(2,1)} %add_convert_fusion.4), channel_id=1, source_target_pairs={{0,2},{1,3},{2,0},{3,1},{4,6},{5,7},{6,4},{7,5},{8,10},{9,11},{10,... | collective-permute-start | bytes 786440 | tf_op jit(solution)/shard_map/ppermute | solution.py:38
  67.9 14.9 %all-to-all-start = ((bf16[4,192,256]{2,1,0:T(8,128)(2,1)}), bf16[4,192,256]{2,1,0:T(8,128)(2,1)S(1)}, u32[]{:S(2)}, u32[]{:S(2)}) async-start(bf16[4,192,256]{2,1,0:T(8,128)(2,1)} %bitcast.24), calls=%async_computation | async-start | bytes 786432 | tf_op jit(solution)/shard_map/all_to_all | solution.py:585
  76.1 6.7 %collective-permute-start.16 = (bf16[1,2,4,128,128]{4,3,2,1,0:T(8,128)(2,1)S(1)}, bf16[1,2,4,128,128]{4,3,2,1,0:T(8,128)(2,1)S(1)}, u32[]{:S(2)}, u32[]{:S(2)}) collective-permute-start(bf16[1,2,4,128,128]{4,3,2,1,0:T(8,128)(2,1)S(1)} %add_convert_fusion.2), channel_id=1, source_target_pairs={{0,2},{1,3},{2,0},{3,1},{4,6},{5,7},{6,4},{7,5},{8,10},{9,11},{10,... | collective-permute-start | bytes 786440 | tf_op jit(solution)/shard_map/ppermute | solution.py:38
  77.7 16.8 %collective-permute-start.19 = (bf16[1,2,4,128,128]{4,3,2,1,0:T(8,128)(2,1)S(1)}, bf16[1,2,4,128,128]{4,3,2,1,0:T(8,128)(2,1)}, u32[]{:S(2)}, u32[]{:S(2)}) collective-permute-start(bf16[1,2,4,128,128]{4,3,2,1,0:T(8,128)(2,1)S(1)} %get-tuple-element.79), channel_id=1, source_target_pairs={{0,1},{1,0},{2,3},{3,2},{4,5},{5,4},{6,7},{7,6},{8,9},{9,8},{10,11... | collective-permute-start | bytes 786440 | tf_op jit(solution)/shard_map/ppermute | solution.py:38
  77.7 16.8 %collective-permute-start.18 = (bf16[2,4,128,128]{3,2,1,0:T(8,128)(2,1)}, bf16[2,4,128,128]{3,2,1,0:T(8,128)(2,1)}, u32[]{:S(2)}, u32[]{:S(2)}) collective-permute-start(bf16[2,4,128,128]{3,2,1,0:T(8,128)(2,1)} %fusion.1), channel_id=1, source_target_pairs={{0,4},{4,8},{8,12},{12,0},{1,5},{5,9},{9,13},{13,1},{2,6},{6,10},{... | collective-permute-start | bytes 786440 | tf_op jit(solution)/shard_map/ppermute | solution.py:33
  77.7 20.0 %collective-permute-start.9 = (bf16[1,2,4,128,128]{4,3,2,1,0:T(8,128)(2,1)S(1)}, bf16[1,2,4,128,128]{4,3,2,1,0:T(8,128)(2,1)S(1)}, u32[]{:S(2)}, u32[]{:S(2)}) collective-permute-start(bf16[1,2,4,128,128]{4,3,2,1,0:T(8,128)(2,1)S(1)} %get-tuple-element.66), channel_id=1, source_target_pairs={{0,1},{1,0},{2,3},{3,2},{4,5},{5,4},{6,7},{7,6},{8,9},{9,8},{10,11... | collective-permute-start | bytes 786440 | tf_op jit(solution)/shard_map/ppermute | solution.py:38
  83.6 21.1 %all-to-all-start.1 = ((bf16[4,192,256]{2,1,0:T(8,128)(2,1)}), bf16[4,192,256]{2,1,0:T(8,128)(2,1)S(1)}, u32[]{:S(2)}, u32[]{:S(2)}) async-start(bf16[4,192,256]{2,1,0:T(8,128)(2,1)} %add_up.1), calls=%async_computation.1 | async-start | bytes 786432 | tf_op jit(solution)/shard_map/all_to_all | solution.py:596
  88.9 9.9 %collective-permute-start.17 = (bf16[1,2,4,128,128]{4,3,2,1,0:T(8,128)(2,1)S(1)}, bf16[1,2,4,128,128]{4,3,2,1,0:T(8,128)(2,1)S(1)}, u32[]{:S(2)}, u32[]{:S(2)}) collective-permute-start(bf16[1,2,4,128,128]{4,3,2,1,0:T(8,128)(2,1)S(1)} %add_convert_fusion.1), channel_id=1, source_target_pairs={{0,2},{1,3},{2,0},{3,1},{4,6},{5,7},{6,4},{7,5},{8,10},{9,11},{10,... | collective-permute-start | bytes 786440 | tf_op jit(solution)/shard_map/ppermute | solution.py:38
  95.6 8.2 %collective-permute-start.20 = (bf16[2,4,128,128]{3,2,1,0:T(8,128)(2,1)S(1)}, bf16[2,4,128,128]{3,2,1,0:T(8,128)(2,1)S(1)}, u32[]{:S(2)}, u32[]{:S(2)}) collective-permute-start(bf16[2,4,128,128]{3,2,1,0:T(8,128)(2,1)S(1)} %fusion), channel_id=1, source_target_pairs={{0,4},{4,8},{8,12},{12,0},{1,5},{5,9},{9,13},{13,1},{2,6},{6,10},{... | collective-permute-start | bytes 786440 | tf_op jit(solution)/shard_map/ppermute | solution.py:33
  (7 other events, 102.5 us)

commit v10 on v9

--- a/solution.py
+++ b/solution.py
@@ -111,10 +111,9 @@
     shares = len(offs)
     pieces = refs[: 1 + (REACH - 1) * shares]
     eig_in, amps_in, tables_in, coef_in = refs[len(pieces):len(pieces) + 4]
-    eigen_send, eigen_keep = refs[len(pieces) + 4:len(pieces) + 6], refs[len(pieces) + 6:len(pieces) + 8]
-    grads_out, coef = refs[len(pieces) + 8:len(pieces) + 10]
+    eigen_send, eigen_keep, grads_out, coef = refs[len(pieces) + 4:len(pieces) + 8]
     (staged, table, probe, amps, eig, obj, ex, mid, far, patch, d_high, d_low, eigen, out_eigen, cross,
-     weights, weights_t, piece_sem, table_sem, amps_sem, eig_sem, grad_sem, out_sem) = refs[len(pieces) + 10:]
+     weights, weights_t, piece_sem, table_sem, amps_sem, eig_sem, grad_sem, out_sem) = refs[len(pieces) + 8:]
     pos_dev, _, frame, _ = probe.shape
     modes = eig.shape[0]
     side = staged.shape[2]
@@ -301,11 +300,14 @@
         copy.start()
         pending.append(copy)
 
-    for h in far_first(shares):
+    parts, _, share = out_eigen.shape[:3]
+    for h in range(shares // 2):
         mine, other = slabs_of(member, h)
-        out_eigen[h] = eigen[other].astype(jnp.bfloat16)
-        start(out_eigen.at[h], eigen_send[h % 2].at[h // 2])
-        start(eigen.at[mine], eigen_keep[h % 2].at[h // 2])
+        for i in range(parts):
+            of_part = pl.ds(i * share, share)
+            out_eigen[i, h] = eigen[other, of_part].astype(jnp.bfloat16)
+            start(eigen.at[mine, of_part], eigen_keep.at[i, h])
+    start(out_eigen, eigen_send)
 
     total = exact(one_hot(by_position[::-1], 1), diagonals(cross[...]))
     coef[...] = lax.dot_general(
@@ -331,13 +333,14 @@
     smem = pl.BlockSpec(memory_space=SMEM)
     whole = pl.BlockSpec(memory_space=VMEM)
     anywhere = pl.BlockSpec(memory_space=pl.ANY)
-    eigen_half = (shares // 2, 2 * modes, frame // shares, frame)
-    eigen_part = (shares // 4,) + eigen_half[1:]
+    peers = lax.axis_size("blk")
+    parts = peers if 2 * modes % peers == 0 else 1
+    eigen_half = (parts, shares // 2, 2 * modes // parts, frame // shares, frame)
     grads = (pos_dev, 2, frame, frame)
     return pl.pallas_call(
         functools.partial(position_kernel, offs, scale),
         in_specs=[smem] * 3 + [anywhere] * (len(pieces) + 3) + [whole],
-        out_specs=[anywhere] * 5 + [whole],
+        out_specs=[anywhere] * 3 + [whole],
         scratch_shapes=[
             pltpu.VMEM((REACH, 2, side, side), jnp.bfloat16),
             pltpu.VMEM(table.shape, jnp.bfloat16),
@@ -361,13 +364,11 @@
             pltpu.SemaphoreType.DMA,
             pltpu.SemaphoreType.DMA,
             pltpu.SemaphoreType.DMA((pos_dev,)),
-            pltpu.SemaphoreType.DMA((shares,)),
+            pltpu.SemaphoreType.DMA((parts * (shares // 2) + 1,)),
         ],
         out_shape=[
-            jax.ShapeDtypeStruct(eigen_part, jnp.bfloat16),
-            jax.ShapeDtypeStruct(eigen_part, jnp.bfloat16),
-            jax.ShapeDtypeStruct(eigen_part, jnp.float32),
-            jax.ShapeDtypeStruct(eigen_part, jnp.float32),
+            jax.ShapeDtypeStruct(eigen_half, jnp.bfloat16),
+            jax.ShapeDtypeStruct(eigen_half, jnp.float32),
             jax.ShapeDtypeStruct(grads, jnp.float32),
             jax.ShapeDtypeStruct((modes, pos_dev), jnp.float32),
         ],
@@ -482,27 +483,39 @@
     return lax.optimization_barrier(tuple(arrays) + others)[:len(arrays)]
 
 
-def halve(keep, send, before_core=(), before_cross=()):
-    far = [keep[1], after(swap(after(send[1], *before_core), "probe", 1), *before_cross)]
-    terms = [keep[0], swap(send[0], "probe", 1)]
+def cross(far, terms):
     leaving = None
     bit = 2
     while True:
         sending = sum(term.astype(jnp.float32) for term in far).astype(jnp.bfloat16)
         leaving = sending if leaving is None else leaving
-        terms.append(swap(sending, "probe", bit))
+        terms = terms + [swap(sending, "probe", bit)]
         if terms[0].shape[0] == 1:
-            return sum(term[0].astype(jnp.float32) for term in terms), leaving, terms[-1]
-        pick = lambda term, which: term.reshape((term.shape[0] // 2, 2) + term.shape[1:])[:, which]
-        far, terms = [pick(term, 1) for term in terms], [pick(term, 0) for term in terms]
+            return [term[0] for term in terms], leaving, terms[-1]
+        far, terms = halves(terms)
         bit *= 2
+
+
+def halves(terms):
+    pick = lambda term, which: term.reshape((term.shape[0] // 2, 2) + term.shape[1:])[:, which]
+    return [pick(term, 1) for term in terms], [pick(term, 0) for term in terms]
+
+
+def halve(keep, send, *before_cross):
+    far = [keep[1], after(swap(send[1], "probe", 1), *before_cross)]
+    terms, leaving, arrived = cross(far, [keep[0], swap(send[0], "probe", 1)])
+    return sum(term.astype(jnp.float32) for term in terms), leaving, arrived
 
 
 def add_up_kernel(shares, out):
     total = shares[0].astype(jnp.float32)
     for i in range(1, shares.shape[0]):
         total += shares[i].astype(jnp.float32)
-    total = total.astype(jnp.bfloat16)
+    out[...] = total
+
+
+def copies_kernel(first, second, out):
+    total = (first[...].astype(jnp.float32) + second[...].astype(jnp.float32)).astype(jnp.bfloat16)
     for i in range(out.shape[0]):
         out[i] = total
 
@@ -511,15 +524,15 @@
     out[...] = array[...].astype(jnp.float32)
 
 
-def small_call(kernel, array, kind, name):
+def small_call(kernel, shape, kind, name, *arrays):
     return pl.pallas_call(
         kernel,
-        in_specs=[pl.BlockSpec(memory_space=VMEM)],
+        in_specs=[pl.BlockSpec(memory_space=VMEM)] * len(arrays),
         out_specs=pl.BlockSpec(memory_space=VMEM),
-        out_shape=jax.ShapeDtypeStruct(array.shape, kind),
+        out_shape=jax.ShapeDtypeStruct(shape, kind),
         compiler_params=pltpu.CompilerParams(vmem_limit_bytes=8 * 1024 * 1024),
         name=name,
-    )(array)
+    )(*arrays)
 
 
 def finish_kernel(first, second, out):
@@ -574,27 +587,35 @@
     out = positions(
         tuple(offs), scale, indices, [tile] + held[0] + held[1], eig, amps, table, coef_t
     )
-    eigen_send, eigen_keep, grads, coef_rows = out[:2], out[2:4], out[4], out[5]
-
-    eigen, leaving, crossed = halve(eigen_keep, eigen_send)
-    out = scatter(shares, side, indices, after(grads, leaving))
+    eigen_send, eigen_keep, grads, coef_rows = out
+
+    partial = (eigen_keep + swap(eigen_send, "probe", 1).astype(jnp.float32)).astype(jnp.bfloat16)
+    if partial.shape[0] == blocks:
+        partial = partial.reshape(blocks, shares // 2, -1, frame)
+    else:
+        partial = jnp.moveaxis(partial.reshape(shares // 2, blocks, -1, frame), 1, 0)
+    scattered = lax.all_to_all(partial, "blk", 0, 0)
+    out = scatter(shares, side, indices, after(grads, partial))
     send, keep = ([out[at + 2 * i:at + 2 * i + 2] for i in range(REACH)] for at in (0, 2 * REACH))
     last = REACH - 1
-    mine, leaving, _ = halve(keep[last], send[last], before_cross=(crossed,))
-    scattered = after(eigen, leaving).reshape(blocks, -1, frame).astype(jnp.bfloat16)
-    scattered = lax.all_to_all(scattered, "blk", 0, 0)
+    mine, _, _ = halve(keep[last], send[last])
     moving = mine.astype(jnp.bfloat16)
     gate = moving
     for section in range(last - 1, -1, -1):
-        mine, _, gate = halve(keep[section], send[section], before_cross=(gate,))
+        mine, leaving, gate = halve(keep[section], send[section], gate)
         if section == last - 1:
-            scattered = after(scattered, gate)
+            scattered = after(scattered, leaving)
         arrived = shift(moving, "blk", 1)
         if section > 0:
             moving = (arrived.astype(jnp.float32) + mine).astype(jnp.bfloat16)
-    copies = small_call(add_up_kernel, scattered, jnp.bfloat16, "add_up")
+    total = small_call(add_up_kernel, scattered.shape[1:], jnp.float32, "add_up", scattered)
+    terms, _, _ = cross(*halves([total]))
+    first = sum(terms[:-1]) if len(terms) > 2 else terms[0]
+    copies = small_call(
+        copies_kernel, (blocks,) + first.shape, jnp.bfloat16, "copies", first, terms[-1]
+    )
     gathered = lax.all_to_all(copies, "blk", 0, 0)
-    eigen_share = small_call(widen_kernel, gathered, jnp.float32, "widen")
+    eigen_share = small_call(widen_kernel, gathered.shape, jnp.float32, "widen", gathered)
     eigen_share = eigen_share.reshape(modes, 2, frame // shares, frame)
     summed = finish(mine, arrived)
     return (summed[None], eigen_share, coef_rows.T)

time: 106 us -> 123 us (1.16)
  waiting for transfers between devices: 28.5 us -> 46.8 us
  starting transfers between devices: 34.7 us -> 30.4 us
  local copies, waits for them, and re-layouts: 3.73 us -> 7.36 us
  other arithmetic: 6.92 us -> 4.37 us
  Pallas kernels: 30.3 us -> 32.4 us
    all_to_all x1, waiting for transfers between devices: 0.01 us -> 7.82 us  [on_device(): scattered = lax.all_to_all(partial, 'blk', 0, 0)]
    ppermute x18 -> x17, waiting for transfers between devices: 17.8 us -> 24.8 us  [swap(): return lax.ppermute(array, axis, [(i, i ^ bit) for i in range(peers)])]
    ppermute x18 -> x17, starting transfers between devices: 15.6 us -> 9.72 us  [swap(): return lax.ppermute(array, axis, [(i, i ^ bit) for i in range(peers)])]
    unnamed x14 -> x26, local copies, waits for them, and re-layouts: 2.75 us -> 6.35 us
    ppermute x4, waiting for transfers between devices: 10.8 us -> 14 us  [shift(): lax.ppermute(array, axis, [(i, (i + by) % peers) for i in range(peers)])]
    pallas_call x1, Pallas kernels: 20.9 us -> 22.8 us  [positions(): pl.pallas_call(functools.partial(position_kernel, offs, scale), in_specs=...]
    ppermute x4, starting transfers between devices: 11.4 us -> 13.3 us  [shift(): lax.ppermute(array, axis, [(i, (i + by) % peers) for i in range(peers)])]
  transfers between devices with their start and end apart: 24 -> 23, of which waited for: 12 -> 13; matrix products, arithmetic and copies ran while one was open for 6% -> 3% of each run, Pallas kernels for 8% -> 2%
where the time goes in v10:
time: 123 us
  waiting for transfers between devices  46.8 us (38%)
  Pallas kernels  32.4 us (26%)
  starting transfers between devices  30.4 us (25%)
  local copies, waits for them, and re-layouts  7.36 us (6%)
  other arithmetic  4.37 us (4%)
  between operations  1.5 us (1%)
    ppermute x17, waiting for transfers between devices, swap(): return lax.ppermute(array, axis, [(i, i ^ bit) for i in range(peers)])  24.8 us
    pallas_call x1, Pallas kernels, positions(): pl.pallas_call(functools.partial(position_kernel, offs, scale), in_specs=...  22.8 us
    ppermute x4, waiting for transfers between devices, shift(): lax.ppermute(array, axis, [(i, (i + by) % peers) for i in range(peers)])  14 us
    ppermute x4, starting transfers between devices, shift(): lax.ppermute(array, axis, [(i, (i + by) % peers) for i in range(peers)])  13.3 us
    ppermute x17, starting transfers between devices, swap(): return lax.ppermute(array, axis, [(i, i ^ bit) for i in range(peers)])  9.72 us
    all_to_all x1, waiting for transfers between devices, on_device(): scattered = lax.all_to_all(partial, 'blk', 0, 0)  7.82 us
    pallas_call x1, Pallas kernels, scatter(): pl.pallas_call(functools.partial(scatter_kernel, shares), in_specs=[pl.Bl...  6.48 us
    unnamed x26, local copies, waits for them, and re-layouts  6.35 us
  transfers between devices with their start and end apart: 23, of which 13 were waited for; matrix products, arithmetic and copies ran while one was open for 3% of the time, Pallas kernels for 2%

profile of v10, /device:TPU:0, one launch (start us, length us, event | category | flops | bytes accessed | tf_op | source)
XLA Modules:
  0.0 122.9 jit_solution(10066563845817232275)
XLA Ops:
  1.7 5.1 %collective-permute-start = (bf16[2,128,512]{2,1,0:T(8,128)(2,1)S(1)}, bf16[2,128,512]{2,1,0:T(8,128)(2,1)S(1)}, u32[]{:S(2)}, u32[]{:S(2)}) collective-permute-start(bf16[2,128,512]{2,1,0:T(8,128)(2,1)S(1)} %dynamic-slice_bitcast_fusion), channel_id=1, source_target_pairs={{0,12},{4,0},{8,4},{12,8},{1,13},{5,1},{9,5},{13,9},{2,14},{6,2},{... | collective-permute-start | bytes 786440 | tf_op jit(solution)/shard_map/ppermute | solution.py:33
  6.8 5.6 %collective-permute-done.refs_1_ = bf16[2,128,512]{2,1,0:T(8,128)(2,1)S(1)} collective-permute-done((bf16[2,128,512]{2,1,0:T(8,128)(2,1)S(1)}, bf16[2,128,512]{2,1,0:T(8,128)(2,1)S(1)}, u32[]{:S(2)}, u32[]{:S(2)}) %collective-permute-start) | collective-permute-done | bytes 262176 | tf_op jit(solution)/shard_map/ppermute | solution.py:33
  12.3 4.3 %collective-permute-start.1 = (bf16[2,128,512]{2,1,0:T(8,128)(2,1)S(1)}, bf16[2,128,512]{2,1,0:T(8,128)(2,1)S(1)}, u32[]{:S(2)}, u32[]{:S(2)}) collective-permute-start(bf16[2,128,512]{2,1,0:T(8,128)(2,1)S(1)} %collective-permute-done.refs_1_), channel_id=1, source_target_pairs={{0,12},{4,0},{8,4},{12,8},{1,13},{5,1},{9,5},{13,9},{2,14},{6,2},{... | collective-permute-start | bytes 786440 | tf_op jit(solution)/shard_map/ppermute | solution.py:33
  16.6 1.5 %collective-permute-start.2 = (bf16[2,128,512]{2,1,0:T(8,128)(2,1)S(1)}, bf16[2,128,512]{2,1,0:T(8,128)(2,1)S(1)}, u32[]{:S(2)}, u32[]{:S(2)}) collective-permute-start(bf16[2,128,512]{2,1,0:T(8,128)(2,1)S(1)} %collective-permute-done.refs_1_), channel_id=1, source_target_pairs={{0,2},{1,3},{2,0},{3,1},{4,6},{5,7},{6,4},{7,5},{8,10},{9,11},{10,... | collective-permute-start | bytes 786440 | tf_op jit(solution)/shard_map/ppermute | solution.py:38
  18.1 1.4 %copy-done.1 = bf16[6,2,256,256]{3,2,1,0:T(8,128)(2,1)S(1)} copy-done((bf16[6,2,256,256]{3,2,1,0:T(8,128)(2,1)S(1)}, bf16[6,2,256,256]{3,2,1,0:T(8,128)(2,1)}, u32[]{:S(2)}) %copy-start.1) | copy-done | bytes 1572888
  19.5 1.3 %copy-done.2 = bf16[10,256,256]{2,1,0:T(8,128)(2,1)S(1)} copy-done((bf16[10,256,256]{2,1,0:T(8,128)(2,1)S(1)}, bf16[10,256,256]{2,1,0:T(8,128)(2,1)}, u32[]{:S(2)}) %copy-start.2) | copy-done | bytes 1310744
  21.3 1.5 %collective-permute-start.5 = (bf16[2,128,512]{2,1,0:T(8,128)(2,1)S(1)}, bf16[2,128,512]{2,1,0:T(8,128)(2,1)S(1)}, u32[]{:S(2)}, u32[]{:S(2)}) collective-permute-start(bf16[2,128,512]{2,1,0:T(8,128)(2,1)S(1)} %collective-permute-done.1.refs_5_), channel_id=1, source_target_pairs={{0,2},{1,3},{2,0},{3,1},{4,6},{5,7},{6,4},{7,5},{8,10},{9,11},{10,... | collective-permute-start | bytes 786440 | tf_op jit(solution)/shard_map/ppermute | solution.py:38
  23.3 1.5 %collective-permute-done.2.refs_2_ = bf16[2,128,512]{2,1,0:T(8,128)(2,1)S(1)} collective-permute-done((bf16[2,128,512]{2,1,0:T(8,128)(2,1)S(1)}, bf16[2,128,512]{2,1,0:T(8,128)(2,1)S(1)}, u32[]{:S(2)}, u32[]{:S(2)}) %collective-permute-start.2) | collective-permute-done | bytes 262176 | tf_op jit(solution)/shard_map/ppermute | solution.py:38
  25.1 4.1 %collective-permute-done.5.refs_6_ = bf16[2,128,512]{2,1,0:T(8,128)(2,1)S(1)} collective-permute-done((bf16[2,128,512]{2,1,0:T(8,128)(2,1)S(1)}, bf16[2,128,512]{2,1,0:T(8,128)(2,1)S(1)}, u32[]{:S(2)}, u32[]{:S(2)}) %collective-permute-start.5) | collective-permute-done | bytes 262176 | tf_op jit(solution)/shard_map/ppermute | solution.py:38
  30.7 22.8 %positions.1 = (bf16[4,2,3,64,256]{4,3,2,1,0:T(8,128)(2,1)S(1)}, f32[4,2,3,64,256]{4,3,2,1,0:T(8,128)S(1)}, f32[10,2,256,256]{3,2,1,0:T(8,128)S(1)}, f32[6,10]{1,0:T(8,128)}) custom-call(s32[2,10]{1,0:T(2,128)S(1)} %get-tuple-element.49.tile_list, s32[4,10]{1,0:T(4,128)S(1)} %get-tuple-element.50.offsets, s32[1]{0:T(128)S(6)} %copy.11.group_counts, ...), custom_call_target="tpu_custom_call" | custom-call | tf_op jit(solution)/shard_map/positions/pallas_call | solution.py:340
  53.7 2.1 %collective-permute-done.8 = bf16[4,2,3,64,256]{4,3,2,1,0:T(8,128)(2,1)S(1)} collective-permute-done((bf16[4,2,3,64,256]{4,3,2,1,0:T(8,128)(2,1)S(1)}, bf16[4,2,3,64,256]{4,3,2,1,0:T(8,128)(2,1)S(1)}, u32[]{:S(2)}, u32[]{:S(2)}) %collective-permute-start.8) | collective-permute-done | bytes 786464 | tf_op jit(solution)/shard_map/ppermute | solution.py:38
  57.0 6.5 %scatter.1 = (bf16[1,2,4,128,128]{4,3,2,1,0:T(8,128)(2,1)}, bf16[1,2,4,128,128]{4,3,2,1,0:T(8,128)(2,1)S(1)}, bf16[1,2,4,128,128]{4,3,2,1,0:T(8,128)(2,1)}, bf16...) custom-call(s32[2,10]{1,0:T(2,128)S(1)} %get-tuple-element.49.tile_l, ...), custom_call_target="tpu_custom_call" | custom-call | flops 16777216 | bytes 16777216 | tf_op jit(solution)/shard_map/scatter/pallas_call | solution.py:459
  66.6 4.0 %all-to-all-start = ((bf16[4,2,192,256]{3,2,1,0:T(8,128)(2,1)}), bf16[4,2,192,256]{3,2,1,0:T(8,128)(2,1)S(1)}, u32[]{:S(2)}, u32[]{:S(2)}) async-start(bf16[4,2,192,256]{3,2,1,0:T(8,128)(2,1)} %bitcast.31), calls=%async_computation | async-start | bytes 1572864 | tf_op jit(solution)/shard_map/all_to_all | solution.py:597
  70.8 1.2 add_convert_fusion.4
  72.0 1.2 %collective-permute-start.14 = (bf16[1,2,4,128,128]{4,3,2,1,0:T(8,128)(2,1)S(1)}, bf16[1,2,4,128,128]{4,3,2,1,0:T(8,128)(2,1)S(1)}, u32[]{:S(2)}, u32[]{:S(2)}) collective-permute-start(bf16[1,2,4,128,128]{4,3,2,1,0:T(8,128)(2,1)S(1)} %add_convert_fusion.4), channel_id=1, source_target_pairs={{0,2},{1,3},{2,0},{3,1},{4,6},{5,7},{6,4},{7,5},{8,10},{9,11},{10,... | collective-permute-start | bytes 786440 | tf_op jit(solution)/shard_map/ppermute | solution.py:38
  73.7 6.8 %collective-permute-done.14 = bf16[1,2,4,128,128]{4,3,2,1,0:T(8,128)(2,1)S(1)} collective-permute-done((bf16[1,2,4,128,128]{4,3,2,1,0:T(8,128)(2,1)S(1)}, bf16[1,2,4,128,128]{4,3,2,1,0:T(8,128)(2,1)S(1)}, u32[]{:S(2)}, u32[]{:S(2)}) %collective-permute-start.14) | collective-permute-done | bytes 262176 | tf_op jit(solution)/shard_map/ppermute | solution.py:38
  82.9 1.9 %collective-permute-start.17 = (bf16[2,4,128,128]{3,2,1,0:T(8,128)(2,1)}, bf16[2,4,128,128]{3,2,1,0:T(8,128)(2,1)}, u32[]{:S(2)}, u32[]{:S(2)}) collective-permute-start(bf16[2,4,128,128]{3,2,1,0:T(8,128)(2,1)} %fusion.1), channel_id=1, source_target_pairs={{0,4},{4,8},{8,12},{12,0},{1,5},{5,9},{9,13},{13,1},{2,6},{6,10},{... | collective-permute-start | bytes 786440 | tf_op jit(solution)/shard_map/ppermute | solution.py:33
  85.5 3.6 %collective-permute-done.15 = bf16[1,2,4,128,128]{4,3,2,1,0:T(8,128)(2,1)S(1)} collective-permute-done((bf16[1,2,4,128,128]{4,3,2,1,0:T(8,128)(2,1)S(1)}, bf16[1,2,4,128,128]{4,3,2,1,0:T(8,128)(2,1)S(1)}, u32[]{:S(2)}, u32[]{:S(2)}) %collective-permute-start.15) | collective-permute-done | bytes 262176 | tf_op jit(solution)/shard_map/ppermute | solution.py:38
  89.2 7.8 %all-to-all-done.shares = bf16[4,2,192,256]{3,2,1,0:T(8,128)(2,1)S(1)} async-done(((bf16[4,2,192,256]{3,2,1,0:T(8,128)(2,1)}), bf16[4,2,192,256]{3,2,1,0:T(8,128)(2,1)S(1)}, u32[]{:S(2)}, u32[]{:S(2)}) %all-to-all-start) | async-done | bytes 786464 | tf_op jit(solution)/shard_map/all_to_all | solution.py:597
  98.3 3.5 %collective-permute-done.20 = bf16[1,192,256]{2,1,0:T(8,128)(2,1)S(1)} collective-permute-done((bf16[1,192,256]{2,1,0:T(8,128)(2,1)S(1)}, bf16[1,192,256]{2,1,0:T(8,128)(2,1)S(1)}, u32[]{:S(2)}, u32[]{:S(2)}) %collective-permute-start.20) | collective-permute-done | bytes 98336 | tf_op jit(solution)/shard_map/ppermute | solution.py:38
  102.5 3.5 %all-to-all-start.1 = ((bf16[4,192,256]{2,1,0:T(8,128)(2,1)}), bf16[4,192,256]{2,1,0:T(8,128)(2,1)S(1)}, u32[]{:S(2)}, u32[]{:S(2)}) async-start(bf16[4,192,256]{2,1,0:T(8,128)(2,1)} %copies.1), calls=%async_computation.1 | async-start | bytes 786432 | tf_op jit(solution)/shard_map/all_to_all | solution.py:617
  108.3 2.0 %collective-permute-start.19 = (bf16[2,4,128,128]{3,2,1,0:T(8,128)(2,1)S(1)}, bf16[2,4,128,128]{3,2,1,0:T(8,128)(2,1)S(1)}, u32[]{:S(2)}, u32[]{:S(2)}) collective-permute-start(bf16[2,4,128,128]{3,2,1,0:T(8,128)(2,1)S(1)} %fusion), channel_id=1, source_target_pairs={{0,4},{4,8},{8,12},{12,0},{1,5},{5,9},{9,13},{13,1},{2,6},{6,10},{... | collective-permute-start | bytes 786440 | tf_op jit(solution)/shard_map/ppermute | solution.py:33
  110.4 2.3 %collective-permute-done.16 = bf16[1,2,4,128,128]{4,3,2,1,0:T(8,128)(2,1)S(1)} collective-permute-done((bf16[1,2,4,128,128]{4,3,2,1,0:T(8,128)(2,1)S(1)}, bf16[1,2,4,128,128]{4,3,2,1,0:T(8,128)(2,1)S(1)}, u32[]{:S(2)}, u32[]{:S(2)}) %collective-permute-start.16) | collective-permute-done | bytes 262176 | tf_op jit(solution)/shard_map/ppermute | solution.py:38
  112.7 8.2 %collective-permute-done.19.second = bf16[2,4,128,128]{3,2,1,0:T(8,128)(2,1)S(1)} collective-permute-done((bf16[2,4,128,128]{3,2,1,0:T(8,128)(2,1)S(1)}, bf16[2,4,128,128]{3,2,1,0:T(8,128)(2,1)S(1)}, u32[]{:S(2)}, u32[]{:S(2)}) %collective-permute-start.19) | collective-permute-done | bytes 262176 | tf_op jit(solution)/shard_map/ppermute | solution.py:33
  (66 shorter events, 17.7 us)
Async XLA Ops:
  0.6 24.2 %copy-start.5 = (f32[10,6]{0,1:T(8,128)S(1)}, f32[10,6]{0,1:T(8,128)}, u32[]{:S(2)}) copy-start(f32[10,6]{0,1:T(8,128)} %param.10) | copy-start | bytes 724
  1.7 10.7 %collective-permute-start = (bf16[2,128,512]{2,1,0:T(8,128)(2,1)S(1)}, bf16[2,128,512]{2,1,0:T(8,128)(2,1)S(1)}, u32[]{:S(2)}, u32[]{:S(2)}) collective-permute-start(bf16[2,128,512]{2,1,0:T(8,128)(2,1)S(1)} %dynamic-slice_bitcast_fusion), channel_id=1, source_target_pairs={{0,12},{4,0},{8,4},{12,8},{1,13},{5,1},{9,5},{13,9},{2,14},{6,2},{... | collective-permute-start | bytes 786440 | tf_op jit(solution)/shard_map/ppermute | solution.py:33
  12.3 9.0 %collective-permute-start.1 = (bf16[2,128,512]{2,1,0:T(8,128)(2,1)S(1)}, bf16[2,128,512]{2,1,0:T(8,128)(2,1)S(1)}, u32[]{:S(2)}, u32[]{:S(2)}) collective-permute-start(bf16[2,128,512]{2,1,0:T(8,128)(2,1)S(1)} %collective-permute-done.refs_1_), channel_id=1, source_target_pairs={{0,12},{4,0},{8,4},{12,8},{1,13},{5,1},{9,5},{13,9},{2,14},{6,2},{... | collective-permute-start | bytes 786440 | tf_op jit(solution)/shard_map/ppermute | solution.py:33
  16.6 8.2 %collective-permute-start.2 = (bf16[2,128,512]{2,1,0:T(8,128)(2,1)S(1)}, bf16[2,128,512]{2,1,0:T(8,128)(2,1)S(1)}, u32[]{:S(2)}, u32[]{:S(2)}) collective-permute-start(bf16[2,128,512]{2,1,0:T(8,128)(2,1)S(1)} %collective-permute-done.refs_1_), channel_id=1, source_target_pairs={{0,2},{1,3},{2,0},{3,1},{4,6},{5,7},{6,4},{7,5},{8,10},{9,11},{10,... | collective-permute-start | bytes 786440 | tf_op jit(solution)/shard_map/ppermute | solution.py:38
  21.3 7.8 %collective-permute-start.5 = (bf16[2,128,512]{2,1,0:T(8,128)(2,1)S(1)}, bf16[2,128,512]{2,1,0:T(8,128)(2,1)S(1)}, u32[]{:S(2)}, u32[]{:S(2)}) collective-permute-start(bf16[2,128,512]{2,1,0:T(8,128)(2,1)S(1)} %collective-permute-done.1.refs_5_), channel_id=1, source_target_pairs={{0,2},{1,3},{2,0},{3,1},{4,6},{5,7},{6,4},{7,5},{8,10},{9,11},{10,... | collective-permute-start | bytes 786440 | tf_op jit(solution)/shard_map/ppermute | solution.py:38
  22.8 7.0 %collective-permute-start.3 = (bf16[2,128,512]{2,1,0:T(8,128)(2,1)S(1)}, bf16[2,128,512]{2,1,0:T(8,128)(2,1)S(1)}, u32[]{:S(2)}, u32[]{:S(2)}) collective-permute-start(bf16[2,128,512]{2,1,0:T(8,128)(2,1)S(1)} %collective-permute-done.refs_1_), channel_id=1, source_target_pairs={{0,1},{1,0},{2,3},{3,2},{4,5},{5,4},{6,7},{7,6},{8,9},{9,8},{10,11... | collective-permute-start | bytes 786440 | tf_op jit(solution)/shard_map/ppermute | solution.py:38
  22.8 7.0 %collective-permute-start.6 = (bf16[2,128,512]{2,1,0:T(8,128)(2,1)S(1)}, bf16[2,128,512]{2,1,0:T(8,128)(2,1)S(1)}, u32[]{:S(2)}, u32[]{:S(2)}) collective-permute-start(bf16[2,128,512]{2,1,0:T(8,128)(2,1)S(1)} %collective-permute-done.1.refs_5_), channel_id=1, source_target_pairs={{0,1},{1,0},{2,3},{3,2},{4,5},{5,4},{6,7},{7,6},{8,9},{9,8},{10,11... | collective-permute-start | bytes 786440 | tf_op jit(solution)/shard_map/ppermute | solution.py:38
  24.8 5.0 %collective-permute-start.4 = (bf16[2,128,512]{2,1,0:T(8,128)(2,1)S(1)}, bf16[2,128,512]{2,1,0:T(8,128)(2,1)S(1)}, u32[]{:S(2)}, u32[]{:S(2)}) collective-permute-start(bf16[2,128,512]{2,1,0:T(8,128)(2,1)S(1)} %collective-permute-done.2.refs_2_), channel_id=1, source_target_pairs={{0,1},{1,0},{2,3},{3,2},{4,5},{5,4},{6,7},{7,6},{8,9},{9,8},{10,11... | collective-permute-start | bytes 786440 | tf_op jit(solution)/shard_map/ppermute | solution.py:38
  29.1 1.5 %collective-permute-start.7 = (bf16[2,128,512]{2,1,0:T(8,128)(2,1)S(1)}, bf16[2,128,512]{2,1,0:T(8,128)(2,1)S(1)}, u32[]{:S(2)}, u32[]{:S(2)}) collective-permute-start(bf16[2,128,512]{2,1,0:T(8,128)(2,1)S(1)} %collective-permute-done.5.refs_6_), channel_id=1, source_target_pairs={{0,1},{1,0},{2,3},{3,2},{4,5},{5,4},{6,7},{7,6},{8,9},{9,8},{10,11... | collective-permute-start | bytes 786440 | tf_op jit(solution)/shard_map/ppermute | solution.py:38
  53.5 2.4 %collective-permute-start.8 = (bf16[4,2,3,64,256]{4,3,2,1,0:T(8,128)(2,1)S(1)}, bf16[4,2,3,64,256]{4,3,2,1,0:T(8,128)(2,1)S(1)}, u32[]{:S(2)}, u32[]{:S(2)}) collective-permute-start(bf16[4,2,3,64,256]{4,3,2,1,0:T(8,128)(2,1)S(1)} %get-tuple-element.59), channel_id=1, source_target_pairs={{0,1},{1,0},{2,3},{3,2},{4,5},{5,4},{6,7},{7,6},{8,9},{9,8},{10,11... | collective-permute-start | bytes 2359304 | tf_op jit(solution)/shard_map/ppermute | solution.py:38
  66.4 4.4 %collective-permute-start.13 = (bf16[1,2,4,128,128]{4,3,2,1,0:T(8,128)(2,1)}, bf16[1,2,4,128,128]{4,3,2,1,0:T(8,128)(2,1)}, u32[]{:S(2)}, u32[]{:S(2)}) collective-permute-start(bf16[1,2,4,128,128]{4,3,2,1,0:T(8,128)(2,1)} %get-tuple-element.70), channel_id=1, source_target_pairs={{0,1},{1,0},{2,3},{3,2},{4,5},{5,4},{6,7},{7,6},{8,9},{9,8},{10,11... | collective-permute-start | bytes 786440 | tf_op jit(solution)/shard_map/ppermute | solution.py:38
  66.6 30.4 %all-to-all-start = ((bf16[4,2,192,256]{3,2,1,0:T(8,128)(2,1)}), bf16[4,2,192,256]{3,2,1,0:T(8,128)(2,1)S(1)}, u32[]{:S(2)}, u32[]{:S(2)}) async-start(bf16[4,2,192,256]{3,2,1,0:T(8,128)(2,1)} %bitcast.31), calls=%async_computation | async-start | bytes 1572864 | tf_op jit(solution)/shard_map/all_to_all | solution.py:597
  70.6 3.2 %collective-permute-start.12 = (bf16[1,2,4,128,128]{4,3,2,1,0:T(8,128)(2,1)}, bf16[1,2,4,128,128]{4,3,2,1,0:T(8,128)(2,1)S(1)}, u32[]{:S(2)}, u32[]{:S(2)}) collective-permute-start(bf16[1,2,4,128,128]{4,3,2,1,0:T(8,128)(2,1)} %copy-done.10), channel_id=1, source_target_pairs={{0,1},{1,0},{2,3},{3,2},{4,5},{5,4},{6,7},{7,6},{8,9},{9,8},{10,11... | collective-permute-start | bytes 786440 | tf_op jit(solution)/shard_map/ppermute | solution.py:38
  72.0 8.6 %collective-permute-start.14 = (bf16[1,2,4,128,128]{4,3,2,1,0:T(8,128)(2,1)S(1)}, bf16[1,2,4,128,128]{4,3,2,1,0:T(8,128)(2,1)S(1)}, u32[]{:S(2)}, u32[]{:S(2)}) collective-permute-start(bf16[1,2,4,128,128]{4,3,2,1,0:T(8,128)(2,1)S(1)} %add_convert_fusion.4), channel_id=1, source_target_pairs={{0,2},{1,3},{2,0},{3,1},{4,6},{5,7},{6,4},{7,5},{8,10},{9,11},{10,... | collective-permute-start | bytes 786440 | tf_op jit(solution)/shard_map/ppermute | solution.py:38
  73.2 8.1 %collective-permute-start.11 = (bf16[1,2,4,128,128]{4,3,2,1,0:T(8,128)(2,1)}, bf16[1,2,4,128,128]{4,3,2,1,0:T(8,128)(2,1)S(1)}, u32[]{:S(2)}, u32[]{:S(2)}) collective-permute-start(bf16[1,2,4,128,128]{4,3,2,1,0:T(8,128)(2,1)} %copy-done.9), channel_id=1, source_target_pairs={{0,1},{1,0},{2,3},{3,2},{4,5},{5,4},{6,7},{7,6},{8,9},{9,8},{10,11... | collective-permute-start | bytes 786440 | tf_op jit(solution)/shard_map/ppermute | solution.py:38
  73.2 11.6 %collective-permute-start.10 = (bf16[1,2,4,128,128]{4,3,2,1,0:T(8,128)(2,1)}, bf16[1,2,4,128,128]{4,3,2,1,0:T(8,128)(2,1)S(1)}, u32[]{:S(2)}, u32[]{:S(2)}) collective-permute-start(bf16[1,2,4,128,128]{4,3,2,1,0:T(8,128)(2,1)} %copy-done.8), channel_id=1, source_target_pairs={{0,1},{1,0},{2,3},{3,2},{4,5},{5,4},{6,7},{7,6},{8,9},{9,8},{10,11... | collective-permute-start | bytes 786440 | tf_op jit(solution)/shard_map/ppermute | solution.py:38
  81.4 7.7 %collective-permute-start.15 = (bf16[1,2,4,128,128]{4,3,2,1,0:T(8,128)(2,1)S(1)}, bf16[1,2,4,128,128]{4,3,2,1,0:T(8,128)(2,1)S(1)}, u32[]{:S(2)}, u32[]{:S(2)}) collective-permute-start(bf16[1,2,4,128,128]{4,3,2,1,0:T(8,128)(2,1)S(1)} %add_convert_fusion.2), channel_id=1, source_target_pairs={{0,2},{1,3},{2,0},{3,1},{4,6},{5,7},{6,4},{7,5},{8,10},{9,11},{10,... | collective-permute-start | bytes 786440 | tf_op jit(solution)/shard_map/ppermute | solution.py:38
  82.4 28.0 %collective-permute-start.9 = (bf16[1,2,4,128,128]{4,3,2,1,0:T(8,128)(2,1)}, bf16[1,2,4,128,128]{4,3,2,1,0:T(8,128)(2,1)S(1)}, u32[]{:S(2)}, u32[]{:S(2)}) collective-permute-start(bf16[1,2,4,128,128]{4,3,2,1,0:T(8,128)(2,1)} %get-tuple-element.62), channel_id=1, source_target_pairs={{0,1},{1,0},{2,3},{3,2},{4,5},{5,4},{6,7},{7,6},{8,9},{9,8},{10,11... | collective-permute-start | bytes 786440 | tf_op jit(solution)/shard_map/ppermute | solution.py:38
  82.4 24.8 %collective-permute-start.18 = (bf16[1,2,4,128,128]{4,3,2,1,0:T(8,128)(2,1)}, bf16[1,2,4,128,128]{4,3,2,1,0:T(8,128)(2,1)S(1)}, u32[]{:S(2)}, u32[]{:S(2)}) collective-permute-start(bf16[1,2,4,128,128]{4,3,2,1,0:T(8,128)(2,1)} %get-tuple-element.74), channel_id=1, source_target_pairs={{0,1},{1,0},{2,3},{3,2},{4,5},{5,4},{6,7},{7,6},{8,9},{9,8},{10,11... | collective-permute-start | bytes 786440 | tf_op jit(solution)/shard_map/ppermute | solution.py:38
  82.9 24.3 %collective-permute-start.17 = (bf16[2,4,128,128]{3,2,1,0:T(8,128)(2,1)}, bf16[2,4,128,128]{3,2,1,0:T(8,128)(2,1)}, u32[]{:S(2)}, u32[]{:S(2)}) collective-permute-start(bf16[2,4,128,128]{3,2,1,0:T(8,128)(2,1)} %fusion.1), channel_id=1, source_target_pairs={{0,4},{4,8},{8,12},{12,0},{1,5},{5,9},{9,13},{13,1},{2,6},{6,10},{... | collective-permute-start | bytes 786440 | tf_op jit(solution)/shard_map/ppermute | solution.py:33
  97.1 4.7 %collective-permute-start.20 = (bf16[1,192,256]{2,1,0:T(8,128)(2,1)S(1)}, bf16[1,192,256]{2,1,0:T(8,128)(2,1)S(1)}, u32[]{:S(2)}, u32[]{:S(2)}) collective-permute-start(bf16[1,192,256]{2,1,0:T(8,128)(2,1)S(1)} %fusion.2), channel_id=1, source_target_pairs={{0,2},{1,3},{2,0},{3,1},{4,6},{5,7},{6,4},{7,5},{8,10},{9,11},{10,... | collective-permute-start | bytes 294920 | tf_op jit(solution)/shard_map/ppermute | solution.py:38
  102.5 19.4 %all-to-all-start.1 = ((bf16[4,192,256]{2,1,0:T(8,128)(2,1)}), bf16[4,192,256]{2,1,0:T(8,128)(2,1)S(1)}, u32[]{:S(2)}, u32[]{:S(2)}) async-start(bf16[4,192,256]{2,1,0:T(8,128)(2,1)} %copies.1), calls=%async_computation.1 | async-start | bytes 786432 | tf_op jit(solution)/shard_map/all_to_all | solution.py:617
  106.1 6.5 %collective-permute-start.16 = (bf16[1,2,4,128,128]{4,3,2,1,0:T(8,128)(2,1)S(1)}, bf16[1,2,4,128,128]{4,3,2,1,0:T(8,128)(2,1)S(1)}, u32[]{:S(2)}, u32[]{:S(2)}) collective-permute-start(bf16[1,2,4,128,128]{4,3,2,1,0:T(8,128)(2,1)S(1)} %add_convert_fusion.1), channel_id=1, source_target_pairs={{0,2},{1,3},{2,0},{3,1},{4,6},{5,7},{6,4},{7,5},{8,10},{9,11},{10,... | collective-permute-start | bytes 786440 | tf_op jit(solution)/shard_map/ppermute | solution.py:38
  108.3 12.6 %collective-permute-start.19 = (bf16[2,4,128,128]{3,2,1,0:T(8,128)(2,1)S(1)}, bf16[2,4,128,128]{3,2,1,0:T(8,128)(2,1)S(1)}, u32[]{:S(2)}, u32[]{:S(2)}) collective-permute-start(bf16[2,4,128,128]{3,2,1,0:T(8,128)(2,1)S(1)} %fusion), channel_id=1, source_target_pairs={{0,4},{4,8},{8,12},{12,0},{1,5},{5,9},{9,13},{13,1},{2,6},{6,10},{... | collective-permute-start | bytes 786440 | tf_op jit(solution)/shard_map/ppermute | solution.py:33
  (12 other events, 98.8 us)

commit v11 on v5

--- a/solution.py
+++ b/solution.py
@@ -152,7 +152,7 @@
         one_hot(by_position, 0), coef_in[...], (((1,), (1,)), ((), ())),
         precision=lax.Precision.HIGHEST, preferred_element_type=jnp.float32,
     )
-    high, low = two_terms(diagonals(exact(spread, one_hot(by_mode[::-1], 1))))
+    high, low = two_terms(diagonals(0.5 * exact(spread, one_hot(by_mode[::-1], 1))))
     weights[...] = jnp.concatenate([high, low], 1)
     eig_copy.wait()
 
@@ -204,7 +204,7 @@
                     ]
                     block = [jnp.where(keep_lane, rolled[b], rolled[b + 1]) for b in range(2)]
                     total = block if total is None else [x + y for x, y in zip(total, block)]
-                parts.append([0.5 * x for x in total])
+                parts.append(total)
             for b in range(2):
                 cols = slice(b * LANES, (b + 1) * LANES)
                 o_re, o_im = parts[0][b], parts[1][b]
@@ -244,8 +244,8 @@
                 high = d.astype(jnp.bfloat16)
                 d_high[j, c, rows] = high
                 d_low[j, c, rows] = (d - high.astype(jnp.float32)).astype(jnp.bfloat16)
-            probe[j, 0, rows] = 0.5 * (p_re * b_re + p_im * b_im)
-            probe[j, 1, rows] = 0.5 * (p_re * b_im - p_im * b_re)
+            probe[j, 0, rows] = p_re * b_re + p_im * b_im
+            probe[j, 1, rows] = p_re * b_im - p_im * b_re
 
     def grad_copy(j):
         return pltpu.make_async_copy(probe.at[j], grads_out.at[j], grad_sem.at[j])
@@ -291,7 +291,7 @@
             e = eig[:, c, rows, :].reshape(modes * STRIP, frame)
             both = jnp.dot(weights_t[...], high, preferred_element_type=jnp.float32)
             rest = jnp.dot(weights_t[:modes * STRIP], low, preferred_element_type=jnp.float32)
-            grad = (both[:modes * STRIP] + both[modes * STRIP:] + rest) * scale
+            grad = (both[:modes * STRIP] + both[modes * STRIP:] + rest) * (0.5 * scale)
             for k in range(modes):
                 group = 2 * k + c
                 if share:
@@ -320,7 +320,7 @@
     coef[...] = lax.dot_general(
         one_hot(by_mode[::-1], 1), total, (((1,), (1,)), ((), ())),
         precision=lax.Precision.HIGHEST, preferred_element_type=jnp.float32,
-    ) * (1.0 / frame)
+    ) * (0.5 / frame)
 
     def drain(j, carry):
         grad_copy(j).wait()
@@ -507,32 +507,40 @@
         bit *= 2
 
 
+def add_up_kernel(own, *refs):
+    arrived, out = refs[:-1], refs[-1]
+    total = own[...]
+    for term in arrived:
+        total += term[...].astype(jnp.float32)
+    total = total.astype(jnp.bfloat16)
+    for i in range(out.shape[0]):
+        out[i] = total
+
+
+def widen_kernel(array, out):
+    out[...] = array[...].astype(jnp.float32)
+
+
+def small_call(kernel, shape, kind, name, *arrays):
+    return pl.pallas_call(
+        kernel,
+        in_specs=[pl.BlockSpec(memory_space=VMEM)] * len(arrays),
+        out_specs=pl.BlockSpec(memory_space=VMEM),
+        out_shape=jax.ShapeDtypeStruct(shape, kind),
+        compiler_params=pltpu.CompilerParams(vmem_limit_bytes=8 * 1024 * 1024),
+        name=name,
+    )(*arrays)
+
+
 def scatter_sum(axis, value, relative):
-    me = lax.axis_index(axis)
+    peers, me = lax.axis_size(axis), lax.axis_index(axis)
     share = (lambda i: value[i]) if relative else (lambda i: lax.dynamic_index_in_dim(value, me ^ i, 0, False))
-    total = share(0)
-    sent = [share(i).astype(jnp.bfloat16) for i in range(1, lax.axis_size(axis))]
-    for i, sending in enumerate(sent, 1):
-        total += swap(sending, axis, i).astype(jnp.float32)
-    return total.astype(jnp.bfloat16), sent
-
-
-def place_kernel(axis, *refs):
-    pieces, out = refs[:-1], refs[-1]
-    me = lax.axis_index(axis)
-    for i, piece in enumerate(pieces):
-        out[me ^ i] = piece[...].astype(jnp.float32)
-
-
-def place(axis, held):
-    return pl.pallas_call(
-        functools.partial(place_kernel, axis),
-        in_specs=[pl.BlockSpec(memory_space=VMEM)] * len(held),
-        out_specs=pl.BlockSpec(memory_space=VMEM),
-        out_shape=jax.ShapeDtypeStruct((len(held),) + held[0].shape, jnp.float32),
-        compiler_params=pltpu.CompilerParams(vmem_limit_bytes=8 * 1024 * 1024),
-        name="place",
-    )(*held)
+    sent = [share(i).astype(jnp.bfloat16) for i in range(1, peers)]
+    arrived = [swap(sending, axis, i) for i, sending in enumerate(sent, 1)]
+    total = small_call(
+        add_up_kernel, (peers,) + value.shape[1:], jnp.bfloat16, "add_up", share(0), *arrived
+    )
+    return total, sent
 
 
 def finish_kernel(first, second, out):
@@ -597,15 +605,16 @@
     total, sent = scatter_sum("blk", eigen.reshape(blocks, -1, frame), relative)
     mine, leaving, _ = halve(keep[last], send[last], before_cross=sent)
     moving = after(mine.astype(jnp.bfloat16), total)
+    gate = moving
     for section in range(last - 1, -1, -1):
-        mine, leaving, _ = halve(keep[section], send[section], before_cross=(moving,))
+        mine, leaving, gate = halve(keep[section], send[section], before_cross=(gate,))
         if section == last - 1:
             total = after(total, leaving)
         arrived = shift(moving, "blk", 1)
         if section > 0:
             moving = (arrived.astype(jnp.float32) + mine).astype(jnp.bfloat16)
-    gathered = [swap(total, "blk", i) for i in range(1, blocks)]
-    eigen_share = place("blk", [after(total, arrived)] + gathered)
+    gathered = lax.all_to_all(total, "blk", 0, 0)
+    eigen_share = small_call(widen_kernel, gathered.shape, jnp.float32, "widen", gathered)
     eigen_share = eigen_share.reshape(modes, 2, frame // shares, frame)
     summed = finish(mine, arrived)
     return (summed[None], eigen_share, coef_rows.T)

time: 106 us -> 104 us (0.981)
  waiting for transfers between devices: 42.4 us -> 37.3 us
  other arithmetic: 0.85 us -> 2.59 us
  starting transfers between devices: 28 us -> 29.2 us
    ppermute x24 -> x21, waiting for transfers between devices: 25.2 us -> 20.4 us  [swap(): return lax.ppermute(array, axis, [(i, i ^ bit) for i in range(peers)])]
    all_to_all x0 -> x1, starting transfers between devices: none -> 3.47 us  [on_device(): gathered = lax.all_to_all(total, 'blk', 0, 0)]
    ppermute x24 -> x21, starting transfers between devices: 17.2 us -> 14.2 us  [swap(): return lax.ppermute(array, axis, [(i, i ^ bit) for i in range(peers)])]
    ppermute x4, waiting for transfers between devices: 17.1 us -> 15.9 us  [shift(): lax.ppermute(array, axis, [(i, (i + by) % peers) for i in range(peers)])]
    all_to_all x0 -> x1, waiting for transfers between devices: none -> 1.1 us  [on_device(): gathered = lax.all_to_all(total, 'blk', 0, 0)]
    convert_element_type x1, other arithmetic: 0.14 us -> 1.23 us  [on_device(): moving = (arrived.astype(jnp.float32) + mine).astype(jnp.bfloat16)]
  transfers between devices with their start and end apart: 28 -> 26, of which waited for: 15 -> 14; matrix products, arithmetic and copies ran while one was open for 1% -> 3% of each run, Pallas kernels for 7% -> 8%
where the time goes in v11:
time: 104 us
  waiting for transfers between devices  37.3 us (36%)
  Pallas kernels  29.3 us (28%)
  starting transfers between devices  29.2 us (28%)
  local copies, waits for them, and re-layouts  3.77 us (4%)
  other arithmetic  2.59 us (2%)
  between operations  1.52 us (1%)
    pallas_call x1, Pallas kernels, positions(): pl.pallas_call(functools.partial(position_kernel, offs, scale), in_specs=...  20.4 us
    ppermute x21, waiting for transfers between devices, swap(): return lax.ppermute(array, axis, [(i, i ^ bit) for i in range(peers)])  20.4 us
    ppermute x4, waiting for transfers between devices, shift(): lax.ppermute(array, axis, [(i, (i + by) % peers) for i in range(peers)])  15.9 us
    ppermute x21, starting transfers between devices, swap(): return lax.ppermute(array, axis, [(i, i ^ bit) for i in range(peers)])  14.2 us
    ppermute x4, starting transfers between devices, shift(): lax.ppermute(array, axis, [(i, (i + by) % peers) for i in range(peers)])  11.5 us
    pallas_call x1, Pallas kernels, scatter(): pl.pallas_call(functools.partial(scatter_kernel, shares), in_specs=[pl.Bl...  5.88 us
    all_to_all x1, starting transfers between devices, on_device(): gathered = lax.all_to_all(total, 'blk', 0, 0)  3.47 us
    unnamed x14, local copies, waits for them, and re-layouts  2.75 us
  transfers between devices with their start and end apart: 26, of which 14 were waited for; matrix products, arithmetic and copies ran while one was open for 3% of the time, Pallas kernels for 8%

profile of v11, /device:TPU:0, one launch (start us, length us, event | category | flops | bytes accessed | tf_op | source)
XLA Modules:
  0.0 103.7 jit_solution(14210823689283497337)
XLA Ops:
  1.7 5.1 %collective-permute-start = (bf16[2,128,512]{2,1,0:T(8,128)(2,1)S(1)}, bf16[2,128,512]{2,1,0:T(8,128)(2,1)S(1)}, u32[]{:S(2)}, u32[]{:S(2)}) collective-permute-start(bf16[2,128,512]{2,1,0:T(8,128)(2,1)S(1)} %dynamic-slice_bitcast_fusion), channel_id=1, source_target_pairs={{0,12},{4,0},{8,4},{12,8},{1,13},{5,1},{9,5},{13,9},{2,14},{6,2},{... | collective-permute-start | bytes 786440 | tf_op jit(solution)/shard_map/ppermute | solution.py:33
  6.8 5.6 %collective-permute-done.refs_1_ = bf16[2,128,512]{2,1,0:T(8,128)(2,1)S(1)} collective-permute-done((bf16[2,128,512]{2,1,0:T(8,128)(2,1)S(1)}, bf16[2,128,512]{2,1,0:T(8,128)(2,1)S(1)}, u32[]{:S(2)}, u32[]{:S(2)}) %collective-permute-start) | collective-permute-done | bytes 262176 | tf_op jit(solution)/shard_map/ppermute | solution.py:33
  12.3 4.3 %collective-permute-start.1 = (bf16[2,128,512]{2,1,0:T(8,128)(2,1)S(1)}, bf16[2,128,512]{2,1,0:T(8,128)(2,1)S(1)}, u32[]{:S(2)}, u32[]{:S(2)}) collective-permute-start(bf16[2,128,512]{2,1,0:T(8,128)(2,1)S(1)} %collective-permute-done.refs_1_), channel_id=1, source_target_pairs={{0,12},{4,0},{8,4},{12,8},{1,13},{5,1},{9,5},{13,9},{2,14},{6,2},{... | collective-permute-start | bytes 786440 | tf_op jit(solution)/shard_map/ppermute | solution.py:33
  16.6 1.5 %collective-permute-start.2 = (bf16[2,128,512]{2,1,0:T(8,128)(2,1)S(1)}, bf16[2,128,512]{2,1,0:T(8,128)(2,1)S(1)}, u32[]{:S(2)}, u32[]{:S(2)}) collective-permute-start(bf16[2,128,512]{2,1,0:T(8,128)(2,1)S(1)} %collective-permute-done.refs_1_), channel_id=1, source_target_pairs={{0,2},{1,3},{2,0},{3,1},{4,6},{5,7},{6,4},{7,5},{8,10},{9,11},{10,... | collective-permute-start | bytes 786440 | tf_op jit(solution)/shard_map/ppermute | solution.py:38
  18.1 1.4 %copy-done.1 = bf16[6,2,256,256]{3,2,1,0:T(8,128)(2,1)S(1)} copy-done((bf16[6,2,256,256]{3,2,1,0:T(8,128)(2,1)S(1)}, bf16[6,2,256,256]{3,2,1,0:T(8,128)(2,1)}, u32[]{:S(2)}) %copy-start.1) | copy-done | bytes 1572888
  19.5 1.3 %copy-done.2 = bf16[10,256,256]{2,1,0:T(8,128)(2,1)S(1)} copy-done((bf16[10,256,256]{2,1,0:T(8,128)(2,1)S(1)}, bf16[10,256,256]{2,1,0:T(8,128)(2,1)}, u32[]{:S(2)}) %copy-start.2) | copy-done | bytes 1310744
  21.3 1.5 %collective-permute-start.5 = (bf16[2,128,512]{2,1,0:T(8,128)(2,1)S(1)}, bf16[2,128,512]{2,1,0:T(8,128)(2,1)S(1)}, u32[]{:S(2)}, u32[]{:S(2)}) collective-permute-start(bf16[2,128,512]{2,1,0:T(8,128)(2,1)S(1)} %collective-permute-done.1.refs_5_), channel_id=1, source_target_pairs={{0,2},{1,3},{2,0},{3,1},{4,6},{5,7},{6,4},{7,5},{8,10},{9,11},{10,... | collective-permute-start | bytes 786440 | tf_op jit(solution)/shard_map/ppermute | solution.py:38
  23.3 1.5 %collective-permute-done.2.refs_2_ = bf16[2,128,512]{2,1,0:T(8,128)(2,1)S(1)} collective-permute-done((bf16[2,128,512]{2,1,0:T(8,128)(2,1)S(1)}, bf16[2,128,512]{2,1,0:T(8,128)(2,1)S(1)}, u32[]{:S(2)}, u32[]{:S(2)}) %collective-permute-start.2) | collective-permute-done | bytes 262176 | tf_op jit(solution)/shard_map/ppermute | solution.py:38
  25.1 4.1 %collective-permute-done.5.refs_6_ = bf16[2,128,512]{2,1,0:T(8,128)(2,1)S(1)} collective-permute-done((bf16[2,128,512]{2,1,0:T(8,128)(2,1)S(1)}, bf16[2,128,512]{2,1,0:T(8,128)(2,1)S(1)}, u32[]{:S(2)}, u32[]{:S(2)}) %collective-permute-start.5) | collective-permute-done | bytes 262176 | tf_op jit(solution)/shard_map/ppermute | solution.py:38
  30.7 20.4 %positions.1 = (bf16[1,12,64,256]{3,2,1,0:T(8,128)(2,1)S(1)}, bf16[1,12,64,256]{3,2,1,0:T(8,128)(2,1)S(1)}, f32[1,12,64,256]{3,2,1,0:T(8,128)S(1)}, f32[1,12,64,...) custom-call(s32[2,10]{1,0:T(2,128)S(1)} %get-tuple-element.53.tile_list, ...), custom_call_target="tpu_custom_call" | custom-call | tf_op jit(solution)/shard_map/positions/pallas_call | solution.py:346
  53.0 1.5 %collective-permute-start.15 = (bf16[1,12,64,256]{3,2,1,0:T(8,128)(2,1)S(1)}, bf16[1,12,64,256]{3,2,1,0:T(8,128)(2,1)S(1)}, u32[]{:S(2)}, u32[]{:S(2)}) collective-permute-start(bf16[1,12,64,256]{3,2,1,0:T(8,128)(2,1)S(1)} %add_convert_fusion), channel_id=1, source_target_pairs={{0,2},{1,3},{2,0},{3,1},{4,6},{5,7},{6,4},{7,5},{8,10},{9,11},{10,... | collective-permute-start | bytes 1179656 | tf_op jit(solution)/shard_map/ppermute | solution.py:38
  54.5 5.9 %scatter.1 = (bf16[1,2,4,128,128]{4,3,2,1,0:T(8,128)(2,1)S(1)}, bf16[1,2,4,128,128]{4,3,2,1,0:T(8,128)(2,1)S(1)}, bf16[1,2,4,128,128]{4,3,2,1,0:T(8,128)(2,1)S(1...) custom-call(s32[2,10]{1,0:T(2,128)S(1)} %get-tuple-element.53.tile_l, ...), custom_call_target="tpu_custom_call" | custom-call | flops 16777216 | bytes 16777216 | tf_op jit(solution)/shard_map/scatter/pallas_call | solution.py:467
  61.0 3.2 %collective-permute-done.15 = bf16[1,12,64,256]{3,2,1,0:T(8,128)(2,1)S(1)} collective-permute-done((bf16[1,12,64,256]{3,2,1,0:T(8,128)(2,1)S(1)}, bf16[1,12,64,256]{3,2,1,0:T(8,128)(2,1)S(1)}, u32[]{:S(2)}, u32[]{:S(2)}) %collective-permute-start.15) | collective-permute-done | bytes 393248 | tf_op jit(solution)/shard_map/ppermute | solution.py:38
  64.5 1.6 %collective-permute-start.16 = (bf16[1,2,4,128,128]{4,3,2,1,0:T(8,128)(2,1)S(1)}, bf16[1,2,4,128,128]{4,3,2,1,0:T(8,128)(2,1)S(1)}, u32[]{:S(2)}, u32[]{:S(2)}) collective-permute-start(bf16[1,2,4,128,128]{4,3,2,1,0:T(8,128)(2,1)S(1)} %add_convert_fusion.4), channel_id=1, source_target_pairs={{0,2},{1,3},{2,0},{3,1},{4,6},{5,7},{6,4},{7,5},{8,10},{9,11},{10,... | collective-permute-start | bytes 786440 | tf_op jit(solution)/shard_map/ppermute | solution.py:38
  66.1 1.6 %collective-permute-start.19 = (bf16[192,256]{1,0:T(8,128)(2,1)S(1)}, bf16[192,256]{1,0:T(8,128)(2,1)S(1)}, u32[]{:S(2)}, u32[]{:S(2)}) collective-permute-start(bf16[192,256]{1,0:T(8,128)(2,1)S(1)} %bitcast.29), channel_id=1, source_target_pairs={{0,12},{4,8},{8,4},{12,0},{1,13},{5,9},{9,5},{13,1},{2,14},{6,10},... | collective-permute-start | bytes 294920 | tf_op jit(solution)/shard_map/ppermute | solution.py:38
  67.7 1.9 %collective-permute-start.17 = (bf16[192,256]{1,0:T(8,128)(2,1)S(1)}, bf16[192,256]{1,0:T(8,128)(2,1)S(1)}, u32[]{:S(2)}, u32[]{:S(2)}) collective-permute-start(bf16[192,256]{1,0:T(8,128)(2,1)S(1)} %bitcast.28), channel_id=1, source_target_pairs={{0,4},{4,0},{8,12},{12,8},{1,5},{5,1},{9,13},{13,9},{2,6},{6,2},{1... | collective-permute-start | bytes 294920 | tf_op jit(solution)/shard_map/ppermute | solution.py:38
  69.6 5.0 %collective-permute-done.18.refs_1_ = bf16[192,256]{1,0:T(8,128)(2,1)S(1)} collective-permute-done((bf16[192,256]{1,0:T(8,128)(2,1)S(1)}, bf16[192,256]{1,0:T(8,128)(2,1)S(1)}, u32[]{:S(2)}, u32[]{:S(2)}) %collective-permute-start.18) | collective-permute-done | bytes 98336 | tf_op jit(solution)/shard_map/ppermute | solution.py:38
  78.2 1.8 %collective-permute-start.22 = (bf16[2,4,128,128]{3,2,1,0:T(8,128)(2,1)S(1)}, bf16[2,4,128,128]{3,2,1,0:T(8,128)(2,1)}, u32[]{:S(2)}, u32[]{:S(2)}) collective-permute-start(bf16[2,4,128,128]{3,2,1,0:T(8,128)(2,1)S(1)} %fusion.1), channel_id=1, source_target_pairs={{0,4},{4,8},{8,12},{12,0},{1,5},{5,9},{9,13},{13,1},{2,6},{6,10},{... | collective-permute-start | bytes 786440 | tf_op jit(solution)/shard_map/ppermute | solution.py:33
  80.1 3.5 %all-to-all-start = ((bf16[4,192,256]{2,1,0:T(8,128)(2,1)}), bf16[4,192,256]{2,1,0:T(8,128)(2,1)S(1)}, u32[]{:S(2)}, u32[]{:S(2)}) async-start(bf16[4,192,256]{2,1,0:T(8,128)(2,1)} %add_up.1), calls=%async_computation | async-start | bytes 786432 | tf_op jit(solution)/shard_map/all_to_all | solution.py:616
  83.5 2.0 %collective-permute-done.20 = bf16[1,2,4,128,128]{4,3,2,1,0:T(8,128)(2,1)} collective-permute-done((bf16[1,2,4,128,128]{4,3,2,1,0:T(8,128)(2,1)}, bf16[1,2,4,128,128]{4,3,2,1,0:T(8,128)(2,1)}, u32[]{:S(2)}, u32[]{:S(2)}) %collective-permute-start.20) | collective-permute-done | bytes 262176 | tf_op jit(solution)/shard_map/ppermute | solution.py:38
  85.6 1.3 %collective-permute-start.21 = (bf16[1,2,4,128,128]{4,3,2,1,0:T(8,128)(2,1)S(1)}, bf16[1,2,4,128,128]{4,3,2,1,0:T(8,128)(2,1)S(1)}, u32[]{:S(2)}, u32[]{:S(2)}) collective-permute-start(bf16[1,2,4,128,128]{4,3,2,1,0:T(8,128)(2,1)S(1)} %add_convert_fusion.1), channel_id=1, source_target_pairs={{0,2},{1,3},{2,0},{3,1},{4,6},{5,7},{6,4},{7,5},{8,10},{9,11},{10,... | collective-permute-start | bytes 786440 | tf_op jit(solution)/shard_map/ppermute | solution.py:38
  86.8 2.2 %collective-permute-done.22 = bf16[2,4,128,128]{3,2,1,0:T(8,128)(2,1)} collective-permute-done((bf16[2,4,128,128]{3,2,1,0:T(8,128)(2,1)S(1)}, bf16[2,4,128,128]{3,2,1,0:T(8,128)(2,1)}, u32[]{:S(2)}, u32[]{:S(2)}) %collective-permute-start.22) | collective-permute-done | bytes 262176 | tf_op jit(solution)/shard_map/ppermute | solution.py:33
  90.6 2.3 %collective-permute-done.21 = bf16[1,2,4,128,128]{4,3,2,1,0:T(8,128)(2,1)S(1)} collective-permute-done((bf16[1,2,4,128,128]{4,3,2,1,0:T(8,128)(2,1)S(1)}, bf16[1,2,4,128,128]{4,3,2,1,0:T(8,128)(2,1)S(1)}, u32[]{:S(2)}, u32[]{:S(2)}) %collective-permute-start.21) | collective-permute-done | bytes 262176 | tf_op jit(solution)/shard_map/ppermute | solution.py:38
  93.0 7.8 %collective-permute-done.24.second = bf16[2,4,128,128]{3,2,1,0:T(8,128)(2,1)S(1)} collective-permute-done((bf16[2,4,128,128]{3,2,1,0:T(8,128)(2,1)S(1)}, bf16[2,4,128,128]{3,2,1,0:T(8,128)(2,1)S(1)}, u32[]{:S(2)}, u32[]{:S(2)}) %collective-permute-start.24) | collective-permute-done | bytes 262176 | tf_op jit(solution)/shard_map/ppermute | solution.py:33
  (60 shorter events, 14.0 us)
Async XLA Ops:
  1.7 10.7 %collective-permute-start = (bf16[2,128,512]{2,1,0:T(8,128)(2,1)S(1)}, bf16[2,128,512]{2,1,0:T(8,128)(2,1)S(1)}, u32[]{:S(2)}, u32[]{:S(2)}) collective-permute-start(bf16[2,128,512]{2,1,0:T(8,128)(2,1)S(1)} %dynamic-slice_bitcast_fusion), channel_id=1, source_target_pairs={{0,12},{4,0},{8,4},{12,8},{1,13},{5,1},{9,5},{13,9},{2,14},{6,2},{... | collective-permute-start | bytes 786440 | tf_op jit(solution)/shard_map/ppermute | solution.py:33
  12.3 9.0 %collective-permute-start.1 = (bf16[2,128,512]{2,1,0:T(8,128)(2,1)S(1)}, bf16[2,128,512]{2,1,0:T(8,128)(2,1)S(1)}, u32[]{:S(2)}, u32[]{:S(2)}) collective-permute-start(bf16[2,128,512]{2,1,0:T(8,128)(2,1)S(1)} %collective-permute-done.refs_1_), channel_id=1, source_target_pairs={{0,12},{4,0},{8,4},{12,8},{1,13},{5,1},{9,5},{13,9},{2,14},{6,2},{... | collective-permute-start | bytes 786440 | tf_op jit(solution)/shard_map/ppermute | solution.py:33
  16.6 8.2 %collective-permute-start.2 = (bf16[2,128,512]{2,1,0:T(8,128)(2,1)S(1)}, bf16[2,128,512]{2,1,0:T(8,128)(2,1)S(1)}, u32[]{:S(2)}, u32[]{:S(2)}) collective-permute-start(bf16[2,128,512]{2,1,0:T(8,128)(2,1)S(1)} %collective-permute-done.refs_1_), channel_id=1, source_target_pairs={{0,2},{1,3},{2,0},{3,1},{4,6},{5,7},{6,4},{7,5},{8,10},{9,11},{10,... | collective-permute-start | bytes 786440 | tf_op jit(solution)/shard_map/ppermute | solution.py:38
  21.3 7.8 %collective-permute-start.5 = (bf16[2,128,512]{2,1,0:T(8,128)(2,1)S(1)}, bf16[2,128,512]{2,1,0:T(8,128)(2,1)S(1)}, u32[]{:S(2)}, u32[]{:S(2)}) collective-permute-start(bf16[2,128,512]{2,1,0:T(8,128)(2,1)S(1)} %collective-permute-done.1.refs_5_), channel_id=1, source_target_pairs={{0,2},{1,3},{2,0},{3,1},{4,6},{5,7},{6,4},{7,5},{8,10},{9,11},{10,... | collective-permute-start | bytes 786440 | tf_op jit(solution)/shard_map/ppermute | solution.py:38
  22.8 7.0 %collective-permute-start.3 = (bf16[2,128,512]{2,1,0:T(8,128)(2,1)S(1)}, bf16[2,128,512]{2,1,0:T(8,128)(2,1)S(1)}, u32[]{:S(2)}, u32[]{:S(2)}) collective-permute-start(bf16[2,128,512]{2,1,0:T(8,128)(2,1)S(1)} %collective-permute-done.refs_1_), channel_id=1, source_target_pairs={{0,1},{1,0},{2,3},{3,2},{4,5},{5,4},{6,7},{7,6},{8,9},{9,8},{10,11... | collective-permute-start | bytes 786440 | tf_op jit(solution)/shard_map/ppermute | solution.py:38
  22.8 7.0 %collective-permute-start.6 = (bf16[2,128,512]{2,1,0:T(8,128)(2,1)S(1)}, bf16[2,128,512]{2,1,0:T(8,128)(2,1)S(1)}, u32[]{:S(2)}, u32[]{:S(2)}) collective-permute-start(bf16[2,128,512]{2,1,0:T(8,128)(2,1)S(1)} %collective-permute-done.1.refs_5_), channel_id=1, source_target_pairs={{0,1},{1,0},{2,3},{3,2},{4,5},{5,4},{6,7},{7,6},{8,9},{9,8},{10,11... | collective-permute-start | bytes 786440 | tf_op jit(solution)/shard_map/ppermute | solution.py:38
  24.8 5.0 %collective-permute-start.4 = (bf16[2,128,512]{2,1,0:T(8,128)(2,1)S(1)}, bf16[2,128,512]{2,1,0:T(8,128)(2,1)S(1)}, u32[]{:S(2)}, u32[]{:S(2)}) collective-permute-start(bf16[2,128,512]{2,1,0:T(8,128)(2,1)S(1)} %collective-permute-done.2.refs_2_), channel_id=1, source_target_pairs={{0,1},{1,0},{2,3},{3,2},{4,5},{5,4},{6,7},{7,6},{8,9},{9,8},{10,11... | collective-permute-start | bytes 786440 | tf_op jit(solution)/shard_map/ppermute | solution.py:38
  51.1 1.8 %collective-permute-start.8 = (bf16[1,12,64,256]{3,2,1,0:T(8,128)(2,1)S(1)}, bf16[1,12,64,256]{3,2,1,0:T(8,128)(2,1)S(1)}, u32[]{:S(2)}, u32[]{:S(2)}) collective-permute-start(bf16[1,12,64,256]{3,2,1,0:T(8,128)(2,1)S(1)} %get-tuple-element.63), channel_id=1, source_target_pairs={{0,1},{1,0},{2,3},{3,2},{4,5},{5,4},{6,7},{7,6},{8,9},{9,8},{10,11... | collective-permute-start | bytes 1179656 | tf_op jit(solution)/shard_map/ppermute | solution.py:38
  51.3 9.7 %collective-permute-start.14 = (bf16[1,12,64,256]{3,2,1,0:T(8,128)(2,1)S(1)}, bf16[1,12,64,256]{3,2,1,0:T(8,128)(2,1)S(1)}, u32[]{:S(2)}, u32[]{:S(2)}) collective-permute-start(bf16[1,12,64,256]{3,2,1,0:T(8,128)(2,1)S(1)} %get-tuple-element.76), channel_id=1, source_target_pairs={{0,1},{1,0},{2,3},{3,2},{4,5},{5,4},{6,7},{7,6},{8,9},{9,8},{10,11... | collective-permute-start | bytes 1179656 | tf_op jit(solution)/shard_map/ppermute | solution.py:38
  53.0 11.2 %collective-permute-start.15 = (bf16[1,12,64,256]{3,2,1,0:T(8,128)(2,1)S(1)}, bf16[1,12,64,256]{3,2,1,0:T(8,128)(2,1)S(1)}, u32[]{:S(2)}, u32[]{:S(2)}) collective-permute-start(bf16[1,12,64,256]{3,2,1,0:T(8,128)(2,1)S(1)} %add_convert_fusion), channel_id=1, source_target_pairs={{0,2},{1,3},{2,0},{3,1},{4,6},{5,7},{6,4},{7,5},{8,10},{9,11},{10,... | collective-permute-start | bytes 1179656 | tf_op jit(solution)/shard_map/ppermute | solution.py:38
  60.4 15.7 %collective-permute-start.12 = (bf16[1,2,4,128,128]{4,3,2,1,0:T(8,128)(2,1)S(1)}, bf16[1,2,4,128,128]{4,3,2,1,0:T(8,128)(2,1)S(1)}, u32[]{:S(2)}, u32[]{:S(2)}) collective-permute-start(bf16[1,2,4,128,128]{4,3,2,1,0:T(8,128)(2,1)S(1)} %get-tuple-element.72), channel_id=1, source_target_pairs={{0,1},{1,0},{2,3},{3,2},{4,5},{5,4},{6,7},{7,6},{8,9},{9,8},{10,11... | collective-permute-start | bytes 786440 | tf_op jit(solution)/shard_map/ppermute | solution.py:38
  60.5 3.9 %collective-permute-start.13 = (bf16[1,2,4,128,128]{4,3,2,1,0:T(8,128)(2,1)S(1)}, bf16[1,2,4,128,128]{4,3,2,1,0:T(8,128)(2,1)S(1)}, u32[]{:S(2)}, u32[]{:S(2)}) collective-permute-start(bf16[1,2,4,128,128]{4,3,2,1,0:T(8,128)(2,1)S(1)} %get-tuple-element.74), channel_id=1, source_target_pairs={{0,1},{1,0},{2,3},{3,2},{4,5},{5,4},{6,7},{7,6},{8,9},{9,8},{10,11... | collective-permute-start | bytes 786440 | tf_op jit(solution)/shard_map/ppermute | solution.py:38
  64.5 11.7 %collective-permute-start.16 = (bf16[1,2,4,128,128]{4,3,2,1,0:T(8,128)(2,1)S(1)}, bf16[1,2,4,128,128]{4,3,2,1,0:T(8,128)(2,1)S(1)}, u32[]{:S(2)}, u32[]{:S(2)}) collective-permute-start(bf16[1,2,4,128,128]{4,3,2,1,0:T(8,128)(2,1)S(1)} %add_convert_fusion.4), channel_id=1, source_target_pairs={{0,2},{1,3},{2,0},{3,1},{4,6},{5,7},{6,4},{7,5},{8,10},{9,11},{10,... | collective-permute-start | bytes 786440 | tf_op jit(solution)/shard_map/ppermute | solution.py:38
  66.1 8.5 %collective-permute-start.18 = (bf16[192,256]{1,0:T(8,128)(2,1)S(1)}, bf16[192,256]{1,0:T(8,128)(2,1)S(1)}, u32[]{:S(2)}, u32[]{:S(2)}) collective-permute-start(bf16[192,256]{1,0:T(8,128)(2,1)S(1)} %bitcast.30), channel_id=1, source_target_pairs={{0,8},{4,12},{8,0},{12,4},{1,9},{5,13},{9,1},{13,5},{2,10},{6,14},... | collective-permute-start | bytes 294920 | tf_op jit(solution)/shard_map/ppermute | solution.py:38
  66.1 8.5 %collective-permute-start.19 = (bf16[192,256]{1,0:T(8,128)(2,1)S(1)}, bf16[192,256]{1,0:T(8,128)(2,1)S(1)}, u32[]{:S(2)}, u32[]{:S(2)}) collective-permute-start(bf16[192,256]{1,0:T(8,128)(2,1)S(1)} %bitcast.29), channel_id=1, source_target_pairs={{0,12},{4,8},{8,4},{12,0},{1,13},{5,9},{9,5},{13,1},{2,14},{6,10},... | collective-permute-start | bytes 294920 | tf_op jit(solution)/shard_map/ppermute | solution.py:38
  67.7 7.7 %collective-permute-start.17 = (bf16[192,256]{1,0:T(8,128)(2,1)S(1)}, bf16[192,256]{1,0:T(8,128)(2,1)S(1)}, u32[]{:S(2)}, u32[]{:S(2)}) collective-permute-start(bf16[192,256]{1,0:T(8,128)(2,1)S(1)} %bitcast.28), channel_id=1, source_target_pairs={{0,4},{4,0},{8,12},{12,8},{1,5},{5,1},{9,13},{13,9},{2,6},{6,2},{1... | collective-permute-start | bytes 294920 | tf_op jit(solution)/shard_map/ppermute | solution.py:38
  74.6 9.0 %collective-permute-start.10 = (bf16[1,2,4,128,128]{4,3,2,1,0:T(8,128)(2,1)S(1)}, bf16[1,2,4,128,128]{4,3,2,1,0:T(8,128)(2,1)S(1)}, u32[]{:S(2)}, u32[]{:S(2)}) collective-permute-start(bf16[1,2,4,128,128]{4,3,2,1,0:T(8,128)(2,1)S(1)} %get-tuple-element.68), channel_id=1, source_target_pairs={{0,1},{1,0},{2,3},{3,2},{4,5},{5,4},{6,7},{7,6},{8,9},{9,8},{10,11... | collective-permute-start | bytes 786440 | tf_op jit(solution)/shard_map/ppermute | solution.py:38
  77.1 8.4 %collective-permute-start.20 = (bf16[1,2,4,128,128]{4,3,2,1,0:T(8,128)(2,1)}, bf16[1,2,4,128,128]{4,3,2,1,0:T(8,128)(2,1)}, u32[]{:S(2)}, u32[]{:S(2)}) collective-permute-start(bf16[1,2,4,128,128]{4,3,2,1,0:T(8,128)(2,1)} %add_convert_fusion.2), channel_id=1, source_target_pairs={{0,2},{1,3},{2,0},{3,1},{4,6},{5,7},{6,4},{7,5},{8,10},{9,11},{10,... | collective-permute-start | bytes 786440 | tf_op jit(solution)/shard_map/ppermute | solution.py:38
  78.2 8.6 %collective-permute-start.23 = (bf16[1,2,4,128,128]{4,3,2,1,0:T(8,128)(2,1)S(1)}, bf16[1,2,4,128,128]{4,3,2,1,0:T(8,128)(2,1)}, u32[]{:S(2)}, u32[]{:S(2)}) collective-permute-start(bf16[1,2,4,128,128]{4,3,2,1,0:T(8,128)(2,1)S(1)} %get-tuple-element.82), channel_id=1, source_target_pairs={{0,1},{1,0},{2,3},{3,2},{4,5},{5,4},{6,7},{7,6},{8,9},{9,8},{10,11... | collective-permute-start | bytes 786440 | tf_op jit(solution)/shard_map/ppermute | solution.py:38
  78.2 10.8 %collective-permute-start.22 = (bf16[2,4,128,128]{3,2,1,0:T(8,128)(2,1)S(1)}, bf16[2,4,128,128]{3,2,1,0:T(8,128)(2,1)}, u32[]{:S(2)}, u32[]{:S(2)}) collective-permute-start(bf16[2,4,128,128]{3,2,1,0:T(8,128)(2,1)S(1)} %fusion.1), channel_id=1, source_target_pairs={{0,4},{4,8},{8,12},{12,0},{1,5},{5,9},{9,13},{13,1},{2,6},{6,10},{... | collective-permute-start | bytes 786440 | tf_op jit(solution)/shard_map/ppermute | solution.py:33
  80.1 10.5 %collective-permute-start.9 = (bf16[1,2,4,128,128]{4,3,2,1,0:T(8,128)(2,1)S(1)}, bf16[1,2,4,128,128]{4,3,2,1,0:T(8,128)(2,1)S(1)}, u32[]{:S(2)}, u32[]{:S(2)}) collective-permute-start(bf16[1,2,4,128,128]{4,3,2,1,0:T(8,128)(2,1)S(1)} %get-tuple-element.66), channel_id=1, source_target_pairs={{0,1},{1,0},{2,3},{3,2},{4,5},{5,4},{6,7},{7,6},{8,9},{9,8},{10,11... | collective-permute-start | bytes 786440 | tf_op jit(solution)/shard_map/ppermute | solution.py:38
  80.1 22.7 %all-to-all-start = ((bf16[4,192,256]{2,1,0:T(8,128)(2,1)}), bf16[4,192,256]{2,1,0:T(8,128)(2,1)S(1)}, u32[]{:S(2)}, u32[]{:S(2)}) async-start(bf16[4,192,256]{2,1,0:T(8,128)(2,1)} %add_up.1), calls=%async_computation | async-start | bytes 786432 | tf_op jit(solution)/shard_map/all_to_all | solution.py:616
  85.6 7.3 %collective-permute-start.21 = (bf16[1,2,4,128,128]{4,3,2,1,0:T(8,128)(2,1)S(1)}, bf16[1,2,4,128,128]{4,3,2,1,0:T(8,128)(2,1)S(1)}, u32[]{:S(2)}, u32[]{:S(2)}) collective-permute-start(bf16[1,2,4,128,128]{4,3,2,1,0:T(8,128)(2,1)S(1)} %add_convert_fusion.1), channel_id=1, source_target_pairs={{0,2},{1,3},{2,0},{3,1},{4,6},{5,7},{6,4},{7,5},{8,10},{9,11},{10,... | collective-permute-start | bytes 786440 | tf_op jit(solution)/shard_map/ppermute | solution.py:38
  90.3 10.5 %collective-permute-start.24 = (bf16[2,4,128,128]{3,2,1,0:T(8,128)(2,1)S(1)}, bf16[2,4,128,128]{3,2,1,0:T(8,128)(2,1)S(1)}, u32[]{:S(2)}, u32[]{:S(2)}) collective-permute-start(bf16[2,4,128,128]{3,2,1,0:T(8,128)(2,1)S(1)} %fusion), channel_id=1, source_target_pairs={{0,4},{4,8},{8,12},{12,0},{1,5},{5,9},{9,13},{13,1},{2,6},{6,10},{... | collective-permute-start | bytes 786440 | tf_op jit(solution)/shard_map/ppermute | solution.py:33
  (9 other events, 105.8 us)

commit v12 on v11

--- a/solution.py
+++ b/solution.py
@@ -512,13 +512,15 @@
     total = own[...]
     for term in arrived:
         total += term[...].astype(jnp.float32)
-    total = total.astype(jnp.bfloat16)
-    for i in range(out.shape[0]):
-        out[i] = total
-
-
-def widen_kernel(array, out):
-    out[...] = array[...].astype(jnp.float32)
+    out[...] = total.astype(jnp.bfloat16)
+
+
+def place_kernel(axis, offs, *refs):
+    pieces, out = refs[:-1], refs[-1]
+    me = lax.axis_index(axis)
+    each = pieces[0].shape[0]
+    for i, off in enumerate(offs):
+        out[me ^ off] = pieces[i // each][i % each].astype(jnp.float32)
 
 
 def small_call(kernel, shape, kind, name, *arrays):
@@ -532,13 +534,26 @@
     )(*arrays)
 
 
+def gather_shares(axis, held):
+    offs, first = [0], None
+    bit = lax.axis_size(axis) // 2
+    while True:
+        arrived = swap(held, axis, bit)
+        first = arrived if first is None else first
+        offs = offs + [o ^ bit for o in offs]
+        if bit == 1:
+            return [held, arrived], offs, first
+        held = jnp.concatenate([held, arrived], 0)
+        bit //= 2
+
+
 def scatter_sum(axis, value, relative):
     peers, me = lax.axis_size(axis), lax.axis_index(axis)
     share = (lambda i: value[i]) if relative else (lambda i: lax.dynamic_index_in_dim(value, me ^ i, 0, False))
     sent = [share(i).astype(jnp.bfloat16) for i in range(1, peers)]
     arrived = [swap(sending, axis, i) for i, sending in enumerate(sent, 1)]
     total = small_call(
-        add_up_kernel, (peers,) + value.shape[1:], jnp.bfloat16, "add_up", share(0), *arrived
+        add_up_kernel, value.shape[1:], jnp.bfloat16, "add_up", share(0), *arrived
     )
     return total, sent
 
@@ -609,12 +624,14 @@
     for section in range(last - 1, -1, -1):
         mine, leaving, gate = halve(keep[section], send[section], before_cross=(gate,))
         if section == last - 1:
-            total = after(total, leaving)
+            pieces, order, first = gather_shares("blk", after(total, leaving)[None])
         arrived = shift(moving, "blk", 1)
         if section > 0:
             moving = (arrived.astype(jnp.float32) + mine).astype(jnp.bfloat16)
-    gathered = lax.all_to_all(total, "blk", 0, 0)
-    eigen_share = small_call(widen_kernel, gathered.shape, jnp.float32, "widen", gathered)
+            gate = after(moving, first)
+    eigen_share = small_call(
+        functools.partial(place_kernel, "blk", order), (blocks,) + total.shape, jnp.float32, "place", *pieces
+    )
     eigen_share = eigen_share.reshape(modes, 2, frame // shares, frame)
     summed = finish(mine, arrived)
     return (summed[None], eigen_share, coef_rows.T)

time: 104 us -> 107 us (1.029)
  waiting for transfers between devices: 37.3 us -> 43.9 us
  other arithmetic: 2.59 us -> 0.82 us
  starting transfers between devices: 29.2 us -> 27.6 us
    ppermute x21 -> x23, waiting for transfers between devices: 20.4 us -> 38.1 us  [swap(): return lax.ppermute(array, axis, [(i, i ^ bit) for i in range(peers)])]
    ppermute x4, waiting for transfers between devices: 15.9 us -> 5.82 us  [shift(): lax.ppermute(array, axis, [(i, (i + by) % peers) for i in range(peers)])]
    all_to_all x1 -> x0, starting transfers between devices: 3.47 us -> none  [on_device(): gathered = lax.all_to_all(total, 'blk', 0, 0)]
    ppermute x4, starting transfers between devices: 11.5 us -> 13 us  [shift(): lax.ppermute(array, axis, [(i, (i + by) % peers) for i in range(peers)])]
    all_to_all x1 -> x0, waiting for transfers between devices: 1.1 us -> none  [on_device(): gathered = lax.all_to_all(total, 'blk', 0, 0)]
    convert_element_type x1, other arithmetic: 1.23 us -> 0.14 us  [on_device(): moving = (arrived.astype(jnp.float32) + mine).astype(jnp.bfloat16)]
    ppermute x21 -> x23, starting transfers between devices: 14.2 us -> 14.6 us  [swap(): return lax.ppermute(array, axis, [(i, i ^ bit) for i in range(peers)])]
  transfers between devices with their start and end apart: 26 -> 27, of which waited for: 14 -> 13; matrix products, arithmetic and copies ran while one was open for 3% -> 1% of each run, Pallas kernels for 8% -> 7%
where the time goes in v12:
time: 107 us; the launch traced here: 106 us
  waiting for transfers between devices  43.9 us (41%)
  Pallas kernels  28.7 us (27%)
  starting transfers between devices  27.6 us (26%)
  local copies, waits for them, and re-layouts  3.77 us (4%)
  between operations  1.56 us (1%)
    ppermute x23, waiting for transfers between devices, swap(): return lax.ppermute(array, axis, [(i, i ^ bit) for i in range(peers)])  38.1 us
    pallas_call x1, Pallas kernels, positions(): pl.pallas_call(functools.partial(position_kernel, offs, scale), in_specs=...  20.5 us
    ppermute x23, starting transfers between devices, swap(): return lax.ppermute(array, axis, [(i, i ^ bit) for i in range(peers)])  14.6 us
    ppermute x4, starting transfers between devices, shift(): lax.ppermute(array, axis, [(i, (i + by) % peers) for i in range(peers)])  13 us
    pallas_call x1, Pallas kernels, scatter(): pl.pallas_call(functools.partial(scatter_kernel, shares), in_specs=[pl.Bl...  5.97 us
    ppermute x4, waiting for transfers between devices, shift(): lax.ppermute(array, axis, [(i, (i + by) % peers) for i in range(peers)])  5.82 us
    unnamed x14, local copies, waits for them, and re-layouts  2.75 us
  transfers between devices with their start and end apart: 27, of which 13 were waited for; matrix products, arithmetic and copies ran while one was open for 1% of the time, Pallas kernels for 7%

profile of v12, /device:TPU:0, one launch (start us, length us, event | category | flops | bytes accessed | tf_op | source)
XLA Modules:
  0.0 106.4 jit_solution(4786428446126506672)
XLA Ops:
  1.7 5.1 %collective-permute-start = (bf16[2,128,512]{2,1,0:T(8,128)(2,1)S(1)}, bf16[2,128,512]{2,1,0:T(8,128)(2,1)S(1)}, u32[]{:S(2)}, u32[]{:S(2)}) collective-permute-start(bf16[2,128,512]{2,1,0:T(8,128)(2,1)S(1)} %dynamic-slice_bitcast_fusion), channel_id=1, source_target_pairs={{0,12},{4,0},{8,4},{12,8},{1,13},{5,1},{9,5},{13,9},{2,14},{6,2},{... | collective-permute-start | bytes 786440 | tf_op jit(solution)/shard_map/ppermute | solution.py:33
  6.8 5.6 %collective-permute-done.refs_1_ = bf16[2,128,512]{2,1,0:T(8,128)(2,1)S(1)} collective-permute-done((bf16[2,128,512]{2,1,0:T(8,128)(2,1)S(1)}, bf16[2,128,512]{2,1,0:T(8,128)(2,1)S(1)}, u32[]{:S(2)}, u32[]{:S(2)}) %collective-permute-start) | collective-permute-done | bytes 262176 | tf_op jit(solution)/shard_map/ppermute | solution.py:33
  12.3 4.3 %collective-permute-start.1 = (bf16[2,128,512]{2,1,0:T(8,128)(2,1)S(1)}, bf16[2,128,512]{2,1,0:T(8,128)(2,1)S(1)}, u32[]{:S(2)}, u32[]{:S(2)}) collective-permute-start(bf16[2,128,512]{2,1,0:T(8,128)(2,1)S(1)} %collective-permute-done.refs_1_), channel_id=1, source_target_pairs={{0,12},{4,0},{8,4},{12,8},{1,13},{5,1},{9,5},{13,9},{2,14},{6,2},{... | collective-permute-start | bytes 786440 | tf_op jit(solution)/shard_map/ppermute | solution.py:33
  16.6 1.5 %collective-permute-start.2 = (bf16[2,128,512]{2,1,0:T(8,128)(2,1)S(1)}, bf16[2,128,512]{2,1,0:T(8,128)(2,1)S(1)}, u32[]{:S(2)}, u32[]{:S(2)}) collective-permute-start(bf16[2,128,512]{2,1,0:T(8,128)(2,1)S(1)} %collective-permute-done.refs_1_), channel_id=1, source_target_pairs={{0,2},{1,3},{2,0},{3,1},{4,6},{5,7},{6,4},{7,5},{8,10},{9,11},{10,... | collective-permute-start | bytes 786440 | tf_op jit(solution)/shard_map/ppermute | solution.py:38
  18.1 1.4 %copy-done.1 = bf16[6,2,256,256]{3,2,1,0:T(8,128)(2,1)S(1)} copy-done((bf16[6,2,256,256]{3,2,1,0:T(8,128)(2,1)S(1)}, bf16[6,2,256,256]{3,2,1,0:T(8,128)(2,1)}, u32[]{:S(2)}) %copy-start.1) | copy-done | bytes 1572888
  19.5 1.3 %copy-done.2 = bf16[10,256,256]{2,1,0:T(8,128)(2,1)S(1)} copy-done((bf16[10,256,256]{2,1,0:T(8,128)(2,1)S(1)}, bf16[10,256,256]{2,1,0:T(8,128)(2,1)}, u32[]{:S(2)}) %copy-start.2) | copy-done | bytes 1310744
  21.3 1.5 %collective-permute-start.5 = (bf16[2,128,512]{2,1,0:T(8,128)(2,1)S(1)}, bf16[2,128,512]{2,1,0:T(8,128)(2,1)S(1)}, u32[]{:S(2)}, u32[]{:S(2)}) collective-permute-start(bf16[2,128,512]{2,1,0:T(8,128)(2,1)S(1)} %collective-permute-done.1.refs_5_), channel_id=1, source_target_pairs={{0,2},{1,3},{2,0},{3,1},{4,6},{5,7},{6,4},{7,5},{8,10},{9,11},{10,... | collective-permute-start | bytes 786440 | tf_op jit(solution)/shard_map/ppermute | solution.py:38
  23.3 1.5 %collective-permute-done.2.refs_2_ = bf16[2,128,512]{2,1,0:T(8,128)(2,1)S(1)} collective-permute-done((bf16[2,128,512]{2,1,0:T(8,128)(2,1)S(1)}, bf16[2,128,512]{2,1,0:T(8,128)(2,1)S(1)}, u32[]{:S(2)}, u32[]{:S(2)}) %collective-permute-start.2) | collective-permute-done | bytes 262176 | tf_op jit(solution)/shard_map/ppermute | solution.py:38
  25.1 4.1 %collective-permute-done.5.refs_6_ = bf16[2,128,512]{2,1,0:T(8,128)(2,1)S(1)} collective-permute-done((bf16[2,128,512]{2,1,0:T(8,128)(2,1)S(1)}, bf16[2,128,512]{2,1,0:T(8,128)(2,1)S(1)}, u32[]{:S(2)}, u32[]{:S(2)}) %collective-permute-start.5) | collective-permute-done | bytes 262176 | tf_op jit(solution)/shard_map/ppermute | solution.py:38
  30.7 20.5 %positions.1 = (bf16[1,12,64,256]{3,2,1,0:T(8,128)(2,1)S(1)}, bf16[1,12,64,256]{3,2,1,0:T(8,128)(2,1)S(1)}, f32[1,12,64,256]{3,2,1,0:T(8,128)S(1)}, f32[1,12,64,...) custom-call(s32[2,10]{1,0:T(2,128)S(1)} %get-tuple-element.52.tile_list, ...), custom_call_target="tpu_custom_call" | custom-call | tf_op jit(solution)/shard_map/positions/pallas_call | solution.py:346
  51.7 1.2 %collective-permute-done.8 = bf16[1,12,64,256]{3,2,1,0:T(8,128)(2,1)S(1)} collective-permute-done((bf16[1,12,64,256]{3,2,1,0:T(8,128)(2,1)S(1)}, bf16[1,12,64,256]{3,2,1,0:T(8,128)(2,1)S(1)}, u32[]{:S(2)}, u32[]{:S(2)}) %collective-permute-start.8) | collective-permute-done | bytes 393248 | tf_op jit(solution)/shard_map/ppermute | solution.py:38
  53.1 1.5 %collective-permute-start.15 = (bf16[1,12,64,256]{3,2,1,0:T(8,128)(2,1)S(1)}, bf16[1,12,64,256]{3,2,1,0:T(8,128)(2,1)S(1)}, u32[]{:S(2)}, u32[]{:S(2)}) collective-permute-start(bf16[1,12,64,256]{3,2,1,0:T(8,128)(2,1)S(1)} %add_convert_fusion), channel_id=1, source_target_pairs={{0,2},{1,3},{2,0},{3,1},{4,6},{5,7},{6,4},{7,5},{8,10},{9,11},{10,... | collective-permute-start | bytes 1179656 | tf_op jit(solution)/shard_map/ppermute | solution.py:38
  54.6 6.0 %scatter.1 = (bf16[1,2,4,128,128]{4,3,2,1,0:T(8,128)(2,1)S(1)}, bf16[1,2,4,128,128]{4,3,2,1,0:T(8,128)(2,1)S(1)}, bf16[1,2,4,128,128]{4,3,2,1,0:T(8,128)(2,1)S(1...) custom-call(s32[2,10]{1,0:T(2,128)S(1)} %get-tuple-element.52.tile_l, ...), custom_call_target="tpu_custom_call" | custom-call | flops 16777216 | bytes 16777216 | tf_op jit(solution)/shard_map/scatter/pallas_call | solution.py:467
  61.2 3.1 %collective-permute-done.15 = bf16[1,12,64,256]{3,2,1,0:T(8,128)(2,1)S(1)} collective-permute-done((bf16[1,12,64,256]{3,2,1,0:T(8,128)(2,1)S(1)}, bf16[1,12,64,256]{3,2,1,0:T(8,128)(2,1)S(1)}, u32[]{:S(2)}, u32[]{:S(2)}) %collective-permute-start.15) | collective-permute-done | bytes 393248 | tf_op jit(solution)/shard_map/ppermute | solution.py:38
  64.6 1.5 %collective-permute-start.16 = (bf16[1,2,4,128,128]{4,3,2,1,0:T(8,128)(2,1)S(1)}, bf16[1,2,4,128,128]{4,3,2,1,0:T(8,128)(2,1)S(1)}, u32[]{:S(2)}, u32[]{:S(2)}) collective-permute-start(bf16[1,2,4,128,128]{4,3,2,1,0:T(8,128)(2,1)S(1)} %add_convert_fusion.3), channel_id=1, source_target_pairs={{0,2},{1,3},{2,0},{3,1},{4,6},{5,7},{6,4},{7,5},{8,10},{9,11},{10,... | collective-permute-start | bytes 786440 | tf_op jit(solution)/shard_map/ppermute | solution.py:38
  66.1 1.6 %collective-permute-start.19 = (bf16[192,256]{1,0:T(8,128)(2,1)S(1)}, bf16[192,256]{1,0:T(8,128)(2,1)S(1)}, u32[]{:S(2)}, u32[]{:S(2)}) collective-permute-start(bf16[192,256]{1,0:T(8,128)(2,1)S(1)} %bitcast.32), channel_id=1, source_target_pairs={{0,12},{4,8},{8,4},{12,0},{1,13},{5,9},{9,5},{13,1},{2,14},{6,10},... | collective-permute-start | bytes 294920 | tf_op jit(solution)/shard_map/ppermute | solution.py:38
  67.7 1.9 %collective-permute-start.17 = (bf16[192,256]{1,0:T(8,128)(2,1)S(1)}, bf16[192,256]{1,0:T(8,128)(2,1)S(1)}, u32[]{:S(2)}, u32[]{:S(2)}) collective-permute-start(bf16[192,256]{1,0:T(8,128)(2,1)S(1)} %bitcast.31), channel_id=1, source_target_pairs={{0,4},{4,0},{8,12},{12,8},{1,5},{5,1},{9,13},{13,9},{2,6},{6,2},{1... | collective-permute-start | bytes 294920 | tf_op jit(solution)/shard_map/ppermute | solution.py:38
  69.6 5.0 %collective-permute-done.18.refs_1_ = bf16[192,256]{1,0:T(8,128)(2,1)S(1)} collective-permute-done((bf16[192,256]{1,0:T(8,128)(2,1)S(1)}, bf16[192,256]{1,0:T(8,128)(2,1)S(1)}, u32[]{:S(2)}, u32[]{:S(2)}) %collective-permute-start.18) | collective-permute-done | bytes 98336 | tf_op jit(solution)/shard_map/ppermute | solution.py:38
  76.2 1.3 %collective-permute-start.23 = (bf16[1,2,4,128,128]{4,3,2,1,0:T(8,128)(2,1)S(1)}, bf16[1,2,4,128,128]{4,3,2,1,0:T(8,128)(2,1)S(1)}, u32[]{:S(2)}, u32[]{:S(2)}) collective-permute-start(bf16[1,2,4,128,128]{4,3,2,1,0:T(8,128)(2,1)S(1)} %add_convert_fusion.1), channel_id=1, source_target_pairs={{0,2},{1,3},{2,0},{3,1},{4,6},{5,7},{6,4},{7,5},{8,10},{9,11},{10,... | collective-permute-start | bytes 786440 | tf_op jit(solution)/shard_map/ppermute | solution.py:38
  77.4 1.6 %collective-permute-start.20 = (bf16[2,4,128,128]{3,2,1,0:T(8,128)(2,1)S(1)}, bf16[2,4,128,128]{3,2,1,0:T(8,128)(2,1)S(1)}, u32[]{:S(2)}, u32[]{:S(2)}) collective-permute-start(bf16[2,4,128,128]{3,2,1,0:T(8,128)(2,1)S(1)} %fusion.1), channel_id=1, source_target_pairs={{0,4},{4,8},{8,12},{12,0},{1,5},{5,9},{9,13},{13,1},{2,6},{6,10},{... | collective-permute-start | bytes 786440 | tf_op jit(solution)/shard_map/ppermute | solution.py:33
  79.7 11.8 %collective-permute-done.25 = bf16[1,192,256]{2,1,0:T(8,128)(2,1)S(1)} collective-permute-done((bf16[1,192,256]{2,1,0:T(8,128)(2,1)S(1)}, bf16[1,192,256]{2,1,0:T(8,128)(2,1)S(1)}, u32[]{:S(2)}, u32[]{:S(2)}) %collective-permute-start.25) | collective-permute-done | bytes 98336 | tf_op jit(solution)/shard_map/ppermute | solution.py:38
  92.6 2.1 %collective-permute-start.24 = (bf16[2,4,128,128]{3,2,1,0:T(8,128)(2,1)S(1)}, bf16[2,4,128,128]{3,2,1,0:T(8,128)(2,1)S(1)}, u32[]{:S(2)}, u32[]{:S(2)}) collective-permute-start(bf16[2,4,128,128]{3,2,1,0:T(8,128)(2,1)S(1)} %fusion), channel_id=1, source_target_pairs={{0,4},{4,8},{8,12},{12,0},{1,5},{5,9},{9,13},{13,1},{2,6},{6,10},{... | collective-permute-start | bytes 786440 | tf_op jit(solution)/shard_map/ppermute | solution.py:33
  94.7 5.1 %collective-permute-done.11 = bf16[1,2,4,128,128]{4,3,2,1,0:T(8,128)(2,1)S(1)} collective-permute-done((bf16[1,2,4,128,128]{4,3,2,1,0:T(8,128)(2,1)S(1)}, bf16[1,2,4,128,128]{4,3,2,1,0:T(8,128)(2,1)S(1)}, u32[]{:S(2)}, u32[]{:S(2)}) %collective-permute-start.11) | collective-permute-done | bytes 262176 | tf_op jit(solution)/shard_map/ppermute | solution.py:38
  99.8 4.8 %collective-permute-done.26.refs_1_ = bf16[2,192,256]{2,1,0:T(8,128)(2,1)S(1)} collective-permute-done((bf16[2,192,256]{2,1,0:T(8,128)(2,1)S(1)}, bf16[2,192,256]{2,1,0:T(8,128)(2,1)S(1)}, u32[]{:S(2)}, u32[]{:S(2)}) %collective-permute-start.26) | collective-permute-done | bytes 196640 | tf_op jit(solution)/shard_map/ppermute | solution.py:38
  (63 shorter events, 9.8 us)
Async XLA Ops:
  1.7 10.7 %collective-permute-start = (bf16[2,128,512]{2,1,0:T(8,128)(2,1)S(1)}, bf16[2,128,512]{2,1,0:T(8,128)(2,1)S(1)}, u32[]{:S(2)}, u32[]{:S(2)}) collective-permute-start(bf16[2,128,512]{2,1,0:T(8,128)(2,1)S(1)} %dynamic-slice_bitcast_fusion), channel_id=1, source_target_pairs={{0,12},{4,0},{8,4},{12,8},{1,13},{5,1},{9,5},{13,9},{2,14},{6,2},{... | collective-permute-start | bytes 786440 | tf_op jit(solution)/shard_map/ppermute | solution.py:33
  12.3 9.0 %collective-permute-start.1 = (bf16[2,128,512]{2,1,0:T(8,128)(2,1)S(1)}, bf16[2,128,512]{2,1,0:T(8,128)(2,1)S(1)}, u32[]{:S(2)}, u32[]{:S(2)}) collective-permute-start(bf16[2,128,512]{2,1,0:T(8,128)(2,1)S(1)} %collective-permute-done.refs_1_), channel_id=1, source_target_pairs={{0,12},{4,0},{8,4},{12,8},{1,13},{5,1},{9,5},{13,9},{2,14},{6,2},{... | collective-permute-start | bytes 786440 | tf_op jit(solution)/shard_map/ppermute | solution.py:33
  16.6 8.2 %collective-permute-start.2 = (bf16[2,128,512]{2,1,0:T(8,128)(2,1)S(1)}, bf16[2,128,512]{2,1,0:T(8,128)(2,1)S(1)}, u32[]{:S(2)}, u32[]{:S(2)}) collective-permute-start(bf16[2,128,512]{2,1,0:T(8,128)(2,1)S(1)} %collective-permute-done.refs_1_), channel_id=1, source_target_pairs={{0,2},{1,3},{2,0},{3,1},{4,6},{5,7},{6,4},{7,5},{8,10},{9,11},{10,... | collective-permute-start | bytes 786440 | tf_op jit(solution)/shard_map/ppermute | solution.py:38
  21.3 7.8 %collective-permute-start.5 = (bf16[2,128,512]{2,1,0:T(8,128)(2,1)S(1)}, bf16[2,128,512]{2,1,0:T(8,128)(2,1)S(1)}, u32[]{:S(2)}, u32[]{:S(2)}) collective-permute-start(bf16[2,128,512]{2,1,0:T(8,128)(2,1)S(1)} %collective-permute-done.1.refs_5_), channel_id=1, source_target_pairs={{0,2},{1,3},{2,0},{3,1},{4,6},{5,7},{6,4},{7,5},{8,10},{9,11},{10,... | collective-permute-start | bytes 786440 | tf_op jit(solution)/shard_map/ppermute | solution.py:38
  22.8 7.0 %collective-permute-start.3 = (bf16[2,128,512]{2,1,0:T(8,128)(2,1)S(1)}, bf16[2,128,512]{2,1,0:T(8,128)(2,1)S(1)}, u32[]{:S(2)}, u32[]{:S(2)}) collective-permute-start(bf16[2,128,512]{2,1,0:T(8,128)(2,1)S(1)} %collective-permute-done.refs_1_), channel_id=1, source_target_pairs={{0,1},{1,0},{2,3},{3,2},{4,5},{5,4},{6,7},{7,6},{8,9},{9,8},{10,11... | collective-permute-start | bytes 786440 | tf_op jit(solution)/shard_map/ppermute | solution.py:38
  22.8 7.0 %collective-permute-start.6 = (bf16[2,128,512]{2,1,0:T(8,128)(2,1)S(1)}, bf16[2,128,512]{2,1,0:T(8,128)(2,1)S(1)}, u32[]{:S(2)}, u32[]{:S(2)}) collective-permute-start(bf16[2,128,512]{2,1,0:T(8,128)(2,1)S(1)} %collective-permute-done.1.refs_5_), channel_id=1, source_target_pairs={{0,1},{1,0},{2,3},{3,2},{4,5},{5,4},{6,7},{7,6},{8,9},{9,8},{10,11... | collective-permute-start | bytes 786440 | tf_op jit(solution)/shard_map/ppermute | solution.py:38
  24.8 5.0 %collective-permute-start.4 = (bf16[2,128,512]{2,1,0:T(8,128)(2,1)S(1)}, bf16[2,128,512]{2,1,0:T(8,128)(2,1)S(1)}, u32[]{:S(2)}, u32[]{:S(2)}) collective-permute-start(bf16[2,128,512]{2,1,0:T(8,128)(2,1)S(1)} %collective-permute-done.2.refs_2_), channel_id=1, source_target_pairs={{0,1},{1,0},{2,3},{3,2},{4,5},{5,4},{6,7},{7,6},{8,9},{9,8},{10,11... | collective-permute-start | bytes 786440 | tf_op jit(solution)/shard_map/ppermute | solution.py:38
  51.3 9.9 %collective-permute-start.14 = (bf16[1,12,64,256]{3,2,1,0:T(8,128)(2,1)S(1)}, bf16[1,12,64,256]{3,2,1,0:T(8,128)(2,1)S(1)}, u32[]{:S(2)}, u32[]{:S(2)}) collective-permute-start(bf16[1,12,64,256]{3,2,1,0:T(8,128)(2,1)S(1)} %get-tuple-element.73), channel_id=1, source_target_pairs={{0,1},{1,0},{2,3},{3,2},{4,5},{5,4},{6,7},{7,6},{8,9},{9,8},{10,11... | collective-permute-start | bytes 1179656 | tf_op jit(solution)/shard_map/ppermute | solution.py:38
  53.1 11.2 %collective-permute-start.15 = (bf16[1,12,64,256]{3,2,1,0:T(8,128)(2,1)S(1)}, bf16[1,12,64,256]{3,2,1,0:T(8,128)(2,1)S(1)}, u32[]{:S(2)}, u32[]{:S(2)}) collective-permute-start(bf16[1,12,64,256]{3,2,1,0:T(8,128)(2,1)S(1)} %add_convert_fusion), channel_id=1, source_target_pairs={{0,2},{1,3},{2,0},{3,1},{4,6},{5,7},{6,4},{7,5},{8,10},{9,11},{10,... | collective-permute-start | bytes 1179656 | tf_op jit(solution)/shard_map/ppermute | solution.py:38
  60.5 7.2 %collective-permute-start.10 = (bf16[1,2,4,128,128]{4,3,2,1,0:T(8,128)(2,1)S(1)}, bf16[1,2,4,128,128]{4,3,2,1,0:T(8,128)(2,1)S(1)}, u32[]{:S(2)}, u32[]{:S(2)}) collective-permute-start(bf16[1,2,4,128,128]{4,3,2,1,0:T(8,128)(2,1)S(1)} %get-tuple-element.67), channel_id=1, source_target_pairs={{0,1},{1,0},{2,3},{3,2},{4,5},{5,4},{6,7},{7,6},{8,9},{9,8},{10,11... | collective-permute-start | bytes 786440 | tf_op jit(solution)/shard_map/ppermute | solution.py:38
  60.6 14.8 %collective-permute-start.12 = (bf16[1,2,4,128,128]{4,3,2,1,0:T(8,128)(2,1)S(1)}, bf16[1,2,4,128,128]{4,3,2,1,0:T(8,128)(2,1)S(1)}, u32[]{:S(2)}, u32[]{:S(2)}) collective-permute-start(bf16[1,2,4,128,128]{4,3,2,1,0:T(8,128)(2,1)S(1)} %get-tuple-element.69), channel_id=1, source_target_pairs={{0,1},{1,0},{2,3},{3,2},{4,5},{5,4},{6,7},{7,6},{8,9},{9,8},{10,11... | collective-permute-start | bytes 786440 | tf_op jit(solution)/shard_map/ppermute | solution.py:38
  61.1 3.4 %collective-permute-start.13 = (bf16[1,2,4,128,128]{4,3,2,1,0:T(8,128)(2,1)S(1)}, bf16[1,2,4,128,128]{4,3,2,1,0:T(8,128)(2,1)S(1)}, u32[]{:S(2)}, u32[]{:S(2)}) collective-permute-start(bf16[1,2,4,128,128]{4,3,2,1,0:T(8,128)(2,1)S(1)} %get-tuple-element.71), channel_id=1, source_target_pairs={{0,1},{1,0},{2,3},{3,2},{4,5},{5,4},{6,7},{7,6},{8,9},{9,8},{10,11... | collective-permute-start | bytes 786440 | tf_op jit(solution)/shard_map/ppermute | solution.py:38
  64.6 10.9 %collective-permute-start.16 = (bf16[1,2,4,128,128]{4,3,2,1,0:T(8,128)(2,1)S(1)}, bf16[1,2,4,128,128]{4,3,2,1,0:T(8,128)(2,1)S(1)}, u32[]{:S(2)}, u32[]{:S(2)}) collective-permute-start(bf16[1,2,4,128,128]{4,3,2,1,0:T(8,128)(2,1)S(1)} %add_convert_fusion.3), channel_id=1, source_target_pairs={{0,2},{1,3},{2,0},{3,1},{4,6},{5,7},{6,4},{7,5},{8,10},{9,11},{10,... | collective-permute-start | bytes 786440 | tf_op jit(solution)/shard_map/ppermute | solution.py:38
  66.1 8.5 %collective-permute-start.18 = (bf16[192,256]{1,0:T(8,128)(2,1)S(1)}, bf16[192,256]{1,0:T(8,128)(2,1)S(1)}, u32[]{:S(2)}, u32[]{:S(2)}) collective-permute-start(bf16[192,256]{1,0:T(8,128)(2,1)S(1)} %bitcast.33), channel_id=1, source_target_pairs={{0,8},{4,12},{8,0},{12,4},{1,9},{5,13},{9,1},{13,5},{2,10},{6,14},... | collective-permute-start | bytes 294920 | tf_op jit(solution)/shard_map/ppermute | solution.py:38
  66.1 8.5 %collective-permute-start.19 = (bf16[192,256]{1,0:T(8,128)(2,1)S(1)}, bf16[192,256]{1,0:T(8,128)(2,1)S(1)}, u32[]{:S(2)}, u32[]{:S(2)}) collective-permute-start(bf16[192,256]{1,0:T(8,128)(2,1)S(1)} %bitcast.32), channel_id=1, source_target_pairs={{0,12},{4,8},{8,4},{12,0},{1,13},{5,9},{9,5},{13,1},{2,14},{6,10},... | collective-permute-start | bytes 294920 | tf_op jit(solution)/shard_map/ppermute | solution.py:38
  67.7 7.7 %collective-permute-start.17 = (bf16[192,256]{1,0:T(8,128)(2,1)S(1)}, bf16[192,256]{1,0:T(8,128)(2,1)S(1)}, u32[]{:S(2)}, u32[]{:S(2)}) collective-permute-start(bf16[192,256]{1,0:T(8,128)(2,1)S(1)} %bitcast.31), channel_id=1, source_target_pairs={{0,4},{4,0},{8,12},{12,8},{1,5},{5,1},{9,13},{13,9},{2,6},{6,2},{1... | collective-permute-start | bytes 294920 | tf_op jit(solution)/shard_map/ppermute | solution.py:38
  74.6 20.1 %collective-permute-start.9 = (bf16[1,2,4,128,128]{4,3,2,1,0:T(8,128)(2,1)S(1)}, bf16[1,2,4,128,128]{4,3,2,1,0:T(8,128)(2,1)S(1)}, u32[]{:S(2)}, u32[]{:S(2)}) collective-permute-start(bf16[1,2,4,128,128]{4,3,2,1,0:T(8,128)(2,1)S(1)} %get-tuple-element.65), channel_id=1, source_target_pairs={{0,1},{1,0},{2,3},{3,2},{4,5},{5,4},{6,7},{7,6},{8,9},{9,8},{10,11... | collective-permute-start | bytes 786440 | tf_op jit(solution)/shard_map/ppermute | solution.py:38
  75.4 16.9 %collective-permute-start.21 = (bf16[1,2,4,128,128]{4,3,2,1,0:T(8,128)(2,1)S(1)}, bf16[1,2,4,128,128]{4,3,2,1,0:T(8,128)(2,1)S(1)}, u32[]{:S(2)}, u32[]{:S(2)}) collective-permute-start(bf16[1,2,4,128,128]{4,3,2,1,0:T(8,128)(2,1)S(1)} %get-tuple-element.77), channel_id=1, source_target_pairs={{0,1},{1,0},{2,3},{3,2},{4,5},{5,4},{6,7},{7,6},{8,9},{9,8},{10,11... | collective-permute-start | bytes 786440 | tf_op jit(solution)/shard_map/ppermute | solution.py:38
  76.2 16.3 %collective-permute-start.23 = (bf16[1,2,4,128,128]{4,3,2,1,0:T(8,128)(2,1)S(1)}, bf16[1,2,4,128,128]{4,3,2,1,0:T(8,128)(2,1)S(1)}, u32[]{:S(2)}, u32[]{:S(2)}) collective-permute-start(bf16[1,2,4,128,128]{4,3,2,1,0:T(8,128)(2,1)S(1)} %add_convert_fusion.1), channel_id=1, source_target_pairs={{0,2},{1,3},{2,0},{3,1},{4,6},{5,7},{6,4},{7,5},{8,10},{9,11},{10,... | collective-permute-start | bytes 786440 | tf_op jit(solution)/shard_map/ppermute | solution.py:38
  77.4 15.0 %collective-permute-start.20 = (bf16[2,4,128,128]{3,2,1,0:T(8,128)(2,1)S(1)}, bf16[2,4,128,128]{3,2,1,0:T(8,128)(2,1)S(1)}, u32[]{:S(2)}, u32[]{:S(2)}) collective-permute-start(bf16[2,4,128,128]{3,2,1,0:T(8,128)(2,1)S(1)} %fusion.1), channel_id=1, source_target_pairs={{0,4},{4,8},{8,12},{12,0},{1,5},{5,9},{9,13},{13,1},{2,6},{6,10},{... | collective-permute-start | bytes 786440 | tf_op jit(solution)/shard_map/ppermute | solution.py:33
  79.0 12.5 %collective-permute-start.25 = (bf16[1,192,256]{2,1,0:T(8,128)(2,1)S(1)}, bf16[1,192,256]{2,1,0:T(8,128)(2,1)S(1)}, u32[]{:S(2)}, u32[]{:S(2)}) collective-permute-start(bf16[1,192,256]{2,1,0:T(8,128)(2,1)S(1)} %bitcast.24), channel_id=1, source_target_pairs={{0,8},{4,12},{8,0},{12,4},{1,9},{5,13},{9,1},{13,5},{2,10},{6,14},... | collective-permute-start | bytes 294920 | tf_op jit(solution)/shard_map/ppermute | solution.py:38
  91.5 8.2 %collective-permute-start.11 = (bf16[1,2,4,128,128]{4,3,2,1,0:T(8,128)(2,1)S(1)}, bf16[1,2,4,128,128]{4,3,2,1,0:T(8,128)(2,1)S(1)}, u32[]{:S(2)}, u32[]{:S(2)}) collective-permute-start(bf16[1,2,4,128,128]{4,3,2,1,0:T(8,128)(2,1)S(1)} %add_convert_fusion.4), channel_id=1, source_target_pairs={{0,2},{1,3},{2,0},{3,1},{4,6},{5,7},{6,4},{7,5},{8,10},{9,11},{10,... | collective-permute-start | bytes 786440 | tf_op jit(solution)/shard_map/ppermute | solution.py:38
  92.4 12.2 %collective-permute-start.26 = (bf16[2,192,256]{2,1,0:T(8,128)(2,1)S(1)}, bf16[2,192,256]{2,1,0:T(8,128)(2,1)S(1)}, u32[]{:S(2)}, u32[]{:S(2)}) collective-permute-start(bf16[2,192,256]{2,1,0:T(8,128)(2,1)S(1)} %pad_maximum_fusion.refs_0_), channel_id=1, source_target_pairs={{0,4},{4,0},{8,12},{12,8},{1,5},{5,1},{9,13},{13,9},{2,6},{6,2},{1... | collective-permute-start | bytes 589832 | tf_op jit(solution)/shard_map/ppermute | solution.py:38
  92.6 12.9 %collective-permute-start.24 = (bf16[2,4,128,128]{3,2,1,0:T(8,128)(2,1)S(1)}, bf16[2,4,128,128]{3,2,1,0:T(8,128)(2,1)S(1)}, u32[]{:S(2)}, u32[]{:S(2)}) collective-permute-start(bf16[2,4,128,128]{3,2,1,0:T(8,128)(2,1)S(1)} %fusion), channel_id=1, source_target_pairs={{0,4},{4,8},{8,12},{12,0},{1,5},{5,9},{9,13},{13,1},{2,6},{6,10},{... | collective-permute-start | bytes 786440 | tf_op jit(solution)/shard_map/ppermute | solution.py:33
  (10 other events, 107.3 us)

commit v13 on v11

--- a/solution.py
+++ b/solution.py
@@ -117,7 +117,7 @@
     eig_in, amps_in, tables_in, coef_in = refs[len(pieces):len(pieces) + 4]
     eigen_send, eigen_keep = refs[len(pieces) + 4:len(pieces) + 6], refs[len(pieces) + 6:len(pieces) + 8]
     grads_out, coef = refs[len(pieces) + 8:len(pieces) + 10]
-    (staged, table, probe, amps, eig, obj, ex, mid, far, patch, d_high, d_low, eigen, out_eigen, cross,
+    (staged, table, probe, amps, eig, obj, ex, mid, far, patch, dprobe, eigen, out_eigen, cross,
      weights, weights_t, piece_sem, table_sem, amps_sem, eig_sem, grad_sem, out_sem) = refs[len(pieces) + 10:]
     pos_dev, _, frame, _ = probe.shape
     modes = eig.shape[0]
@@ -166,7 +166,7 @@
             probe[:, c, rows, :] = made.reshape(pos_dev, STRIP, frame)
         return carry
 
-    lax.fori_loop(0, frame // STRIP, synth, 0, unroll=4)
+    lax.fori_loop(0, frame // STRIP, synth, 0, unroll=8)
     for copy in copies:
         copy.wait()
 
@@ -241,9 +241,7 @@
             o_re, o_im = patch[slot, 0, rows], patch[slot, 1, rows]
             p_re, p_im = probe[j, 0, rows], probe[j, 1, rows]
             for c, d in enumerate((o_re * b_re + o_im * b_im, o_re * b_im - o_im * b_re)):
-                high = d.astype(jnp.bfloat16)
-                d_high[j, c, rows] = high
-                d_low[j, c, rows] = (d - high.astype(jnp.float32)).astype(jnp.bfloat16)
+                dprobe[j, c, rows] = d.astype(jnp.bfloat16)
             probe[j, 0, rows] = p_re * b_re + p_im * b_im
             probe[j, 1, rows] = p_re * b_im - p_im * b_re
 
@@ -270,8 +268,7 @@
     lax.fori_loop(0, pairs, visit, 0)
 
     def skip(j, carry):
-        d_high[j] = jnp.zeros((2, frame, frame), jnp.bfloat16)
-        d_low[j] = jnp.zeros((2, frame, frame), jnp.bfloat16)
+        dprobe[j] = jnp.zeros((2, frame, frame), jnp.bfloat16)
         return carry
 
     lax.fori_loop(2 * pairs, pos_dev, skip, 0)
@@ -286,23 +283,21 @@
         q = i // (rows_q // STRIP)
         inner = pl.ds(pl.multiple_of(i % (rows_q // STRIP) * STRIP, STRIP), STRIP)
         for c in range(2):
-            high = d_high[:, c, rows, :].reshape(pos_dev * STRIP, frame)
-            low = d_low[:, c, rows, :].reshape(pos_dev * STRIP, frame)
+            d = dprobe[:, c, rows, :].reshape(pos_dev * STRIP, frame)
             e = eig[:, c, rows, :].reshape(modes * STRIP, frame)
-            both = jnp.dot(weights_t[...], high, preferred_element_type=jnp.float32)
-            rest = jnp.dot(weights_t[:modes * STRIP], low, preferred_element_type=jnp.float32)
-            grad = (both[:modes * STRIP] + both[modes * STRIP:] + rest) * (0.5 * scale)
+            both = jnp.dot(weights_t[...], d, preferred_element_type=jnp.float32)
+            grad = (both[:modes * STRIP] + both[modes * STRIP:]) * (0.5 * scale)
             for k in range(modes):
                 group = 2 * k + c
                 if share:
                     group = (group // share ^ my_block) * share + group % share
                 eigen[q, group, inner, :] = grad[k * STRIP:(k + 1) * STRIP]
             cross[...] += lax.dot_general(
-                high, e, (((1,), (1,)), ((), ())), preferred_element_type=jnp.float32
+                d, e, (((1,), (1,)), ((), ())), preferred_element_type=jnp.float32
             )
         return carry
 
-    lax.fori_loop(0, frame // STRIP, eigen_strip, 0, unroll=4)
+    lax.fori_loop(0, frame // STRIP, eigen_strip, 0, unroll=8)
     pending = []
 
     def start(source, target):
@@ -359,7 +354,6 @@
             pltpu.VMEM((2, 2 * frame, frame), jnp.float32),
             pltpu.VMEM((2, 2, frame, frame), jnp.float32),
             pltpu.VMEM(grads, jnp.bfloat16),
-            pltpu.VMEM(grads, jnp.bfloat16),
             pltpu.VMEM((shares, 2 * modes, frame // shares, frame), jnp.float32),
             pltpu.VMEM(eigen_half, jnp.bfloat16),
             pltpu.VMEM((pos_dev * STRIP, modes * STRIP), jnp.float32),

time: 104 us -> 103 us (level)
  waiting for transfers between devices: 37.3 us -> 39.4 us
  starting transfers between devices: 29.2 us -> 27.1 us
  Pallas kernels: 29.3 us -> 28.1 us
    ppermute x21, waiting for transfers between devices: 20.4 us -> 23.3 us  [swap(): return lax.ppermute(array, axis, [(i, i ^ bit) for i in range(peers)])]
    ppermute x21, starting transfers between devices: 14.2 us -> 12.1 us  [swap(): return lax.ppermute(array, axis, [(i, i ^ bit) for i in range(peers)])]
    pallas_call x1, Pallas kernels: 20.4 us -> 19.2 us  [positions(): pl.pallas_call(functools.partial(position_kernel, offs, scale), in_specs=...]
  transfers between devices with their start and end apart: 26 -> 26, of which waited for: 14 -> 13; matrix products, arithmetic and copies ran while one was open for 3% -> 3% of each run, Pallas kernels for 8% -> 8%
where the time goes in v13:
time: 103 us; the launch traced here: 102 us
  waiting for transfers between devices  39.4 us (38%)
  Pallas kernels  28.1 us (27%)
  starting transfers between devices  27.1 us (26%)
  local copies, waits for them, and re-layouts  3.77 us (4%)
  other arithmetic  2.59 us (3%)
  between operations  1.5 us (1%)
    ppermute x21, waiting for transfers between devices, swap(): return lax.ppermute(array, axis, [(i, i ^ bit) for i in range(peers)])  23.3 us
    pallas_call x1, Pallas kernels, positions(): pl.pallas_call(functools.partial(position_kernel, offs, scale), in_specs=...  19.2 us
    ppermute x4, waiting for transfers between devices, shift(): lax.ppermute(array, axis, [(i, (i + by) % peers) for i in range(peers)])  15 us
    ppermute x21, starting transfers between devices, swap(): return lax.ppermute(array, axis, [(i, i ^ bit) for i in range(peers)])  12.1 us
    ppermute x4, starting transfers between devices, shift(): lax.ppermute(array, axis, [(i, (i + by) % peers) for i in range(peers)])  11.5 us
    pallas_call x1, Pallas kernels, scatter(): pl.pallas_call(functools.partial(scatter_kernel, shares), in_specs=[pl.Bl...  5.97 us
    all_to_all x1, starting transfers between devices, on_device(): gathered = lax.all_to_all(total, 'blk', 0, 0)  3.48 us
    unnamed x14, local copies, waits for them, and re-layouts  2.75 us
  transfers between devices with their start and end apart: 26, of which 13 were waited for; matrix products, arithmetic and copies ran while one was open for 3% of the time, Pallas kernels for 8%

profile of v13, /device:TPU:0, one launch (start us, length us, event | category | flops | bytes accessed | tf_op | source)
XLA Modules:
  0.0 102.4 jit_solution(13951105582316619199)
XLA Ops:
  1.7 5.1 %collective-permute-start = (bf16[2,128,512]{2,1,0:T(8,128)(2,1)S(1)}, bf16[2,128,512]{2,1,0:T(8,128)(2,1)S(1)}, u32[]{:S(2)}, u32[]{:S(2)}) collective-permute-start(bf16[2,128,512]{2,1,0:T(8,128)(2,1)S(1)} %dynamic-slice_bitcast_fusion), channel_id=1, source_target_pairs={{0,12},{4,0},{8,4},{12,8},{1,13},{5,1},{9,5},{13,9},{2,14},{6,2},{... | collective-permute-start | bytes 786440 | tf_op jit(solution)/shard_map/ppermute | solution.py:33
  6.8 5.6 %collective-permute-done.refs_1_ = bf16[2,128,512]{2,1,0:T(8,128)(2,1)S(1)} collective-permute-done((bf16[2,128,512]{2,1,0:T(8,128)(2,1)S(1)}, bf16[2,128,512]{2,1,0:T(8,128)(2,1)S(1)}, u32[]{:S(2)}, u32[]{:S(2)}) %collective-permute-start) | collective-permute-done | bytes 262176 | tf_op jit(solution)/shard_map/ppermute | solution.py:33
  12.3 4.3 %collective-permute-start.1 = (bf16[2,128,512]{2,1,0:T(8,128)(2,1)S(1)}, bf16[2,128,512]{2,1,0:T(8,128)(2,1)S(1)}, u32[]{:S(2)}, u32[]{:S(2)}) collective-permute-start(bf16[2,128,512]{2,1,0:T(8,128)(2,1)S(1)} %collective-permute-done.refs_1_), channel_id=1, source_target_pairs={{0,12},{4,0},{8,4},{12,8},{1,13},{5,1},{9,5},{13,9},{2,14},{6,2},{... | collective-permute-start | bytes 786440 | tf_op jit(solution)/shard_map/ppermute | solution.py:33
  16.6 1.5 %collective-permute-start.2 = (bf16[2,128,512]{2,1,0:T(8,128)(2,1)S(1)}, bf16[2,128,512]{2,1,0:T(8,128)(2,1)S(1)}, u32[]{:S(2)}, u32[]{:S(2)}) collective-permute-start(bf16[2,128,512]{2,1,0:T(8,128)(2,1)S(1)} %collective-permute-done.refs_1_), channel_id=1, source_target_pairs={{0,2},{1,3},{2,0},{3,1},{4,6},{5,7},{6,4},{7,5},{8,10},{9,11},{10,... | collective-permute-start | bytes 786440 | tf_op jit(solution)/shard_map/ppermute | solution.py:38
  18.1 1.4 %copy-done.1 = bf16[6,2,256,256]{3,2,1,0:T(8,128)(2,1)S(1)} copy-done((bf16[6,2,256,256]{3,2,1,0:T(8,128)(2,1)S(1)}, bf16[6,2,256,256]{3,2,1,0:T(8,128)(2,1)}, u32[]{:S(2)}) %copy-start.1) | copy-done | bytes 1572888
  19.5 1.3 %copy-done.2 = bf16[10,256,256]{2,1,0:T(8,128)(2,1)S(1)} copy-done((bf16[10,256,256]{2,1,0:T(8,128)(2,1)S(1)}, bf16[10,256,256]{2,1,0:T(8,128)(2,1)}, u32[]{:S(2)}) %copy-start.2) | copy-done | bytes 1310744
  21.3 1.5 %collective-permute-start.5 = (bf16[2,128,512]{2,1,0:T(8,128)(2,1)S(1)}, bf16[2,128,512]{2,1,0:T(8,128)(2,1)S(1)}, u32[]{:S(2)}, u32[]{:S(2)}) collective-permute-start(bf16[2,128,512]{2,1,0:T(8,128)(2,1)S(1)} %collective-permute-done.1.refs_5_), channel_id=1, source_target_pairs={{0,2},{1,3},{2,0},{3,1},{4,6},{5,7},{6,4},{7,5},{8,10},{9,11},{10,... | collective-permute-start | bytes 786440 | tf_op jit(solution)/shard_map/ppermute | solution.py:38
  23.3 1.5 %collective-permute-done.2.refs_2_ = bf16[2,128,512]{2,1,0:T(8,128)(2,1)S(1)} collective-permute-done((bf16[2,128,512]{2,1,0:T(8,128)(2,1)S(1)}, bf16[2,128,512]{2,1,0:T(8,128)(2,1)S(1)}, u32[]{:S(2)}, u32[]{:S(2)}) %collective-permute-start.2) | collective-permute-done | bytes 262176 | tf_op jit(solution)/shard_map/ppermute | solution.py:38
  25.1 4.1 %collective-permute-done.5.refs_6_ = bf16[2,128,512]{2,1,0:T(8,128)(2,1)S(1)} collective-permute-done((bf16[2,128,512]{2,1,0:T(8,128)(2,1)S(1)}, bf16[2,128,512]{2,1,0:T(8,128)(2,1)S(1)}, u32[]{:S(2)}, u32[]{:S(2)}) %collective-permute-start.5) | collective-permute-done | bytes 262176 | tf_op jit(solution)/shard_map/ppermute | solution.py:38
  30.7 19.2 %positions.1 = (bf16[1,12,64,256]{3,2,1,0:T(8,128)(2,1)S(1)}, bf16[1,12,64,256]{3,2,1,0:T(8,128)(2,1)S(1)}, f32[1,12,64,256]{3,2,1,0:T(8,128)S(1)}, f32[1,12,64,...) custom-call(s32[2,10]{1,0:T(2,128)S(1)} %get-tuple-element.53.tile_list, ...), custom_call_target="tpu_custom_call" | custom-call | tf_op jit(solution)/shard_map/positions/pallas_call | solution.py:341
  50.4 1.2 %collective-permute-done.8 = bf16[1,12,64,256]{3,2,1,0:T(8,128)(2,1)S(1)} collective-permute-done((bf16[1,12,64,256]{3,2,1,0:T(8,128)(2,1)S(1)}, bf16[1,12,64,256]{3,2,1,0:T(8,128)(2,1)S(1)}, u32[]{:S(2)}, u32[]{:S(2)}) %collective-permute-start.8) | collective-permute-done | bytes 393248 | tf_op jit(solution)/shard_map/ppermute | solution.py:38
  51.8 6.0 %scatter.1 = (bf16[1,2,4,128,128]{4,3,2,1,0:T(8,128)(2,1)S(1)}, bf16[1,2,4,128,128]{4,3,2,1,0:T(8,128)(2,1)S(1)}, bf16[1,2,4,128,128]{4,3,2,1,0:T(8,128)(2,1)S(1...) custom-call(s32[2,10]{1,0:T(2,128)S(1)} %get-tuple-element.53.tile_l, ...), custom_call_target="tpu_custom_call" | custom-call | flops 16777216 | bytes 16777216 | tf_op jit(solution)/shard_map/scatter/pallas_call | solution.py:461
  58.4 4.6 %collective-permute-done.15 = bf16[1,12,64,256]{3,2,1,0:T(8,128)(2,1)S(1)} collective-permute-done((bf16[1,12,64,256]{3,2,1,0:T(8,128)(2,1)S(1)}, bf16[1,12,64,256]{3,2,1,0:T(8,128)(2,1)S(1)}, u32[]{:S(2)}, u32[]{:S(2)}) %collective-permute-start.15) | collective-permute-done | bytes 393248 | tf_op jit(solution)/shard_map/ppermute | solution.py:38
  63.6 1.2 %collective-permute-start.18 = (bf16[192,256]{1,0:T(8,128)(2,1)S(1)}, bf16[192,256]{1,0:T(8,128)(2,1)S(1)}, u32[]{:S(2)}, u32[]{:S(2)}) collective-permute-start(bf16[192,256]{1,0:T(8,128)(2,1)S(1)} %bitcast.30), channel_id=1, source_target_pairs={{0,8},{4,12},{8,0},{12,4},{1,9},{5,13},{9,1},{13,5},{2,10},{6,14},... | collective-permute-start | bytes 294920 | tf_op jit(solution)/shard_map/ppermute | solution.py:38
  64.8 2.8 %collective-permute-start.19 = (bf16[192,256]{1,0:T(8,128)(2,1)S(1)}, bf16[192,256]{1,0:T(8,128)(2,1)S(1)}, u32[]{:S(2)}, u32[]{:S(2)}) collective-permute-start(bf16[192,256]{1,0:T(8,128)(2,1)S(1)} %bitcast.29), channel_id=1, source_target_pairs={{0,12},{4,8},{8,4},{12,0},{1,13},{5,9},{9,5},{13,1},{2,14},{6,10},... | collective-permute-start | bytes 294920 | tf_op jit(solution)/shard_map/ppermute | solution.py:38
  68.2 5.5 %collective-permute-done.18.refs_1_ = bf16[192,256]{1,0:T(8,128)(2,1)S(1)} collective-permute-done((bf16[192,256]{1,0:T(8,128)(2,1)S(1)}, bf16[192,256]{1,0:T(8,128)(2,1)S(1)}, u32[]{:S(2)}, u32[]{:S(2)}) %collective-permute-start.18) | collective-permute-done | bytes 98336 | tf_op jit(solution)/shard_map/ppermute | solution.py:38
  77.0 1.8 %collective-permute-start.22 = (bf16[2,4,128,128]{3,2,1,0:T(8,128)(2,1)S(1)}, bf16[2,4,128,128]{3,2,1,0:T(8,128)(2,1)}, u32[]{:S(2)}, u32[]{:S(2)}) collective-permute-start(bf16[2,4,128,128]{3,2,1,0:T(8,128)(2,1)S(1)} %fusion.1), channel_id=1, source_target_pairs={{0,4},{4,8},{8,12},{12,0},{1,5},{5,9},{9,13},{13,1},{2,6},{6,10},{... | collective-permute-start | bytes 786440 | tf_op jit(solution)/shard_map/ppermute | solution.py:33
  78.8 3.5 %all-to-all-start = ((bf16[4,192,256]{2,1,0:T(8,128)(2,1)}), bf16[4,192,256]{2,1,0:T(8,128)(2,1)S(1)}, u32[]{:S(2)}, u32[]{:S(2)}) async-start(bf16[4,192,256]{2,1,0:T(8,128)(2,1)} %add_up.1), calls=%async_computation | async-start | bytes 786432 | tf_op jit(solution)/shard_map/all_to_all | solution.py:610
  82.3 2.4 %collective-permute-done.20 = bf16[1,2,4,128,128]{4,3,2,1,0:T(8,128)(2,1)} collective-permute-done((bf16[1,2,4,128,128]{4,3,2,1,0:T(8,128)(2,1)}, bf16[1,2,4,128,128]{4,3,2,1,0:T(8,128)(2,1)}, u32[]{:S(2)}, u32[]{:S(2)}) %collective-permute-start.20) | collective-permute-done | bytes 262176 | tf_op jit(solution)/shard_map/ppermute | solution.py:38
  85.7 2.1 %collective-permute-done.22 = bf16[2,4,128,128]{3,2,1,0:T(8,128)(2,1)} collective-permute-done((bf16[2,4,128,128]{3,2,1,0:T(8,128)(2,1)S(1)}, bf16[2,4,128,128]{3,2,1,0:T(8,128)(2,1)}, u32[]{:S(2)}, u32[]{:S(2)}) %collective-permute-start.22) | collective-permute-done | bytes 262176 | tf_op jit(solution)/shard_map/ppermute | solution.py:33
  87.8 1.2 %fusion = bf16[2,4,128,128]{3,2,1,0:T(8,128)(2,1)S(1)} fusion(bf16[1,2,4,128,128]{4,3,2,1,0:T(8,128)(2,1)} %collective-permute-done.20, f32[1,2,4,128,128]{4,3,2,1,0:T(8,128)S(1)} %get-tuple-element.81, bf16[1,2,4,128,128]{4,3,2,1,0:T(8,128)(2,1)} %collective-permute-done.23, bf16[2,4,128,128]{3,2,1,0:T(8,128)(2,1)} %collective-permute-done.22), kind=kLoop, calls=%fused_computation.3 | loop fusion | flops 917504 | bytes 1572864 | tf_op jit(solution)/shard_map/convert_element_type | solution.py:609
  89.3 3.0 %collective-permute-done.21 = bf16[1,2,4,128,128]{4,3,2,1,0:T(8,128)(2,1)S(1)} collective-permute-done((bf16[1,2,4,128,128]{4,3,2,1,0:T(8,128)(2,1)S(1)}, bf16[1,2,4,128,128]{4,3,2,1,0:T(8,128)(2,1)S(1)}, u32[]{:S(2)}, u32[]{:S(2)}) %collective-permute-start.21) | collective-permute-done | bytes 262176 | tf_op jit(solution)/shard_map/ppermute | solution.py:38
  92.4 7.1 %collective-permute-done.24.second = bf16[2,4,128,128]{3,2,1,0:T(8,128)(2,1)S(1)} collective-permute-done((bf16[2,4,128,128]{3,2,1,0:T(8,128)(2,1)S(1)}, bf16[2,4,128,128]{3,2,1,0:T(8,128)(2,1)S(1)}, u32[]{:S(2)}, u32[]{:S(2)}) %collective-permute-start.24) | collective-permute-done | bytes 262176 | tf_op jit(solution)/shard_map/ppermute | solution.py:33
  100.4 1.1 %all-to-all-done.array = bf16[4,192,256]{2,1,0:T(8,128)(2,1)S(1)} async-done(((bf16[4,192,256]{2,1,0:T(8,128)(2,1)}), bf16[4,192,256]{2,1,0:T(8,128)(2,1)S(1)}, u32[]{:S(2)}, u32[]{:S(2)}) %all-to-all-start) | async-done | bytes 393248 | tf_op jit(solution)/shard_map/all_to_all | solution.py:610
  (60 shorter events, 11.9 us)
Async XLA Ops:
  1.7 10.7 %collective-permute-start = (bf16[2,128,512]{2,1,0:T(8,128)(2,1)S(1)}, bf16[2,128,512]{2,1,0:T(8,128)(2,1)S(1)}, u32[]{:S(2)}, u32[]{:S(2)}) collective-permute-start(bf16[2,128,512]{2,1,0:T(8,128)(2,1)S(1)} %dynamic-slice_bitcast_fusion), channel_id=1, source_target_pairs={{0,12},{4,0},{8,4},{12,8},{1,13},{5,1},{9,5},{13,9},{2,14},{6,2},{... | collective-permute-start | bytes 786440 | tf_op jit(solution)/shard_map/ppermute | solution.py:33
  12.3 9.0 %collective-permute-start.1 = (bf16[2,128,512]{2,1,0:T(8,128)(2,1)S(1)}, bf16[2,128,512]{2,1,0:T(8,128)(2,1)S(1)}, u32[]{:S(2)}, u32[]{:S(2)}) collective-permute-start(bf16[2,128,512]{2,1,0:T(8,128)(2,1)S(1)} %collective-permute-done.refs_1_), channel_id=1, source_target_pairs={{0,12},{4,0},{8,4},{12,8},{1,13},{5,1},{9,5},{13,9},{2,14},{6,2},{... | collective-permute-start | bytes 786440 | tf_op jit(solution)/shard_map/ppermute | solution.py:33
  16.6 8.2 %collective-permute-start.2 = (bf16[2,128,512]{2,1,0:T(8,128)(2,1)S(1)}, bf16[2,128,512]{2,1,0:T(8,128)(2,1)S(1)}, u32[]{:S(2)}, u32[]{:S(2)}) collective-permute-start(bf16[2,128,512]{2,1,0:T(8,128)(2,1)S(1)} %collective-permute-done.refs_1_), channel_id=1, source_target_pairs={{0,2},{1,3},{2,0},{3,1},{4,6},{5,7},{6,4},{7,5},{8,10},{9,11},{10,... | collective-permute-start | bytes 786440 | tf_op jit(solution)/shard_map/ppermute | solution.py:38
  21.3 7.8 %collective-permute-start.5 = (bf16[2,128,512]{2,1,0:T(8,128)(2,1)S(1)}, bf16[2,128,512]{2,1,0:T(8,128)(2,1)S(1)}, u32[]{:S(2)}, u32[]{:S(2)}) collective-permute-start(bf16[2,128,512]{2,1,0:T(8,128)(2,1)S(1)} %collective-permute-done.1.refs_5_), channel_id=1, source_target_pairs={{0,2},{1,3},{2,0},{3,1},{4,6},{5,7},{6,4},{7,5},{8,10},{9,11},{10,... | collective-permute-start | bytes 786440 | tf_op jit(solution)/shard_map/ppermute | solution.py:38
  22.8 7.0 %collective-permute-start.3 = (bf16[2,128,512]{2,1,0:T(8,128)(2,1)S(1)}, bf16[2,128,512]{2,1,0:T(8,128)(2,1)S(1)}, u32[]{:S(2)}, u32[]{:S(2)}) collective-permute-start(bf16[2,128,512]{2,1,0:T(8,128)(2,1)S(1)} %collective-permute-done.refs_1_), channel_id=1, source_target_pairs={{0,1},{1,0},{2,3},{3,2},{4,5},{5,4},{6,7},{7,6},{8,9},{9,8},{10,11... | collective-permute-start | bytes 786440 | tf_op jit(solution)/shard_map/ppermute | solution.py:38
  22.8 7.0 %collective-permute-start.6 = (bf16[2,128,512]{2,1,0:T(8,128)(2,1)S(1)}, bf16[2,128,512]{2,1,0:T(8,128)(2,1)S(1)}, u32[]{:S(2)}, u32[]{:S(2)}) collective-permute-start(bf16[2,128,512]{2,1,0:T(8,128)(2,1)S(1)} %collective-permute-done.1.refs_5_), channel_id=1, source_target_pairs={{0,1},{1,0},{2,3},{3,2},{4,5},{5,4},{6,7},{7,6},{8,9},{9,8},{10,11... | collective-permute-start | bytes 786440 | tf_op jit(solution)/shard_map/ppermute | solution.py:38
  24.8 5.0 %collective-permute-start.4 = (bf16[2,128,512]{2,1,0:T(8,128)(2,1)S(1)}, bf16[2,128,512]{2,1,0:T(8,128)(2,1)S(1)}, u32[]{:S(2)}, u32[]{:S(2)}) collective-permute-start(bf16[2,128,512]{2,1,0:T(8,128)(2,1)S(1)} %collective-permute-done.2.refs_2_), channel_id=1, source_target_pairs={{0,1},{1,0},{2,3},{3,2},{4,5},{5,4},{6,7},{7,6},{8,9},{9,8},{10,11... | collective-permute-start | bytes 786440 | tf_op jit(solution)/shard_map/ppermute | solution.py:38
  49.8 1.8 %collective-permute-start.8 = (bf16[1,12,64,256]{3,2,1,0:T(8,128)(2,1)S(1)}, bf16[1,12,64,256]{3,2,1,0:T(8,128)(2,1)S(1)}, u32[]{:S(2)}, u32[]{:S(2)}) collective-permute-start(bf16[1,12,64,256]{3,2,1,0:T(8,128)(2,1)S(1)} %get-tuple-element.63), channel_id=1, source_target_pairs={{0,1},{1,0},{2,3},{3,2},{4,5},{5,4},{6,7},{7,6},{8,9},{9,8},{10,11... | collective-permute-start | bytes 1179656 | tf_op jit(solution)/shard_map/ppermute | solution.py:38
  50.0 8.3 %collective-permute-start.14 = (bf16[1,12,64,256]{3,2,1,0:T(8,128)(2,1)S(1)}, bf16[1,12,64,256]{3,2,1,0:T(8,128)(2,1)S(1)}, u32[]{:S(2)}, u32[]{:S(2)}) collective-permute-start(bf16[1,12,64,256]{3,2,1,0:T(8,128)(2,1)S(1)} %get-tuple-element.76), channel_id=1, source_target_pairs={{0,1},{1,0},{2,3},{3,2},{4,5},{5,4},{6,7},{7,6},{8,9},{9,8},{10,11... | collective-permute-start | bytes 1179656 | tf_op jit(solution)/shard_map/ppermute | solution.py:38
  51.7 11.2 %collective-permute-start.15 = (bf16[1,12,64,256]{3,2,1,0:T(8,128)(2,1)S(1)}, bf16[1,12,64,256]{3,2,1,0:T(8,128)(2,1)S(1)}, u32[]{:S(2)}, u32[]{:S(2)}) collective-permute-start(bf16[1,12,64,256]{3,2,1,0:T(8,128)(2,1)S(1)} %add_convert_fusion), channel_id=1, source_target_pairs={{0,2},{1,3},{2,0},{3,1},{4,6},{5,7},{6,4},{7,5},{8,10},{9,11},{10,... | collective-permute-start | bytes 1179656 | tf_op jit(solution)/shard_map/ppermute | solution.py:38
  57.8 17.4 %collective-permute-start.12 = (bf16[1,2,4,128,128]{4,3,2,1,0:T(8,128)(2,1)S(1)}, bf16[1,2,4,128,128]{4,3,2,1,0:T(8,128)(2,1)S(1)}, u32[]{:S(2)}, u32[]{:S(2)}) collective-permute-start(bf16[1,2,4,128,128]{4,3,2,1,0:T(8,128)(2,1)S(1)} %get-tuple-element.72), channel_id=1, source_target_pairs={{0,1},{1,0},{2,3},{3,2},{4,5},{5,4},{6,7},{7,6},{8,9},{9,8},{10,11... | collective-permute-start | bytes 786440 | tf_op jit(solution)/shard_map/ppermute | solution.py:38
  58.0 5.2 %collective-permute-start.13 = (bf16[1,2,4,128,128]{4,3,2,1,0:T(8,128)(2,1)S(1)}, bf16[1,2,4,128,128]{4,3,2,1,0:T(8,128)(2,1)S(1)}, u32[]{:S(2)}, u32[]{:S(2)}) collective-permute-start(bf16[1,2,4,128,128]{4,3,2,1,0:T(8,128)(2,1)S(1)} %get-tuple-element.74), channel_id=1, source_target_pairs={{0,1},{1,0},{2,3},{3,2},{4,5},{5,4},{6,7},{7,6},{8,9},{9,8},{10,11... | collective-permute-start | bytes 786440 | tf_op jit(solution)/shard_map/ppermute | solution.py:38
  63.3 11.9 %collective-permute-start.16 = (bf16[1,2,4,128,128]{4,3,2,1,0:T(8,128)(2,1)S(1)}, bf16[1,2,4,128,128]{4,3,2,1,0:T(8,128)(2,1)S(1)}, u32[]{:S(2)}, u32[]{:S(2)}) collective-permute-start(bf16[1,2,4,128,128]{4,3,2,1,0:T(8,128)(2,1)S(1)} %add_convert_fusion.4), channel_id=1, source_target_pairs={{0,2},{1,3},{2,0},{3,1},{4,6},{5,7},{6,4},{7,5},{8,10},{9,11},{10,... | collective-permute-start | bytes 786440 | tf_op jit(solution)/shard_map/ppermute | solution.py:38
  63.6 10.1 %collective-permute-start.18 = (bf16[192,256]{1,0:T(8,128)(2,1)S(1)}, bf16[192,256]{1,0:T(8,128)(2,1)S(1)}, u32[]{:S(2)}, u32[]{:S(2)}) collective-permute-start(bf16[192,256]{1,0:T(8,128)(2,1)S(1)} %bitcast.30), channel_id=1, source_target_pairs={{0,8},{4,12},{8,0},{12,4},{1,9},{5,13},{9,1},{13,5},{2,10},{6,14},... | collective-permute-start | bytes 294920 | tf_op jit(solution)/shard_map/ppermute | solution.py:38
  64.8 9.0 %collective-permute-start.19 = (bf16[192,256]{1,0:T(8,128)(2,1)S(1)}, bf16[192,256]{1,0:T(8,128)(2,1)S(1)}, u32[]{:S(2)}, u32[]{:S(2)}) collective-permute-start(bf16[192,256]{1,0:T(8,128)(2,1)S(1)} %bitcast.29), channel_id=1, source_target_pairs={{0,12},{4,8},{8,4},{12,0},{1,13},{5,9},{9,5},{13,1},{2,14},{6,10},... | collective-permute-start | bytes 294920 | tf_op jit(solution)/shard_map/ppermute | solution.py:38
  67.6 6.7 %collective-permute-start.17 = (bf16[192,256]{1,0:T(8,128)(2,1)S(1)}, bf16[192,256]{1,0:T(8,128)(2,1)S(1)}, u32[]{:S(2)}, u32[]{:S(2)}) collective-permute-start(bf16[192,256]{1,0:T(8,128)(2,1)S(1)} %bitcast.28), channel_id=1, source_target_pairs={{0,4},{4,0},{8,12},{12,8},{1,5},{5,1},{9,13},{13,9},{2,6},{6,2},{1... | collective-permute-start | bytes 294920 | tf_op jit(solution)/shard_map/ppermute | solution.py:38
  73.8 8.5 %collective-permute-start.10 = (bf16[1,2,4,128,128]{4,3,2,1,0:T(8,128)(2,1)S(1)}, bf16[1,2,4,128,128]{4,3,2,1,0:T(8,128)(2,1)S(1)}, u32[]{:S(2)}, u32[]{:S(2)}) collective-permute-start(bf16[1,2,4,128,128]{4,3,2,1,0:T(8,128)(2,1)S(1)} %get-tuple-element.68), channel_id=1, source_target_pairs={{0,1},{1,0},{2,3},{3,2},{4,5},{5,4},{6,7},{7,6},{8,9},{9,8},{10,11... | collective-permute-start | bytes 786440 | tf_op jit(solution)/shard_map/ppermute | solution.py:38
  76.1 8.7 %collective-permute-start.20 = (bf16[1,2,4,128,128]{4,3,2,1,0:T(8,128)(2,1)}, bf16[1,2,4,128,128]{4,3,2,1,0:T(8,128)(2,1)}, u32[]{:S(2)}, u32[]{:S(2)}) collective-permute-start(bf16[1,2,4,128,128]{4,3,2,1,0:T(8,128)(2,1)} %add_convert_fusion.2), channel_id=1, source_target_pairs={{0,2},{1,3},{2,0},{3,1},{4,6},{5,7},{6,4},{7,5},{8,10},{9,11},{10,... | collective-permute-start | bytes 786440 | tf_op jit(solution)/shard_map/ppermute | solution.py:38
  76.9 8.8 %collective-permute-start.23 = (bf16[1,2,4,128,128]{4,3,2,1,0:T(8,128)(2,1)S(1)}, bf16[1,2,4,128,128]{4,3,2,1,0:T(8,128)(2,1)}, u32[]{:S(2)}, u32[]{:S(2)}) collective-permute-start(bf16[1,2,4,128,128]{4,3,2,1,0:T(8,128)(2,1)S(1)} %get-tuple-element.82), channel_id=1, source_target_pairs={{0,1},{1,0},{2,3},{3,2},{4,5},{5,4},{6,7},{7,6},{8,9},{9,8},{10,11... | collective-permute-start | bytes 786440 | tf_op jit(solution)/shard_map/ppermute | solution.py:38
  77.0 10.8 %collective-permute-start.22 = (bf16[2,4,128,128]{3,2,1,0:T(8,128)(2,1)S(1)}, bf16[2,4,128,128]{3,2,1,0:T(8,128)(2,1)}, u32[]{:S(2)}, u32[]{:S(2)}) collective-permute-start(bf16[2,4,128,128]{3,2,1,0:T(8,128)(2,1)S(1)} %fusion.1), channel_id=1, source_target_pairs={{0,4},{4,8},{8,12},{12,0},{1,5},{5,9},{9,13},{13,1},{2,6},{6,10},{... | collective-permute-start | bytes 786440 | tf_op jit(solution)/shard_map/ppermute | solution.py:33
  78.8 10.5 %collective-permute-start.9 = (bf16[1,2,4,128,128]{4,3,2,1,0:T(8,128)(2,1)S(1)}, bf16[1,2,4,128,128]{4,3,2,1,0:T(8,128)(2,1)S(1)}, u32[]{:S(2)}, u32[]{:S(2)}) collective-permute-start(bf16[1,2,4,128,128]{4,3,2,1,0:T(8,128)(2,1)S(1)} %get-tuple-element.66), channel_id=1, source_target_pairs={{0,1},{1,0},{2,3},{3,2},{4,5},{5,4},{6,7},{7,6},{8,9},{9,8},{10,11... | collective-permute-start | bytes 786440 | tf_op jit(solution)/shard_map/ppermute | solution.py:38
  78.8 22.7 %all-to-all-start = ((bf16[4,192,256]{2,1,0:T(8,128)(2,1)}), bf16[4,192,256]{2,1,0:T(8,128)(2,1)S(1)}, u32[]{:S(2)}, u32[]{:S(2)}) async-start(bf16[4,192,256]{2,1,0:T(8,128)(2,1)} %add_up.1), calls=%async_computation | async-start | bytes 786432 | tf_op jit(solution)/shard_map/all_to_all | solution.py:610
  84.8 7.6 %collective-permute-start.21 = (bf16[1,2,4,128,128]{4,3,2,1,0:T(8,128)(2,1)S(1)}, bf16[1,2,4,128,128]{4,3,2,1,0:T(8,128)(2,1)S(1)}, u32[]{:S(2)}, u32[]{:S(2)}) collective-permute-start(bf16[1,2,4,128,128]{4,3,2,1,0:T(8,128)(2,1)S(1)} %add_convert_fusion.1), channel_id=1, source_target_pairs={{0,2},{1,3},{2,0},{3,1},{4,6},{5,7},{6,4},{7,5},{8,10},{9,11},{10,... | collective-permute-start | bytes 786440 | tf_op jit(solution)/shard_map/ppermute | solution.py:38
  89.0 10.5 %collective-permute-start.24 = (bf16[2,4,128,128]{3,2,1,0:T(8,128)(2,1)S(1)}, bf16[2,4,128,128]{3,2,1,0:T(8,128)(2,1)S(1)}, u32[]{:S(2)}, u32[]{:S(2)}) collective-permute-start(bf16[2,4,128,128]{3,2,1,0:T(8,128)(2,1)S(1)} %fusion), channel_id=1, source_target_pairs={{0,4},{4,8},{8,12},{12,0},{1,5},{5,9},{9,13},{13,1},{2,6},{6,10},{... | collective-permute-start | bytes 786440 | tf_op jit(solution)/shard_map/ppermute | solution.py:33
  (9 other events, 105.6 us)

commit v14 on v13

--- a/solution.py
+++ b/solution.py
@@ -87,15 +87,22 @@
 
 def stage_kernel(*refs):
     count = len(refs) // 2
-    sem = refs[-1]
+    move(refs[:count], refs[count:2 * count], refs[-1])()
+
+
+def move(sources, targets, sem):
     copies = [
         pltpu.make_async_copy(source, target, sem.at[i])
-        for i, (source, target) in enumerate(zip(refs[:count], refs[count:2 * count]))
+        for i, (source, target) in enumerate(zip(sources, targets))
     ]
     for copy in copies:
         copy.start()
-    for copy in copies:
-        copy.wait()
+
+    def finish():
+        for copy in copies:
+            copy.wait()
+
+    return finish
 
 
 def stage(*arrays):
@@ -111,14 +118,52 @@
     )(*arrays)
 
 
+def weights_kernel(coef_in, *refs):
+    count = (len(refs) - 3) // 2
+    weights, weights_t = refs[count:count + 2]
+    finish = move(refs[:count], refs[count + 2:-1], refs[-1])
+    modes, pos_dev = coef_in.shape
+    by_position = (pos_dev * STRIP, pos_dev)
+    by_mode = (modes * STRIP, modes)
+    tall_t = exact(exact(one_hot(by_mode, 0), coef_in[...]), one_hot(by_position[::-1], 1))
+    high, low = two_terms(diagonals(tall_t))
+    weights_t[...] = jnp.concatenate([high, low], 0)
+    spread = lax.dot_general(
+        one_hot(by_position, 0), coef_in[...], (((1,), (1,)), ((), ())),
+        precision=lax.Precision.HIGHEST, preferred_element_type=jnp.float32,
+    )
+    high, low = two_terms(diagonals(0.5 * exact(spread, one_hot(by_mode[::-1], 1))))
+    weights[...] = jnp.concatenate([high, low], 1)
+    finish()
+
+
+def expand(coef_t, *arrays):
+    modes, pos_dev = coef_t.shape
+    whole = pl.BlockSpec(memory_space=VMEM)
+    anywhere = pl.BlockSpec(memory_space=pl.ANY)
+    return pl.pallas_call(
+        weights_kernel,
+        in_specs=[whole] + [anywhere] * len(arrays),
+        out_specs=[whole] * 2 + [anywhere] * len(arrays),
+        scratch_shapes=[pltpu.SemaphoreType.DMA((len(arrays),))],
+        out_shape=[
+            jax.ShapeDtypeStruct((pos_dev * STRIP, 2 * modes * STRIP), jnp.bfloat16),
+            jax.ShapeDtypeStruct((2 * modes * STRIP, pos_dev * STRIP), jnp.bfloat16),
+        ]
+        + [jax.ShapeDtypeStruct(x.shape, x.dtype) for x in arrays],
+        compiler_params=pltpu.CompilerParams(vmem_limit_bytes=4 * 1024 * 1024),
+        name="expand",
+    )(coef_t, *arrays)
+
+
 def position_kernel(offs, scale, tile_list, offsets, group_counts, *refs):
     shares = len(offs)
     pieces = refs[: 1 + (REACH - 1) * shares]
-    eig_in, amps_in, tables_in, coef_in = refs[len(pieces):len(pieces) + 4]
-    eigen_send, eigen_keep = refs[len(pieces) + 4:len(pieces) + 6], refs[len(pieces) + 6:len(pieces) + 8]
-    grads_out, coef = refs[len(pieces) + 8:len(pieces) + 10]
+    eig_in, amps_in, tables_in, weights, weights_t = refs[len(pieces):len(pieces) + 5]
+    eigen_send, eigen_keep = refs[len(pieces) + 5:len(pieces) + 7], refs[len(pieces) + 7:len(pieces) + 9]
+    grads_out, coef = refs[len(pieces) + 9:len(pieces) + 11]
     (staged, table, probe, amps, eig, obj, ex, mid, far, patch, dprobe, eigen, out_eigen, cross,
-     weights, weights_t, piece_sem, table_sem, amps_sem, eig_sem, grad_sem, out_sem) = refs[len(pieces) + 10:]
+     piece_sem, table_sem, amps_sem, eig_sem, grad_sem, out_sem) = refs[len(pieces) + 11:]
     pos_dev, _, frame, _ = probe.shape
     modes = eig.shape[0]
     side = staged.shape[2]
@@ -143,17 +188,6 @@
     for copy in [eig_copy] + copies + [table_copy, amps_copy]:
         copy.start()
 
-    by_position = (pos_dev * STRIP, pos_dev)
-    by_mode = (modes * STRIP, modes)
-    tall_t = exact(exact(one_hot(by_mode, 0), coef_in[...]), one_hot(by_position[::-1], 1))
-    high, low = two_terms(diagonals(tall_t))
-    weights_t[...] = jnp.concatenate([high, low], 0)
-    spread = lax.dot_general(
-        one_hot(by_position, 0), coef_in[...], (((1,), (1,)), ((), ())),
-        precision=lax.Precision.HIGHEST, preferred_element_type=jnp.float32,
-    )
-    high, low = two_terms(diagonals(0.5 * exact(spread, one_hot(by_mode[::-1], 1))))
-    weights[...] = jnp.concatenate([high, low], 1)
     eig_copy.wait()
 
     def synth(i, carry):
@@ -311,6 +345,8 @@
         start(out_eigen.at[h], eigen_send[h % 2].at[h // 2])
         start(eigen.at[mine], eigen_keep[h % 2].at[h // 2])
 
+    by_position = (pos_dev * STRIP, pos_dev)
+    by_mode = (modes * STRIP, modes)
     total = exact(one_hot(by_position[::-1], 1), diagonals(cross[...]))
     coef[...] = lax.dot_general(
         one_hot(by_mode[::-1], 1), total, (((1,), (1,)), ((), ())),
@@ -326,7 +362,7 @@
         copy.wait()
 
 
-def positions(offs, scale, indices, pieces, eigenprobes, amps, table, coef_t):
+def positions(offs, scale, indices, pieces, eigenprobes, amps, table, weights, weights_t):
     modes, _, frame, _ = eigenprobes.shape
     pos_dev = amps.shape[0]
     side = pieces[0].shape[2]
@@ -340,7 +376,7 @@
     grads = (pos_dev, 2, frame, frame)
     return pl.pallas_call(
         functools.partial(position_kernel, offs, scale),
-        in_specs=[smem] * 3 + [anywhere] * (len(pieces) + 3) + [whole],
+        in_specs=[smem] * 3 + [anywhere] * (len(pieces) + 3) + [whole] * 2,
         out_specs=[anywhere] * 5 + [whole],
         scratch_shapes=[
             pltpu.VMEM((REACH, 2, side, side), jnp.bfloat16),
@@ -357,8 +393,6 @@
             pltpu.VMEM((shares, 2 * modes, frame // shares, frame), jnp.float32),
             pltpu.VMEM(eigen_half, jnp.bfloat16),
             pltpu.VMEM((pos_dev * STRIP, modes * STRIP), jnp.float32),
-            pltpu.VMEM((pos_dev * STRIP, 2 * modes * STRIP), jnp.bfloat16),
-            pltpu.VMEM((2 * modes * STRIP, pos_dev * STRIP), jnp.bfloat16),
             pltpu.SemaphoreType.DMA((len(pieces),)),
             pltpu.SemaphoreType.DMA,
             pltpu.SemaphoreType.DMA,
@@ -376,7 +410,7 @@
         ],
         compiler_params=pltpu.CompilerParams(vmem_limit_bytes=VMEM_LIMIT),
         name="positions",
-    )(*indices, *pieces, eigenprobes, amps, table, coef_t)
+    )(*indices, *pieces, eigenprobes, amps, table, weights, weights_t)
 
 
 def scatter_kernel(shares, tile_list, offsets, group_counts, grads_in, *refs):
@@ -574,8 +608,8 @@
     held = [[near], [shift(near, "blk", -1)]]
     eig, amps = stage(*after_all((eigenprobes, amplitudes), near))
     held[1][0] = after(held[1][0], eig)
-    table, tile, coef_t, lists, corners = stage(
-        *after_all((tables(frame), tiles[0], coefficients.T, tile_list.T, offsets.T), held[1][0])
+    weights, weights_t, table, tile, lists, corners = expand(
+        *after_all((coefficients.T, tables(frame), tiles[0], tile_list.T, offsets.T), held[1][0])
     )
     for bit in reversed(bits):
         for part in held:
@@ -587,7 +621,7 @@
     indices = (lists, corners, group_counts)
     scale = (pos_dev * blocks * shares) ** (-0.5)
     out = positions(
-        tuple(offs), scale, indices, [tile] + held[0] + held[1], eig, amps, table, coef_t
+        tuple(offs), scale, indices, [tile] + held[0] + held[1], eig, amps, table, weights, weights_t
     )
     eigen_send, eigen_keep, grads, coef_rows = out[:2], out[2:4], out[4], out[5]
 
@@ -598,7 +632,7 @@
     relative = share_of(2 * modes, blocks) > 0
     total, sent = scatter_sum("blk", eigen.reshape(blocks, -1, frame), relative)
     mine, leaving, _ = halve(keep[last], send[last], before_cross=sent)
-    moving = after(mine.astype(jnp.bfloat16), total)
+    moving = after(mine.astype(jnp.bfloat16), *sent)
     gate = moving
     for section in range(last - 1, -1, -1):
         mine, leaving, gate = halve(keep[section], send[section], before_cross=(gate,))

time: 103 us -> 107 us (1.039)
  waiting for transfers between devices: 39.4 us -> 43 us
    ppermute x21, waiting for transfers between devices: 23.3 us -> 26.2 us  [swap(): return lax.ppermute(array, axis, [(i, i ^ bit) for i in range(peers)])]
    ppermute x4, waiting for transfers between devices: 15 us -> 16.4 us  [shift(): lax.ppermute(array, axis, [(i, (i + by) % peers) for i in range(peers)])]
where the time goes in v14:
time: 107 us; the launch traced here: 106 us
  waiting for transfers between devices  43 us (40%)
  Pallas kernels  28.1 us (26%)
  starting transfers between devices  26.4 us (25%)
  local copies, waits for them, and re-layouts  3.77 us (4%)
  other arithmetic  3.43 us (3%)
  between operations  1.54 us (1%)
    ppermute x21, waiting for transfers between devices, swap(): return lax.ppermute(array, axis, [(i, i ^ bit) for i in range(peers)])  26.2 us
    pallas_call x1, Pallas kernels, positions(): pl.pallas_call(functools.partial(position_kernel, offs, scale), in_specs=...  18.4 us
    ppermute x4, waiting for transfers between devices, shift(): lax.ppermute(array, axis, [(i, (i + by) % peers) for i in range(peers)])  16.4 us
    ppermute x21, starting transfers between devices, swap(): return lax.ppermute(array, axis, [(i, i ^ bit) for i in range(peers)])  11.6 us
    ppermute x4, starting transfers between devices, shift(): lax.ppermute(array, axis, [(i, (i + by) % peers) for i in range(peers)])  11.2 us
    pallas_call x1, Pallas kernels, scatter(): pl.pallas_call(functools.partial(scatter_kernel, shares), in_specs=[pl.Bl...  5.9 us
    all_to_all x1, starting transfers between devices, on_device(): gathered = lax.all_to_all(total, 'blk', 0, 0)  3.53 us
    unnamed x14, local copies, waits for them, and re-layouts  2.75 us
  transfers between devices with their start and end apart: 26, of which 13 were waited for; matrix products, arithmetic and copies ran while one was open for 3% of the time, Pallas kernels for 8%

profile of v14, /device:TPU:0, one launch (start us, length us, event | category | flops | bytes accessed | tf_op | source)
XLA Modules:
  0.0 106.2 jit_solution(14914247791667863507)
XLA Ops:
  1.7 5.1 %collective-permute-start = (bf16[2,128,512]{2,1,0:T(8,128)(2,1)S(1)}, bf16[2,128,512]{2,1,0:T(8,128)(2,1)S(1)}, u32[]{:S(2)}, u32[]{:S(2)}) collective-permute-start(bf16[2,128,512]{2,1,0:T(8,128)(2,1)S(1)} %dynamic-slice_bitcast_fusion), channel_id=1, source_target_pairs={{0,12},{4,0},{8,4},{12,8},{1,13},{5,1},{9,5},{13,9},{2,14},{6,2},{... | collective-permute-start | bytes 786440 | tf_op jit(solution)/shard_map/ppermute | solution.py:33
  6.8 5.6 %collective-permute-done.refs_1_ = bf16[2,128,512]{2,1,0:T(8,128)(2,1)S(1)} collective-permute-done((bf16[2,128,512]{2,1,0:T(8,128)(2,1)S(1)}, bf16[2,128,512]{2,1,0:T(8,128)(2,1)S(1)}, u32[]{:S(2)}, u32[]{:S(2)}) %collective-permute-start) | collective-permute-done | bytes 262176 | tf_op jit(solution)/shard_map/ppermute | solution.py:33
  12.3 4.3 %collective-permute-start.1 = (bf16[2,128,512]{2,1,0:T(8,128)(2,1)S(1)}, bf16[2,128,512]{2,1,0:T(8,128)(2,1)S(1)}, u32[]{:S(2)}, u32[]{:S(2)}) collective-permute-start(bf16[2,128,512]{2,1,0:T(8,128)(2,1)S(1)} %collective-permute-done.refs_1_), channel_id=1, source_target_pairs={{0,12},{4,0},{8,4},{12,8},{1,13},{5,1},{9,5},{13,9},{2,14},{6,2},{... | collective-permute-start | bytes 786440 | tf_op jit(solution)/shard_map/ppermute | solution.py:33
  16.6 1.5 %collective-permute-start.2 = (bf16[2,128,512]{2,1,0:T(8,128)(2,1)S(1)}, bf16[2,128,512]{2,1,0:T(8,128)(2,1)S(1)}, u32[]{:S(2)}, u32[]{:S(2)}) collective-permute-start(bf16[2,128,512]{2,1,0:T(8,128)(2,1)S(1)} %collective-permute-done.refs_1_), channel_id=1, source_target_pairs={{0,2},{1,3},{2,0},{3,1},{4,6},{5,7},{6,4},{7,5},{8,10},{9,11},{10,... | collective-permute-start | bytes 786440 | tf_op jit(solution)/shard_map/ppermute | solution.py:38
  18.1 1.4 %copy-done.1 = bf16[6,2,256,256]{3,2,1,0:T(8,128)(2,1)S(1)} copy-done((bf16[6,2,256,256]{3,2,1,0:T(8,128)(2,1)S(1)}, bf16[6,2,256,256]{3,2,1,0:T(8,128)(2,1)}, u32[]{:S(2)}) %copy-start.1) | copy-done | bytes 1572888
  19.5 1.3 %copy-done.2 = bf16[10,256,256]{2,1,0:T(8,128)(2,1)S(1)} copy-done((bf16[10,256,256]{2,1,0:T(8,128)(2,1)S(1)}, bf16[10,256,256]{2,1,0:T(8,128)(2,1)}, u32[]{:S(2)}) %copy-start.2) | copy-done | bytes 1310744
  21.3 1.5 %collective-permute-start.5 = (bf16[2,128,512]{2,1,0:T(8,128)(2,1)S(1)}, bf16[2,128,512]{2,1,0:T(8,128)(2,1)S(1)}, u32[]{:S(2)}, u32[]{:S(2)}) collective-permute-start(bf16[2,128,512]{2,1,0:T(8,128)(2,1)S(1)} %collective-permute-done.1.refs_5_), channel_id=1, source_target_pairs={{0,2},{1,3},{2,0},{3,1},{4,6},{5,7},{6,4},{7,5},{8,10},{9,11},{10,... | collective-permute-start | bytes 786440 | tf_op jit(solution)/shard_map/ppermute | solution.py:38
  23.3 1.5 %collective-permute-done.2.refs_2_ = bf16[2,128,512]{2,1,0:T(8,128)(2,1)S(1)} collective-permute-done((bf16[2,128,512]{2,1,0:T(8,128)(2,1)S(1)}, bf16[2,128,512]{2,1,0:T(8,128)(2,1)S(1)}, u32[]{:S(2)}, u32[]{:S(2)}) %collective-permute-start.2) | collective-permute-done | bytes 262176 | tf_op jit(solution)/shard_map/ppermute | solution.py:38
  25.9 3.3 %collective-permute-done.5.refs_6_ = bf16[2,128,512]{2,1,0:T(8,128)(2,1)S(1)} collective-permute-done((bf16[2,128,512]{2,1,0:T(8,128)(2,1)S(1)}, bf16[2,128,512]{2,1,0:T(8,128)(2,1)S(1)}, u32[]{:S(2)}, u32[]{:S(2)}) %collective-permute-start.5) | collective-permute-done | bytes 262176 | tf_op jit(solution)/shard_map/ppermute | solution.py:38
  30.7 18.4 %positions.1 = (bf16[1,12,64,256]{3,2,1,0:T(8,128)(2,1)S(1)}, bf16[1,12,64,256]{3,2,1,0:T(8,128)(2,1)S(1)}, f32[1,12,64,256]{3,2,1,0:T(8,128)S(1)}, f32[1,12,64,...) custom-call(s32[2,10]{1,0:T(2,128)S(1)} %get-tuple-element.54.tile_list, ...), custom_call_target="tpu_custom_call" | custom-call | tf_op jit(solution)/shard_map/positions/pallas_call | solution.py:377
  49.7 1.2 %collective-permute-done.8 = bf16[1,12,64,256]{3,2,1,0:T(8,128)(2,1)S(1)} collective-permute-done((bf16[1,12,64,256]{3,2,1,0:T(8,128)(2,1)S(1)}, bf16[1,12,64,256]{3,2,1,0:T(8,128)(2,1)S(1)}, u32[]{:S(2)}, u32[]{:S(2)}) %collective-permute-start.8) | collective-permute-done | bytes 393248 | tf_op jit(solution)/shard_map/ppermute | solution.py:38
  51.1 5.9 %scatter.1 = (bf16[1,2,4,128,128]{4,3,2,1,0:T(8,128)(2,1)S(1)}, bf16[1,2,4,128,128]{4,3,2,1,0:T(8,128)(2,1)S(1)}, bf16[1,2,4,128,128]{4,3,2,1,0:T(8,128)(2,1)S(1...) custom-call(s32[2,10]{1,0:T(2,128)S(1)} %get-tuple-element.54.tile_l, ...), custom_call_target="tpu_custom_call" | custom-call | flops 16777216 | bytes 16777216 | tf_op jit(solution)/shard_map/scatter/pallas_call | solution.py:495
  57.6 4.7 %collective-permute-done.15 = bf16[1,12,64,256]{3,2,1,0:T(8,128)(2,1)S(1)} collective-permute-done((bf16[1,12,64,256]{3,2,1,0:T(8,128)(2,1)S(1)}, bf16[1,12,64,256]{3,2,1,0:T(8,128)(2,1)S(1)}, u32[]{:S(2)}, u32[]{:S(2)}) %collective-permute-start.15) | collective-permute-done | bytes 393248 | tf_op jit(solution)/shard_map/ppermute | solution.py:38
  63.4 6.7 %collective-permute-done.16 = bf16[1,2,4,128,128]{4,3,2,1,0:T(8,128)(2,1)S(1)} collective-permute-done((bf16[1,2,4,128,128]{4,3,2,1,0:T(8,128)(2,1)S(1)}, bf16[1,2,4,128,128]{4,3,2,1,0:T(8,128)(2,1)S(1)}, u32[]{:S(2)}, u32[]{:S(2)}) %collective-permute-start.16) | collective-permute-done | bytes 262176 | tf_op jit(solution)/shard_map/ppermute | solution.py:38
  72.4 2.9 %collective-permute-start.24 = (bf16[192,256]{1,0:T(8,128)(2,1)S(1)}, bf16[192,256]{1,0:T(8,128)(2,1)S(1)}, u32[]{:S(2)}, u32[]{:S(2)}) collective-permute-start(bf16[192,256]{1,0:T(8,128)(2,1)S(1)} %bitcast.29), channel_id=1, source_target_pairs={{0,12},{4,8},{8,4},{12,0},{1,13},{5,9},{9,5},{13,1},{2,14},{6,10},... | collective-permute-start | bytes 294920 | tf_op jit(solution)/shard_map/ppermute | solution.py:38
  75.9 4.9 %collective-permute-done.23.refs_1_ = bf16[192,256]{1,0:T(8,128)(2,1)S(1)} collective-permute-done((bf16[192,256]{1,0:T(8,128)(2,1)S(1)}, bf16[192,256]{1,0:T(8,128)(2,1)S(1)}, u32[]{:S(2)}, u32[]{:S(2)}) %collective-permute-start.23) | collective-permute-done | bytes 98336 | tf_op jit(solution)/shard_map/ppermute | solution.py:38
  80.7 1.8 %collective-permute-start.19 = (bf16[2,4,128,128]{3,2,1,0:T(8,128)(2,1)S(1)}, bf16[2,4,128,128]{3,2,1,0:T(8,128)(2,1)}, u32[]{:S(2)}, u32[]{:S(2)}) collective-permute-start(bf16[2,4,128,128]{3,2,1,0:T(8,128)(2,1)S(1)} %fusion.1), channel_id=1, source_target_pairs={{0,4},{4,8},{8,12},{12,0},{1,5},{5,9},{9,13},{13,1},{2,6},{6,10},{... | collective-permute-start | bytes 786440 | tf_op jit(solution)/shard_map/ppermute | solution.py:33
  83.4 3.5 %all-to-all-start = ((bf16[4,192,256]{2,1,0:T(8,128)(2,1)}), bf16[4,192,256]{2,1,0:T(8,128)(2,1)S(1)}, u32[]{:S(2)}, u32[]{:S(2)}) async-start(bf16[4,192,256]{2,1,0:T(8,128)(2,1)} %add_up.1), calls=%async_computation | async-start | bytes 786432 | tf_op jit(solution)/shard_map/all_to_all | solution.py:644
  87.0 1.1 %collective-permute-start.18 = (bf16[1,2,4,128,128]{4,3,2,1,0:T(8,128)(2,1)S(1)}, bf16[1,2,4,128,128]{4,3,2,1,0:T(8,128)(2,1)S(1)}, u32[]{:S(2)}, u32[]{:S(2)}) collective-permute-start(bf16[1,2,4,128,128]{4,3,2,1,0:T(8,128)(2,1)S(1)} %add_convert_fusion.1), channel_id=1, source_target_pairs={{0,2},{1,3},{2,0},{3,1},{4,6},{5,7},{6,4},{7,5},{8,10},{9,11},{10,... | collective-permute-start | bytes 786440 | tf_op jit(solution)/shard_map/ppermute | solution.py:38
  88.1 3.3 %collective-permute-done.19 = bf16[2,4,128,128]{3,2,1,0:T(8,128)(2,1)} collective-permute-done((bf16[2,4,128,128]{3,2,1,0:T(8,128)(2,1)S(1)}, bf16[2,4,128,128]{3,2,1,0:T(8,128)(2,1)}, u32[]{:S(2)}, u32[]{:S(2)}) %collective-permute-start.19) | collective-permute-done | bytes 262176 | tf_op jit(solution)/shard_map/ppermute | solution.py:33
  91.5 1.2 %fusion = bf16[2,4,128,128]{3,2,1,0:T(8,128)(2,1)S(1)} fusion(bf16[1,2,4,128,128]{4,3,2,1,0:T(8,128)(2,1)S(1)} %collective-permute-done.17, f32[1,2,4,128,128]{4,3,2,1,0:T(8,128)S(1)} %get-tuple-element.83, bf16[1,2,4,128,128]{4,3,2,1,0:T(8,128)(2,1)} %collective-permute-done.20, bf16[2,4,128,128]{3,2,1,0:T(8,128)(2,1)} %collective-permute-done.19), kind=kLoop, calls=%fused_computation.3 | loop fusion | flops 917504 | bytes 1572864 | tf_op jit(solution)/shard_map/convert_element_type | solution.py:643
  92.7 3.0 %collective-permute-done.18 = bf16[1,2,4,128,128]{4,3,2,1,0:T(8,128)(2,1)S(1)} collective-permute-done((bf16[1,2,4,128,128]{4,3,2,1,0:T(8,128)(2,1)S(1)}, bf16[1,2,4,128,128]{4,3,2,1,0:T(8,128)(2,1)S(1)}, u32[]{:S(2)}, u32[]{:S(2)}) %collective-permute-start.18) | collective-permute-done | bytes 262176 | tf_op jit(solution)/shard_map/ppermute | solution.py:38
  95.7 1.0 add_bitcast_fusion.first
  96.8 7.3 %collective-permute-done.21.second = bf16[2,4,128,128]{3,2,1,0:T(8,128)(2,1)S(1)} collective-permute-done((bf16[2,4,128,128]{3,2,1,0:T(8,128)(2,1)S(1)}, bf16[2,4,128,128]{3,2,1,0:T(8,128)(2,1)S(1)}, u32[]{:S(2)}, u32[]{:S(2)}) %collective-permute-start.21) | collective-permute-done | bytes 262176 | tf_op jit(solution)/shard_map/ppermute | solution.py:33
  (60 shorter events, 12.4 us)
Async XLA Ops:
  1.7 10.7 %collective-permute-start = (bf16[2,128,512]{2,1,0:T(8,128)(2,1)S(1)}, bf16[2,128,512]{2,1,0:T(8,128)(2,1)S(1)}, u32[]{:S(2)}, u32[]{:S(2)}) collective-permute-start(bf16[2,128,512]{2,1,0:T(8,128)(2,1)S(1)} %dynamic-slice_bitcast_fusion), channel_id=1, source_target_pairs={{0,12},{4,0},{8,4},{12,8},{1,13},{5,1},{9,5},{13,9},{2,14},{6,2},{... | collective-permute-start | bytes 786440 | tf_op jit(solution)/shard_map/ppermute | solution.py:33
  12.3 9.0 %collective-permute-start.1 = (bf16[2,128,512]{2,1,0:T(8,128)(2,1)S(1)}, bf16[2,128,512]{2,1,0:T(8,128)(2,1)S(1)}, u32[]{:S(2)}, u32[]{:S(2)}) collective-permute-start(bf16[2,128,512]{2,1,0:T(8,128)(2,1)S(1)} %collective-permute-done.refs_1_), channel_id=1, source_target_pairs={{0,12},{4,0},{8,4},{12,8},{1,13},{5,1},{9,5},{13,9},{2,14},{6,2},{... | collective-permute-start | bytes 786440 | tf_op jit(solution)/shard_map/ppermute | solution.py:33
  16.6 8.2 %collective-permute-start.2 = (bf16[2,128,512]{2,1,0:T(8,128)(2,1)S(1)}, bf16[2,128,512]{2,1,0:T(8,128)(2,1)S(1)}, u32[]{:S(2)}, u32[]{:S(2)}) collective-permute-start(bf16[2,128,512]{2,1,0:T(8,128)(2,1)S(1)} %collective-permute-done.refs_1_), channel_id=1, source_target_pairs={{0,2},{1,3},{2,0},{3,1},{4,6},{5,7},{6,4},{7,5},{8,10},{9,11},{10,... | collective-permute-start | bytes 786440 | tf_op jit(solution)/shard_map/ppermute | solution.py:38
  21.3 7.8 %collective-permute-start.5 = (bf16[2,128,512]{2,1,0:T(8,128)(2,1)S(1)}, bf16[2,128,512]{2,1,0:T(8,128)(2,1)S(1)}, u32[]{:S(2)}, u32[]{:S(2)}) collective-permute-start(bf16[2,128,512]{2,1,0:T(8,128)(2,1)S(1)} %collective-permute-done.1.refs_5_), channel_id=1, source_target_pairs={{0,2},{1,3},{2,0},{3,1},{4,6},{5,7},{6,4},{7,5},{8,10},{9,11},{10,... | collective-permute-start | bytes 786440 | tf_op jit(solution)/shard_map/ppermute | solution.py:38
  22.8 7.0 %collective-permute-start.3 = (bf16[2,128,512]{2,1,0:T(8,128)(2,1)S(1)}, bf16[2,128,512]{2,1,0:T(8,128)(2,1)S(1)}, u32[]{:S(2)}, u32[]{:S(2)}) collective-permute-start(bf16[2,128,512]{2,1,0:T(8,128)(2,1)S(1)} %collective-permute-done.refs_1_), channel_id=1, source_target_pairs={{0,1},{1,0},{2,3},{3,2},{4,5},{5,4},{6,7},{7,6},{8,9},{9,8},{10,11... | collective-permute-start | bytes 786440 | tf_op jit(solution)/shard_map/ppermute | solution.py:38
  22.8 7.0 %collective-permute-start.6 = (bf16[2,128,512]{2,1,0:T(8,128)(2,1)S(1)}, bf16[2,128,512]{2,1,0:T(8,128)(2,1)S(1)}, u32[]{:S(2)}, u32[]{:S(2)}) collective-permute-start(bf16[2,128,512]{2,1,0:T(8,128)(2,1)S(1)} %collective-permute-done.1.refs_5_), channel_id=1, source_target_pairs={{0,1},{1,0},{2,3},{3,2},{4,5},{5,4},{6,7},{7,6},{8,9},{9,8},{10,11... | collective-permute-start | bytes 786440 | tf_op jit(solution)/shard_map/ppermute | solution.py:38
  24.8 5.0 %collective-permute-start.4 = (bf16[2,128,512]{2,1,0:T(8,128)(2,1)S(1)}, bf16[2,128,512]{2,1,0:T(8,128)(2,1)S(1)}, u32[]{:S(2)}, u32[]{:S(2)}) collective-permute-start(bf16[2,128,512]{2,1,0:T(8,128)(2,1)S(1)} %collective-permute-done.2.refs_2_), channel_id=1, source_target_pairs={{0,1},{1,0},{2,3},{3,2},{4,5},{5,4},{6,7},{7,6},{8,9},{9,8},{10,11... | collective-permute-start | bytes 786440 | tf_op jit(solution)/shard_map/ppermute | solution.py:38
  49.2 8.3 %collective-permute-start.14 = (bf16[1,12,64,256]{3,2,1,0:T(8,128)(2,1)S(1)}, bf16[1,12,64,256]{3,2,1,0:T(8,128)(2,1)S(1)}, u32[]{:S(2)}, u32[]{:S(2)}) collective-permute-start(bf16[1,12,64,256]{3,2,1,0:T(8,128)(2,1)S(1)} %get-tuple-element.78), channel_id=1, source_target_pairs={{0,1},{1,0},{2,3},{3,2},{4,5},{5,4},{6,7},{7,6},{8,9},{9,8},{10,11... | collective-permute-start | bytes 1179656 | tf_op jit(solution)/shard_map/ppermute | solution.py:38
  51.0 11.2 %collective-permute-start.15 = (bf16[1,12,64,256]{3,2,1,0:T(8,128)(2,1)S(1)}, bf16[1,12,64,256]{3,2,1,0:T(8,128)(2,1)S(1)}, u32[]{:S(2)}, u32[]{:S(2)}) collective-permute-start(bf16[1,12,64,256]{3,2,1,0:T(8,128)(2,1)S(1)} %add_convert_fusion), channel_id=1, source_target_pairs={{0,2},{1,3},{2,0},{3,1},{4,6},{5,7},{6,4},{7,5},{8,10},{9,11},{10,... | collective-permute-start | bytes 1179656 | tf_op jit(solution)/shard_map/ppermute | solution.py:38
  57.0 6.4 %collective-permute-start.12 = (bf16[1,2,4,128,128]{4,3,2,1,0:T(8,128)(2,1)S(1)}, bf16[1,2,4,128,128]{4,3,2,1,0:T(8,128)(2,1)S(1)}, u32[]{:S(2)}, u32[]{:S(2)}) collective-permute-start(bf16[1,2,4,128,128]{4,3,2,1,0:T(8,128)(2,1)S(1)} %get-tuple-element.74), channel_id=1, source_target_pairs={{0,1},{1,0},{2,3},{3,2},{4,5},{5,4},{6,7},{7,6},{8,9},{9,8},{10,11... | collective-permute-start | bytes 786440 | tf_op jit(solution)/shard_map/ppermute | solution.py:38
  57.3 5.2 %collective-permute-start.13 = (bf16[1,2,4,128,128]{4,3,2,1,0:T(8,128)(2,1)S(1)}, bf16[1,2,4,128,128]{4,3,2,1,0:T(8,128)(2,1)S(1)}, u32[]{:S(2)}, u32[]{:S(2)}) collective-permute-start(bf16[1,2,4,128,128]{4,3,2,1,0:T(8,128)(2,1)S(1)} %get-tuple-element.76), channel_id=1, source_target_pairs={{0,1},{1,0},{2,3},{3,2},{4,5},{5,4},{6,7},{7,6},{8,9},{9,8},{10,11... | collective-permute-start | bytes 786440 | tf_op jit(solution)/shard_map/ppermute | solution.py:38
  62.5 7.6 %collective-permute-start.16 = (bf16[1,2,4,128,128]{4,3,2,1,0:T(8,128)(2,1)S(1)}, bf16[1,2,4,128,128]{4,3,2,1,0:T(8,128)(2,1)S(1)}, u32[]{:S(2)}, u32[]{:S(2)}) collective-permute-start(bf16[1,2,4,128,128]{4,3,2,1,0:T(8,128)(2,1)S(1)} %add_convert_fusion.4), channel_id=1, source_target_pairs={{0,2},{1,3},{2,0},{3,1},{4,6},{5,7},{6,4},{7,5},{8,10},{9,11},{10,... | collective-permute-start | bytes 786440 | tf_op jit(solution)/shard_map/ppermute | solution.py:38
  62.9 7.3 %collective-permute-start.11 = (bf16[1,2,4,128,128]{4,3,2,1,0:T(8,128)(2,1)S(1)}, bf16[1,2,4,128,128]{4,3,2,1,0:T(8,128)(2,1)S(1)}, u32[]{:S(2)}, u32[]{:S(2)}) collective-permute-start(bf16[1,2,4,128,128]{4,3,2,1,0:T(8,128)(2,1)S(1)} %get-tuple-element.72), channel_id=1, source_target_pairs={{0,1},{1,0},{2,3},{3,2},{4,5},{5,4},{6,7},{7,6},{8,9},{9,8},{10,11... | collective-permute-start | bytes 786440 | tf_op jit(solution)/shard_map/ppermute | solution.py:38
  62.9 24.1 %collective-permute-start.10 = (bf16[1,2,4,128,128]{4,3,2,1,0:T(8,128)(2,1)S(1)}, bf16[1,2,4,128,128]{4,3,2,1,0:T(8,128)(2,1)S(1)}, u32[]{:S(2)}, u32[]{:S(2)}) collective-permute-start(bf16[1,2,4,128,128]{4,3,2,1,0:T(8,128)(2,1)S(1)} %get-tuple-element.70), channel_id=1, source_target_pairs={{0,1},{1,0},{2,3},{3,2},{4,5},{5,4},{6,7},{7,6},{8,9},{9,8},{10,11... | collective-permute-start | bytes 786440 | tf_op jit(solution)/shard_map/ppermute | solution.py:38
  71.0 16.0 %collective-permute-start.17 = (bf16[1,2,4,128,128]{4,3,2,1,0:T(8,128)(2,1)}, bf16[1,2,4,128,128]{4,3,2,1,0:T(8,128)(2,1)S(1)}, u32[]{:S(2)}, u32[]{:S(2)}) collective-permute-start(bf16[1,2,4,128,128]{4,3,2,1,0:T(8,128)(2,1)} %add_convert_fusion.2), channel_id=1, source_target_pairs={{0,2},{1,3},{2,0},{3,1},{4,6},{5,7},{6,4},{7,5},{8,10},{9,11},{10,... | collective-permute-start | bytes 786440 | tf_op jit(solution)/shard_map/ppermute | solution.py:38
  71.6 9.2 %collective-permute-start.23 = (bf16[192,256]{1,0:T(8,128)(2,1)S(1)}, bf16[192,256]{1,0:T(8,128)(2,1)S(1)}, u32[]{:S(2)}, u32[]{:S(2)}) collective-permute-start(bf16[192,256]{1,0:T(8,128)(2,1)S(1)} %bitcast.30), channel_id=1, source_target_pairs={{0,8},{4,12},{8,0},{12,4},{1,9},{5,13},{9,1},{13,5},{2,10},{6,14},... | collective-permute-start | bytes 294920 | tf_op jit(solution)/shard_map/ppermute | solution.py:38
  72.4 8.3 %collective-permute-start.24 = (bf16[192,256]{1,0:T(8,128)(2,1)S(1)}, bf16[192,256]{1,0:T(8,128)(2,1)S(1)}, u32[]{:S(2)}, u32[]{:S(2)}) collective-permute-start(bf16[192,256]{1,0:T(8,128)(2,1)S(1)} %bitcast.29), channel_id=1, source_target_pairs={{0,12},{4,8},{8,4},{12,0},{1,13},{5,9},{9,5},{13,1},{2,14},{6,10},... | collective-permute-start | bytes 294920 | tf_op jit(solution)/shard_map/ppermute | solution.py:38
  75.3 7.2 %collective-permute-start.22 = (bf16[192,256]{1,0:T(8,128)(2,1)S(1)}, bf16[192,256]{1,0:T(8,128)(2,1)S(1)}, u32[]{:S(2)}, u32[]{:S(2)}) collective-permute-start(bf16[192,256]{1,0:T(8,128)(2,1)S(1)} %bitcast.28), channel_id=1, source_target_pairs={{0,4},{4,0},{8,12},{12,8},{1,5},{5,1},{9,13},{13,9},{2,6},{6,2},{1... | collective-permute-start | bytes 294920 | tf_op jit(solution)/shard_map/ppermute | solution.py:38
  80.7 7.4 %collective-permute-start.20 = (bf16[1,2,4,128,128]{4,3,2,1,0:T(8,128)(2,1)S(1)}, bf16[1,2,4,128,128]{4,3,2,1,0:T(8,128)(2,1)}, u32[]{:S(2)}, u32[]{:S(2)}) collective-permute-start(bf16[1,2,4,128,128]{4,3,2,1,0:T(8,128)(2,1)S(1)} %get-tuple-element.84), channel_id=1, source_target_pairs={{0,1},{1,0},{2,3},{3,2},{4,5},{5,4},{6,7},{7,6},{8,9},{9,8},{10,11... | collective-permute-start | bytes 786440 | tf_op jit(solution)/shard_map/ppermute | solution.py:38
  80.7 10.7 %collective-permute-start.19 = (bf16[2,4,128,128]{3,2,1,0:T(8,128)(2,1)S(1)}, bf16[2,4,128,128]{3,2,1,0:T(8,128)(2,1)}, u32[]{:S(2)}, u32[]{:S(2)}) collective-permute-start(bf16[2,4,128,128]{3,2,1,0:T(8,128)(2,1)S(1)} %fusion.1), channel_id=1, source_target_pairs={{0,4},{4,8},{8,12},{12,0},{1,5},{5,9},{9,13},{13,1},{2,6},{6,10},{... | collective-permute-start | bytes 786440 | tf_op jit(solution)/shard_map/ppermute | solution.py:33
  82.5 10.2 %collective-permute-start.9 = (bf16[1,2,4,128,128]{4,3,2,1,0:T(8,128)(2,1)S(1)}, bf16[1,2,4,128,128]{4,3,2,1,0:T(8,128)(2,1)}, u32[]{:S(2)}, u32[]{:S(2)}) collective-permute-start(bf16[1,2,4,128,128]{4,3,2,1,0:T(8,128)(2,1)S(1)} %get-tuple-element.68), channel_id=1, source_target_pairs={{0,1},{1,0},{2,3},{3,2},{4,5},{5,4},{6,7},{7,6},{8,9},{9,8},{10,11... | collective-permute-start | bytes 786440 | tf_op jit(solution)/shard_map/ppermute | solution.py:38
  83.4 21.9 %all-to-all-start = ((bf16[4,192,256]{2,1,0:T(8,128)(2,1)}), bf16[4,192,256]{2,1,0:T(8,128)(2,1)S(1)}, u32[]{:S(2)}, u32[]{:S(2)}) async-start(bf16[4,192,256]{2,1,0:T(8,128)(2,1)} %add_up.1), calls=%async_computation | async-start | bytes 786432 | tf_op jit(solution)/shard_map/all_to_all | solution.py:644
  87.0 8.7 %collective-permute-start.18 = (bf16[1,2,4,128,128]{4,3,2,1,0:T(8,128)(2,1)S(1)}, bf16[1,2,4,128,128]{4,3,2,1,0:T(8,128)(2,1)S(1)}, u32[]{:S(2)}, u32[]{:S(2)}) collective-permute-start(bf16[1,2,4,128,128]{4,3,2,1,0:T(8,128)(2,1)S(1)} %add_convert_fusion.1), channel_id=1, source_target_pairs={{0,2},{1,3},{2,0},{3,1},{4,6},{5,7},{6,4},{7,5},{8,10},{9,11},{10,... | collective-permute-start | bytes 786440 | tf_op jit(solution)/shard_map/ppermute | solution.py:38
  92.6 11.4 %collective-permute-start.21 = (bf16[2,4,128,128]{3,2,1,0:T(8,128)(2,1)S(1)}, bf16[2,4,128,128]{3,2,1,0:T(8,128)(2,1)S(1)}, u32[]{:S(2)}, u32[]{:S(2)}) collective-permute-start(bf16[2,4,128,128]{3,2,1,0:T(8,128)(2,1)S(1)} %fusion), channel_id=1, source_target_pairs={{0,4},{4,8},{8,12},{12,0},{1,5},{5,9},{9,13},{13,1},{2,6},{6,10},{... | collective-permute-start | bytes 786440 | tf_op jit(solution)/shard_map/ppermute | solution.py:33
  (9 other events, 105.8 us)

commit v15 on v14

--- a/solution.py
+++ b/solution.py
@@ -632,7 +632,7 @@
     relative = share_of(2 * modes, blocks) > 0
     total, sent = scatter_sum("blk", eigen.reshape(blocks, -1, frame), relative)
     mine, leaving, _ = halve(keep[last], send[last], before_cross=sent)
-    moving = after(mine.astype(jnp.bfloat16), *sent)
+    moving = after(mine.astype(jnp.bfloat16), total)
     gate = moving
     for section in range(last - 1, -1, -1):
         mine, leaving, gate = halve(keep[section], send[section], before_cross=(gate,))

time: 107 us -> 102 us (0.953)
  waiting for transfers between devices: 43 us -> 37.7 us
  starting transfers between devices: 26.4 us -> 28 us
    ppermute x21, waiting for transfers between devices: 26.2 us -> 21.5 us  [swap(): return lax.ppermute(array, axis, [(i, i ^ bit) for i in range(peers)])]
    ppermute x4, waiting for transfers between devices: 16.4 us -> 15.1 us  [shift(): lax.ppermute(array, axis, [(i, (i + by) % peers) for i in range(peers)])]
    ppermute x21, starting transfers between devices: 11.6 us -> 13 us  [swap(): return lax.ppermute(array, axis, [(i, i ^ bit) for i in range(peers)])]
  transfers between devices with their start and end apart: 26 -> 26, of which waited for: 13 -> 14; matrix products, arithmetic and copies ran while one was open for 3% -> 3% of each run, Pallas kernels for 8% -> 9%
where the time goes in v15:
time: 102 us
  waiting for transfers between devices  37.7 us (37%)
  Pallas kernels  28.2 us (28%)
  starting transfers between devices  28 us (27%)
  local copies, waits for them, and re-layouts  3.77 us (4%)
  other arithmetic  2.56 us (3%)
  between operations  1.52 us (1%)
    ppermute x21, waiting for transfers between devices, swap(): return lax.ppermute(array, axis, [(i, i ^ bit) for i in range(peers)])  21.5 us
    pallas_call x1, Pallas kernels, positions(): pl.pallas_call(functools.partial(position_kernel, offs, scale), in_specs=...  18.4 us
    ppermute x4, waiting for transfers between devices, shift(): lax.ppermute(array, axis, [(i, (i + by) % peers) for i in range(peers)])  15.1 us
    ppermute x21, starting transfers between devices, swap(): return lax.ppermute(array, axis, [(i, i ^ bit) for i in range(peers)])  13 us
    ppermute x4, starting transfers between devices, shift(): lax.ppermute(array, axis, [(i, (i + by) % peers) for i in range(peers)])  11.5 us
    pallas_call x1, Pallas kernels, scatter(): pl.pallas_call(functools.partial(scatter_kernel, shares), in_specs=[pl.Bl...  5.98 us
    all_to_all x1, starting transfers between devices, on_device(): gathered = lax.all_to_all(total, 'blk', 0, 0)  3.47 us
    unnamed x14, local copies, waits for them, and re-layouts  2.75 us
  transfers between devices with their start and end apart: 26, of which 14 were waited for; matrix products, arithmetic and copies ran while one was open for 3% of the time, Pallas kernels for 9%

profile of v15, /device:TPU:0, one launch (start us, length us, event | category | flops | bytes accessed | tf_op | source)
XLA Modules:
  0.0 101.7 jit_solution(14975735206877266122)
XLA Ops:
  1.7 5.1 %collective-permute-start = (bf16[2,128,512]{2,1,0:T(8,128)(2,1)S(1)}, bf16[2,128,512]{2,1,0:T(8,128)(2,1)S(1)}, u32[]{:S(2)}, u32[]{:S(2)}) collective-permute-start(bf16[2,128,512]{2,1,0:T(8,128)(2,1)S(1)} %dynamic-slice_bitcast_fusion), channel_id=1, source_target_pairs={{0,12},{4,0},{8,4},{12,8},{1,13},{5,1},{9,5},{13,9},{2,14},{6,2},{... | collective-permute-start | bytes 786440 | tf_op jit(solution)/shard_map/ppermute | solution.py:33
  6.8 5.6 %collective-permute-done.refs_1_ = bf16[2,128,512]{2,1,0:T(8,128)(2,1)S(1)} collective-permute-done((bf16[2,128,512]{2,1,0:T(8,128)(2,1)S(1)}, bf16[2,128,512]{2,1,0:T(8,128)(2,1)S(1)}, u32[]{:S(2)}, u32[]{:S(2)}) %collective-permute-start) | collective-permute-done | bytes 262176 | tf_op jit(solution)/shard_map/ppermute | solution.py:33
  12.3 4.3 %collective-permute-start.1 = (bf16[2,128,512]{2,1,0:T(8,128)(2,1)S(1)}, bf16[2,128,512]{2,1,0:T(8,128)(2,1)S(1)}, u32[]{:S(2)}, u32[]{:S(2)}) collective-permute-start(bf16[2,128,512]{2,1,0:T(8,128)(2,1)S(1)} %collective-permute-done.refs_1_), channel_id=1, source_target_pairs={{0,12},{4,0},{8,4},{12,8},{1,13},{5,1},{9,5},{13,9},{2,14},{6,2},{... | collective-permute-start | bytes 786440 | tf_op jit(solution)/shard_map/ppermute | solution.py:33
  16.6 1.5 %collective-permute-start.2 = (bf16[2,128,512]{2,1,0:T(8,128)(2,1)S(1)}, bf16[2,128,512]{2,1,0:T(8,128)(2,1)S(1)}, u32[]{:S(2)}, u32[]{:S(2)}) collective-permute-start(bf16[2,128,512]{2,1,0:T(8,128)(2,1)S(1)} %collective-permute-done.refs_1_), channel_id=1, source_target_pairs={{0,2},{1,3},{2,0},{3,1},{4,6},{5,7},{6,4},{7,5},{8,10},{9,11},{10,... | collective-permute-start | bytes 786440 | tf_op jit(solution)/shard_map/ppermute | solution.py:38
  18.1 1.4 %copy-done.1 = bf16[6,2,256,256]{3,2,1,0:T(8,128)(2,1)S(1)} copy-done((bf16[6,2,256,256]{3,2,1,0:T(8,128)(2,1)S(1)}, bf16[6,2,256,256]{3,2,1,0:T(8,128)(2,1)}, u32[]{:S(2)}) %copy-start.1) | copy-done | bytes 1572888
  19.5 1.3 %copy-done.2 = bf16[10,256,256]{2,1,0:T(8,128)(2,1)S(1)} copy-done((bf16[10,256,256]{2,1,0:T(8,128)(2,1)S(1)}, bf16[10,256,256]{2,1,0:T(8,128)(2,1)}, u32[]{:S(2)}) %copy-start.2) | copy-done | bytes 1310744
  21.3 1.5 %collective-permute-start.5 = (bf16[2,128,512]{2,1,0:T(8,128)(2,1)S(1)}, bf16[2,128,512]{2,1,0:T(8,128)(2,1)S(1)}, u32[]{:S(2)}, u32[]{:S(2)}) collective-permute-start(bf16[2,128,512]{2,1,0:T(8,128)(2,1)S(1)} %collective-permute-done.1.refs_5_), channel_id=1, source_target_pairs={{0,2},{1,3},{2,0},{3,1},{4,6},{5,7},{6,4},{7,5},{8,10},{9,11},{10,... | collective-permute-start | bytes 786440 | tf_op jit(solution)/shard_map/ppermute | solution.py:38
  23.3 1.5 %collective-permute-done.2.refs_2_ = bf16[2,128,512]{2,1,0:T(8,128)(2,1)S(1)} collective-permute-done((bf16[2,128,512]{2,1,0:T(8,128)(2,1)S(1)}, bf16[2,128,512]{2,1,0:T(8,128)(2,1)S(1)}, u32[]{:S(2)}, u32[]{:S(2)}) %collective-permute-start.2) | collective-permute-done | bytes 262176 | tf_op jit(solution)/shard_map/ppermute | solution.py:38
  25.9 3.3 %collective-permute-done.5.refs_6_ = bf16[2,128,512]{2,1,0:T(8,128)(2,1)S(1)} collective-permute-done((bf16[2,128,512]{2,1,0:T(8,128)(2,1)S(1)}, bf16[2,128,512]{2,1,0:T(8,128)(2,1)S(1)}, u32[]{:S(2)}, u32[]{:S(2)}) %collective-permute-start.5) | collective-permute-done | bytes 262176 | tf_op jit(solution)/shard_map/ppermute | solution.py:38
  30.7 18.4 %positions.1 = (bf16[1,12,64,256]{3,2,1,0:T(8,128)(2,1)S(1)}, bf16[1,12,64,256]{3,2,1,0:T(8,128)(2,1)S(1)}, f32[1,12,64,256]{3,2,1,0:T(8,128)S(1)}, f32[1,12,64,...) custom-call(s32[2,10]{1,0:T(2,128)S(1)} %get-tuple-element.54.tile_list, ...), custom_call_target="tpu_custom_call" | custom-call | tf_op jit(solution)/shard_map/positions/pallas_call | solution.py:377
  49.7 1.2 %collective-permute-done.8 = bf16[1,12,64,256]{3,2,1,0:T(8,128)(2,1)S(1)} collective-permute-done((bf16[1,12,64,256]{3,2,1,0:T(8,128)(2,1)S(1)}, bf16[1,12,64,256]{3,2,1,0:T(8,128)(2,1)S(1)}, u32[]{:S(2)}, u32[]{:S(2)}) %collective-permute-start.8) | collective-permute-done | bytes 393248 | tf_op jit(solution)/shard_map/ppermute | solution.py:38
  51.0 1.6 %collective-permute-start.15 = (bf16[1,12,64,256]{3,2,1,0:T(8,128)(2,1)S(1)}, bf16[1,12,64,256]{3,2,1,0:T(8,128)(2,1)S(1)}, u32[]{:S(2)}, u32[]{:S(2)}) collective-permute-start(bf16[1,12,64,256]{3,2,1,0:T(8,128)(2,1)S(1)} %add_convert_fusion), channel_id=1, source_target_pairs={{0,2},{1,3},{2,0},{3,1},{4,6},{5,7},{6,4},{7,5},{8,10},{9,11},{10,... | collective-permute-start | bytes 1179656 | tf_op jit(solution)/shard_map/ppermute | solution.py:38
  52.6 6.0 %scatter.1 = (bf16[1,2,4,128,128]{4,3,2,1,0:T(8,128)(2,1)S(1)}, bf16[1,2,4,128,128]{4,3,2,1,0:T(8,128)(2,1)S(1)}, bf16[1,2,4,128,128]{4,3,2,1,0:T(8,128)(2,1)S(1...) custom-call(s32[2,10]{1,0:T(2,128)S(1)} %get-tuple-element.54.tile_l, ...), custom_call_target="tpu_custom_call" | custom-call | flops 16777216 | bytes 16777216 | tf_op jit(solution)/shard_map/scatter/pallas_call | solution.py:495
  59.1 3.1 %collective-permute-done.15 = bf16[1,12,64,256]{3,2,1,0:T(8,128)(2,1)S(1)} collective-permute-done((bf16[1,12,64,256]{3,2,1,0:T(8,128)(2,1)S(1)}, bf16[1,12,64,256]{3,2,1,0:T(8,128)(2,1)S(1)}, u32[]{:S(2)}, u32[]{:S(2)}) %collective-permute-start.15) | collective-permute-done | bytes 393248 | tf_op jit(solution)/shard_map/ppermute | solution.py:38
  62.5 1.5 %collective-permute-start.16 = (bf16[1,2,4,128,128]{4,3,2,1,0:T(8,128)(2,1)S(1)}, bf16[1,2,4,128,128]{4,3,2,1,0:T(8,128)(2,1)S(1)}, u32[]{:S(2)}, u32[]{:S(2)}) collective-permute-start(bf16[1,2,4,128,128]{4,3,2,1,0:T(8,128)(2,1)S(1)} %add_convert_fusion.4), channel_id=1, source_target_pairs={{0,2},{1,3},{2,0},{3,1},{4,6},{5,7},{6,4},{7,5},{8,10},{9,11},{10,... | collective-permute-start | bytes 786440 | tf_op jit(solution)/shard_map/ppermute | solution.py:38
  64.1 2.8 %collective-permute-start.19 = (bf16[192,256]{1,0:T(8,128)(2,1)S(1)}, bf16[192,256]{1,0:T(8,128)(2,1)S(1)}, u32[]{:S(2)}, u32[]{:S(2)}) collective-permute-start(bf16[192,256]{1,0:T(8,128)(2,1)S(1)} %bitcast.29), channel_id=1, source_target_pairs={{0,12},{4,8},{8,4},{12,0},{1,13},{5,9},{9,5},{13,1},{2,14},{6,10},... | collective-permute-start | bytes 294920 | tf_op jit(solution)/shard_map/ppermute | solution.py:38
  67.5 5.7 %collective-permute-done.18.refs_1_ = bf16[192,256]{1,0:T(8,128)(2,1)S(1)} collective-permute-done((bf16[192,256]{1,0:T(8,128)(2,1)S(1)}, bf16[192,256]{1,0:T(8,128)(2,1)S(1)}, u32[]{:S(2)}, u32[]{:S(2)}) %collective-permute-start.18) | collective-permute-done | bytes 98336 | tf_op jit(solution)/shard_map/ppermute | solution.py:38
  76.2 1.8 %collective-permute-start.22 = (bf16[2,4,128,128]{3,2,1,0:T(8,128)(2,1)S(1)}, bf16[2,4,128,128]{3,2,1,0:T(8,128)(2,1)}, u32[]{:S(2)}, u32[]{:S(2)}) collective-permute-start(bf16[2,4,128,128]{3,2,1,0:T(8,128)(2,1)S(1)} %fusion.1), channel_id=1, source_target_pairs={{0,4},{4,8},{8,12},{12,0},{1,5},{5,9},{9,13},{13,1},{2,6},{6,10},{... | collective-permute-start | bytes 786440 | tf_op jit(solution)/shard_map/ppermute | solution.py:33
  78.1 3.5 %all-to-all-start = ((bf16[4,192,256]{2,1,0:T(8,128)(2,1)}), bf16[4,192,256]{2,1,0:T(8,128)(2,1)S(1)}, u32[]{:S(2)}, u32[]{:S(2)}) async-start(bf16[4,192,256]{2,1,0:T(8,128)(2,1)} %add_up.1), calls=%async_computation | async-start | bytes 786432 | tf_op jit(solution)/shard_map/all_to_all | solution.py:644
  81.6 2.6 %collective-permute-done.20 = bf16[1,2,4,128,128]{4,3,2,1,0:T(8,128)(2,1)} collective-permute-done((bf16[1,2,4,128,128]{4,3,2,1,0:T(8,128)(2,1)}, bf16[1,2,4,128,128]{4,3,2,1,0:T(8,128)(2,1)}, u32[]{:S(2)}, u32[]{:S(2)}) %collective-permute-start.20) | collective-permute-done | bytes 262176 | tf_op jit(solution)/shard_map/ppermute | solution.py:38
  84.8 2.2 %collective-permute-done.22 = bf16[2,4,128,128]{3,2,1,0:T(8,128)(2,1)} collective-permute-done((bf16[2,4,128,128]{3,2,1,0:T(8,128)(2,1)S(1)}, bf16[2,4,128,128]{3,2,1,0:T(8,128)(2,1)}, u32[]{:S(2)}, u32[]{:S(2)}) %collective-permute-start.22) | collective-permute-done | bytes 262176 | tf_op jit(solution)/shard_map/ppermute | solution.py:33
  87.1 1.2 %fusion = bf16[2,4,128,128]{3,2,1,0:T(8,128)(2,1)S(1)} fusion(bf16[1,2,4,128,128]{4,3,2,1,0:T(8,128)(2,1)} %collective-permute-done.20, f32[1,2,4,128,128]{4,3,2,1,0:T(8,128)S(1)} %get-tuple-element.83, bf16[1,2,4,128,128]{4,3,2,1,0:T(8,128)(2,1)} %collective-permute-done.23, bf16[2,4,128,128]{3,2,1,0:T(8,128)(2,1)} %collective-permute-done.22), kind=kLoop, calls=%fused_computation.3 | loop fusion | flops 917504 | bytes 1572864 | tf_op jit(solution)/shard_map/convert_element_type | solution.py:643
  88.6 3.1 %collective-permute-done.21 = bf16[1,2,4,128,128]{4,3,2,1,0:T(8,128)(2,1)S(1)} collective-permute-done((bf16[1,2,4,128,128]{4,3,2,1,0:T(8,128)(2,1)S(1)}, bf16[1,2,4,128,128]{4,3,2,1,0:T(8,128)(2,1)S(1)}, u32[]{:S(2)}, u32[]{:S(2)}) %collective-permute-start.21) | collective-permute-done | bytes 262176 | tf_op jit(solution)/shard_map/ppermute | solution.py:38
  91.8 7.1 %collective-permute-done.24.second = bf16[2,4,128,128]{3,2,1,0:T(8,128)(2,1)S(1)} collective-permute-done((bf16[2,4,128,128]{3,2,1,0:T(8,128)(2,1)S(1)}, bf16[2,4,128,128]{3,2,1,0:T(8,128)(2,1)S(1)}, u32[]{:S(2)}, u32[]{:S(2)}) %collective-permute-start.24) | collective-permute-done | bytes 262176 | tf_op jit(solution)/shard_map/ppermute | solution.py:33
  (60 shorter events, 12.9 us)
Async XLA Ops:
  1.7 10.7 %collective-permute-start = (bf16[2,128,512]{2,1,0:T(8,128)(2,1)S(1)}, bf16[2,128,512]{2,1,0:T(8,128)(2,1)S(1)}, u32[]{:S(2)}, u32[]{:S(2)}) collective-permute-start(bf16[2,128,512]{2,1,0:T(8,128)(2,1)S(1)} %dynamic-slice_bitcast_fusion), channel_id=1, source_target_pairs={{0,12},{4,0},{8,4},{12,8},{1,13},{5,1},{9,5},{13,9},{2,14},{6,2},{... | collective-permute-start | bytes 786440 | tf_op jit(solution)/shard_map/ppermute | solution.py:33
  12.3 9.0 %collective-permute-start.1 = (bf16[2,128,512]{2,1,0:T(8,128)(2,1)S(1)}, bf16[2,128,512]{2,1,0:T(8,128)(2,1)S(1)}, u32[]{:S(2)}, u32[]{:S(2)}) collective-permute-start(bf16[2,128,512]{2,1,0:T(8,128)(2,1)S(1)} %collective-permute-done.refs_1_), channel_id=1, source_target_pairs={{0,12},{4,0},{8,4},{12,8},{1,13},{5,1},{9,5},{13,9},{2,14},{6,2},{... | collective-permute-start | bytes 786440 | tf_op jit(solution)/shard_map/ppermute | solution.py:33
  16.6 8.2 %collective-permute-start.2 = (bf16[2,128,512]{2,1,0:T(8,128)(2,1)S(1)}, bf16[2,128,512]{2,1,0:T(8,128)(2,1)S(1)}, u32[]{:S(2)}, u32[]{:S(2)}) collective-permute-start(bf16[2,128,512]{2,1,0:T(8,128)(2,1)S(1)} %collective-permute-done.refs_1_), channel_id=1, source_target_pairs={{0,2},{1,3},{2,0},{3,1},{4,6},{5,7},{6,4},{7,5},{8,10},{9,11},{10,... | collective-permute-start | bytes 786440 | tf_op jit(solution)/shard_map/ppermute | solution.py:38
  21.3 7.8 %collective-permute-start.5 = (bf16[2,128,512]{2,1,0:T(8,128)(2,1)S(1)}, bf16[2,128,512]{2,1,0:T(8,128)(2,1)S(1)}, u32[]{:S(2)}, u32[]{:S(2)}) collective-permute-start(bf16[2,128,512]{2,1,0:T(8,128)(2,1)S(1)} %collective-permute-done.1.refs_5_), channel_id=1, source_target_pairs={{0,2},{1,3},{2,0},{3,1},{4,6},{5,7},{6,4},{7,5},{8,10},{9,11},{10,... | collective-permute-start | bytes 786440 | tf_op jit(solution)/shard_map/ppermute | solution.py:38
  22.8 7.0 %collective-permute-start.3 = (bf16[2,128,512]{2,1,0:T(8,128)(2,1)S(1)}, bf16[2,128,512]{2,1,0:T(8,128)(2,1)S(1)}, u32[]{:S(2)}, u32[]{:S(2)}) collective-permute-start(bf16[2,128,512]{2,1,0:T(8,128)(2,1)S(1)} %collective-permute-done.refs_1_), channel_id=1, source_target_pairs={{0,1},{1,0},{2,3},{3,2},{4,5},{5,4},{6,7},{7,6},{8,9},{9,8},{10,11... | collective-permute-start | bytes 786440 | tf_op jit(solution)/shard_map/ppermute | solution.py:38
  22.8 7.0 %collective-permute-start.6 = (bf16[2,128,512]{2,1,0:T(8,128)(2,1)S(1)}, bf16[2,128,512]{2,1,0:T(8,128)(2,1)S(1)}, u32[]{:S(2)}, u32[]{:S(2)}) collective-permute-start(bf16[2,128,512]{2,1,0:T(8,128)(2,1)S(1)} %collective-permute-done.1.refs_5_), channel_id=1, source_target_pairs={{0,1},{1,0},{2,3},{3,2},{4,5},{5,4},{6,7},{7,6},{8,9},{9,8},{10,11... | collective-permute-start | bytes 786440 | tf_op jit(solution)/shard_map/ppermute | solution.py:38
  24.8 5.0 %collective-permute-start.4 = (bf16[2,128,512]{2,1,0:T(8,128)(2,1)S(1)}, bf16[2,128,512]{2,1,0:T(8,128)(2,1)S(1)}, u32[]{:S(2)}, u32[]{:S(2)}) collective-permute-start(bf16[2,128,512]{2,1,0:T(8,128)(2,1)S(1)} %collective-permute-done.2.refs_2_), channel_id=1, source_target_pairs={{0,1},{1,0},{2,3},{3,2},{4,5},{5,4},{6,7},{7,6},{8,9},{9,8},{10,11... | collective-permute-start | bytes 786440 | tf_op jit(solution)/shard_map/ppermute | solution.py:38
  49.1 1.8 %collective-permute-start.8 = (bf16[1,12,64,256]{3,2,1,0:T(8,128)(2,1)S(1)}, bf16[1,12,64,256]{3,2,1,0:T(8,128)(2,1)S(1)}, u32[]{:S(2)}, u32[]{:S(2)}) collective-permute-start(bf16[1,12,64,256]{3,2,1,0:T(8,128)(2,1)S(1)} %get-tuple-element.65), channel_id=1, source_target_pairs={{0,1},{1,0},{2,3},{3,2},{4,5},{5,4},{6,7},{7,6},{8,9},{9,8},{10,11... | collective-permute-start | bytes 1179656 | tf_op jit(solution)/shard_map/ppermute | solution.py:38
  49.3 9.8 %collective-permute-start.14 = (bf16[1,12,64,256]{3,2,1,0:T(8,128)(2,1)S(1)}, bf16[1,12,64,256]{3,2,1,0:T(8,128)(2,1)S(1)}, u32[]{:S(2)}, u32[]{:S(2)}) collective-permute-start(bf16[1,12,64,256]{3,2,1,0:T(8,128)(2,1)S(1)} %get-tuple-element.78), channel_id=1, source_target_pairs={{0,1},{1,0},{2,3},{3,2},{4,5},{5,4},{6,7},{7,6},{8,9},{9,8},{10,11... | collective-permute-start | bytes 1179656 | tf_op jit(solution)/shard_map/ppermute | solution.py:38
  51.0 11.2 %collective-permute-start.15 = (bf16[1,12,64,256]{3,2,1,0:T(8,128)(2,1)S(1)}, bf16[1,12,64,256]{3,2,1,0:T(8,128)(2,1)S(1)}, u32[]{:S(2)}, u32[]{:S(2)}) collective-permute-start(bf16[1,12,64,256]{3,2,1,0:T(8,128)(2,1)S(1)} %add_convert_fusion), channel_id=1, source_target_pairs={{0,2},{1,3},{2,0},{3,1},{4,6},{5,7},{6,4},{7,5},{8,10},{9,11},{10,... | collective-permute-start | bytes 1179656 | tf_op jit(solution)/shard_map/ppermute | solution.py:38
  58.5 16.2 %collective-permute-start.12 = (bf16[1,2,4,128,128]{4,3,2,1,0:T(8,128)(2,1)S(1)}, bf16[1,2,4,128,128]{4,3,2,1,0:T(8,128)(2,1)S(1)}, u32[]{:S(2)}, u32[]{:S(2)}) collective-permute-start(bf16[1,2,4,128,128]{4,3,2,1,0:T(8,128)(2,1)S(1)} %get-tuple-element.74), channel_id=1, source_target_pairs={{0,1},{1,0},{2,3},{3,2},{4,5},{5,4},{6,7},{7,6},{8,9},{9,8},{10,11... | collective-permute-start | bytes 786440 | tf_op jit(solution)/shard_map/ppermute | solution.py:38
  58.6 3.8 %collective-permute-start.13 = (bf16[1,2,4,128,128]{4,3,2,1,0:T(8,128)(2,1)S(1)}, bf16[1,2,4,128,128]{4,3,2,1,0:T(8,128)(2,1)S(1)}, u32[]{:S(2)}, u32[]{:S(2)}) collective-permute-start(bf16[1,2,4,128,128]{4,3,2,1,0:T(8,128)(2,1)S(1)} %get-tuple-element.76), channel_id=1, source_target_pairs={{0,1},{1,0},{2,3},{3,2},{4,5},{5,4},{6,7},{7,6},{8,9},{9,8},{10,11... | collective-permute-start | bytes 786440 | tf_op jit(solution)/shard_map/ppermute | solution.py:38
  62.5 12.2 %collective-permute-start.16 = (bf16[1,2,4,128,128]{4,3,2,1,0:T(8,128)(2,1)S(1)}, bf16[1,2,4,128,128]{4,3,2,1,0:T(8,128)(2,1)S(1)}, u32[]{:S(2)}, u32[]{:S(2)}) collective-permute-start(bf16[1,2,4,128,128]{4,3,2,1,0:T(8,128)(2,1)S(1)} %add_convert_fusion.4), channel_id=1, source_target_pairs={{0,2},{1,3},{2,0},{3,1},{4,6},{5,7},{6,4},{7,5},{8,10},{9,11},{10,... | collective-permute-start | bytes 786440 | tf_op jit(solution)/shard_map/ppermute | solution.py:38
  64.1 9.2 %collective-permute-start.18 = (bf16[192,256]{1,0:T(8,128)(2,1)S(1)}, bf16[192,256]{1,0:T(8,128)(2,1)S(1)}, u32[]{:S(2)}, u32[]{:S(2)}) collective-permute-start(bf16[192,256]{1,0:T(8,128)(2,1)S(1)} %bitcast.30), channel_id=1, source_target_pairs={{0,8},{4,12},{8,0},{12,4},{1,9},{5,13},{9,1},{13,5},{2,10},{6,14},... | collective-permute-start | bytes 294920 | tf_op jit(solution)/shard_map/ppermute | solution.py:38
  64.1 9.2 %collective-permute-start.19 = (bf16[192,256]{1,0:T(8,128)(2,1)S(1)}, bf16[192,256]{1,0:T(8,128)(2,1)S(1)}, u32[]{:S(2)}, u32[]{:S(2)}) collective-permute-start(bf16[192,256]{1,0:T(8,128)(2,1)S(1)} %bitcast.29), channel_id=1, source_target_pairs={{0,12},{4,8},{8,4},{12,0},{1,13},{5,9},{9,5},{13,1},{2,14},{6,10},... | collective-permute-start | bytes 294920 | tf_op jit(solution)/shard_map/ppermute | solution.py:38
  66.9 7.1 %collective-permute-start.17 = (bf16[192,256]{1,0:T(8,128)(2,1)S(1)}, bf16[192,256]{1,0:T(8,128)(2,1)S(1)}, u32[]{:S(2)}, u32[]{:S(2)}) collective-permute-start(bf16[192,256]{1,0:T(8,128)(2,1)S(1)} %bitcast.28), channel_id=1, source_target_pairs={{0,4},{4,0},{8,12},{12,8},{1,5},{5,1},{9,13},{13,9},{2,6},{6,2},{1... | collective-permute-start | bytes 294920 | tf_op jit(solution)/shard_map/ppermute | solution.py:38
  73.2 8.3 %collective-permute-start.10 = (bf16[1,2,4,128,128]{4,3,2,1,0:T(8,128)(2,1)S(1)}, bf16[1,2,4,128,128]{4,3,2,1,0:T(8,128)(2,1)S(1)}, u32[]{:S(2)}, u32[]{:S(2)}) collective-permute-start(bf16[1,2,4,128,128]{4,3,2,1,0:T(8,128)(2,1)S(1)} %get-tuple-element.70), channel_id=1, source_target_pairs={{0,1},{1,0},{2,3},{3,2},{4,5},{5,4},{6,7},{7,6},{8,9},{9,8},{10,11... | collective-permute-start | bytes 786440 | tf_op jit(solution)/shard_map/ppermute | solution.py:38
  75.6 8.5 %collective-permute-start.20 = (bf16[1,2,4,128,128]{4,3,2,1,0:T(8,128)(2,1)}, bf16[1,2,4,128,128]{4,3,2,1,0:T(8,128)(2,1)}, u32[]{:S(2)}, u32[]{:S(2)}) collective-permute-start(bf16[1,2,4,128,128]{4,3,2,1,0:T(8,128)(2,1)} %add_convert_fusion.2), channel_id=1, source_target_pairs={{0,2},{1,3},{2,0},{3,1},{4,6},{5,7},{6,4},{7,5},{8,10},{9,11},{10,... | collective-permute-start | bytes 786440 | tf_op jit(solution)/shard_map/ppermute | solution.py:38
  76.2 8.6 %collective-permute-start.23 = (bf16[1,2,4,128,128]{4,3,2,1,0:T(8,128)(2,1)S(1)}, bf16[1,2,4,128,128]{4,3,2,1,0:T(8,128)(2,1)}, u32[]{:S(2)}, u32[]{:S(2)}) collective-permute-start(bf16[1,2,4,128,128]{4,3,2,1,0:T(8,128)(2,1)S(1)} %get-tuple-element.84), channel_id=1, source_target_pairs={{0,1},{1,0},{2,3},{3,2},{4,5},{5,4},{6,7},{7,6},{8,9},{9,8},{10,11... | collective-permute-start | bytes 786440 | tf_op jit(solution)/shard_map/ppermute | solution.py:38
  76.2 10.8 %collective-permute-start.22 = (bf16[2,4,128,128]{3,2,1,0:T(8,128)(2,1)S(1)}, bf16[2,4,128,128]{3,2,1,0:T(8,128)(2,1)}, u32[]{:S(2)}, u32[]{:S(2)}) collective-permute-start(bf16[2,4,128,128]{3,2,1,0:T(8,128)(2,1)S(1)} %fusion.1), channel_id=1, source_target_pairs={{0,4},{4,8},{8,12},{12,0},{1,5},{5,9},{9,13},{13,1},{2,6},{6,10},{... | collective-permute-start | bytes 786440 | tf_op jit(solution)/shard_map/ppermute | solution.py:33
  78.1 10.5 %collective-permute-start.9 = (bf16[1,2,4,128,128]{4,3,2,1,0:T(8,128)(2,1)S(1)}, bf16[1,2,4,128,128]{4,3,2,1,0:T(8,128)(2,1)S(1)}, u32[]{:S(2)}, u32[]{:S(2)}) collective-permute-start(bf16[1,2,4,128,128]{4,3,2,1,0:T(8,128)(2,1)S(1)} %get-tuple-element.68), channel_id=1, source_target_pairs={{0,1},{1,0},{2,3},{3,2},{4,5},{5,4},{6,7},{7,6},{8,9},{9,8},{10,11... | collective-permute-start | bytes 786440 | tf_op jit(solution)/shard_map/ppermute | solution.py:38
  78.1 22.7 %all-to-all-start = ((bf16[4,192,256]{2,1,0:T(8,128)(2,1)}), bf16[4,192,256]{2,1,0:T(8,128)(2,1)S(1)}, u32[]{:S(2)}, u32[]{:S(2)}) async-start(bf16[4,192,256]{2,1,0:T(8,128)(2,1)} %add_up.1), calls=%async_computation | async-start | bytes 786432 | tf_op jit(solution)/shard_map/all_to_all | solution.py:644
  84.2 7.4 %collective-permute-start.21 = (bf16[1,2,4,128,128]{4,3,2,1,0:T(8,128)(2,1)S(1)}, bf16[1,2,4,128,128]{4,3,2,1,0:T(8,128)(2,1)S(1)}, u32[]{:S(2)}, u32[]{:S(2)}) collective-permute-start(bf16[1,2,4,128,128]{4,3,2,1,0:T(8,128)(2,1)S(1)} %add_convert_fusion.1), channel_id=1, source_target_pairs={{0,2},{1,3},{2,0},{3,1},{4,6},{5,7},{6,4},{7,5},{8,10},{9,11},{10,... | collective-permute-start | bytes 786440 | tf_op jit(solution)/shard_map/ppermute | solution.py:38
  88.3 10.5 %collective-permute-start.24 = (bf16[2,4,128,128]{3,2,1,0:T(8,128)(2,1)S(1)}, bf16[2,4,128,128]{3,2,1,0:T(8,128)(2,1)S(1)}, u32[]{:S(2)}, u32[]{:S(2)}) collective-permute-start(bf16[2,4,128,128]{3,2,1,0:T(8,128)(2,1)S(1)} %fusion), channel_id=1, source_target_pairs={{0,4},{4,8},{8,12},{12,0},{1,5},{5,9},{9,13},{13,1},{2,6},{6,10},{... | collective-permute-start | bytes 786440 | tf_op jit(solution)/shard_map/ppermute | solution.py:33
  (9 other events, 105.7 us)

commit v16 on v15

--- a/solution.py
+++ b/solution.py
@@ -192,15 +192,13 @@
 
     def synth(i, carry):
         rows = pl.ds(pl.multiple_of(i * STRIP, STRIP), STRIP)
+        e = jnp.concatenate([eig[:, c, rows, :].reshape(modes * STRIP, frame) for c in range(2)], 1)
+        made = jnp.dot(weights[...], jnp.concatenate([e, e], 0), preferred_element_type=jnp.float32)
         for c in range(2):
-            e = eig[:, c, rows, :].reshape(modes * STRIP, frame)
-            made = jnp.dot(
-                weights[...], jnp.concatenate([e, e], 0), preferred_element_type=jnp.float32
-            )
-            probe[:, c, rows, :] = made.reshape(pos_dev, STRIP, frame)
-        return carry
-
-    lax.fori_loop(0, frame // STRIP, synth, 0, unroll=8)
+            probe[:, c, rows, :] = made[:, c * frame:(c + 1) * frame].reshape(pos_dev, STRIP, frame)
+        return carry
+
+    lax.fori_loop(0, frame // STRIP, synth, 0, unroll=16)
     for copy in copies:
         copy.wait()
 
@@ -316,22 +314,20 @@
         rows = pl.ds(pl.multiple_of(i * STRIP, STRIP), STRIP)
         q = i // (rows_q // STRIP)
         inner = pl.ds(pl.multiple_of(i % (rows_q // STRIP) * STRIP, STRIP), STRIP)
+        d = jnp.concatenate([dprobe[:, c, rows, :].reshape(pos_dev * STRIP, frame) for c in range(2)], 1)
+        e = jnp.concatenate([eig[:, c, rows, :].reshape(modes * STRIP, frame) for c in range(2)], 1)
+        both = jnp.dot(weights_t[...], d, preferred_element_type=jnp.float32)
+        grad = (both[:modes * STRIP] + both[modes * STRIP:]) * (0.5 * scale)
         for c in range(2):
-            d = dprobe[:, c, rows, :].reshape(pos_dev * STRIP, frame)
-            e = eig[:, c, rows, :].reshape(modes * STRIP, frame)
-            both = jnp.dot(weights_t[...], d, preferred_element_type=jnp.float32)
-            grad = (both[:modes * STRIP] + both[modes * STRIP:]) * (0.5 * scale)
             for k in range(modes):
                 group = 2 * k + c
                 if share:
                     group = (group // share ^ my_block) * share + group % share
-                eigen[q, group, inner, :] = grad[k * STRIP:(k + 1) * STRIP]
-            cross[...] += lax.dot_general(
-                d, e, (((1,), (1,)), ((), ())), preferred_element_type=jnp.float32
-            )
-        return carry
-
-    lax.fori_loop(0, frame // STRIP, eigen_strip, 0, unroll=8)
+                eigen[q, group, inner, :] = grad[k * STRIP:(k + 1) * STRIP, c * frame:(c + 1) * frame]
+        cross[...] += lax.dot_general(d, e, (((1,), (1,)), ((), ())), preferred_element_type=jnp.float32)
+        return carry
+
+    lax.fori_loop(0, frame // STRIP, eigen_strip, 0, unroll=16)
     pending = []
 
     def start(source, target):

time: 102 us -> 102 us (level)
  waiting for transfers between devices: 37.7 us -> 36.5 us
  starting transfers between devices: 28 us -> 29.2 us
    ppermute x21, waiting for transfers between devices: 21.5 us -> 19.6 us  [swap(): return lax.ppermute(array, axis, [(i, i ^ bit) for i in range(peers)])]
    ppermute x21, starting transfers between devices: 13 us -> 14.2 us  [swap(): return lax.ppermute(array, axis, [(i, i ^ bit) for i in range(peers)])]
where the time goes in v16:
time: 102 us; the launch traced here: 101 us
  waiting for transfers between devices  36.5 us (36%)
  starting transfers between devices  29.2 us (29%)
  Pallas kernels  27.8 us (27%)
  local copies, waits for them, and re-layouts  3.77 us (4%)
  other arithmetic  2.56 us (3%)
  between operations  1.52 us (1%)
    ppermute x21, waiting for transfers between devices, swap(): return lax.ppermute(array, axis, [(i, i ^ bit) for i in range(peers)])  19.6 us
    pallas_call x1, Pallas kernels, positions(): pl.pallas_call(functools.partial(position_kernel, offs, scale), in_specs=...  18.1 us
    ppermute x4, waiting for transfers between devices, shift(): lax.ppermute(array, axis, [(i, (i + by) % peers) for i in range(peers)])  15.9 us
    ppermute x21, starting transfers between devices, swap(): return lax.ppermute(array, axis, [(i, i ^ bit) for i in range(peers)])  14.2 us
    ppermute x4, starting transfers between devices, shift(): lax.ppermute(array, axis, [(i, (i + by) % peers) for i in range(peers)])  11.5 us
    pallas_call x1, Pallas kernels, scatter(): pl.pallas_call(functools.partial(scatter_kernel, shares), in_specs=[pl.Bl...  5.9 us
    all_to_all x1, starting transfers between devices, on_device(): gathered = lax.all_to_all(total, 'blk', 0, 0)  3.47 us
    unnamed x14, local copies, waits for them, and re-layouts  2.75 us
  transfers between devices with their start and end apart: 26, of which 14 were waited for; matrix products, arithmetic and copies ran while one was open for 3% of the time, Pallas kernels for 9%

profile of v16, /device:TPU:0, one launch (start us, length us, event | category | flops | bytes accessed | tf_op | source)
XLA Modules:
  0.0 101.4 jit_solution(4141791949411131125)
XLA Ops:
  1.7 5.1 %collective-permute-start = (bf16[2,128,512]{2,1,0:T(8,128)(2,1)S(1)}, bf16[2,128,512]{2,1,0:T(8,128)(2,1)S(1)}, u32[]{:S(2)}, u32[]{:S(2)}) collective-permute-start(bf16[2,128,512]{2,1,0:T(8,128)(2,1)S(1)} %dynamic-slice_bitcast_fusion), channel_id=1, source_target_pairs={{0,12},{4,0},{8,4},{12,8},{1,13},{5,1},{9,5},{13,9},{2,14},{6,2},{... | collective-permute-start | bytes 786440 | tf_op jit(solution)/shard_map/ppermute | solution.py:33
  6.8 5.6 %collective-permute-done.refs_1_ = bf16[2,128,512]{2,1,0:T(8,128)(2,1)S(1)} collective-permute-done((bf16[2,128,512]{2,1,0:T(8,128)(2,1)S(1)}, bf16[2,128,512]{2,1,0:T(8,128)(2,1)S(1)}, u32[]{:S(2)}, u32[]{:S(2)}) %collective-permute-start) | collective-permute-done | bytes 262176 | tf_op jit(solution)/shard_map/ppermute | solution.py:33
  12.3 4.3 %collective-permute-start.1 = (bf16[2,128,512]{2,1,0:T(8,128)(2,1)S(1)}, bf16[2,128,512]{2,1,0:T(8,128)(2,1)S(1)}, u32[]{:S(2)}, u32[]{:S(2)}) collective-permute-start(bf16[2,128,512]{2,1,0:T(8,128)(2,1)S(1)} %collective-permute-done.refs_1_), channel_id=1, source_target_pairs={{0,12},{4,0},{8,4},{12,8},{1,13},{5,1},{9,5},{13,9},{2,14},{6,2},{... | collective-permute-start | bytes 786440 | tf_op jit(solution)/shard_map/ppermute | solution.py:33
  16.6 1.5 %collective-permute-start.2 = (bf16[2,128,512]{2,1,0:T(8,128)(2,1)S(1)}, bf16[2,128,512]{2,1,0:T(8,128)(2,1)S(1)}, u32[]{:S(2)}, u32[]{:S(2)}) collective-permute-start(bf16[2,128,512]{2,1,0:T(8,128)(2,1)S(1)} %collective-permute-done.refs_1_), channel_id=1, source_target_pairs={{0,2},{1,3},{2,0},{3,1},{4,6},{5,7},{6,4},{7,5},{8,10},{9,11},{10,... | collective-permute-start | bytes 786440 | tf_op jit(solution)/shard_map/ppermute | solution.py:38
  18.1 1.4 %copy-done.1 = bf16[6,2,256,256]{3,2,1,0:T(8,128)(2,1)S(1)} copy-done((bf16[6,2,256,256]{3,2,1,0:T(8,128)(2,1)S(1)}, bf16[6,2,256,256]{3,2,1,0:T(8,128)(2,1)}, u32[]{:S(2)}) %copy-start.1) | copy-done | bytes 1572888
  19.5 1.3 %copy-done.2 = bf16[10,256,256]{2,1,0:T(8,128)(2,1)S(1)} copy-done((bf16[10,256,256]{2,1,0:T(8,128)(2,1)S(1)}, bf16[10,256,256]{2,1,0:T(8,128)(2,1)}, u32[]{:S(2)}) %copy-start.2) | copy-done | bytes 1310744
  21.3 1.5 %collective-permute-start.5 = (bf16[2,128,512]{2,1,0:T(8,128)(2,1)S(1)}, bf16[2,128,512]{2,1,0:T(8,128)(2,1)S(1)}, u32[]{:S(2)}, u32[]{:S(2)}) collective-permute-start(bf16[2,128,512]{2,1,0:T(8,128)(2,1)S(1)} %collective-permute-done.1.refs_5_), channel_id=1, source_target_pairs={{0,2},{1,3},{2,0},{3,1},{4,6},{5,7},{6,4},{7,5},{8,10},{9,11},{10,... | collective-permute-start | bytes 786440 | tf_op jit(solution)/shard_map/ppermute | solution.py:38
  23.3 1.5 %collective-permute-done.2.refs_2_ = bf16[2,128,512]{2,1,0:T(8,128)(2,1)S(1)} collective-permute-done((bf16[2,128,512]{2,1,0:T(8,128)(2,1)S(1)}, bf16[2,128,512]{2,1,0:T(8,128)(2,1)S(1)}, u32[]{:S(2)}, u32[]{:S(2)}) %collective-permute-start.2) | collective-permute-done | bytes 262176 | tf_op jit(solution)/shard_map/ppermute | solution.py:38
  25.9 3.3 %collective-permute-done.5.refs_6_ = bf16[2,128,512]{2,1,0:T(8,128)(2,1)S(1)} collective-permute-done((bf16[2,128,512]{2,1,0:T(8,128)(2,1)S(1)}, bf16[2,128,512]{2,1,0:T(8,128)(2,1)S(1)}, u32[]{:S(2)}, u32[]{:S(2)}) %collective-permute-start.5) | collective-permute-done | bytes 262176 | tf_op jit(solution)/shard_map/ppermute | solution.py:38
  30.7 18.1 %positions.1 = (bf16[1,12,64,256]{3,2,1,0:T(8,128)(2,1)S(1)}, bf16[1,12,64,256]{3,2,1,0:T(8,128)(2,1)S(1)}, f32[1,12,64,256]{3,2,1,0:T(8,128)S(1)}, f32[1,12,64,...) custom-call(s32[2,10]{1,0:T(2,128)S(1)} %get-tuple-element.54.tile_list, ...), custom_call_target="tpu_custom_call" | custom-call | tf_op jit(solution)/shard_map/positions/pallas_call | solution.py:373
  50.7 1.6 %collective-permute-start.15 = (bf16[1,12,64,256]{3,2,1,0:T(8,128)(2,1)S(1)}, bf16[1,12,64,256]{3,2,1,0:T(8,128)(2,1)S(1)}, u32[]{:S(2)}, u32[]{:S(2)}) collective-permute-start(bf16[1,12,64,256]{3,2,1,0:T(8,128)(2,1)S(1)} %add_convert_fusion), channel_id=1, source_target_pairs={{0,2},{1,3},{2,0},{3,1},{4,6},{5,7},{6,4},{7,5},{8,10},{9,11},{10,... | collective-permute-start | bytes 1179656 | tf_op jit(solution)/shard_map/ppermute | solution.py:38
  52.3 5.9 %scatter.1 = (bf16[1,2,4,128,128]{4,3,2,1,0:T(8,128)(2,1)S(1)}, bf16[1,2,4,128,128]{4,3,2,1,0:T(8,128)(2,1)S(1)}, bf16[1,2,4,128,128]{4,3,2,1,0:T(8,128)(2,1)S(1...) custom-call(s32[2,10]{1,0:T(2,128)S(1)} %get-tuple-element.54.tile_l, ...), custom_call_target="tpu_custom_call" | custom-call | flops 16777216 | bytes 16777216 | tf_op jit(solution)/shard_map/scatter/pallas_call | solution.py:491
  58.7 3.2 %collective-permute-done.15 = bf16[1,12,64,256]{3,2,1,0:T(8,128)(2,1)S(1)} collective-permute-done((bf16[1,12,64,256]{3,2,1,0:T(8,128)(2,1)S(1)}, bf16[1,12,64,256]{3,2,1,0:T(8,128)(2,1)S(1)}, u32[]{:S(2)}, u32[]{:S(2)}) %collective-permute-start.15) | collective-permute-done | bytes 393248 | tf_op jit(solution)/shard_map/ppermute | solution.py:38
  62.2 1.5 %collective-permute-start.16 = (bf16[1,2,4,128,128]{4,3,2,1,0:T(8,128)(2,1)S(1)}, bf16[1,2,4,128,128]{4,3,2,1,0:T(8,128)(2,1)S(1)}, u32[]{:S(2)}, u32[]{:S(2)}) collective-permute-start(bf16[1,2,4,128,128]{4,3,2,1,0:T(8,128)(2,1)S(1)} %add_convert_fusion.4), channel_id=1, source_target_pairs={{0,2},{1,3},{2,0},{3,1},{4,6},{5,7},{6,4},{7,5},{8,10},{9,11},{10,... | collective-permute-start | bytes 786440 | tf_op jit(solution)/shard_map/ppermute | solution.py:38
  63.8 1.6 %collective-permute-start.19 = (bf16[192,256]{1,0:T(8,128)(2,1)S(1)}, bf16[192,256]{1,0:T(8,128)(2,1)S(1)}, u32[]{:S(2)}, u32[]{:S(2)}) collective-permute-start(bf16[192,256]{1,0:T(8,128)(2,1)S(1)} %bitcast.29), channel_id=1, source_target_pairs={{0,12},{4,8},{8,4},{12,0},{1,13},{5,9},{9,5},{13,1},{2,14},{6,10},... | collective-permute-start | bytes 294920 | tf_op jit(solution)/shard_map/ppermute | solution.py:38
  65.4 1.9 %collective-permute-start.17 = (bf16[192,256]{1,0:T(8,128)(2,1)S(1)}, bf16[192,256]{1,0:T(8,128)(2,1)S(1)}, u32[]{:S(2)}, u32[]{:S(2)}) collective-permute-start(bf16[192,256]{1,0:T(8,128)(2,1)S(1)} %bitcast.28), channel_id=1, source_target_pairs={{0,4},{4,0},{8,12},{12,8},{1,5},{5,1},{9,13},{13,9},{2,6},{6,2},{1... | collective-permute-start | bytes 294920 | tf_op jit(solution)/shard_map/ppermute | solution.py:38
  67.2 5.0 %collective-permute-done.18.refs_1_ = bf16[192,256]{1,0:T(8,128)(2,1)S(1)} collective-permute-done((bf16[192,256]{1,0:T(8,128)(2,1)S(1)}, bf16[192,256]{1,0:T(8,128)(2,1)S(1)}, u32[]{:S(2)}, u32[]{:S(2)}) %collective-permute-start.18) | collective-permute-done | bytes 98336 | tf_op jit(solution)/shard_map/ppermute | solution.py:38
  75.9 1.8 %collective-permute-start.22 = (bf16[2,4,128,128]{3,2,1,0:T(8,128)(2,1)S(1)}, bf16[2,4,128,128]{3,2,1,0:T(8,128)(2,1)}, u32[]{:S(2)}, u32[]{:S(2)}) collective-permute-start(bf16[2,4,128,128]{3,2,1,0:T(8,128)(2,1)S(1)} %fusion.1), channel_id=1, source_target_pairs={{0,4},{4,8},{8,12},{12,0},{1,5},{5,9},{9,13},{13,1},{2,6},{6,10},{... | collective-permute-start | bytes 786440 | tf_op jit(solution)/shard_map/ppermute | solution.py:33
  77.7 3.5 %all-to-all-start = ((bf16[4,192,256]{2,1,0:T(8,128)(2,1)}), bf16[4,192,256]{2,1,0:T(8,128)(2,1)S(1)}, u32[]{:S(2)}, u32[]{:S(2)}) async-start(bf16[4,192,256]{2,1,0:T(8,128)(2,1)} %add_up.1), calls=%async_computation | async-start | bytes 786432 | tf_op jit(solution)/shard_map/all_to_all | solution.py:640
  81.2 2.0 %collective-permute-done.20 = bf16[1,2,4,128,128]{4,3,2,1,0:T(8,128)(2,1)} collective-permute-done((bf16[1,2,4,128,128]{4,3,2,1,0:T(8,128)(2,1)}, bf16[1,2,4,128,128]{4,3,2,1,0:T(8,128)(2,1)}, u32[]{:S(2)}, u32[]{:S(2)}) %collective-permute-start.20) | collective-permute-done | bytes 262176 | tf_op jit(solution)/shard_map/ppermute | solution.py:38
  83.3 1.3 %collective-permute-start.21 = (bf16[1,2,4,128,128]{4,3,2,1,0:T(8,128)(2,1)S(1)}, bf16[1,2,4,128,128]{4,3,2,1,0:T(8,128)(2,1)S(1)}, u32[]{:S(2)}, u32[]{:S(2)}) collective-permute-start(bf16[1,2,4,128,128]{4,3,2,1,0:T(8,128)(2,1)S(1)} %add_convert_fusion.1), channel_id=1, source_target_pairs={{0,2},{1,3},{2,0},{3,1},{4,6},{5,7},{6,4},{7,5},{8,10},{9,11},{10,... | collective-permute-start | bytes 786440 | tf_op jit(solution)/shard_map/ppermute | solution.py:38
  84.5 2.2 %collective-permute-done.22 = bf16[2,4,128,128]{3,2,1,0:T(8,128)(2,1)} collective-permute-done((bf16[2,4,128,128]{3,2,1,0:T(8,128)(2,1)S(1)}, bf16[2,4,128,128]{3,2,1,0:T(8,128)(2,1)}, u32[]{:S(2)}, u32[]{:S(2)}) %collective-permute-start.22) | collective-permute-done | bytes 262176 | tf_op jit(solution)/shard_map/ppermute | solution.py:33
  88.3 2.3 %collective-permute-done.21 = bf16[1,2,4,128,128]{4,3,2,1,0:T(8,128)(2,1)S(1)} collective-permute-done((bf16[1,2,4,128,128]{4,3,2,1,0:T(8,128)(2,1)S(1)}, bf16[1,2,4,128,128]{4,3,2,1,0:T(8,128)(2,1)S(1)}, u32[]{:S(2)}, u32[]{:S(2)}) %collective-permute-start.21) | collective-permute-done | bytes 262176 | tf_op jit(solution)/shard_map/ppermute | solution.py:38
  90.7 7.8 %collective-permute-done.24.second = bf16[2,4,128,128]{3,2,1,0:T(8,128)(2,1)S(1)} collective-permute-done((bf16[2,4,128,128]{3,2,1,0:T(8,128)(2,1)S(1)}, bf16[2,4,128,128]{3,2,1,0:T(8,128)(2,1)S(1)}, u32[]{:S(2)}, u32[]{:S(2)}) %collective-permute-start.24) | collective-permute-done | bytes 262176 | tf_op jit(solution)/shard_map/ppermute | solution.py:33
  (60 shorter events, 14.8 us)
Async XLA Ops:
  1.7 10.7 %collective-permute-start = (bf16[2,128,512]{2,1,0:T(8,128)(2,1)S(1)}, bf16[2,128,512]{2,1,0:T(8,128)(2,1)S(1)}, u32[]{:S(2)}, u32[]{:S(2)}) collective-permute-start(bf16[2,128,512]{2,1,0:T(8,128)(2,1)S(1)} %dynamic-slice_bitcast_fusion), channel_id=1, source_target_pairs={{0,12},{4,0},{8,4},{12,8},{1,13},{5,1},{9,5},{13,9},{2,14},{6,2},{... | collective-permute-start | bytes 786440 | tf_op jit(solution)/shard_map/ppermute | solution.py:33
  12.3 9.0 %collective-permute-start.1 = (bf16[2,128,512]{2,1,0:T(8,128)(2,1)S(1)}, bf16[2,128,512]{2,1,0:T(8,128)(2,1)S(1)}, u32[]{:S(2)}, u32[]{:S(2)}) collective-permute-start(bf16[2,128,512]{2,1,0:T(8,128)(2,1)S(1)} %collective-permute-done.refs_1_), channel_id=1, source_target_pairs={{0,12},{4,0},{8,4},{12,8},{1,13},{5,1},{9,5},{13,9},{2,14},{6,2},{... | collective-permute-start | bytes 786440 | tf_op jit(solution)/shard_map/ppermute | solution.py:33
  16.6 8.2 %collective-permute-start.2 = (bf16[2,128,512]{2,1,0:T(8,128)(2,1)S(1)}, bf16[2,128,512]{2,1,0:T(8,128)(2,1)S(1)}, u32[]{:S(2)}, u32[]{:S(2)}) collective-permute-start(bf16[2,128,512]{2,1,0:T(8,128)(2,1)S(1)} %collective-permute-done.refs_1_), channel_id=1, source_target_pairs={{0,2},{1,3},{2,0},{3,1},{4,6},{5,7},{6,4},{7,5},{8,10},{9,11},{10,... | collective-permute-start | bytes 786440 | tf_op jit(solution)/shard_map/ppermute | solution.py:38
  21.3 7.8 %collective-permute-start.5 = (bf16[2,128,512]{2,1,0:T(8,128)(2,1)S(1)}, bf16[2,128,512]{2,1,0:T(8,128)(2,1)S(1)}, u32[]{:S(2)}, u32[]{:S(2)}) collective-permute-start(bf16[2,128,512]{2,1,0:T(8,128)(2,1)S(1)} %collective-permute-done.1.refs_5_), channel_id=1, source_target_pairs={{0,2},{1,3},{2,0},{3,1},{4,6},{5,7},{6,4},{7,5},{8,10},{9,11},{10,... | collective-permute-start | bytes 786440 | tf_op jit(solution)/shard_map/ppermute | solution.py:38
  22.8 7.0 %collective-permute-start.3 = (bf16[2,128,512]{2,1,0:T(8,128)(2,1)S(1)}, bf16[2,128,512]{2,1,0:T(8,128)(2,1)S(1)}, u32[]{:S(2)}, u32[]{:S(2)}) collective-permute-start(bf16[2,128,512]{2,1,0:T(8,128)(2,1)S(1)} %collective-permute-done.refs_1_), channel_id=1, source_target_pairs={{0,1},{1,0},{2,3},{3,2},{4,5},{5,4},{6,7},{7,6},{8,9},{9,8},{10,11... | collective-permute-start | bytes 786440 | tf_op jit(solution)/shard_map/ppermute | solution.py:38
  22.8 7.0 %collective-permute-start.6 = (bf16[2,128,512]{2,1,0:T(8,128)(2,1)S(1)}, bf16[2,128,512]{2,1,0:T(8,128)(2,1)S(1)}, u32[]{:S(2)}, u32[]{:S(2)}) collective-permute-start(bf16[2,128,512]{2,1,0:T(8,128)(2,1)S(1)} %collective-permute-done.1.refs_5_), channel_id=1, source_target_pairs={{0,1},{1,0},{2,3},{3,2},{4,5},{5,4},{6,7},{7,6},{8,9},{9,8},{10,11... | collective-permute-start | bytes 786440 | tf_op jit(solution)/shard_map/ppermute | solution.py:38
  24.8 5.0 %collective-permute-start.4 = (bf16[2,128,512]{2,1,0:T(8,128)(2,1)S(1)}, bf16[2,128,512]{2,1,0:T(8,128)(2,1)S(1)}, u32[]{:S(2)}, u32[]{:S(2)}) collective-permute-start(bf16[2,128,512]{2,1,0:T(8,128)(2,1)S(1)} %collective-permute-done.2.refs_2_), channel_id=1, source_target_pairs={{0,1},{1,0},{2,3},{3,2},{4,5},{5,4},{6,7},{7,6},{8,9},{9,8},{10,11... | collective-permute-start | bytes 786440 | tf_op jit(solution)/shard_map/ppermute | solution.py:38
  48.8 1.8 %collective-permute-start.8 = (bf16[1,12,64,256]{3,2,1,0:T(8,128)(2,1)S(1)}, bf16[1,12,64,256]{3,2,1,0:T(8,128)(2,1)S(1)}, u32[]{:S(2)}, u32[]{:S(2)}) collective-permute-start(bf16[1,12,64,256]{3,2,1,0:T(8,128)(2,1)S(1)} %get-tuple-element.65), channel_id=1, source_target_pairs={{0,1},{1,0},{2,3},{3,2},{4,5},{5,4},{6,7},{7,6},{8,9},{9,8},{10,11... | collective-permute-start | bytes 1179656 | tf_op jit(solution)/shard_map/ppermute | solution.py:38
  49.0 9.7 %collective-permute-start.14 = (bf16[1,12,64,256]{3,2,1,0:T(8,128)(2,1)S(1)}, bf16[1,12,64,256]{3,2,1,0:T(8,128)(2,1)S(1)}, u32[]{:S(2)}, u32[]{:S(2)}) collective-permute-start(bf16[1,12,64,256]{3,2,1,0:T(8,128)(2,1)S(1)} %get-tuple-element.78), channel_id=1, source_target_pairs={{0,1},{1,0},{2,3},{3,2},{4,5},{5,4},{6,7},{7,6},{8,9},{9,8},{10,11... | collective-permute-start | bytes 1179656 | tf_op jit(solution)/shard_map/ppermute | solution.py:38
  50.7 11.2 %collective-permute-start.15 = (bf16[1,12,64,256]{3,2,1,0:T(8,128)(2,1)S(1)}, bf16[1,12,64,256]{3,2,1,0:T(8,128)(2,1)S(1)}, u32[]{:S(2)}, u32[]{:S(2)}) collective-permute-start(bf16[1,12,64,256]{3,2,1,0:T(8,128)(2,1)S(1)} %add_convert_fusion), channel_id=1, source_target_pairs={{0,2},{1,3},{2,0},{3,1},{4,6},{5,7},{6,4},{7,5},{8,10},{9,11},{10,... | collective-permute-start | bytes 1179656 | tf_op jit(solution)/shard_map/ppermute | solution.py:38
  58.2 15.7 %collective-permute-start.12 = (bf16[1,2,4,128,128]{4,3,2,1,0:T(8,128)(2,1)S(1)}, bf16[1,2,4,128,128]{4,3,2,1,0:T(8,128)(2,1)S(1)}, u32[]{:S(2)}, u32[]{:S(2)}) collective-permute-start(bf16[1,2,4,128,128]{4,3,2,1,0:T(8,128)(2,1)S(1)} %get-tuple-element.74), channel_id=1, source_target_pairs={{0,1},{1,0},{2,3},{3,2},{4,5},{5,4},{6,7},{7,6},{8,9},{9,8},{10,11... | collective-permute-start | bytes 786440 | tf_op jit(solution)/shard_map/ppermute | solution.py:38
  58.2 3.9 %collective-permute-start.13 = (bf16[1,2,4,128,128]{4,3,2,1,0:T(8,128)(2,1)S(1)}, bf16[1,2,4,128,128]{4,3,2,1,0:T(8,128)(2,1)S(1)}, u32[]{:S(2)}, u32[]{:S(2)}) collective-permute-start(bf16[1,2,4,128,128]{4,3,2,1,0:T(8,128)(2,1)S(1)} %get-tuple-element.76), channel_id=1, source_target_pairs={{0,1},{1,0},{2,3},{3,2},{4,5},{5,4},{6,7},{7,6},{8,9},{9,8},{10,11... | collective-permute-start | bytes 786440 | tf_op jit(solution)/shard_map/ppermute | solution.py:38
  62.2 11.7 %collective-permute-start.16 = (bf16[1,2,4,128,128]{4,3,2,1,0:T(8,128)(2,1)S(1)}, bf16[1,2,4,128,128]{4,3,2,1,0:T(8,128)(2,1)S(1)}, u32[]{:S(2)}, u32[]{:S(2)}) collective-permute-start(bf16[1,2,4,128,128]{4,3,2,1,0:T(8,128)(2,1)S(1)} %add_convert_fusion.4), channel_id=1, source_target_pairs={{0,2},{1,3},{2,0},{3,1},{4,6},{5,7},{6,4},{7,5},{8,10},{9,11},{10,... | collective-permute-start | bytes 786440 | tf_op jit(solution)/shard_map/ppermute | solution.py:38
  63.7 8.5 %collective-permute-start.18 = (bf16[192,256]{1,0:T(8,128)(2,1)S(1)}, bf16[192,256]{1,0:T(8,128)(2,1)S(1)}, u32[]{:S(2)}, u32[]{:S(2)}) collective-permute-start(bf16[192,256]{1,0:T(8,128)(2,1)S(1)} %bitcast.30), channel_id=1, source_target_pairs={{0,8},{4,12},{8,0},{12,4},{1,9},{5,13},{9,1},{13,5},{2,10},{6,14},... | collective-permute-start | bytes 294920 | tf_op jit(solution)/shard_map/ppermute | solution.py:38
  63.8 8.5 %collective-permute-start.19 = (bf16[192,256]{1,0:T(8,128)(2,1)S(1)}, bf16[192,256]{1,0:T(8,128)(2,1)S(1)}, u32[]{:S(2)}, u32[]{:S(2)}) collective-permute-start(bf16[192,256]{1,0:T(8,128)(2,1)S(1)} %bitcast.29), channel_id=1, source_target_pairs={{0,12},{4,8},{8,4},{12,0},{1,13},{5,9},{9,5},{13,1},{2,14},{6,10},... | collective-permute-start | bytes 294920 | tf_op jit(solution)/shard_map/ppermute | solution.py:38
  65.4 7.7 %collective-permute-start.17 = (bf16[192,256]{1,0:T(8,128)(2,1)S(1)}, bf16[192,256]{1,0:T(8,128)(2,1)S(1)}, u32[]{:S(2)}, u32[]{:S(2)}) collective-permute-start(bf16[192,256]{1,0:T(8,128)(2,1)S(1)} %bitcast.28), channel_id=1, source_target_pairs={{0,4},{4,0},{8,12},{12,8},{1,5},{5,1},{9,13},{13,9},{2,6},{6,2},{1... | collective-permute-start | bytes 294920 | tf_op jit(solution)/shard_map/ppermute | solution.py:38
  72.3 9.0 %collective-permute-start.10 = (bf16[1,2,4,128,128]{4,3,2,1,0:T(8,128)(2,1)S(1)}, bf16[1,2,4,128,128]{4,3,2,1,0:T(8,128)(2,1)S(1)}, u32[]{:S(2)}, u32[]{:S(2)}) collective-permute-start(bf16[1,2,4,128,128]{4,3,2,1,0:T(8,128)(2,1)S(1)} %get-tuple-element.70), channel_id=1, source_target_pairs={{0,1},{1,0},{2,3},{3,2},{4,5},{5,4},{6,7},{7,6},{8,9},{9,8},{10,11... | collective-permute-start | bytes 786440 | tf_op jit(solution)/shard_map/ppermute | solution.py:38
  74.8 8.4 %collective-permute-start.20 = (bf16[1,2,4,128,128]{4,3,2,1,0:T(8,128)(2,1)}, bf16[1,2,4,128,128]{4,3,2,1,0:T(8,128)(2,1)}, u32[]{:S(2)}, u32[]{:S(2)}) collective-permute-start(bf16[1,2,4,128,128]{4,3,2,1,0:T(8,128)(2,1)} %add_convert_fusion.2), channel_id=1, source_target_pairs={{0,2},{1,3},{2,0},{3,1},{4,6},{5,7},{6,4},{7,5},{8,10},{9,11},{10,... | collective-permute-start | bytes 786440 | tf_op jit(solution)/shard_map/ppermute | solution.py:38
  75.9 8.6 %collective-permute-start.23 = (bf16[1,2,4,128,128]{4,3,2,1,0:T(8,128)(2,1)S(1)}, bf16[1,2,4,128,128]{4,3,2,1,0:T(8,128)(2,1)}, u32[]{:S(2)}, u32[]{:S(2)}) collective-permute-start(bf16[1,2,4,128,128]{4,3,2,1,0:T(8,128)(2,1)S(1)} %get-tuple-element.84), channel_id=1, source_target_pairs={{0,1},{1,0},{2,3},{3,2},{4,5},{5,4},{6,7},{7,6},{8,9},{9,8},{10,11... | collective-permute-start | bytes 786440 | tf_op jit(solution)/shard_map/ppermute | solution.py:38
  75.9 10.8 %collective-permute-start.22 = (bf16[2,4,128,128]{3,2,1,0:T(8,128)(2,1)S(1)}, bf16[2,4,128,128]{3,2,1,0:T(8,128)(2,1)}, u32[]{:S(2)}, u32[]{:S(2)}) collective-permute-start(bf16[2,4,128,128]{3,2,1,0:T(8,128)(2,1)S(1)} %fusion.1), channel_id=1, source_target_pairs={{0,4},{4,8},{8,12},{12,0},{1,5},{5,9},{9,13},{13,1},{2,6},{6,10},{... | collective-permute-start | bytes 786440 | tf_op jit(solution)/shard_map/ppermute | solution.py:33
  77.7 10.5 %collective-permute-start.9 = (bf16[1,2,4,128,128]{4,3,2,1,0:T(8,128)(2,1)S(1)}, bf16[1,2,4,128,128]{4,3,2,1,0:T(8,128)(2,1)S(1)}, u32[]{:S(2)}, u32[]{:S(2)}) collective-permute-start(bf16[1,2,4,128,128]{4,3,2,1,0:T(8,128)(2,1)S(1)} %get-tuple-element.68), channel_id=1, source_target_pairs={{0,1},{1,0},{2,3},{3,2},{4,5},{5,4},{6,7},{7,6},{8,9},{9,8},{10,11... | collective-permute-start | bytes 786440 | tf_op jit(solution)/shard_map/ppermute | solution.py:38
  77.7 22.7 %all-to-all-start = ((bf16[4,192,256]{2,1,0:T(8,128)(2,1)}), bf16[4,192,256]{2,1,0:T(8,128)(2,1)S(1)}, u32[]{:S(2)}, u32[]{:S(2)}) async-start(bf16[4,192,256]{2,1,0:T(8,128)(2,1)} %add_up.1), calls=%async_computation | async-start | bytes 786432 | tf_op jit(solution)/shard_map/all_to_all | solution.py:640
  83.3 7.3 %collective-permute-start.21 = (bf16[1,2,4,128,128]{4,3,2,1,0:T(8,128)(2,1)S(1)}, bf16[1,2,4,128,128]{4,3,2,1,0:T(8,128)(2,1)S(1)}, u32[]{:S(2)}, u32[]{:S(2)}) collective-permute-start(bf16[1,2,4,128,128]{4,3,2,1,0:T(8,128)(2,1)S(1)} %add_convert_fusion.1), channel_id=1, source_target_pairs={{0,2},{1,3},{2,0},{3,1},{4,6},{5,7},{6,4},{7,5},{8,10},{9,11},{10,... | collective-permute-start | bytes 786440 | tf_op jit(solution)/shard_map/ppermute | solution.py:38
  88.0 10.5 %collective-permute-start.24 = (bf16[2,4,128,128]{3,2,1,0:T(8,128)(2,1)S(1)}, bf16[2,4,128,128]{3,2,1,0:T(8,128)(2,1)S(1)}, u32[]{:S(2)}, u32[]{:S(2)}) collective-permute-start(bf16[2,4,128,128]{3,2,1,0:T(8,128)(2,1)S(1)} %fusion), channel_id=1, source_target_pairs={{0,4},{4,8},{8,12},{12,0},{1,5},{5,9},{9,13},{13,1},{2,6},{6,10},{... | collective-permute-start | bytes 786440 | tf_op jit(solution)/shard_map/ppermute | solution.py:33
  (9 other events, 105.8 us)
